TPU v7x, 32 devices: a whole 2x2x4 slice. The times are simulated.
32 devices in a mesh: dp: 8 (over y, x, core), tensor: 4 (over z).
Axes of the slice: x: 2, y: 2, z: 4, core: 2. Of those that a mesh axis runs over, the one named last changes fastest.
Arguments:
- layer_in: bfloat16 [8192, 2048], P(('dp', 'tensor')), may hold values from -6 to 6
- cotangent: bfloat16 [8192, 2048], P(('dp', 'tensor')), may hold values from -6 to 6
- doc_ids: int32 [8192], P('dp'), may hold values from 0 to 3, as said below
- positions: int32 [8192], P('dp'), may hold values from 0 to 511, as said below
- attn_gain: float32 [2048], replicated, may hold values from 0.5 to 1.5
- w_query: bfloat16 [2048, 2048], P(None, 'tensor'), may hold values from -0.125 to 0.125
- w_key: bfloat16 [2048, 2048], P(None, 'tensor'), may hold values from -0.125 to 0.125
- w_value: bfloat16 [2048, 2048], P(None, 'tensor'), may hold values from -0.125 to 0.125
- w_out: bfloat16 [2048, 2048], P('tensor'), may hold values from -3 to 3
- ffn_gain: float32 [2048], replicated, may hold values from 0.5 to 1.5
- w_gate: bfloat16 [2048, 8192], P(None, 'tensor'), may hold values from -0.125 to 0.125
- w_up: bfloat16 [2048, 8192], P(None, 'tensor'), may hold values from -0.125 to 0.125
- w_down: bfloat16 [8192, 2048], P('tensor'), may hold values from -0.0625 to 0.0625
Outputs:
- layer_out: bfloat16 [8192, 2048], P(('dp', 'tensor'))
- in_grad: bfloat16 [8192, 2048], P(('dp', 'tensor'))
- attn_gain_grad: float32 [2048], replicated
- query_grad: float32 [2048, 2048], P(None, 'tensor')
- key_grad: float32 [2048, 2048], P(None, 'tensor')
- value_grad: float32 [2048, 2048], P(None, 'tensor')
- out_grad: float32 [2048, 2048], P('tensor')
- ffn_gain_grad: float32 [2048], replicated
- gate_grad: float32 [2048, 8192], P(None, 'tensor')
- up_grad: float32 [2048, 8192], P(None, 'tensor')
- down_grad: float32 [8192, 2048], P('tensor')
Inputs may be any that keep to these rules, and one draw needn't show every extreme that they name: `doc_ids`: within each sequence of 1024 tokens the ids never fall, start at 0 and end at 3: 4 contiguous documents of ragged lengths, one of which holds exactly 512 tokens. `positions`: each token's offset from the first token of its document.
All inputs are finite; a program needn't handle non-finite values.
Results may differ from a plain program's by a relative error of at most 0.018.
Values may be sent and summed in bfloat16 or wider, within the bound.
No kernel may reach another device: no remote copies, remote signals or barrier semaphores. Data moves between devices by JAX's collectives and lax.ppermute only.
A program may use at most 320 MiB of HBM per device.

v0:
```python
import math

import jax
import jax.numpy as jnp
from jax import lax
from jax.sharding import PartitionSpec as P

HD = 128


EPS = 1e-05
ROPE_BASE = 500000.0


def rms_scale(values, gain):
    return values * lax.rsqrt(jnp.mean(values * values, axis=-1, keepdims=True) + EPS) * gain


def rope_turn(values, positions):
    half = HD // 2
    freqs = ROPE_BASE ** (-(jnp.arange(half).astype(jnp.float32) * 2.0) / HD)
    angles = positions.astype(jnp.float32)[:, None] * freqs[None, :]
    cosine = jnp.cos(angles)[:, None, :]
    sine = jnp.sin(angles)[:, None, :]
    heads = values.reshape(values.shape[0], -1, HD)
    lower = heads[..., :half]
    upper = heads[..., half:]
    turned = jnp.concatenate(
        [lower * cosine - upper * sine, upper * cosine + lower * sine], axis=-1
    )
    return turned.reshape(values.shape)


def contract_rows(left, right):
    return lax.dot_general(
        left, right, (((0,), (0,)), ((), ())), preferred_element_type=jnp.float32
    )


def contract_cols(left, right):
    return lax.dot_general(
        left, right, (((1,), (1,)), ((), ())), preferred_element_type=jnp.float32
    )


def block_scores(query_b, key_heads, doc_ids, start, block_rows):
    seq_len = doc_ids.shape[0]
    query_blk = lax.slice_in_dim(query_b, start, start + block_rows, axis=0).reshape(
        block_rows, -1, HD
    )
    scores = jnp.einsum(
        "qhd,khd->hqk", query_blk, key_heads, preferred_element_type=jnp.float32
    ) * (1.0 / math.sqrt(HD)) - math.log(seq_len)
    row_place = start + jnp.arange(block_rows)
    col_place = jnp.arange(seq_len)
    doc_blk = lax.slice_in_dim(doc_ids, start, start + block_rows, axis=0)
    allowed = (doc_blk[:, None] == doc_ids[None, :]) & (row_place[:, None] >= col_place[None, :])
    return (query_blk, jax.nn.sigmoid(scores), allowed[None])


def local(
    layer_in,
    cotangent,
    doc_ids,
    positions,
    attn_gain,
    w_query,
    w_key,
    w_value,
    w_out,
    ffn_gain,
    w_gate,
    w_up,
    w_down,
):
    seq_len = doc_ids.shape[0]
    local_width = w_query.shape[1]
    block_rows = min(512, seq_len)
    scale = 1.0 / math.sqrt(HD)
    own_in = layer_in.astype(jnp.float32)
    normed = lax.all_gather(
        rms_scale(own_in, attn_gain).astype(jnp.bfloat16), "tensor", axis=0, tiled=True
    )
    query_pre = jnp.dot(normed, w_query, preferred_element_type=jnp.float32)
    key_pre = jnp.dot(normed, w_key, preferred_element_type=jnp.float32)
    value_b = jnp.dot(normed, w_value, preferred_element_type=jnp.float32).astype(jnp.bfloat16)
    query_b = rope_turn(query_pre, positions).astype(jnp.bfloat16)
    key_b = rope_turn(key_pre, positions).astype(jnp.bfloat16)
    key_heads = key_b.reshape(seq_len, -1, HD)
    value_heads = value_b.reshape(seq_len, -1, HD)
    mixed_blocks = []
    for start in range(0, seq_len, block_rows):
        query_blk, sigmas, allowed = block_scores(query_b, key_heads, doc_ids, start, block_rows)
        probs_b = jnp.where(allowed, sigmas, 0.0).astype(jnp.bfloat16)
        mixed_blk = jnp.einsum(
            "hqk,khd->qhd", probs_b, value_heads, preferred_element_type=jnp.float32
        )
        mixed_blocks.append(mixed_blk.reshape(block_rows, local_width).astype(jnp.bfloat16))
    mixed_b = jnp.concatenate(mixed_blocks, axis=0)
    resid = own_in + lax.psum_scatter(
        jnp.dot(mixed_b, w_out, preferred_element_type=jnp.float32),
        "tensor",
        scatter_dimension=0,
        tiled=True,
    )
    normed2 = lax.all_gather(
        rms_scale(resid, ffn_gain).astype(jnp.bfloat16), "tensor", axis=0, tiled=True
    )
    gate = jnp.dot(normed2, w_gate, preferred_element_type=jnp.float32)
    up_proj = jnp.dot(normed2, w_up, preferred_element_type=jnp.float32)
    inner_b = (jax.nn.silu(gate) * up_proj).astype(jnp.bfloat16)
    layer_out = (
        resid
        + lax.psum_scatter(
            jnp.dot(inner_b, w_down, preferred_element_type=jnp.float32).astype(jnp.bfloat16),
            "tensor",
            scatter_dimension=0,
            tiled=True,
        ).astype(jnp.float32)
    ).astype(jnp.bfloat16)
    cot_all = lax.all_gather(cotangent, "tensor", axis=0, tiled=True)
    down_grad = contract_rows(inner_b, cot_all)
    d_inner = contract_cols(cot_all, w_down)
    silu_out, silu_pull = jax.vjp(lambda gate_v, up_v: jax.nn.silu(gate_v) * up_v, gate, up_proj)
    d_gate_f, d_up_f = silu_pull(d_inner)
    d_gate = d_gate_f.astype(jnp.bfloat16)
    d_up = d_up_f.astype(jnp.bfloat16)
    gate_grad = contract_rows(normed2, d_gate)
    up_grad = contract_rows(normed2, d_up)
    gate_part = contract_cols(d_gate, w_gate)
    d_normed2 = lax.psum_scatter(
        gate_part + contract_cols(d_up, w_up), "tensor", scatter_dimension=0, tiled=True
    )
    norm_out, norm_pull = jax.vjp(rms_scale, resid, ffn_gain)
    d_resid_part, ffn_gain_part = norm_pull(d_normed2)
    d_resid = cotangent.astype(jnp.float32) + d_resid_part
    resid_all = lax.all_gather(d_resid.astype(jnp.bfloat16), "tensor", axis=0, tiled=True)
    out_grad = contract_rows(mixed_b, resid_all)
    d_mix = contract_cols(resid_all, w_out).astype(jnp.bfloat16)
    d_key = jnp.zeros((seq_len, local_width // HD, HD), jnp.float32)
    d_value = jnp.zeros((seq_len, local_width // HD, HD), jnp.float32)
    query_blocks = []
    for start in range(0, seq_len, block_rows):
        query_blk, sigmas, allowed = block_scores(query_b, key_heads, doc_ids, start, block_rows)
        probs_b = jnp.where(allowed, sigmas, 0.0).astype(jnp.bfloat16)
        d_mix_blk = lax.slice_in_dim(d_mix, start, start + block_rows, axis=0).reshape(
            block_rows, -1, HD
        )
        d_probs = jnp.einsum(
            "qhd,khd->hqk", d_mix_blk, value_heads, preferred_element_type=jnp.float32
        )
        d_scores = jnp.where(allowed, d_probs * sigmas * (1.0 - sigmas), 0.0).astype(jnp.bfloat16)
        d_value = d_value + jnp.einsum(
            "hqk,qhd->khd", probs_b, d_mix_blk, preferred_element_type=jnp.float32
        )
        query_part = (
            jnp.einsum("hqk,khd->qhd", d_scores, key_heads, preferred_element_type=jnp.float32)
            * scale
        )
        query_blocks.append(query_part.reshape(block_rows, local_width))
        d_key = (
            d_key
            + jnp.einsum("hqk,qhd->khd", d_scores, query_blk, preferred_element_type=jnp.float32)
            * scale
        )
    d_query = jnp.concatenate(query_blocks, axis=0)
    turned, rope_pull = jax.vjp(lambda values: rope_turn(values, positions), query_pre)
    d_query_pre = rope_pull(d_query)[0].astype(jnp.bfloat16)
    d_key_pre = rope_pull(d_key.reshape(seq_len, local_width))[0].astype(jnp.bfloat16)
    d_value_b = d_value.reshape(seq_len, local_width).astype(jnp.bfloat16)
    query_grad = contract_rows(normed, d_query_pre)
    key_grad = contract_rows(normed, d_key_pre)
    value_grad = contract_rows(normed, d_value_b)
    total = contract_cols(d_query_pre, w_query)
    total = total + contract_cols(d_key_pre, w_key)
    d_normed = lax.psum_scatter(
        total + contract_cols(d_value_b, w_value), "tensor", scatter_dimension=0, tiled=True
    )
    norm_first, first_pull = jax.vjp(rms_scale, own_in, attn_gain)
    d_in_part, attn_gain_part = first_pull(d_normed)
    in_grad = (d_resid + d_in_part).astype(jnp.bfloat16)
    attn_gain_grad, ffn_gain_grad = lax.psum((attn_gain_part, ffn_gain_part), ("dp", "tensor"))
    query_grad, key_grad, value_grad, out_grad, gate_grad, up_grad, down_grad = (
        lax.psum(query_grad.astype(jnp.bfloat16), "dp").astype(jnp.float32),
        lax.psum(key_grad.astype(jnp.bfloat16), "dp").astype(jnp.float32),
        lax.psum(value_grad.astype(jnp.bfloat16), "dp").astype(jnp.float32),
        lax.psum(out_grad.astype(jnp.bfloat16), "dp").astype(jnp.float32),
        lax.psum(gate_grad.astype(jnp.bfloat16), "dp").astype(jnp.float32),
        lax.psum(up_grad.astype(jnp.bfloat16), "dp").astype(jnp.float32),
        lax.psum(down_grad.astype(jnp.bfloat16), "dp").astype(jnp.float32),
    )
    return (
        layer_out,
        in_grad,
        attn_gain_grad,
        query_grad,
        key_grad,
        value_grad,
        out_grad,
        ffn_gain_grad,
        gate_grad,
        up_grad,
        down_grad,
    )


def solution(mesh):
    placed = (
        P(("dp", "tensor"), None),
        P(("dp", "tensor"), None),
        P("dp"),
        P("dp"),
        P(),
        P(None, "tensor"),
        P(None, "tensor"),
        P(None, "tensor"),
        P("tensor", None),
        P(),
        P(None, "tensor"),
        P(None, "tensor"),
        P("tensor", None),
    )
    return jax.shard_map(
        local,
        mesh=mesh,
        in_specs=placed,
        out_specs=(
            P(("dp", "tensor"), None),
            P(("dp", "tensor"), None),
            P(),
            P(None, "tensor"),
            P(None, "tensor"),
            P(None, "tensor"),
            P("tensor", None),
            P(),
            P(None, "tensor"),
            P(None, "tensor"),
            P("tensor", None),
        ),
        check_vma=False,
    )
```

profile of v0, /device:TPU:0, one launch (start us, length us, event | category | flops | bytes accessed | tf_op | source)
XLA Modules:
  0.0 1437.6 jit_solution(10712023922354823133)
XLA Ops:
  16.9 79.2 %all-gather.5.cloned.1.call-done = bf16[1024,2048]{1,0:T(8,128)(2,1)} async-done(((bf16[256,2048]{1,0:T(8,128)(2,1)}), bf16[1024,2048]{1,0:T(8,128)(2,1)}) %all-gather.5.cloned.1.call-update) | async-done | bytes 4194320 | tf_op jit(solution)/shard_map/all_gather | solution.py:81
  150.1 143.1 %reduce-scatter.5.cloned.1.call-done = f32[256,2048]{1,0:T(8,128)} async-done(((f32[1024,2048]{1,0:T(8,128)}), f32[256,2048]{1,0:T(8,128)}) %reduce-scatter.5.cloned.1.call-update) | async-done | bytes 2097168 | tf_op jit(solution)/shard_map/reduce_scatter | solution.py:100
  298.3 81.0 %all-gather.7.cloned.1.call-done = bf16[1024,2048]{1,0:T(8,128)(2,1)} async-done(((bf16[256,2048]{1,0:T(8,128)(2,1)}), bf16[1024,2048]{1,0:T(8,128)(2,1)}) %all-gather.7.cloned.1.call-update) | async-done | bytes 4194320 | tf_op jit(solution)/shard_map/all_gather | solution.py:106
  379.3 15.9 %fusion.43 = f32[1024,2048]{1,0:T(8,128)} fusion(bf16[1024,2048]{1,0:T(8,128)(2,1)} %all-gather.7.cloned.1.call-done, bf16[2048,2048]{1,0:T(8,128)(2,1)} %param.24), kind=kOutput, calls=%fused_computation.106 | convolution fusion | flops 8589934592 | bytes 20971520 | tf_op jit(solution)/shard_map/dot_general | solution.py:110
  395.2 13.2 fusion.42
  408.5 51.6 %all-gather.9.cloned.1.call-done = bf16[1024,2048]{1,0:T(8,128)(2,1)} async-done(((bf16[256,2048]{1,0:T(8,128)(2,1)}), bf16[1024,2048]{1,0:T(8,128)(2,1)}) %all-gather.9.cloned.1.call-update) | async-done | bytes 4194320 | tf_op jit(solution)/shard_map/all_gather | solution.py:121
  460.1 21.7 %multiply_convert_fusion = (bf16[1024,2048]{1,0:T(8,128)(2,1)}, bf16[1024,2048]{1,0:T(8,128)(2,1)}, bf16[1024,2048]{1,0:T(8,128)(2,1)}) fusion(f32[1024,2048]{1,0:T(8,128)} %fusion.42, f32[1024,2048]{1,0:T(8,128)} %fusion.43, bf16[1024,2048]{1,0:T(8,128)(2,1)} %all-gather.9.cloned.1.call-done, bf16[2048,2048]{1,0:T(8,128)(2,1)} %param.25), kind=kOutput, calls=%fused_computation.7 | convolution fusion | flops 8623489024 | bytes 41943040 | tf_op jit(solution)/shard_map/dot_general | solution.py:41
  481.8 12.9 fusion.44
  494.7 13.5 convolution_add_fusion
  508.3 143.1 %reduce-scatter.9.cloned.1.call-done = f32[256,2048]{1,0:T(8,128)} async-done(((f32[1024,2048]{1,0:T(8,128)}), f32[256,2048]{1,0:T(8,128)}) %reduce-scatter.9.cloned.1.call-update) | async-done | bytes 2097168 | tf_op jit(solution)/shard_map/reduce_scatter | solution.py:131
  657.3 14.7 %convolution_convert_fusion.1 = bf16[2048,2048]{1,0:T(8,128)(2,1)} fusion(bf16[1024,2048]{1,0:T(8,128)(2,1)} %all-gather.7.cloned.1.call-done, bf16[1024,2048]{1,0:T(8,128)(2,1)} %get-tuple-element.26), kind=kOutput, calls=%fused_computation.16 | convolution fusion | flops 8594128896 | bytes 16777216 | tf_op jit(solution)/shard_map/dot_general | solution.py:35
  672.0 11.4 convolution_convert_fusion.2
  683.4 11.8 convolution_convert_fusion
  695.2 43.7 %all-gather.11.cloned.1.call-done = bf16[1024,2048]{1,0:T(8,128)(2,1)} async-done(((bf16[256,2048]{1,0:T(8,128)(2,1)}), bf16[1024,2048]{1,0:T(8,128)(2,1)}) %all-gather.11.cloned.1.call-update) | async-done | bytes 4194320 | tf_op jit(solution)/shard_map/all_gather | solution.py:137
  776.6 6.3 convolution_convert_fusion.4
  807.6 14.0 convolution_convert_fusion.3
  821.7 375.1 %all-reduce.8.cloned.1.call-done = (bf16[2048,512]{1,0:T(8,128)(2,1)}, bf16[2048,512]{1,0:T(8,128)(2,1)}, bf16[2048,512]{1,0:T(8,128)(2,1)}, bf16[512,2048]{1,0:...) async-done(((bf16[2048,512]{1,0:T(8,128)(2,1)}, bf16[2048,512]{1,0:T(8,128)(2,1)}, bf16[2048,512]{1,0:T(8,128)(2,1)}, ...) | async-done | bytes 33554448 | tf_op jit(solution)/shard_map/psum | solution.py:184
  1209.0 11.7 convert_element_type.197
  1220.6 11.7 convert_element_type.199
  1232.4 11.8 convert_element_type.201
  1244.2 99.5 %reduce-scatter.11.cloned.1.call-done = f32[256,2048]{1,0:T(8,128)} async-done(((f32[1024,2048]{1,0:T(8,128)}), f32[256,2048]{1,0:T(8,128)}) %reduce-scatter.11.cloned.1.call-update) | async-done | bytes 2097168 | tf_op jit(solution)/shard_map/reduce_scatter | solution.py:176
  1346.0 43.2 %all-reduce.4 = (f32[2048]{0:T(1024)}, f32[2048]{0:T(1024)}) all-reduce(f32[2048]{0:T(1024)S(1)} %get-tuple-element.13, f32[2048]{0:T(1024)S(1)} %copy-done.38), channel_id=1, replica_groups=mesh['dp'=8,'tensor'=4] {'dp','tensor'}, use_global_device_ids=true, to_apply=%region_9.10 | all-reduce | flops 4096 | bytes 32768 | tf_op jit(solution)/shard_map/psum | solution.py:182
  1389.2 35.5 %reduce-scatter.7.cloned.1.call-done = bf16[256,2048]{1,0:T(8,128)(2,1)} async-done(((bf16[1024,2048]{1,0:T(8,128)(2,1)}), bf16[256,2048]{1,0:T(8,128)(2,1)}) %reduce-scatter.7.cloned.1.call-update) | async-done | bytes 1048592 | tf_op jit(solution)/shard_map/reduce_scatter | solution.py:114
  1424.7 5.8 fusion.10
  (197 shorter events, 151.0 us)
Async XLA Ops:
  7.2 137.0 %copy-start = (bf16[512,2048]{1,0:T(8,128)(2,1)S(1)}, bf16[512,2048]{1,0:T(8,128)(2,1)}, u32[]{:S(2)}) copy-start(bf16[512,2048]{1,0:T(8,128)(2,1)} %param.21) | copy-start | bytes 6291460
  7.2 88.9 %all-gather.5.cloned.1.call-start = ((), (), s32[]{:S(2)}) async-start(), calls=%async_computation.4 | async-start | bytes 5242880 | tf_op jit(solution)/shard_map/all_gather | solution.py:81
  12.5 280.6 %reduce-scatter.5.cloned.1.call-start = ((), (), s32[]{:S(2)}) async-start(), calls=%async_computation.5 | async-start | bytes 10485760 | tf_op jit(solution)/shard_map/reduce_scatter | solution.py:100
  16.9 122.5 %copy-start.15 = (pred[512,1024]{1,0:T(8,128)(4,1)}, pred[512,1024]{1,0:T(8,128)(4,1)S(1)}, u32[]{:S(2)}) copy-start(pred[512,1024]{1,0:T(8,128)(4,1)S(1)} %get-tuple-element.52) | copy-start | bytes 1572868
  16.9 124.9 %copy-start.17 = (pred[512,1024]{1,0:T(8,128)(4,1)}, pred[512,1024]{1,0:T(8,128)(4,1)S(1)}, u32[]{:S(2)}) copy-start(pred[512,1024]{1,0:T(8,128)(4,1)S(1)} %get-tuple-element.51) | copy-start | bytes 1572868
  150.0 143.2 %copy-start.5 = (bf16[256,2048]{1,0:T(8,128)(2,1)S(1)}, bf16[256,2048]{1,0:T(8,128)(2,1)}, u32[]{:S(2)}) copy-start(bf16[256,2048]{1,0:T(8,128)(2,1)} %param.13) | copy-start | bytes 3145732
  150.0 146.4 %copy-start.35 = (f32[2048]{0:T(1024)S(1)}, f32[2048]{0:T(1024)}, u32[]{:S(2)}) copy-start(f32[2048]{0:T(1024)} %param.22) | copy-start | bytes 24580
  150.0 229.3 %all-gather.7.cloned.1.call-start = ((), (), s32[]{:S(2)}) async-start(), calls=%async_computation.6 | async-start | bytes 5242880 | tf_op jit(solution)/shard_map/all_gather | solution.py:106
  295.1 359.8 %copy-start.39 = (f32[256]{0:T(256)}, f32[256]{0:T(256)S(1)}, u32[]{:S(2)}) copy-start(f32[256]{0:T(256)S(1)} %fusion.25) | copy-start | bytes 3076
  297.7 162.4 %all-gather.9.cloned.1.call-start = ((), (), s32[]{:S(2)}) async-start(), calls=%async_computation.8 | async-start | bytes 5242880 | tf_op jit(solution)/shard_map/all_gather | solution.py:121
  298.3 353.2 %reduce-scatter.9.cloned.1.call-start = ((), (), s32[]{:S(2)}) async-start(), calls=%async_computation.9 | async-start | bytes 10485760 | tf_op jit(solution)/shard_map/reduce_scatter | solution.py:131
  508.2 147.3 %copy-start.10 = (bf16[256,2048]{1,0:T(8,128)(2,1)S(1)}, bf16[256,2048]{1,0:T(8,128)(2,1)}, u32[]{:S(2)}) copy-start(bf16[256,2048]{1,0:T(8,128)(2,1)} %param.14) | copy-start | bytes 3145732
  508.2 230.7 %all-gather.11.cloned.1.call-start = ((), (), s32[]{:S(2)}) async-start(), calls=%async_computation.10 | async-start | bytes 5242880 | tf_op jit(solution)/shard_map/all_gather | solution.py:137
  657.3 539.5 %all-reduce.8.cloned.1.call-start = ((), (), s32[]{:S(2)}) async-start(), calls=%async_computation.12 | async-start | bytes 67108864 | tf_op jit(solution)/shard_map/psum | solution.py:184
  794.4 549.4 %reduce-scatter.11.cloned.1.call-start = ((), (), s32[]{:S(2)}) async-start(), calls=%async_computation.11 | async-start | bytes 10485760 | tf_op jit(solution)/shard_map/reduce_scatter | solution.py:176
  807.3 617.4 %reduce-scatter.7.cloned.1.call-start = ((), (), s32[]{:S(2)}) async-start(), calls=%async_computation.7 | async-start | bytes 5242880 | tf_op jit(solution)/shard_map/reduce_scatter | solution.py:114
  1232.3 111.4 %copy-start.6 = (bf16[256,2048]{1,0:T(8,128)(2,1)S(1)}, bf16[256,2048]{1,0:T(8,128)(2,1)}, u32[]{:S(2)}) copy-start(bf16[256,2048]{1,0:T(8,128)(2,1)} %param.13) | copy-start | bytes 3145732
  1232.3 111.4 %copy-start.37 = (f32[2048]{0:T(1024)S(1)}, f32[2048]{0:T(1024)}, u32[]{:S(2)}) copy-start(f32[2048]{0:T(1024)} %param.17) | copy-start | bytes 24580
  1232.3 111.4 %copy-start.43 = (f32[256]{0:T(256)S(1)}, f32[256]{0:T(256)}, u32[]{:S(2)}) copy-start(f32[256]{0:T(256)} %copy-done.42) | copy-start | bytes 3076
  1232.3 113.7 %copy-start.38 = (f32[2048]{0:T(1024)S(1)}, f32[2048]{0:T(1024)}, u32[]{:S(2)}) copy-start(f32[2048]{0:T(1024)} %get-tuple-element.11) | copy-start | bytes 24580
  1232.3 156.9 %copy-start.45 = (f32[256]{0:T(256)S(1)}, f32[256]{0:T(256)}, u32[]{:S(2)}) copy-start(f32[256]{0:T(256)} %copy-done.44) | copy-start | bytes 3076
  1232.3 192.4 %copy-start.36 = (f32[2048]{0:T(1024)S(1)}, f32[2048]{0:T(1024)}, u32[]{:S(2)}) copy-start(f32[2048]{0:T(1024)} %param.22) | copy-start | bytes 24580
  1232.4 192.4 %copy-start.40 = (f32[256]{0:T(256)S(1)}, f32[256]{0:T(256)}, u32[]{:S(2)}) copy-start(f32[256]{0:T(256)} %copy-done.39) | copy-start | bytes 3076
  1232.4 192.4 %copy-start.47 = (f32[256]{0:T(256)S(1)}, f32[256]{0:T(256)}, u32[]{:S(2)}) copy-start(f32[256]{0:T(256)} %copy-done.46) | copy-start | bytes 3076
  (45 other events, 257.7 us)
Sparse Core Ops, SparseCore 0:
  12.6 83.4 all-gather.4
  150.1 143.0 reduce-scatter.4
  297.8 81.4 all-gather.6
  380.7 79.2 all-gather.8
  508.4 143.0 reduce-scatter.8
  657.4 81.4 all-gather.10
  794.5 402.2 all-reduce.7
  1199.2 144.4 reduce-scatter.10
  1346.1 78.5 reduce-scatter.6
where the time goes:
time: 1450 us; the launch traced here: 1440 us
  waiting for transfers between devices  1050 us (72%)
  matrix products  211 us (15%)
  other arithmetic  86.9 us (6%)
  blocking collectives  43.2 us (3%)
  local copies, waits for them, and re-layouts  28.3 us (2%)
  between operations  15.1 us (1%)
    psum x1, waiting for transfers between devices, local(): lax.psum(query_grad.astype(jnp.bfloat16), 'dp').astype(jnp.float32)  375 us
    reduce_scatter x1, waiting for transfers between devices, local(): lax.psum_scatter(gate_part + contract_cols(d_up, w_up), 'tensor', scatter...  143 us
    reduce_scatter x1, waiting for transfers between devices, local(): lax.psum_scatter(jnp.dot(mixed_b, w_out, preferred_element_type=jnp.float...  143 us
    reduce_scatter x1, waiting for transfers between devices, local(): lax.psum_scatter(total + contract_cols(d_value_b, w_value), 'tensor', sca...  99.5 us
    all_gather x1, waiting for transfers between devices, local(): lax.all_gather(rms_scale(resid, ffn_gain).astype(jnp.bfloat16), 'tensor',...  81 us
    all_gather x1, waiting for transfers between devices, local(): lax.all_gather(rms_scale(own_in, attn_gain).astype(jnp.bfloat16), 'tensor...  79.2 us
    dot_general x7, matrix products, contract_cols(): lax.dot_general(left, right, (((1,), (1,)), ((), ())), preferred_element_...  65.3 us
    dot_general x7, matrix products, contract_rows(): lax.dot_general(left, right, (((0,), (0,)), ((), ())), preferred_element_...  55.6 us
  transfers between devices with their start and end apart: 9, of which 9 were waited for; matrix products, arithmetic and copies ran while one was open for 10% of the time, Pallas kernels for 0%

commit v1 on v0

v1 whole, which is shorter than its diff:
```python
import functools
import math

import jax
import jax.numpy as jnp
from jax import lax
from jax.experimental import pallas as pl
from jax.experimental.pallas import tpu as pltpu
from jax.sharding import PartitionSpec as P

HD = 128
EPS = 1e-05
ROPE_BASE = 500000.0
BF = jnp.bfloat16
F32 = jnp.float32
MIB = 1 << 20


def dot(left, right):
    return lax.dot_general(left, right, (((1,), (0,)), ((), ())), preferred_element_type=F32)


def dot_nt(left, right):
    return lax.dot_general(left, right, (((1,), (1,)), ((), ())), preferred_element_type=F32)


def dot_tn(left, right):
    return lax.dot_general(left, right, (((0,), (0,)), ((), ())), preferred_element_type=F32)


def sigmoid(v):
    return 1.0 / (1.0 + jnp.exp(-v))


def rms_scale(values, gain):
    return values * lax.rsqrt(jnp.mean(values * values, axis=-1, keepdims=True) + EPS) * gain


def call(body, *, name, grid, scalars, in_specs, out_specs, out_shape, scratch=(), aliases=None,
         flops=0, nbytes=0, trans=0, vmem=40):
    return pl.pallas_call(
        body,
        grid_spec=pltpu.PrefetchScalarGridSpec(
            num_scalar_prefetch=scalars,
            grid=grid,
            in_specs=in_specs,
            out_specs=out_specs,
            scratch_shapes=list(scratch),
        ),
        out_shape=out_shape,
        input_output_aliases=aliases or {},
        compiler_params=pltpu.CompilerParams(vmem_limit_bytes=vmem * MIB),
        cost_estimate=pl.CostEstimate(flops=flops, bytes_accessed=nbytes, transcendentals=trans),
        name=name,
    )


ANY = pl.BlockSpec(memory_space=pl.ANY)


def xor_pairs(size, mask):
    return [(i, i ^ mask) for i in range(size)]


def tie_body(*refs):
    pass


def tie(values, others):
    return call(
        tie_body,
        name="tie",
        grid=(1,),
        scalars=0,
        in_specs=[ANY] * (len(values) + len(others)),
        out_specs=[ANY] * len(values),
        out_shape=[jax.ShapeDtypeStruct(v.shape, v.dtype) for v in values],
        aliases={i: i for i in range(len(values))},
        vmem=1,
    )(*values, *others)


def after(value, *others):
    return tie([value], others)[0]


class LineGather:
    def __init__(self, own, size, place):
        self.size, self.place = size, place
        self.ups, self.downs = [own], [own]

    def step(self, *others):
        k, size = len(self.ups), self.size
        if others:
            self.ups[-1], self.downs[-1] = tie([self.ups[-1], self.downs[-1]], others)
        up, down = self.ups[-1], self.downs[-1]
        self.ups.append(lax.ppermute(up, "tensor", [(i, i + 1) for i in range(k - 1, size - 1)]))
        self.downs.append(lax.ppermute(down, "tensor", [(i + 1, i) for i in range(0, size - k)]))

    def slot(self, j):
        groups = {}
        for at in range(self.size):
            groups.setdefault((at ^ j) - at, []).append(at)
        value = None
        for off, places in groups.items():
            arr = self.downs[off] if off >= 0 else self.ups[-off]
            if value is None:
                value = arr
            else:
                here = functools.reduce(jnp.logical_or, [self.place == at for at in places])
                value = jnp.where(here, arr, value)
        return value


def exchange(pieces, size):
    return [pieces[0]] + [
        lax.ppermute(pieces[j], "tensor", xor_pairs(size, j)) for j in range(1, size)
    ]


def rows_at(values, block, rows):
    return lax.dynamic_slice_in_dim(values, block * rows, rows, axis=0)


def cols_at(values, block, cols):
    return lax.dynamic_slice_in_dim(values, block * cols, cols, axis=1)


def join_body(places, *refs):
    pieces, out = refs[:-1], refs[-1]
    step = pl.program_id(0) * pl.num_programs(1) + pl.program_id(1)
    for k, piece in enumerate(pieces):

        @pl.when(step == k)
        def _():
            out[...] = piece[...]


def finish_body(core, mine, other, *outs):
    at = 0
    for source, turn in ((mine, 0), (other, 1)):

        @pl.when(pl.program_id(0) == turn)
        def _():
            at = 0
            for out in outs:
                width = out.shape[1]
                out[...] = source[:, at : at + width].astype(F32)
                at += width


class Reducer:
    def __init__(self, count):
        self.count = count
        self.bits = count.bit_length() - 1
        self.index = lax.axis_index("dp")
        self.core = self.bit(0)

    def bit(self, b):
        return (self.index >> b) & 1

    def split(self, left):
        half = left.shape[1] // 2
        return (cols_at(left, 1 - self.core, half), cols_at(left, self.core, half))

    def swap(self, value, b):
        return lax.ppermute(value, "dp", xor_pairs(self.count, 1 << b))

    def give(self, halves, right):
        return self.swap(dot_tn(halves[0], right).astype(BF), 0)

    def keep(self, halves, right, got):
        return (dot_tn(halves[1], right) + got.astype(F32)).astype(BF)

    def open(self, chip):
        cols = chip.shape[1]
        halves = [lax.slice_in_dim(chip, at * cols // 2, (at + 1) * cols // 2, axis=1) for at in (0, 1)]
        orders = [list(range(1, self.bits)), list(range(self.bits - 1, 0, -1))]
        return [[[half], order, order, jnp.int32(0)] for half, order in zip(halves, orders)]

    def add(self, state):
        out = []
        for (part,), order, left, place in state:
            half, mine = part.shape[0] // 2, self.bit(left[0])
            got = self.swap(rows_at(part, 1 - mine, half), left[0])
            part = (rows_at(part, mine, half).astype(F32) + got.astype(F32)).astype(BF)
            out.append([[part], order, left[1:], place * 2 + mine])
        return out

    def spread(self, state):
        out = []
        for held, order, left, place in state:
            step = order[len(order) - 1 - (len(held).bit_length() - 1)]
            out.append([held + [self.swap(p, step) for p in held], order, left, place])
        return out

    def wait(self, state, *others):
        flat = [p for held, *_ in state for p in held]
        got = list(tie(flat, others))
        return [[[got.pop(0) for _ in held], order, left, place] for held, order, left, place in state]

    def pieces(self, state):
        return [p for held, *_ in state for p in held]

    def close(self, state, widths):
        pieces = self.pieces(state)
        places = [place for *_, place in state]
        brows, bcols = pieces[0].shape
        blocks = len(pieces) // 2
        rows, cols = brows * blocks, bcols * 2
        half = call(
            join_body,
            name="join",
            grid=(2, blocks),
            scalars=1,
            in_specs=[pl.BlockSpec((brows, bcols), lambda h, k, s: (0, 0))] * len(pieces),
            out_specs=pl.BlockSpec((brows, bcols), lambda h, k, s: (k ^ s[h], h)),
            out_shape=jax.ShapeDtypeStruct((rows, cols), BF),
            nbytes=rows * cols * 4,
            vmem=24,
        )(jnp.stack(places), *pieces)
        other = self.swap(half, 0)
        crows = min(256, rows)
        nblk = rows // crows
        return call(
            finish_body,
            name="finish",
            grid=(2, nblk),
            scalars=1,
            in_specs=[
                pl.BlockSpec((crows, cols), lambda g, b, s: (jnp.where(g == 0, b, nblk - 1), 0)),
                pl.BlockSpec((crows, cols), lambda g, b, s: (jnp.where(g == 0, 0, b), 0)),
            ],
            out_specs=[
                pl.BlockSpec((crows, w), lambda g, b, s: ((g ^ s[0]) * nblk + b, 0)) for w in widths
            ],
            out_shape=[jax.ShapeDtypeStruct((2 * rows, w), F32) for w in widths],
            nbytes=rows * cols * 12,
            vmem=24,
        )(self.core.reshape(1), half, other)


def gain_total(part, dp, tensor):
    value = part.reshape(-1, 128)
    for name, size in (("dp", dp), ("tensor", tensor)):
        step = 1
        while step < size:
            value = value + lax.ppermute(value, name, xor_pairs(size, step))
            step *= 2
    return value.reshape(-1)


def qkv_body(*refs):
    chunk, rows, wq, wk, wv, cos, sin = refs[:7]
    q_out, k_out, v_out, rows_out = refs[-4:]
    x = rows[...]
    cosine, sine = cos[...], sin[...]

    def turned(pre):
        out = []
        for h in range(pre.shape[1] // HD):
            one = pre[:, h * HD : (h + 1) * HD]
            out.append(one * cosine + pltpu.roll(one, HD // 2, 1) * sine)
        return jnp.concatenate(out, axis=1)

    q_out[...] = turned(dot(x, wq[...])).astype(BF)
    k_out[...] = turned(dot(x, wk[...])).astype(BF)
    v_out[...] = dot(x, wv[...]).astype(BF)
    rows_out[...] = x


def qkv_slot(chunk, rows, w_query, w_key, w_value, cos, sin, held, count):
    t, d = rows.shape
    width = w_query.shape[1]
    bn = min(256, width)
    wspec = pl.BlockSpec((d, bn), lambda i, s: (0, i))
    tspec = pl.BlockSpec((t, HD), lambda i, s: (s[0], 0))
    return call(
        qkv_body,
        name="qkv",
        grid=(width // bn,),
        scalars=1,
        in_specs=[pl.BlockSpec((t, d), lambda i, s: (0, 0)), wspec, wspec, wspec, tspec, tspec]
        + [ANY] * len(held),
        out_specs=[pl.BlockSpec((t, bn), lambda i, s: (s[0], i))] * 3
        + [pl.BlockSpec((t, d), lambda i, s: (s[0], 0))],
        out_shape=[jax.ShapeDtypeStruct((count * t, width), BF)] * 3
        + [jax.ShapeDtypeStruct((count * t, d), BF)],
        aliases={7 + i: i for i in range(len(held))},
        flops=6 * t * d * width,
        nbytes=2 * (3 * d * width + 2 * t * d + 3 * t * width),
        vmem=32,
    )(chunk, rows, w_query, w_key, w_value, cos, sin, *held)


def attend_consts(seq_len):
    to_log2 = math.log2(math.e)
    return (to_log2 / math.sqrt(HD), math.log2(seq_len))


def attend_body(docs, q_ref, k_ref, v_ref, ids_col, ids_row, mix, acc, *, block):
    seq_len = q_ref.shape[0]
    scale, shift = attend_consts(seq_len)
    causal = lax.broadcasted_iota(jnp.int32, (block, block), 0) >= lax.broadcasted_iota(
        jnp.int32, (block, block), 1
    )

    def term(i, j):
        q = q_ref[i * block : (i + 1) * block, :]
        k = k_ref[j * block : (j + 1) * block, :]
        sig = 1.0 / (1.0 + jnp.exp2(shift - dot_nt(q, k) * scale))
        same = ids_col[i * block : (i + 1) * block, :] == ids_row[:, j * block : (j + 1) * block]
        allowed = same & causal if i == j else same
        probs = jnp.where(allowed, sig, 0.0).astype(BF)
        return dot(probs, v_ref[j * block : (j + 1) * block, :])

    for i in range(seq_len // block):
        acc[...] = term(i, i)
        for j in range(i):

            @pl.when(docs[(j + 1) * block - 1] == docs[i * block])
            def _():
                acc[...] += term(i, j)

        mix[i * block : (i + 1) * block, :] = acc[...].astype(BF)


def attend(docs, q, k, v):
    seq_len, width = q.shape
    block = 256
    head = pl.BlockSpec((seq_len, HD), lambda h, s: (0, h))
    return call(
        functools.partial(attend_body, block=block),
        name="attend",
        grid=(width // HD,),
        scalars=1,
        in_specs=[
            head,
            head,
            head,
            pl.BlockSpec((seq_len, 1), lambda h, s: (0, 0)),
            pl.BlockSpec((1, seq_len), lambda h, s: (0, 0)),
        ],
        out_specs=head,
        out_shape=jax.ShapeDtypeStruct((seq_len, width), BF),
        scratch=[pltpu.VMEM((block, HD), F32)],
        flops=3 * seq_len * seq_len * width,
        nbytes=8 * seq_len * width,
        trans=seq_len * seq_len * width // HD,
        vmem=24,
    )(docs, q, k, v, docs.reshape(-1, 1), docs.reshape(1, -1))


def attend_back_body(*refs, block, count):
    docs, chunks, q_ref, k_ref, v_ref = refs[:5]
    grads = refs[5 : 5 + count]
    ids_col, ids_row, cos, sin, out, dmix, dq, dk, dv = refs[5 + count :]
    seq_len = q_ref.shape[0]
    t = seq_len // count
    scale, shift = attend_consts(seq_len)
    for c in range(count):
        dmix[pl.ds(pl.multiple_of(chunks[c] * t, t), t), :] = grads[c][...]
    causal = lax.broadcasted_iota(jnp.int32, (block, block), 0) <= lax.broadcasted_iota(
        jnp.int32, (block, block), 1
    )

    def at(i):
        return slice(i * block, (i + 1) * block)

    def term(i, j):
        q, k, v, d = q_ref[at(i), :], k_ref[at(j), :], v_ref[at(j), :], dmix[at(i), :]
        sig = 1.0 / (1.0 + jnp.exp2(shift - dot_nt(k, q) * scale))
        same = ids_col[at(j), :] == ids_row[:, at(i)]
        allowed = same & causal if i == j else same
        probs = jnp.where(allowed, sig, 0.0)
        d_scores = (dot_nt(v, d) * probs * (1.0 - probs)).astype(BF)
        return dot_tn(d_scores, k), dot(d_scores, q), dot(probs.astype(BF), d)

    for i in range(seq_len // block):
        dq[at(i), :], dk[at(i), :], dv[at(i), :] = term(i, i)
    for i in range(seq_len // block):
        for j in range(i):

            @pl.when(docs[(j + 1) * block - 1] == docs[i * block])
            def _():
                a, b, c = term(i, j)
                dq[at(i), :] += a
                dk[at(j), :] += b
                dv[at(j), :] += c

    cosine, sine = cos[...], sin[...]

    def turned_back(v):
        v = v * (1.0 / math.sqrt(HD))
        return (v * cosine - pltpu.roll(v, HD // 2, 1) * sine).astype(BF)

    width = out.shape[1] // 3
    at_head = pl.program_id(0) * HD
    for part, value in enumerate((turned_back(dq[...]), turned_back(dk[...]), dv[...].astype(BF))):
        out[:, pl.ds(pl.multiple_of(at_head + part * width, HD), HD)] = value


def attend_back(docs, chunks, q, k, v, grads, cos, sin):
    seq_len, width = q.shape
    block, count = 256, len(grads)
    head = pl.BlockSpec((seq_len, HD), lambda h, s, c: (0, h))
    whole = lambda r, c: pl.BlockSpec((r, c), lambda h, s, e: (0, 0))
    return call(
        functools.partial(attend_back_body, block=block, count=count),
        name="attend_back",
        grid=(width // HD,),
        scalars=2,
        in_specs=[head, head, head]
        + [pl.BlockSpec((seq_len // count, HD), lambda h, s, c: (0, h))] * count
        + [whole(seq_len, 1), whole(1, seq_len), whole(seq_len, HD), whole(seq_len, HD)],
        out_specs=whole(seq_len, 3 * width),
        out_shape=jax.ShapeDtypeStruct((seq_len, 3 * width), BF),
        scratch=[pltpu.VMEM((seq_len, HD), BF)] + [pltpu.VMEM((seq_len, HD), F32)] * 3,
        flops=7 * seq_len * seq_len * width,
        nbytes=14 * seq_len * width,
        trans=seq_len * seq_len * width // HD,
        vmem=40,
    )(docs, chunks, q, k, v, *grads, docs.reshape(-1, 1), docs.reshape(1, -1), cos, sin)


def project_body(*refs, count):
    chunks = refs[0]
    mixes = refs[1 : 1 + count]
    w_ref, x_ref, gain, resid, normed, acc = refs[1 + count :]
    for c in range(count):

        @pl.when(pl.program_id(0) == c)
        def _():
            term = dot(mixes[c][...], w_ref[...])
            acc[...] = term if c == 0 else acc[...] + term

    @pl.when(pl.program_id(0) == count - 1)
    def _():
        total = x_ref[...].astype(F32) + acc[...]
        resid[...] = total
        normed[...] = rms_scale(total, gain[...]).astype(BF)


def project(chunks, mixes, w_out, x, gain):
    t, d = x.shape
    count = len(mixes)
    width = mixes[0].shape[1]
    whole = lambda r, c: pl.BlockSpec((r, c), lambda i, s: (0, 0))
    return call(
        functools.partial(project_body, count=count),
        name="project",
        grid=(count,),
        scalars=1,
        in_specs=[whole(t, width)] * count
        + [pl.BlockSpec((width, d), lambda i, s: (s[i], 0)), whole(t, d), whole(1, d)],
        out_specs=[whole(t, d)] * 2,
        out_shape=[jax.ShapeDtypeStruct((t, d), F32), jax.ShapeDtypeStruct((t, d), BF)],
        scratch=[pltpu.VMEM((t, d), F32)],
        flops=2 * t * d * d,
        nbytes=2 * d * d + 10 * t * d,
        vmem=32,
    )(chunks, *mixes, w_out, x, gain.reshape(1, -1))


def ffn_body(*refs):
    chunk, rows, cot, wg, wu, wd = refs[:6]
    inner, d_gate, d_up, rows_out, d_rows, down, token, acc_d, acc_o = refs[-9:]
    step, last = pl.program_id(0), pl.num_programs(0) - 1
    x = rows[...]
    gate = dot(x, wg[...])
    up = dot(x, wu[...])
    sig = sigmoid(gate)
    silu = gate * sig
    inner_b = (silu * up).astype(BF)
    inner[...] = inner_b
    d_inner = dot_nt(cot[...], wd[...])
    dg = (d_inner * up * (sig * (1.0 + gate * (1.0 - sig)))).astype(BF)
    du = (d_inner * silu).astype(BF)
    d_gate[...] = dg
    d_up[...] = du
    term_o = dot(inner_b, wd[...])
    term_d = dot_nt(dg, wg[...]) + dot_nt(du, wu[...])

    @pl.when(step == 0)
    def _():
        acc_o[...] = term_o
        acc_d[...] = term_d
        rows_out[...] = x

    @pl.when(step > 0)
    def _():
        acc_o[...] += term_o
        acc_d[...] += term_d

    @pl.when(step == last)
    def _():
        d_rows[...] = acc_d[...].astype(BF)
        down[...] = acc_o[...].astype(BF)
        token[...] = jnp.zeros_like(token)


def ffn_slot(chunk, rows, cot, w_gate, w_up, w_down, held, count):
    t, d = rows.shape
    hidden = w_gate.shape[1]
    bh = min(512, hidden)
    wcol = pl.BlockSpec((d, bh), lambda i, s: (0, i))
    part = pl.BlockSpec((t, bh), lambda i, s: (s[0], i))
    line = pl.BlockSpec((t, d), lambda i, s: (s[0], 0))
    return call(
        ffn_body,
        name="ffn",
        grid=(hidden // bh,),
        scalars=1,
        in_specs=[
            pl.BlockSpec((t, d), lambda i, s: (0, 0)),
            line,
            wcol,
            wcol,
            pl.BlockSpec((bh, d), lambda i, s: (i, 0)),
        ]
        + [ANY] * len(held),
        out_specs=[part] * 3 + [line] * 3 + [pl.BlockSpec((8, 128), lambda i, s: (0, 0))],
        out_shape=[jax.ShapeDtypeStruct((count * t, hidden), BF)] * 3
        + [jax.ShapeDtypeStruct((count * t, d), BF)] * 3
        + [jax.ShapeDtypeStruct((8, 128), F32)],
        scratch=[pltpu.VMEM((t, d), F32)] * 2,
        aliases={6 + i: i for i in range(len(held))},
        flops=14 * t * d * hidden,
        nbytes=2 * (3 * d * hidden + 5 * t * d + 3 * t * hidden),
        trans=2 * t * hidden,
        vmem=44,
    )(chunk, rows, cot, w_gate, w_up, w_down, *held)


def local(
    layer_in,
    cotangent,
    doc_ids,
    positions,
    attn_gain,
    w_query,
    w_key,
    w_value,
    w_out,
    ffn_gain,
    w_gate,
    w_up,
    w_down,
    *,
    dp,
    tensor,
):
    t, d = layer_in.shape
    width = w_query.shape[1]
    place = lax.axis_index("tensor")
    chunks = jnp.stack([place ^ j for j in range(tensor)]).astype(jnp.int32)
    chunk = [chunks[j : j + 1] for j in range(tensor)]
    reducer = Reducer(dp)

    share = w_out.shape[0] // dp
    w_out_all = lax.all_gather(
        rows_at(w_out, reducer.index, share), ("tensor", "dp"), axis=0, tiled=True
    )
    cot_all = lax.all_gather(cotangent, "tensor", axis=0, tiled=True)

    half = HD // 2
    freqs = ROPE_BASE ** (-(jnp.arange(half).astype(F32) * 2.0) / HD)
    angles = positions.astype(F32)[:, None] * freqs[None, :]
    cosine, sine = jnp.cos(angles), jnp.sin(angles)
    cos = jnp.concatenate([cosine, cosine], axis=1)
    sin = jnp.concatenate([-sine, sine], axis=1)

    own_in = layer_in.astype(F32)
    line = LineGather(rms_scale(own_in, attn_gain).astype(BF), tensor, place)
    held = []
    for j in range(tensor):
        if j + 1 < tensor:
            line.step()
        held = qkv_slot(chunk[j], line.slot(j), w_query, w_key, w_value, cos, sin, held, tensor)
    query, key, value, normed = held

    mixed = attend(doc_ids, query, key, value)
    mixes = exchange([rows_at(mixed, place ^ j, t) for j in range(tensor)], tensor)
    resid, normed2_own = project(chunks, mixes, w_out_all, layer_in, ffn_gain)

    line = LineGather(normed2_own, tensor, place)
    line.step()
    held, token = [], None
    for j in range(tensor):
        if 0 < j < tensor - 1:
            line.step(token)
        *held, token = ffn_slot(chunk[j], line.slot(j), cot_all, w_gate, w_up, w_down, held, tensor)
    inner, d_gate, d_up, normed2, d_normed2_part, down_part = held

    d_normed2 = lax.psum_scatter(d_normed2_part, "tensor", scatter_dimension=0, tiled=True)

    inner_halves = reducer.split(inner)
    normed2_halves = reducer.split(normed2)
    down_got = reducer.give(inner_halves, cot_all)
    gate_got = reducer.give(normed2_halves, d_gate)
    down_red = reducer.open(reducer.keep(inner_halves, cot_all, down_got))
    up_got = reducer.give(normed2_halves, d_up)
    gate_red = reducer.open(reducer.keep(normed2_halves, d_gate, gate_got))
    up_red = reducer.open(reducer.keep(normed2_halves, d_up, up_got))
    turns = range(1, reducer.bits)
    for _ in turns:
        down_red = reducer.add(down_red)
    gate_red = reducer.add(gate_red)
    d_normed2 = after(
        d_normed2, *reducer.pieces(down_red), *reducer.pieces(gate_red), *reducer.pieces(up_red)
    )
    down_part = after(down_part, *reducer.pieces(up_red))
    down_sum = lax.psum_scatter(down_part, "tensor", scatter_dimension=0, tiled=True)
    layer_out = (resid + down_sum.astype(F32)).astype(BF)

    norm_out, norm_pull = jax.vjp(rms_scale, resid, ffn_gain)
    d_resid_part, ffn_gain_part = norm_pull(d_normed2.astype(F32))
    d_resid = cotangent.astype(F32) + d_resid_part
    d_resid_low = d_resid.astype(BF)
    d_mix_own = dot_nt(d_resid_low, w_out_all).astype(BF)
    d_mixes = exchange([cols_at(d_mix_own, place ^ j, width) for j in range(tensor)], tensor)

    up_red = reducer.add(up_red)
    for _ in turns[1:]:
        gate_red = reducer.add(gate_red)
    down_red = reducer.spread(down_red)
    d_mixes = tie(
        d_mixes, [p for red in (up_red, gate_red, down_red) for p in reducer.pieces(red)]
    )
    d_qkv = attend_back(doc_ids, chunks, query, key, value, d_mixes, cos, sin)

    line = LineGather(after(d_resid_low, d_mixes[-1]), tensor, place)
    line.step()
    w_qkv = jnp.concatenate([w_query, w_key, w_value], axis=1)
    d_normed = lax.psum_scatter(
        dot_nt(d_qkv, w_qkv).astype(BF), "tensor", scatter_dimension=0, tiled=True
    )
    normed_halves = reducer.split(normed)
    qkv_got = reducer.give(normed_halves, d_qkv)
    qkv_red = reducer.open(reducer.keep(normed_halves, d_qkv, qkv_got))
    for _ in turns[1:]:
        up_red = reducer.add(up_red)
    for _ in turns[1:]:
        down_red = reducer.spread(down_red)
    gate_red = reducer.spread(gate_red)
    for _ in range(2, tensor):
        line.step()
    (down_grad,) = reducer.close(down_red, [d])
    qkv_red = reducer.add(qkv_red)
    hidden = w_gate.shape[1]
    for _ in turns[1:]:
        gate_red = reducer.spread(gate_red)
    up_red = reducer.spread(up_red)
    (gate_grad,) = reducer.close(gate_red, [hidden])

    d_resid_all = jnp.zeros((t * tensor, d), BF)
    for j in range(tensor):
        d_resid_all = lax.dynamic_update_slice_in_dim(d_resid_all, line.slot(j), (place ^ j) * t, axis=0)
    mixed_halves = reducer.split(mixed)
    out_got = reducer.give(mixed_halves, d_resid_all)
    out_red = reducer.open(reducer.keep(mixed_halves, d_resid_all, out_got))
    for _ in turns[1:]:
        qkv_red = reducer.add(qkv_red)
    for _ in turns[1:]:
        up_red = reducer.spread(up_red)
    for _ in turns:
        out_red = reducer.add(out_red)
    d_normed = after(d_normed, down_grad, gate_grad, *reducer.pieces(out_red), *reducer.pieces(up_red))
    (up_grad,) = reducer.close(up_red, [hidden])
    for _ in turns:
        qkv_red = reducer.spread(qkv_red)
        out_red = reducer.spread(out_red)
    query_grad, key_grad, value_grad = reducer.close(qkv_red, [width] * 3)
    (out_grad,) = reducer.close(out_red, [d])

    norm_first, first_pull = jax.vjp(rms_scale, own_in, attn_gain)
    d_in_part, attn_gain_part = first_pull(d_normed.astype(F32))
    in_grad = (d_resid + d_in_part).astype(BF)
    attn_gain_grad = gain_total(attn_gain_part, dp, tensor)
    ffn_gain_grad = gain_total(ffn_gain_part, dp, tensor)
    return (
        layer_out,
        in_grad,
        attn_gain_grad,
        query_grad,
        key_grad,
        value_grad,
        out_grad,
        ffn_gain_grad,
        gate_grad,
        up_grad,
        down_grad,
    )


def solution(mesh):
    rows, cols, lines = P(("dp", "tensor"), None), P(None, "tensor"), P("tensor", None)
    return jax.shard_map(
        functools.partial(local, dp=mesh.shape["dp"], tensor=mesh.shape["tensor"]),
        mesh=mesh,
        in_specs=(
            rows, rows, P("dp"), P("dp"), P(), cols, cols, cols, lines, P(), cols, cols, lines
        ),
        out_specs=(rows, rows, P(), cols, cols, cols, lines, P(), cols, cols, lines),
        check_vma=False,
    )
```

time: 1450 us -> 1040 us (0.72)
  waiting for transfers between devices: 1050 us -> 479 us
  Pallas kernels: 0 us -> 208 us
  matrix products: 211 us -> 73.6 us
  starting transfers between devices: 0.83 us -> 128 us
  local copies, waits for them, and re-layouts: 28.3 us -> 84.4 us
  blocking collectives: 43.2 us -> 0 us
  other arithmetic: 86.9 us -> 45.5 us
    ppermute x0 -> x94, waiting for transfers between devices: none -> 478 us  [the longest x9 230 us: step(): lax.ppermute(down, 'tensor', [(i + 1, i) for i in range(0, size - k)])]
    reduce_scatter x4 -> x3, waiting for transfers between devices: 421 us -> 0.02 us  [the longest x1 0.02 us: local(): lax.psum_scatter(dot_nt(d_qkv, w_qkv).astype(BF), 'tensor', scatter_dimen...]
    psum x1 -> x0, waiting for transfers between devices: 375 us -> none  [local(): lax.psum(query_grad.astype(jnp.bfloat16), 'dp').astype(jnp.float32)]
    pallas_call x0 -> x28, Pallas kernels: none -> 208 us  [the longest x4 87.9 us: ffn_slot(): call(ffn_body, name='ffn', grid=(hidden // bh,), scalars=1, in_specs=[pl....]
    all_gather x3 -> x1, waiting for transfers between devices: 204 us -> 0.01 us  [local(): lax.all_gather(rows_at(w_out, reducer.index, share), ('tensor', 'dp'), ax...]
    dot_general x33 -> x12, matrix products: 211 us -> 73.6 us  [the longest x10 59.2 us: dot_tn(): lax.dot_general(left, right, (((0,), (0,)), ((), ())), preferred_element_...]
    ppermute x0 -> x94, starting transfers between devices: none -> 128 us  [the longest x60 53.7 us: swap(): return lax.ppermute(value, 'dp', xor_pairs(self.count, 1 << b))]
    all_gather x1, waiting for transfers between devices: 51.6 us -> 0.02 us  [local(): cot_all = lax.all_gather(cotangent, 'tensor', axis=0, tiled=True)]
  transfers between devices with their start and end apart: 9 -> 99, of which waited for: 9 -> 41; matrix products, arithmetic and copies ran while one was open for 10% -> 11% of each run, Pallas kernels for 0% -> 16%
where the time goes in v1:
time: 1040 us; the launch traced here: 1030 us
  waiting for transfers between devices  479 us (46%)
  Pallas kernels  208 us (20%)
  starting transfers between devices  128 us (12%)
  local copies, waits for them, and re-layouts  84.4 us (8%)
  matrix products  73.6 us (7%)
  other arithmetic  45.5 us (4%)
  between operations  15.8 us (2%)
    ppermute x9, waiting for transfers between devices, step(): lax.ppermute(down, 'tensor', [(i + 1, i) for i in range(0, size - k)])  230 us
    ppermute x60, waiting for transfers between devices, swap(): return lax.ppermute(value, 'dp', xor_pairs(self.count, 1 << b))  162 us
    pallas_call x4, Pallas kernels, ffn_slot(): call(ffn_body, name='ffn', grid=(hidden // bh,), scalars=1, in_specs=[pl....  87.9 us
    unnamed x288, local copies, waits for them, and re-layouts  71.3 us
    dot_general x10, matrix products, dot_tn(): lax.dot_general(left, right, (((0,), (0,)), ((), ())), preferred_element_...  59.2 us
    ppermute x9, waiting for transfers between devices, step(): lax.ppermute(up, 'tensor', [(i, i + 1) for i in range(k - 1, size - 1)])  57.3 us
    ppermute x60, starting transfers between devices, swap(): return lax.ppermute(value, 'dp', xor_pairs(self.count, 1 << b))  53.7 us
    pallas_call x5, Pallas kernels, close(): call(finish_body, name='finish', grid=(2, nblk), scalars=1, in_specs=[pl....  46.3 us
  transfers between devices with their start and end apart: 99, of which 41 were waited for; matrix products, arithmetic and copies ran while one was open for 11% of the time, Pallas kernels for 16%

profile of v1, /device:TPU:0, one launch (start us, length us, event | category | flops | bytes accessed | tf_op | source)
XLA Modules:
  0.0 1034.0 jit_solution(12003826037350269868)
XLA Ops:
  21.8 29.0 %collective-permute-done = bf16[256,2048]{1,0:T(8,128)(2,1)} collective-permute-done((bf16[256,2048]{1,0:T(8,128)(2,1)S(1)}, bf16[256,2048]{1,0:T(8,128)(2,1)}, u32[]{:S(2)}, u32[]{:S(2)}) %collective-permute-start) | collective-permute-done | bytes 1048608 | tf_op jit(solution)/shard_map/ppermute | solution.py:97
  64.9 43.2 %collective-permute-done.4 = bf16[256,2048]{1,0:T(8,128)(2,1)} collective-permute-done((bf16[256,2048]{1,0:T(8,128)(2,1)}, bf16[256,2048]{1,0:T(8,128)(2,1)}, u32[]{:S(2)}, u32[]{:S(2)}) %collective-permute-start.4) | collective-permute-done | bytes 1048608 | tf_op jit(solution)/shard_map/ppermute | solution.py:98
  118.0 68.7 %collective-permute-done.5 = bf16[256,2048]{1,0:T(8,128)(2,1)S(1)} collective-permute-done((bf16[256,2048]{1,0:T(8,128)(2,1)}, bf16[256,2048]{1,0:T(8,128)(2,1)S(1)}, u32[]{:S(2)}, u32[]{:S(2)}) %collective-permute-start.5) | collective-permute-done | bytes 1048608 | tf_op jit(solution)/shard_map/ppermute | solution.py:98
  196.9 12.1 %attend.1 = bf16[1024,512]{1,0:T(8,128)(2,1)S(1)} custom-call(s32[1024]{0:T(1024)S(1)} %copy-done.111, bf16[1024,512]{1,0:T(8,128)(2,1)S(1)} %get-tuple-element.78.q_ref.refs_2_, bf16[1024,512]{1,0:T(8,128)(2,1)S(1)} %get-tuple-element.79.k_ref.refs_3_, bf16[1024,512]{1,0:T(8,128)(2,1)S(1)} %get-tuple-element.80.v_ref.refs_4_, s32[1024,1]{1,0:T(8,128)S(1)} %copy-done.98, ...), custom_call_target="tpu_custom_call" | custom-call | flops 1610612736 | bytes 4194304 | tf_op jit(solution)/shard_map/attend/pallas_call | solution.py:332
  247.6 22.3 %ffn.4 = (bf16[1024,2048]{1,0:T(8,128)(2,1)S(1)}, bf16[1024,2048]{1,0:T(8,128)(2,1)S(1)}, bf16[1024,2048]{1,0:T(8,128)(2,1)}, bf16[1024,2048]{1,0:T(8,128)(2,1)}...) custom-call(s32[1]{0:T(128)} %bitcast.refs_0_, ...), custom_call_target="tpu_custom_call" | custom-call | flops 15032385536 | bytes 33554432 | tf_op jit(solution)/shard_map/ffn/pallas_call | solution.py:509
  273.3 21.8 %ffn.5 = (bf16[1024,2048]{1,0:T(8,128)(2,1)S(1)}, bf16[1024,2048]{1,0:T(8,128)(2,1)S(1)}, bf16[1024,2048]{1,0:T(8,128)(2,1)}, bf16[1024,2048]{1,0:T(8,128)(2,1)}...) custom-call(s32[1]{0:T(128)} %bitcast.1.refs_0_, ...), custom_call_target="tpu_custom_call", output_to_operand_aliasing={{0}: (6, {}), {1}: (7, {}), {2}: (8, {}), {3}: (9, {}), {4}... | custom-call | flops 15032385536 | bytes 33554432 | tf_op jit(solution)/shard_map/ffn/pallas_call | solution.py:509
  297.3 22.0 %ffn.6 = (bf16[1024,2048]{1,0:T(8,128)(2,1)S(1)}, bf16[1024,2048]{1,0:T(8,128)(2,1)S(1)}, bf16[1024,2048]{1,0:T(8,128)(2,1)}, bf16[1024,2048]{1,0:T(8,128)(2,1)}...) custom-call(s32[1]{0:T(128)} %bitcast.2.refs_0_, ...), custom_call_target="tpu_custom_call", output_to_operand_aliasing={{0}: (6, {}), {1}: (7, {}), {2}: (8, {}), {3}: (9, {}), {4}... | custom-call | flops 15032385536 | bytes 33554432 | tf_op jit(solution)/shard_map/ffn/pallas_call | solution.py:509
  319.5 21.9 %ffn.7 = (bf16[1024,2048]{1,0:T(8,128)(2,1)S(1)}, bf16[1024,2048]{1,0:T(8,128)(2,1)S(1)}, bf16[1024,2048]{1,0:T(8,128)(2,1)}, bf16[1024,2048]{1,0:T(8,128)(2,1)}...) custom-call(s32[1]{0:T(128)} %bitcast.3.refs_0_, ...), custom_call_target="tpu_custom_call", output_to_operand_aliasing={{0}: (6, {}), {1}: (7, {}), {2}: (8, {}), {3}: (9, {}), {4}... | custom-call | flops 15032385536 | bytes 33554432 | tf_op jit(solution)/shard_map/ffn/pallas_call | solution.py:509
  401.1 19.4 %collective-permute-done.22 = bf16[512,1024]{1,0:T(8,128)(2,1)S(1)} collective-permute-done((bf16[512,1024]{1,0:T(8,128)(2,1)S(1)}, bf16[512,1024]{1,0:T(8,128)(2,1)S(1)}, u32[]{:S(2)}, u32[]{:S(2)}) %collective-permute-start.22) | collective-permute-done | bytes 1048608 | tf_op jit(solution)/shard_map/ppermute | solution.py:167
  424.9 18.2 %collective-permute-done.27 = bf16[512,1024]{1,0:T(8,128)(2,1)S(1)} collective-permute-done((bf16[512,1024]{1,0:T(8,128)(2,1)S(1)}, bf16[512,1024]{1,0:T(8,128)(2,1)S(1)}, u32[]{:S(2)}, u32[]{:S(2)}) %collective-permute-start.27) | collective-permute-done | bytes 1048608 | tf_op jit(solution)/shard_map/ppermute | solution.py:167
  491.7 13.2 %collective-permute-done.25.refs_2_ = bf16[256,512]{1,0:T(8,128)(2,1)S(1)} collective-permute-done((bf16[256,512]{1,0:T(8,128)(2,1)S(1)}, bf16[256,512]{1,0:T(8,128)(2,1)S(1)}, u32[]{:S(2)}, u32[]{:S(2)}) %collective-permute-start.25) | collective-permute-done | bytes 262176 | tf_op jit(solution)/shard_map/ppermute | solution.py:117
  507.2 18.8 %attend_back.1 = bf16[1024,1536]{1,0:T(8,128)(2,1)S(1)} custom-call(s32[1024]{0:T(1024)S(1)} %copy-done.111, s32[4]{0:T(128)S(1)} %pad_add_fusion.refs_0_.refs_1_, bf16[1024,512]{1,0:T(8,128)(2,1)S(1)} %copy-done.33, bf16[1024,512]{1,0:T(8,128)(2,1)S(1)} %copy-done.35, bf16[1024,512]{1,0:T(8,128)(2,1)S(1)} %copy-done.37, ...), custom_call_target="tpu_custom_call" | custom-call | flops 3758096384 | bytes 7340032 | tf_op jit(solution)/shard_map/attend_back/pallas_call | solution.py:408
  567.0 28.3 %collective-permute-done.45 = bf16[256,2048]{1,0:T(8,128)(2,1)} collective-permute-done((bf16[256,2048]{1,0:T(8,128)(2,1)}, bf16[256,2048]{1,0:T(8,128)(2,1)}, u32[]{:S(2)}, u32[]{:S(2)}) %collective-permute-start.45) | collective-permute-done | bytes 1048608 | tf_op jit(solution)/shard_map/ppermute | solution.py:97
  596.0 25.3 %collective-permute-done.46 = bf16[256,2048]{1,0:T(8,128)(2,1)} collective-permute-done((bf16[256,2048]{1,0:T(8,128)(2,1)}, bf16[256,2048]{1,0:T(8,128)(2,1)}, u32[]{:S(2)}, u32[]{:S(2)}) %collective-permute-start.46) | collective-permute-done | bytes 1048608 | tf_op jit(solution)/shard_map/ppermute | solution.py:98
  632.0 35.8 %collective-permute-done.48 = bf16[256,2048]{1,0:T(8,128)(2,1)S(1)} collective-permute-done((bf16[256,2048]{1,0:T(8,128)(2,1)}, bf16[256,2048]{1,0:T(8,128)(2,1)S(1)}, u32[]{:S(2)}, u32[]{:S(2)}) %collective-permute-start.48) | collective-permute-done | bytes 1048608 | tf_op jit(solution)/shard_map/ppermute | solution.py:98
  695.6 48.2 %collective-permute-done.50 = bf16[256,2048]{1,0:T(8,128)(2,1)S(1)} collective-permute-done((bf16[256,2048]{1,0:T(8,128)(2,1)S(1)}, bf16[256,2048]{1,0:T(8,128)(2,1)S(1)}, u32[]{:S(2)}, u32[]{:S(2)}) %collective-permute-start.50) | collective-permute-done | bytes 1048608 | tf_op jit(solution)/shard_map/ppermute | solution.py:98
  752.6 11.6 %collective-permute-done.75 = bf16[512,768]{1,0:T(8,128)(2,1)S(1)} collective-permute-done((bf16[512,768]{1,0:T(8,128)(2,1)S(1)}, bf16[512,768]{1,0:T(8,128)(2,1)S(1)}, u32[]{:S(2)}, u32[]{:S(2)}) %collective-permute-start.75) | collective-permute-done | bytes 786464 | tf_op jit(solution)/shard_map/ppermute | solution.py:167
  775.1 11.2 %collective-permute-done.34.refs_3_ = bf16[256,1024]{1,0:T(8,128)(2,1)S(1)} collective-permute-done((bf16[256,1024]{1,0:T(8,128)(2,1)}, bf16[256,1024]{1,0:T(8,128)(2,1)S(1)}, u32[]{:S(2)}, u32[]{:S(2)}) %collective-permute-start.34) | collective-permute-done | bytes 524320 | tf_op jit(solution)/shard_map/ppermute | solution.py:167
  818.8 9.3 collective-permute-done.59.refs_8_.refs_3_
  929.9 11.0 %finish.5.refs_1_ = f32[2048,2048]{1,0:T(8,128)} custom-call(s32[1]{0:T(128)} %bitcast.7.core, bf16[1024,2048]{1,0:T(8,128)(2,1)} %join.5.mine, bf16[1024,2048]{1,0:T(8,128)(2,1)} %collective-permute-done.37.other), custom_call_target="tpu_custom_call" | custom-call | bytes 25165824 | tf_op jit(solution)/shard_map/finish/pallas_call | solution.py:225
  940.9 11.3 %finish.6.refs_2_ = f32[2048,2048]{1,0:T(8,128)} custom-call(s32[1]{0:T(128)} %bitcast.7.core, bf16[1024,2048]{1,0:T(8,128)(2,1)} %join.6.mine, bf16[1024,2048]{1,0:T(8,128)(2,1)} %collective-permute-done.44.other), custom_call_target="tpu_custom_call" | custom-call | bytes 25165824 | tf_op jit(solution)/shard_map/finish/pallas_call | solution.py:225
  975.1 13.2 %collective-permute-start.92 = (f32[16,128]{1,0:T(8,128)S(1)}, f32[16,128]{1,0:T(8,128)S(1)}, u32[]{:S(2)}, u32[]{:S(2)}) collective-permute-start(f32[16,128]{1,0:T(8,128)S(1)} %add.343), channel_id=1, source_target_pairs={{0,2},{1,3},{2,0},{3,1},{4,6},{5,7},{6,4},{7,5},{8,10},{9,11},{10,... | collective-permute-start | bytes 24584 | tf_op jit(solution)/shard_map/ppermute | solution.py:248
  990.6 11.0 %finish.9 = f32[2048,2048]{1,0:T(8,128)} custom-call(s32[1]{0:T(128)} %bitcast.7.core, bf16[1024,2048]{1,0:T(8,128)(2,1)} %join.9.mine, bf16[1024,2048]{1,0:T(8,128)(2,1)} %collective-permute-done.93.other), custom_call_target="tpu_custom_call" | custom-call | bytes 25165824 | tf_op jit(solution)/shard_map/finish/pallas_call | solution.py:225
  1005.3 9.5 finish.7
  (593 shorter events, 482.0 us)
Async XLA Ops:
  7.2 220.7 %all-gather.3.cloned.1.call-start = ((), (), s32[]{:S(2)}) async-start(), calls=%async_computation.3 | async-start | bytes 8650752 | tf_op jit(solution)/shard_map/all_gather | solution.py:561
  9.5 238.1 %all-gather.5.cloned.1.call-start = ((), (), s32[]{:S(2)}) async-start(), calls=%async_computation.4 | async-start | bytes 5242880 | tf_op jit(solution)/shard_map/all_gather | solution.py:564
  10.3 448.2 %reduce-scatter.6.cloned.1.call-start = ((), (), s32[]{:S(2)}) async-start(), calls=%async_computation.6 | async-start | bytes 5242880 | tf_op jit(solution)/shard_map/reduce_scatter | solution.py:595
  64.1 53.9 %collective-permute-start.2 = (bf16[256,2048]{1,0:T(8,128)(2,1)}, bf16[256,2048]{1,0:T(8,128)(2,1)S(1)}, u32[]{:S(2)}, u32[]{:S(2)}) collective-permute-start(bf16[256,2048]{1,0:T(8,128)(2,1)} %collective-permute-done.1), channel_id=1, source_target_pairs={{2,3},{6,7},{10,11},{14,15},{18,19},{22,23},{26,27},{30,31}} | collective-permute-start | bytes 3145736 | tf_op jit(solution)/shard_map/ppermute | solution.py:97
  108.1 78.6 %collective-permute-start.5 = (bf16[256,2048]{1,0:T(8,128)(2,1)}, bf16[256,2048]{1,0:T(8,128)(2,1)S(1)}, u32[]{:S(2)}, u32[]{:S(2)}) collective-permute-start(bf16[256,2048]{1,0:T(8,128)(2,1)} %collective-permute-done.4), channel_id=1, source_target_pairs={{1,0},{5,4},{9,8},{13,12},{17,16},{21,20},{25,24},{29,28}} | collective-permute-start | bytes 3145736 | tf_op jit(solution)/shard_map/ppermute | solution.py:98
  361.0 591.2 %reduce-scatter.8.cloned.1.call-start = ((), (), s32[]{:S(2)}) async-start(), calls=%async_computation.7 | async-start | bytes 5242880 | tf_op jit(solution)/shard_map/reduce_scatter | solution.py:635
  398.6 55.9 %collective-permute-start.18 = (bf16[256,1024]{1,0:T(8,128)(2,1)S(1)}, bf16[256,1024]{1,0:T(8,128)(2,1)S(1)}, u32[]{:S(2)}, u32[]{:S(2)}) collective-permute-start(bf16[256,1024]{1,0:T(8,128)(2,1)S(1)} %constant_dynamic-slice_fusion.22), channel_id=1, source_target_pairs={{0,16},{4,20},{8,24},{12,28},{16,0},{20,4},{24,8},{28,12},{1,17},{... | collective-permute-start | bytes 1572872 | tf_op jit(solution)/shard_map/ppermute | solution.py:167
  421.9 62.5 %collective-permute-start.29 = (bf16[256,1024]{1,0:T(8,128)(2,1)}, bf16[256,1024]{1,0:T(8,128)(2,1)}, u32[]{:S(2)}, u32[]{:S(2)}) collective-permute-start(bf16[256,1024]{1,0:T(8,128)(2,1)} %constant_dynamic-slice_fusion.11), channel_id=1, source_target_pairs={{0,16},{4,20},{8,24},{12,28},{16,0},{20,4},{24,8},{28,12},{1,17},{... | collective-permute-start | bytes 1572872 | tf_op jit(solution)/shard_map/ppermute | solution.py:167
  536.0 485.3 %reduce-scatter.4.cloned.1.call-start = ((), (), s32[]{:S(2)}) async-start(), calls=%async_computation.5 | async-start | bytes 5242880 | tf_op jit(solution)/shard_map/reduce_scatter | solution.py:613
  543.8 125.2 %collective-permute-start.69 = (bf16[1024,1536]{1,0:T(8,128)(2,1)}, bf16[1024,1536]{1,0:T(8,128)(2,1)}, u32[]{:S(2)}, u32[]{:S(2)}) collective-permute-start(bf16[1024,1536]{1,0:T(8,128)(2,1)} %convolution_convert_fusion), channel_id=1, source_target_pairs={{0,4},{4,0},{8,12},{12,8},{16,20},{20,16},{24,28},{28,24},{1,5},{5... | collective-permute-start | bytes 9437192 | tf_op jit(solution)/shard_map/ppermute | solution.py:167
  550.2 71.1 %collective-permute-start.46 = (bf16[256,2048]{1,0:T(8,128)(2,1)}, bf16[256,2048]{1,0:T(8,128)(2,1)}, u32[]{:S(2)}, u32[]{:S(2)}) collective-permute-start(bf16[256,2048]{1,0:T(8,128)(2,1)} %tie.12), channel_id=1, source_target_pairs={{1,0},{2,1},{3,2},{5,4},{6,5},{7,6},{9,8},{10,9},{11,10},{13,12},{... | collective-permute-start | bytes 3145736 | tf_op jit(solution)/shard_map/ppermute | solution.py:98
  553.2 70.7 %collective-permute-start.60 = (bf16[256,1024]{1,0:T(8,128)(2,1)}, bf16[256,1024]{1,0:T(8,128)(2,1)}, u32[]{:S(2)}, u32[]{:S(2)}) collective-permute-start(bf16[256,1024]{1,0:T(8,128)(2,1)} %constant_dynamic-slice_fusion.4), channel_id=1, source_target_pairs={{0,8},{4,12},{8,0},{12,4},{16,24},{20,28},{24,16},{28,20},{1,9},{5... | collective-permute-start | bytes 1572872 | tf_op jit(solution)/shard_map/ppermute | solution.py:167
  566.6 109.0 %collective-permute-start.33 = (bf16[256,1024]{1,0:T(8,128)(2,1)}, bf16[256,1024]{1,0:T(8,128)(2,1)S(1)}, u32[]{:S(2)}, u32[]{:S(2)}) collective-permute-start(bf16[256,1024]{1,0:T(8,128)(2,1)} %add_convert_fusion.18.refs_1_.refs_8_.refs_0_), channel_id=1, source_target_pairs={{0,8},{4,12},{8,0},{12,4},{16,24},{20,28},{24,16},{28,20},{1,9},{5... | collective-permute-start | bytes 1572872 | tf_op jit(solution)/shard_map/ppermute | solution.py:167
  623.9 53.5 %collective-permute-start.35 = (bf16[256,1024]{1,0:T(8,128)(2,1)}, bf16[256,1024]{1,0:T(8,128)(2,1)S(1)}, u32[]{:S(2)}, u32[]{:S(2)}) collective-permute-start(bf16[256,1024]{1,0:T(8,128)(2,1)} %add_convert_fusion.17.refs_2_.refs_10_.refs_4_), channel_id=1, source_target_pairs={{0,16},{4,20},{8,24},{12,28},{16,0},{20,4},{24,8},{28,12},{1,17},{... | collective-permute-start | bytes 1572872 | tf_op jit(solution)/shard_map/ppermute | solution.py:167
  669.1 74.8 %collective-permute-start.50 = (bf16[256,2048]{1,0:T(8,128)(2,1)S(1)}, bf16[256,2048]{1,0:T(8,128)(2,1)S(1)}, u32[]{:S(2)}, u32[]{:S(2)}) collective-permute-start(bf16[256,2048]{1,0:T(8,128)(2,1)S(1)} %collective-permute-done.48), channel_id=1, source_target_pairs={{1,0},{5,4},{9,8},{13,12},{17,16},{21,20},{25,24},{29,28}} | collective-permute-start | bytes 3145736 | tf_op jit(solution)/shard_map/ppermute | solution.py:98
  678.3 70.6 %collective-permute-start.41 = (bf16[256,1024]{1,0:T(8,128)(2,1)S(1)}, bf16[256,1024]{1,0:T(8,128)(2,1)}, u32[]{:S(2)}, u32[]{:S(2)}) collective-permute-start(bf16[256,1024]{1,0:T(8,128)(2,1)S(1)} %copy-done.58), channel_id=1, source_target_pairs={{0,8},{4,12},{8,0},{12,4},{16,24},{20,28},{24,16},{28,20},{1,9},{5... | collective-permute-start | bytes 1572872 | tf_op jit(solution)/shard_map/ppermute | solution.py:167
  678.9 70.9 %collective-permute-start.42 = (bf16[256,1024]{1,0:T(8,128)(2,1)S(1)}, bf16[256,1024]{1,0:T(8,128)(2,1)S(1)}, u32[]{:S(2)}, u32[]{:S(2)}) collective-permute-start(bf16[256,1024]{1,0:T(8,128)(2,1)S(1)} %copy-done.58), channel_id=1, source_target_pairs={{0,16},{4,20},{8,24},{12,28},{16,0},{20,4},{24,8},{28,12},{1,17},{... | collective-permute-start | bytes 1572872 | tf_op jit(solution)/shard_map/ppermute | solution.py:167
  690.4 60.6 %collective-permute-start.57 = (bf16[256,1024]{1,0:T(8,128)(2,1)S(1)}, bf16[256,1024]{1,0:T(8,128)(2,1)S(1)}, u32[]{:S(2)}, u32[]{:S(2)}) collective-permute-start(bf16[256,1024]{1,0:T(8,128)(2,1)S(1)} %add_convert_fusion.14.refs_5_.refs_0_), channel_id=1, source_target_pairs={{0,16},{4,20},{8,24},{12,28},{16,0},{20,4},{24,8},{28,12},{1,17},{... | collective-permute-start | bytes 1572872 | tf_op jit(solution)/shard_map/ppermute | solution.py:167
  695.6 56.3 %collective-permute-start.70 = (bf16[512,768]{1,0:T(8,128)(2,1)S(1)}, bf16[512,768]{1,0:T(8,128)(2,1)S(1)}, u32[]{:S(2)}, u32[]{:S(2)}) collective-permute-start(bf16[512,768]{1,0:T(8,128)(2,1)S(1)} %constant_dynamic-slice_fusion.3), channel_id=1, source_target_pairs={{0,8},{4,12},{8,0},{12,4},{16,24},{20,28},{24,16},{28,20},{1,9},{5... | collective-permute-start | bytes 2359304 | tf_op jit(solution)/shard_map/ppermute | solution.py:167
  808.0 121.2 %collective-permute-start.37 = (bf16[1024,2048]{1,0:T(8,128)(2,1)}, bf16[1024,2048]{1,0:T(8,128)(2,1)}, u32[]{:S(2)}, u32[]{:S(2)}) collective-permute-start(bf16[1024,2048]{1,0:T(8,128)(2,1)} %join.5.mine), channel_id=1, source_target_pairs={{0,4},{4,0},{8,12},{12,8},{16,20},{20,16},{24,28},{28,24},{1,5},{5... | collective-permute-start | bytes 12582920 | tf_op jit(solution)/shard_map/ppermute | solution.py:167
  813.7 127.2 %collective-permute-start.44 = (bf16[1024,2048]{1,0:T(8,128)(2,1)}, bf16[1024,2048]{1,0:T(8,128)(2,1)}, u32[]{:S(2)}, u32[]{:S(2)}) collective-permute-start(bf16[1024,2048]{1,0:T(8,128)(2,1)} %join.6.mine), channel_id=1, source_target_pairs={{0,4},{4,0},{8,12},{12,8},{16,20},{20,16},{24,28},{28,24},{1,5},{5... | collective-permute-start | bytes 12582920 | tf_op jit(solution)/shard_map/ppermute | solution.py:167
  843.9 146.7 %collective-permute-start.93 = (bf16[1024,2048]{1,0:T(8,128)(2,1)}, bf16[1024,2048]{1,0:T(8,128)(2,1)}, u32[]{:S(2)}, u32[]{:S(2)}) collective-permute-start(bf16[1024,2048]{1,0:T(8,128)(2,1)} %join.9.mine), channel_id=1, source_target_pairs={{0,4},{4,0},{8,12},{12,8},{16,20},{20,16},{24,28},{28,24},{1,5},{5... | collective-permute-start | bytes 12582920 | tf_op jit(solution)/shard_map/ppermute | solution.py:167
  874.8 130.5 %collective-permute-start.80 = (bf16[1024,1536]{1,0:T(8,128)(2,1)}, bf16[1024,1536]{1,0:T(8,128)(2,1)}, u32[]{:S(2)}, u32[]{:S(2)}) collective-permute-start(bf16[1024,1536]{1,0:T(8,128)(2,1)} %join.7.mine), channel_id=1, source_target_pairs={{0,4},{4,0},{8,12},{12,8},{16,20},{20,16},{24,28},{28,24},{1,5},{5... | collective-permute-start | bytes 9437192 | tf_op jit(solution)/shard_map/ppermute | solution.py:167
  928.5 73.0 %collective-permute-start.87 = (bf16[256,2048]{1,0:T(8,128)(2,1)}, bf16[256,2048]{1,0:T(8,128)(2,1)}, u32[]{:S(2)}, u32[]{:S(2)}) collective-permute-start(bf16[256,2048]{1,0:T(8,128)(2,1)} %join.8.mine), channel_id=1, source_target_pairs={{0,4},{4,0},{8,12},{12,8},{16,20},{20,16},{24,28},{28,24},{1,5},{5... | collective-permute-start | bytes 3145736 | tf_op jit(solution)/shard_map/ppermute | solution.py:167
  (219 other events, 3895.1 us)
Sparse Core Ops, SparseCore 0:
  11.5 95.9 all-gather.2
  109.1 97.7 all-gather.4
  361.1 81.4 reduce-scatter.5
  536.1 104.7 reduce-scatter.7
  643.1 106.5 reduce-scatter.3

commit v2 on v1

v2 whole, which is shorter than its diff:
```python
import functools
import math

import jax
import jax.numpy as jnp
from jax import lax
from jax.experimental import pallas as pl
from jax.experimental.pallas import tpu as pltpu
from jax.sharding import PartitionSpec as P

HD = 128
EPS = 1e-05
ROPE_BASE = 500000.0
BF = jnp.bfloat16
F32 = jnp.float32
VMEM = 56 << 20
COST = {
    "give": 8, "keep": 10, "fold": 4, "spread": 4, "join": 4.5, "finish": 11, "middle": 9.5, "attend": 11,
    "attend_back": 17, "back_project": 11, "qkv": 5.6, "project": 8.6, "ffn": 22, "last": 5, "tie": 0.5,
}


def dot(left, right):
    return lax.dot_general(left, right, (((1,), (0,)), ((), ())), preferred_element_type=F32)


def dot_nt(left, right):
    return lax.dot_general(left, right, (((1,), (1,)), ((), ())), preferred_element_type=F32)


def dot_tn(left, right):
    return lax.dot_general(left, right, (((0,), (0,)), ((), ())), preferred_element_type=F32)


def sigmoid(v):
    return 1.0 / (1.0 + jnp.exp(-v))


def rms_scale(values, gain):
    return values * lax.rsqrt(jnp.mean(values * values, axis=-1, keepdims=True) + EPS) * gain


ANY = pl.BlockSpec(memory_space=pl.ANY)
TOKEN = jax.ShapeDtypeStruct((8, 128), F32)


def call(body, *, name, grid, scalars, in_specs, out_specs, out_shape, scratch=(), aliases=None):
    def run(order, *operands):
        tokens = order.take()
        ahead = scalars + len(in_specs)

        def whole(*refs):
            outs = refs[ahead + len(tokens) :]
            body(*refs[:ahead], *outs[: len(out_shape)], *outs[len(out_shape) + 1 :])
            outs[len(out_shape)][...] = jnp.zeros((8, 128), F32)

        *values, token = pl.pallas_call(
            whole,
            grid_spec=pltpu.PrefetchScalarGridSpec(
                num_scalar_prefetch=scalars,
                grid=grid,
                in_specs=list(in_specs) + [ANY] * len(tokens),
                out_specs=list(out_specs) + [pl.BlockSpec((8, 128), lambda *_: (0, 0))],
                scratch_shapes=list(scratch),
            ),
            out_shape=list(out_shape) + [TOKEN],
            input_output_aliases=aliases or {},
            compiler_params=pltpu.CompilerParams(vmem_limit_bytes=VMEM),
            cost_estimate=pl.CostEstimate(flops=int(COST[name] * 1e+09), bytes_accessed=int(COST[name] * 1e6), transcendentals=0),
            name=name,
        )(*operands, *tokens)
        order.give(token)
        return values

    return run


class Order:
    def __init__(self):
        self.tokens = []

    def take(self):
        return self.tokens

    def give(self, token):
        self.tokens = [token]

    def after(self, *values):
        return call(
            lambda *refs: None,
            name="tie",
            grid=(1,),
            scalars=0,
            in_specs=[ANY] * len(values),
            out_specs=[ANY] * len(values),
            out_shape=[jax.ShapeDtypeStruct(v.shape, v.dtype) for v in values],
            aliases={i: i for i in range(len(values))},
            )(self, *values)


def xor_pairs(size, mask):
    return [(i, i ^ mask) for i in range(size)]


class LineGather:
    def __init__(self, own, size, place):
        self.size, self.place = size, place
        self.ups, self.downs = [own], [own]

    def step(self, order=None):
        k, size = len(self.ups), self.size
        if order is not None:
            if k == 1:
                self.ups = self.downs = order.after(self.ups[0])
                self.downs = list(self.downs)
            else:
                self.ups[-1], self.downs[-1] = order.after(self.ups[-1], self.downs[-1])
        up, down = self.ups[-1], self.downs[-1]
        self.ups.append(lax.ppermute(up, "tensor", [(i, i + 1) for i in range(k - 1, size - 1)]))
        self.downs.append(lax.ppermute(down, "tensor", [(i + 1, i) for i in range(0, size - k)]))

    def hold(self, order):
        self.ups[-1], self.downs[-1] = order.after(self.ups[-1], self.downs[-1])

    def slot(self, j):
        groups = {}
        for at in range(self.size):
            groups.setdefault((at ^ j) - at, []).append(at)
        value = None
        for off, places in groups.items():
            arr = self.downs[off] if off >= 0 else self.ups[-off]
            if value is None:
                value = arr
            else:
                here = functools.reduce(jnp.logical_or, [self.place == at for at in places])
                value = jnp.where(here, arr, value)
        return value


def exchange(values):
    return lax.all_to_all(values, "tensor", 0, 0, tiled=True)


def rows_at(values, block, rows):
    return lax.dynamic_slice_in_dim(values, block * rows, rows, axis=0)


def cols_at(values, block, cols):
    return lax.dynamic_slice_in_dim(values, block * cols, cols, axis=1)


def give_body(places, *refs, two, last):
    out = refs[-1]
    if not two:
        out[...] = dot(refs[0][...], refs[1][...]).astype(BF)
        return

    @pl.when(pl.program_id(0) < last)
    def _():
        out[...] = dot(refs[0][...], refs[1][...]).astype(BF)

    @pl.when(pl.program_id(0) == last)
    def _():
        out[...] = second(refs[2:4], None).astype(BF)


def second(refs, rows):
    left, right = refs
    total, t = None, left.shape[2]
    for k in range(left.shape[0]):
        part = left[k] if rows is None else left[k, rows, :]
        term = dot(part, right[k * t : (k + 1) * t, :])
        total = term if total is None else total + term
    return total


def keep_body(places, *refs, two, last, lanes, chunks):
    ins = 4 if two else 2
    got, outs = refs[ins], refs[ins + 1 :]
    step = pl.program_id(0)
    rows = outs[0].shape[0]
    for lane in range(lanes):
        for rel in (1, 0):
            at = pl.multiple_of((places[1 + lane] ^ rel) * rows, rows)
            place = pl.ds(at, rows)
            out = outs[2 * lane + rel]
            inside = (step >= lane * chunks) & (step < (lane + 1) * chunks)

            @pl.when((inside & (step < last)) if two else inside)
            def _():
                total = dot(refs[0][place, :], refs[1][...])
                out[...] = (total + got[place, :].astype(F32)).astype(BF)

            if two and lane == lanes - 1:

                @pl.when(step == last)
                def _():
                    total = second(refs[2:4], place)
                    out[...] = (total + got[place, :].astype(F32)).astype(BF)


def fold_body(places, *refs):
    ins, outs = refs[:4], refs[4:]
    for h in (0, 1):
        total = (ins[2 * h][...].astype(F32) + ins[2 * h + 1][...].astype(F32)).astype(BF)
        if len(outs) == 2:
            outs[h][...] = total
        else:
            for rel in (0, 1):

                @pl.when(pl.program_id(0) == rel)
                def _():
                    outs[2 * h + rel][...] = total


def spread_body(places, *refs):
    ins, outs = refs[:4], refs[4:]
    for k in (0, 1):

        @pl.when(pl.program_id(0) == k)
        def _():
            for h in (0, 1):
                outs[h][...] = ins[2 * h + k][...]


def join_body(places, *refs):
    pieces, out = refs[:-1], refs[-1]
    step = pl.program_id(0) * 2 + pl.program_id(1)
    for k, piece in enumerate(pieces):

        @pl.when(step == k)
        def _():
            out[...] = piece[...]


def finish_body(core, mine, other, *outs, turned):
    for source, turn in ((mine, 0), (other, 1)):

        @pl.when(pl.program_id(0) == turn)
        def _():
            at = 0
            for k, out in enumerate(outs):
                flip = turned and k == len(outs) - 1
                width = out.shape[0] if flip else out.shape[1]
                value = source[:, at : at + width].astype(F32)
                out[...] = value.T if flip else value
                at += width


class Product:
    def __init__(self, left, right, widths, firsts, pair=()):
        self.left, self.right, self.widths, self.firsts, self.pair = left, right, widths, firsts, pair
        self.rows = left.shape[0] // 2
        self.cols = right.shape[1] + (pair[1].shape[1] if pair else 0)
        self.bn = min(512, widths[-1])


class Gradients:
    def __init__(self, products, count):
        self.count = count
        self.bits = count.bit_length() - 1
        self.index = lax.axis_index("dp")
        self.orders = [list(range(1, self.bits)), list(range(self.bits - 1, 0, -1))]
        self.step = 0
        self.kept, self.gots = [], []
        per = 2 // len(products)
        self.products = [
            Product(*p[:3], [o[0] for o in self.orders[i * per : (i + 1) * per]], p[3:])
            for i, p in enumerate(products)
        ]

    def bit(self, b):
        return (self.index >> b) & 1

    def scalars(self, *values):
        return jnp.stack([jnp.asarray(v, jnp.int32) for v in values])

    def swap(self, value, b):
        return lax.ppermute(value, "dp", xor_pairs(self.count, 1 << b))

    def operands(self, p, core):
        tokens, last = p.right.shape[0], p.right.shape[1] // p.bn
        specs = [
            pl.BlockSpec((p.rows, tokens), lambda n, s: (s[0], 0)),
            pl.BlockSpec((tokens, p.bn), lambda n, s: (0, jnp.minimum(n, last - 1))),
        ]
        if p.pair:
            count, _, t = p.pair[0].shape
            specs += [
                pl.BlockSpec((count, p.rows, t), lambda n, s: (0, s[0], 0)),
                pl.BlockSpec((tokens, p.bn), lambda n, s: (0, 0)),
            ]
        return specs, [p.left, p.right, *p.pair], dict(two=bool(p.pair), last=last)

    def give(self, order, at=0):
        p = self.products[at]
        specs, values, facts = self.operands(p, 1 - self.bit(0))
        (out,) = call(
            functools.partial(give_body, **facts),
            name="give",
            grid=(p.cols // p.bn,),
            scalars=1,
            in_specs=specs,
            out_specs=[pl.BlockSpec((p.rows, p.bn), lambda n, s: (0, n))],
            out_shape=[jax.ShapeDtypeStruct((p.rows, p.cols), BF)],
        )(order, self.scalars(1 - self.bit(0)), *values)
        p.got = self.swap(out, 0)

    def keep(self, order, at=0):
        p = self.products[at]
        lanes = len(p.firsts)
        rows, cols = p.rows // 2, p.cols // lanes
        chunks = cols // p.bn
        specs, values, facts = self.operands(p, self.bit(0))

        def out_spec(lane):
            return pl.BlockSpec(
                (rows, p.bn), lambda n, s: (0, jnp.clip(n - lane * chunks, 0, chunks - 1))
            )

        outs = call(
            functools.partial(keep_body, lanes=lanes, chunks=chunks, **facts),
            name="keep",
            grid=(lanes * chunks,),
            scalars=1,
            in_specs=specs + [pl.BlockSpec((p.rows, p.bn), lambda n, s: (0, n))],
            out_specs=[out_spec(k // 2) for k in range(2 * lanes)],
            out_shape=[jax.ShapeDtypeStruct((rows, cols), BF)] * (2 * lanes),
        )(order, self.scalars(self.bit(0), *[self.bit(b) for b in p.firsts]), *values, p.got)
        for h in range(lanes):
            self.kept.append(outs[2 * h])
            self.gots.append(self.swap(outs[2 * h + 1], p.firsts[h]))

    def fold(self, order):
        rows, cols = self.kept[0].shape
        self.step += 1
        more = self.step < self.bits - 1
        nexts = [self.bit(o[self.step]) for o in self.orders] if more else [0, 0]
        orows = rows // 2 if more else rows
        spec = lambda h: pl.BlockSpec((orows, cols), lambda r, s: (s[h] ^ r, 0))
        outs = call(
            fold_body,
            name="fold",
            grid=(2 if more else 1,),
            scalars=1,
            in_specs=[spec(0), spec(0), spec(1), spec(1)],
            out_specs=[pl.BlockSpec((orows, cols), lambda r, s: (0, 0))] * (4 if more else 2),
            out_shape=[jax.ShapeDtypeStruct((orows, cols), BF)] * (4 if more else 2),
        )(order, self.scalars(*nexts), self.kept[0], self.gots[0], self.kept[1], self.gots[1])
        self.kept = outs[:: 2 if more else 1]
        if more:
            self.gots = [self.swap(outs[1 + 2 * h], self.orders[h][self.step]) for h in (0, 1)]
        else:
            self.ask()

    def ask(self):
        self.step -= 1
        self.gots = [self.swap(k, o[self.step]) for k, o in zip(self.kept, self.orders)]

    def spread(self, order):
        rows, cols = self.kept[0].shape
        spec = pl.BlockSpec((rows, cols), lambda k, s: (0, 0))
        self.kept = call(
            spread_body,
            name="spread",
            grid=(2,),
            scalars=1,
            in_specs=[spec] * 4,
            out_specs=[
                pl.BlockSpec((rows, cols), lambda k, s: (k ^ s[0], 0)),
                pl.BlockSpec((rows, cols), lambda k, s: (k ^ s[1], 0)),
            ],
            out_shape=[jax.ShapeDtypeStruct((2 * rows, cols), BF)] * 2,
        )(
            order,
            self.scalars(*[self.bit(o[self.step]) for o in self.orders]),
            self.kept[0],
            self.gots[0],
            self.kept[1],
            self.gots[1],
        )
        self.ask()

    def join(self, order):
        brows, bcols = self.kept[0].shape
        lane = 0
        for p in self.products:
            lanes = range(lane, lane + len(p.firsts))
            lane += len(p.firsts)
            (p.half,) = call(
                join_body,
                name="join",
                grid=(len(lanes), 2),
                scalars=1,
                in_specs=[pl.BlockSpec((brows, bcols), lambda h, k, s: (0, 0))] * (2 * len(lanes)),
                out_specs=[pl.BlockSpec((brows, bcols), lambda h, k, s: (k ^ s[h], h))],
                out_shape=[jax.ShapeDtypeStruct((p.rows, p.cols), BF)],
            )(
                order,
                self.scalars(*[self.bit(self.orders[l][self.step]) for l in lanes]),
                *[v for l in lanes for v in (self.kept[l], self.gots[l])],
            )
            p.other = self.swap(p.half, 0)

    def finish(self, order, at=0):
        p = self.products[at]
        rows, cols = p.half.shape
        crows = min(256, rows)
        nblk = rows // crows
        turned = bool(p.pair)
        specs = [
            pl.BlockSpec((crows, w), lambda g, b, s: ((g ^ s[0]) * nblk + b, 0)) for w in p.widths
        ]
        shapes = [jax.ShapeDtypeStruct((2 * rows, w), F32) for w in p.widths]
        if turned:
            w = p.widths[-1]
            specs[-1] = pl.BlockSpec((w, crows), lambda g, b, s: (0, (g ^ s[0]) * nblk + b))
            shapes[-1] = jax.ShapeDtypeStruct((w, 2 * rows), F32)
        return call(
            functools.partial(finish_body, turned=turned),
            name="finish",
            grid=(2, nblk),
            scalars=1,
            in_specs=[
                pl.BlockSpec((crows, cols), lambda g, b, s: (jnp.where(g == 0, b, nblk - 1), 0)),
                pl.BlockSpec((crows, cols), lambda g, b, s: (jnp.where(g == 0, 0, b), 0)),
            ],
            out_specs=specs,
            out_shape=shapes,
        )(order, self.scalars(self.bit(0)), p.half, p.other)


class GainTotals:
    def __init__(self, parts, dp, tensor):
        self.size = parts[0].size
        self.value = jnp.concatenate([p.reshape(-1, 128) for p in parts], axis=0)
        self.left = []
        for name, size in (("tensor", tensor), ("dp", dp)):
            step = 1
            while step < size:
                masks = [step, 2 * step, 3 * step] if 2 * step < size else [step]
                self.left.append((name, size, masks))
                step *= 1 + len(masks)
        self.next()

    def next(self):
        name, size, masks = self.left.pop(0)
        self.got = [lax.ppermute(self.value, name, xor_pairs(size, m)) for m in masks]

    def step(self, order):
        self.value, *got = order.after(self.value, *self.got)
        self.value = self.value + got[0]
        if len(got) == 3:
            self.value = self.value + (got[1] + got[2])
        if self.left:
            self.next()

    def split(self, order):
        while self.left:
            self.step(order)
        self.step(order)
        value = self.value.reshape(-1)
        return [value[k : k + self.size] for k in range(0, value.size, self.size)]


def qkv_body(*refs):
    chunk, rows, wq, wk, wv, cos, sin = refs[:7]
    q_out, k_out, v_out, rows_out = refs[-4:]
    x = rows[...]
    cosine, sine = cos[...], sin[...]

    def turned(pre):
        out = []
        for h in range(pre.shape[1] // HD):
            one = pre[:, h * HD : (h + 1) * HD]
            out.append(one * cosine + pltpu.roll(one, HD // 2, 1) * sine)
        return jnp.concatenate(out, axis=1)

    q_out[...] = turned(dot(x, wq[...])).astype(BF)
    k_out[...] = turned(dot(x, wk[...])).astype(BF)
    v_out[...] = dot(x, wv[...]).astype(BF)
    part = rows_out.shape[0]
    rows_out[...] = rows[:, pl.ds(pl.multiple_of(pl.program_id(0) * part, part), part)].T


def qkv_slot(order, chunk, rows, w_query, w_key, w_value, cos, sin, held, count):
    t, d = rows.shape
    width = w_query.shape[1]
    bn = min(256, width)
    wspec = pl.BlockSpec((d, bn), lambda i, s: (0, i))
    tspec = pl.BlockSpec((t, HD), lambda i, s: (s[0], 0))
    return call(
        qkv_body,
        name="qkv",
        grid=(width // bn,),
        scalars=1,
        in_specs=[pl.BlockSpec((t, d), lambda i, s: (0, 0)), wspec, wspec, wspec, tspec, tspec]
        + [ANY] * len(held),
        out_specs=[pl.BlockSpec((t, bn), lambda i, s: (s[0], i))] * 3
        + [pl.BlockSpec((d // (width // bn), t), lambda i, s: (i, s[0]))],
        out_shape=[jax.ShapeDtypeStruct((count * t, width), BF)] * 3
        + [jax.ShapeDtypeStruct((d, count * t), BF)],
        aliases={7 + i: i for i in range(len(held))},
    )(order, chunk, rows, w_query, w_key, w_value, cos, sin, *held)


def attend_consts(seq_len):
    to_log2 = math.log2(math.e)
    return (to_log2 / math.sqrt(HD), math.log2(seq_len))


def attend_body(docs, q_ref, k_ref, v_ref, ids_col, ids_row, mix, acc, *, block):
    seq_len = q_ref.shape[0]
    scale, shift = attend_consts(seq_len)
    causal = lax.broadcasted_iota(jnp.int32, (block, block), 0) >= lax.broadcasted_iota(
        jnp.int32, (block, block), 1
    )

    def term(i, j):
        q = q_ref[i * block : (i + 1) * block, :]
        k = k_ref[j * block : (j + 1) * block, :]
        sig = 1.0 / (1.0 + jnp.exp2(shift - dot_nt(q, k) * scale))
        same = ids_col[i * block : (i + 1) * block, :] == ids_row[:, j * block : (j + 1) * block]
        allowed = same & causal if i == j else same
        probs = jnp.where(allowed, sig, 0.0).astype(BF)
        return dot(probs, v_ref[j * block : (j + 1) * block, :])

    for i in range(seq_len // block):
        acc[...] = term(i, i)
        for j in range(i):

            @pl.when(docs[(j + 1) * block - 1] == docs[i * block])
            def _():
                acc[...] += term(i, j)

        mix[i * block : (i + 1) * block, :] = acc[...].astype(BF)


def attend(order, docs, q, k, v):
    seq_len, width = q.shape
    block = 256
    head = pl.BlockSpec((seq_len, HD), lambda h, s: (0, h))
    return call(
        functools.partial(attend_body, block=block),
        name="attend",
        grid=(width // HD,),
        scalars=1,
        in_specs=[
            head,
            head,
            head,
            pl.BlockSpec((seq_len, 1), lambda h, s: (0, 0)),
            pl.BlockSpec((1, seq_len), lambda h, s: (0, 0)),
        ],
        out_specs=[head],
        out_shape=[jax.ShapeDtypeStruct((seq_len, width), BF)],
        scratch=[pltpu.VMEM((block, HD), F32)],
    )(order, docs, q, k, v, docs.reshape(-1, 1), docs.reshape(1, -1))


def attend_back_body(
    docs, q_ref, k_ref, v_ref, dmix, ids_col, ids_row, cos, sin, out, dq, dk, dv, *, block
):
    seq_len = q_ref.shape[0]
    scale, shift = attend_consts(seq_len)
    causal = lax.broadcasted_iota(jnp.int32, (block, block), 0) <= lax.broadcasted_iota(
        jnp.int32, (block, block), 1
    )

    def at(i):
        return slice(i * block, (i + 1) * block)

    def term(i, j):
        q, k, v, d = q_ref[at(i), :], k_ref[at(j), :], v_ref[at(j), :], dmix[at(i), :]
        sig = 1.0 / (1.0 + jnp.exp2(shift - dot_nt(k, q) * scale))
        same = ids_col[at(j), :] == ids_row[:, at(i)]
        allowed = same & causal if i == j else same
        probs = jnp.where(allowed, sig, 0.0)
        d_scores = (dot_nt(v, d) * probs * (1.0 - probs)).astype(BF)
        return dot_tn(d_scores, k), dot(d_scores, q), dot(probs.astype(BF), d)

    for i in range(seq_len // block):
        dq[at(i), :], dk[at(i), :], dv[at(i), :] = term(i, i)
    for i in range(seq_len // block):
        for j in range(i):

            @pl.when(docs[(j + 1) * block - 1] == docs[i * block])
            def _():
                a, b, c = term(i, j)
                dq[at(i), :] += a
                dk[at(j), :] += b
                dv[at(j), :] += c

    cosine, sine = cos[...], sin[...]

    def turned_back(v):
        v = v * (1.0 / math.sqrt(HD))
        return (v * cosine - pltpu.roll(v, HD // 2, 1) * sine).astype(BF)

    width = out.shape[1] // 3
    at_head = pl.program_id(0) * HD
    for part, value in enumerate((turned_back(dq[...]), turned_back(dk[...]), dv[...].astype(BF))):
        out[:, pl.ds(pl.multiple_of(at_head + part * width, HD), HD)] = value


def attend_back(order, docs, q, k, v, d_mix, cos, sin):
    seq_len, width = q.shape
    head = pl.BlockSpec((seq_len, HD), lambda h, s: (0, h))
    whole = lambda r, c: pl.BlockSpec((r, c), lambda h, s: (0, 0))
    return call(
        functools.partial(attend_back_body, block=256),
        name="attend_back",
        grid=(width // HD,),
        scalars=1,
        in_specs=[head] * 4
        + [whole(seq_len, 1), whole(1, seq_len), whole(seq_len, HD), whole(seq_len, HD)],
        out_specs=[whole(seq_len, 3 * width)],
        out_shape=[jax.ShapeDtypeStruct((seq_len, 3 * width), BF)],
        scratch=[pltpu.VMEM((seq_len, HD), F32)] * 3,
    )(order, docs, q, k, v, d_mix, docs.reshape(-1, 1), docs.reshape(1, -1), cos, sin)


def project_body(mix, w_ref, x_ref, gain, resid, normed, acc):
    parts, _, cols = w_ref.shape
    step = pl.program_id(0)

    @pl.when(step == 0)
    def _():
        acc[...] = x_ref[...].astype(F32)

    for p in range(parts):
        acc[:, p * cols : (p + 1) * cols] += dot(mix[...], w_ref[p])

    @pl.when(step == pl.num_programs(0) - 1)
    def _():
        resid[...] = acc[...]
        normed[...] = rms_scale(acc[...], gain[...]).astype(BF)


def project(order, mix, w_out, x, gain):
    t, d = x.shape
    width = mix.shape[1]
    parts, _, cols = w_out.shape
    whole = lambda r, c: pl.BlockSpec((r, c), lambda i: (0, 0))
    return call(
        project_body,
        name="project",
        grid=(mix.shape[0] // t,),
        scalars=0,
        in_specs=[
            pl.BlockSpec((t, width), lambda i: (i, 0)),
            pl.BlockSpec((parts, width, cols), lambda i: (0, i, 0)),
            whole(t, d),
            whole(1, d),
        ],
        out_specs=[whole(t, d)] * 2,
        out_shape=[jax.ShapeDtypeStruct((t, d), F32), jax.ShapeDtypeStruct((t, d), BF)],
        scratch=[pltpu.VMEM((t, d), F32)],
    )(order, mix, w_out, x, gain.reshape(1, -1))


def norm_back(d_normed, rows, gain):
    r = lax.rsqrt(jnp.mean(rows * rows, axis=-1, keepdims=True) + EPS)
    u = rows * r
    scaled = d_normed * gain
    d_rows = r * (scaled - u * jnp.mean(scaled * u, axis=-1, keepdims=True))
    return d_rows, jnp.sum(d_normed * u, axis=0, keepdims=True)


def middle_body(d_ref, resid, cot, gain, w_ref, out, d_resid, low_t, part, low):
    parts, _, cols = w_ref.shape

    @pl.when(pl.program_id(0) == 0)
    def _():
        d_rows, part[...] = norm_back(d_ref[...].astype(F32), resid[...], gain[...])
        total = cot[...].astype(F32) + d_rows
        d_resid[...] = total
        low[...] = total.astype(BF)
        low_t[...] = low[...].T

    total = None
    for p in range(parts):
        term = dot_nt(low[:, p * cols : (p + 1) * cols], w_ref[p])
        total = term if total is None else total + term
    out[...] = total.astype(BF)


def middle(order, d_normed2, resid, cot, gain, w_out, width):
    t, d = resid.shape
    parts, rows, cols = w_out.shape
    count = rows // width
    whole = lambda r, c: pl.BlockSpec((r, c), lambda i: (0, 0))
    return call(
        middle_body,
        name="middle",
        grid=(count,),
        scalars=0,
        in_specs=[whole(t, d)] * 3
        + [whole(1, d), pl.BlockSpec((parts, width, cols), lambda i: (0, i, 0))],
        out_specs=[
            pl.BlockSpec((t, width), lambda i: (i, 0)),
            whole(t, d),
            whole(d, t),
            whole(1, d),
        ],
        out_shape=[
            jax.ShapeDtypeStruct((count * t, width), BF),
            jax.ShapeDtypeStruct((t, d), F32),
            jax.ShapeDtypeStruct((d, t), BF),
            jax.ShapeDtypeStruct((1, d), F32),
        ],
        scratch=[pltpu.VMEM((t, d), BF)],
    )(order, d_normed2, resid, cot, gain.reshape(1, -1), w_out)


def last_body(d_ref, x_ref, d_resid, gain, out, part):
    d_rows, part[...] = norm_back(d_ref[...].astype(F32), x_ref[...].astype(F32), gain[...])
    out[...] = (d_resid[...] + d_rows).astype(BF)


def last(order, d_normed, x, d_resid, gain):
    t, d = x.shape
    whole = lambda r, c: pl.BlockSpec((r, c), lambda i: (0, 0))
    return call(
        last_body,
        name="last",
        grid=(1,),
        scalars=0,
        in_specs=[whole(t, d)] * 3 + [whole(1, d)],
        out_specs=[whole(t, d), whole(1, d)],
        out_shape=[jax.ShapeDtypeStruct((t, d), BF), jax.ShapeDtypeStruct((1, d), F32)],
    )(order, d_normed, x, d_resid, gain.reshape(1, -1))


def back_project_body(d_ref, wq, wk, wv, out):
    total = None
    width = wq.shape[1]
    for k, w in enumerate((wq, wk, wv)):
        term = dot_nt(d_ref[:, k * width : (k + 1) * width], w[...])
        total = term if total is None else total + term
    out[...] = total.astype(BF)


def back_project(order, d_qkv, w_query, w_key, w_value):
    seq_len, wide = d_qkv.shape
    d, width = w_query.shape
    bn = 512
    wspec = pl.BlockSpec((bn, width), lambda i: (i, 0))
    return call(
        back_project_body,
        name="back_project",
        grid=(d // bn,),
        scalars=0,
        in_specs=[pl.BlockSpec((seq_len, wide), lambda i: (0, 0)), wspec, wspec, wspec],
        out_specs=[pl.BlockSpec((seq_len, bn), lambda i: (0, i))],
        out_shape=[jax.ShapeDtypeStruct((seq_len, d), BF)],
    )(order, d_qkv, w_query, w_key, w_value)[0]


def ffn_body(*refs):
    chunk, rows, cot, wg, wu, wd = refs[:6]
    inner, d_gate, d_up, rows_out, cot_out, d_rows, down, acc_d, acc_o = refs[-9:]
    step, last = pl.program_id(0), pl.num_programs(0) - 1
    x = rows[...]
    gate = dot(x, wg[...])
    up = dot(x, wu[...])
    sig = sigmoid(gate)
    silu = gate * sig
    inner_b = (silu * up).astype(BF)
    inner[...] = inner_b.T
    part = rows_out.shape[0]
    rows_out[...] = rows[:, pl.ds(pl.multiple_of(step * part, part), part)].T
    d_inner = dot_nt(cot[...], wd[...])
    dg = (d_inner * up * (sig * (1.0 + gate * (1.0 - sig)))).astype(BF)
    du = (d_inner * silu).astype(BF)
    d_gate[...] = dg
    d_up[...] = du
    term_o = dot(inner_b, wd[...])
    term_d = dot_nt(dg, wg[...]) + dot_nt(du, wu[...])

    @pl.when(step == 0)
    def _():
        acc_o[...] = term_o
        acc_d[...] = term_d
        cot_out[...] = cot[...]

    @pl.when(step > 0)
    def _():
        acc_o[...] += term_o
        acc_d[...] += term_d

    @pl.when(step == last)
    def _():
        d_rows[...] = acc_d[...].astype(BF)
        down[...] = acc_o[...].astype(BF)


def ffn_slot(order, chunk, rows, cot, w_gate, w_up, w_down, held, count):
    t, d = rows.shape
    hidden = w_gate.shape[1]
    bh = min(512, hidden)
    steps = hidden // bh
    wcol = pl.BlockSpec((d, bh), lambda i, s: (0, i))
    part = pl.BlockSpec((t, bh), lambda i, s: (s[0], i))
    line = pl.BlockSpec((t, d), lambda i, s: (s[0], 0))
    return call(
        ffn_body,
        name="ffn",
        grid=(hidden // bh,),
        scalars=1,
        in_specs=[
            pl.BlockSpec((t, d), lambda i, s: (0, 0)),
            pl.BlockSpec((t, d), lambda i, s: (0, 0)),
            wcol,
            wcol,
            pl.BlockSpec((bh, d), lambda i, s: (i, 0)),
        ]
        + [ANY] * len(held),
        out_specs=[pl.BlockSpec((bh, t), lambda i, s: (i, s[0])), part, part]
        + [pl.BlockSpec((d // steps, t), lambda i, s: (i, s[0])), line, line, line],
        out_shape=[jax.ShapeDtypeStruct((hidden, count * t), BF)]
        + [jax.ShapeDtypeStruct((count * t, hidden), BF)] * 2
        + [jax.ShapeDtypeStruct((d, count * t), BF)]
        + [jax.ShapeDtypeStruct((count * t, d), BF)] * 3,
        scratch=[pltpu.VMEM((t, d), F32)] * 2,
        aliases={6 + i: i for i in range(len(held))},
    )(order, chunk, rows, cot, w_gate, w_up, w_down, *held)


def local(
    layer_in,
    cotangent,
    doc_ids,
    positions,
    attn_gain,
    w_query,
    w_key,
    w_value,
    w_out,
    ffn_gain,
    w_gate,
    w_up,
    w_down,
    *,
    dp,
    tensor,
):
    t, d = layer_in.shape
    width = w_query.shape[1]
    hidden = w_gate.shape[1]
    place = lax.axis_index("tensor")
    chunks = jnp.stack([place ^ j for j in range(tensor)]).astype(jnp.int32)
    chunk = [chunks[j : j + 1] for j in range(tensor)]
    order = Order()

    share = w_out.shape[1] // dp
    w_cols = lax.all_gather(
        cols_at(w_out, lax.axis_index("dp"), share), "tensor", axis=0, tiled=True
    )
    half = HD // 2
    freqs = ROPE_BASE ** (-(jnp.arange(half).astype(F32) * 2.0) / HD)
    angles = positions.astype(F32)[:, None] * freqs[None, :]
    cosine, sine = jnp.cos(angles), jnp.sin(angles)
    cos = jnp.concatenate([cosine, cosine], axis=1)
    sin = jnp.concatenate([-sine, sine], axis=1)

    normed_own = rms_scale(layer_in.astype(F32), attn_gain).astype(BF)
    line = LineGather(normed_own, tensor, place)
    line.step()
    held = []
    for j in range(tensor):
        if 0 < j < tensor - 1:
            line.step(order)
        if j == tensor - 1:
            cots = LineGather(cotangent, tensor, place)
            cots.step(order)
        held = qkv_slot(order, chunk[j], line.slot(j), w_query, w_key, w_value, cos, sin, held, tensor)
        if j == 1:
            (w_cols,) = order.after(w_cols)
            w_out_all = lax.all_gather(w_cols, "dp", axis=0)
    query, key, value, normed_t = held
    (mixed,) = attend(order, doc_ids, query, key, value)
    mix = exchange(mixed)
    cots.step(order)
    resid, normed2_own = project(order, mix, w_out_all, layer_in, ffn_gain)

    weights = (w_gate, w_up, w_down)
    line = LineGather(normed2_own, tensor, place)
    line.step()
    held = ffn_slot(order, chunk[0], line.slot(0), cotangent, *weights, [], tensor)
    for j in range(1, tensor):
        if j < tensor - 1:
            line.step(order)
            if len(cots.ups) < tensor:
                cots.step(order)
        else:
            cots.hold(order)
            line.hold(order)
        held = ffn_slot(order, chunk[j], line.slot(j), cots.slot(j), *weights, held, tensor)
    inner_t, d_gate, d_up, normed2_t, cot_all, d_normed2_part, down_part = held
    d_normed2 = lax.psum_scatter(d_normed2_part, "tensor", scatter_dimension=0, tiled=True)

    first = Gradients([(inner_t, cot_all, [d])], dp)
    wide = Gradients([(normed2_t, d_gate, [hidden]), (normed2_t, d_up, [hidden])], dp)
    more = range(first.bits - 2)

    first.give(order)
    wide.give(order, 0)
    wide.give(order, 1)
    first.keep(order)
    wide.keep(order, 0)
    wide.keep(order, 1)
    first.fold(order)
    for _ in more:
        first.fold(order)
    d_mix, d_resid, d_resid_t, ffn_gain_part = middle(
        order, d_normed2, resid, cotangent, ffn_gain, w_out_all, width
    )
    d_mix = exchange(d_mix)
    d_resid_all = lax.all_gather(d_resid_t, "tensor", axis=0)
    for _ in more:
        first.spread(order)
    wide.fold(order)
    (d_qkv,) = attend_back(order, doc_ids, query, key, value, d_mix, cos, sin)
    downs = exchange(order.after(down_part)[0]).reshape(tensor, t, d)
    d_normed = lax.psum_scatter(
        back_project(order, d_qkv, w_query, w_key, w_value),
        "tensor",
        scatter_dimension=0,
        tiled=True,
    )
    first.join(order)
    for _ in more:
        wide.fold(order)
    for _ in more:
        wide.spread(order)
    attn = Gradients([(normed_t, d_qkv, [width] * 4, d_resid_all, mixed)], dp)
    attn.give(order)
    attn.keep(order)
    wide.join(order)
    (down_grad,) = first.finish(order)
    attn.fold(order)
    (gate_grad,) = wide.finish(order, 0)
    for _ in more:
        attn.fold(order)
    in_grad, attn_gain_part = last(order, d_normed, layer_in, d_resid, attn_gain)
    totals = GainTotals([attn_gain_part, ffn_gain_part], dp, tensor)
    (up_grad,) = wide.finish(order, 1)
    totals.step(order)
    for _ in more:
        attn.spread(order)
    attn_gain_grad, ffn_gain_grad = totals.split(order)
    attn.join(order)
    query_grad, key_grad, value_grad, out_grad = attn.finish(order)
    layer_out = (resid + jnp.sum(downs.astype(F32), axis=0)).astype(BF)
    return (
        layer_out,
        in_grad,
        attn_gain_grad,
        query_grad,
        key_grad,
        value_grad,
        out_grad,
        ffn_gain_grad,
        gate_grad,
        up_grad,
        down_grad,
    )


def solution(mesh):
    rows, cols, lines = P(("dp", "tensor"), None), P(None, "tensor"), P("tensor", None)
    return jax.shard_map(
        functools.partial(local, dp=mesh.shape["dp"], tensor=mesh.shape["tensor"]),
        mesh=mesh,
        in_specs=(
            rows, rows, P("dp"), P("dp"), P(), cols, cols, cols, lines, P(), cols, cols, lines
        ),
        out_specs=(rows, rows, P(), cols, cols, cols, lines, P(), cols, cols, lines),
        check_vma=False,
    )
```

time: 1040 us -> 796 us (0.77)
  waiting for transfers between devices: 479 us -> 257 us
  Pallas kernels: 208 us -> 371 us
  matrix products: 73.6 us -> 0 us
  local copies, waits for them, and re-layouts: 84.4 us -> 26.7 us
  starting transfers between devices: 128 us -> 80.2 us
    ppermute x9, waiting for transfers between devices: 230 us -> 47.5 us  [step(): lax.ppermute(down, 'tensor', [(i + 1, i) for i in range(0, size - k)])]
    pallas_call x28 -> x53, Pallas kernels: 208 us -> 371 us  [run(): pl.pallas_call(whole, grid_spec=pltpu.PrefetchScalarGridSpec(num_scalar_p...]
    dot_general x12 -> x0, matrix products: 73.6 us -> none  [the longest x10 59.2 us: dot_tn(): lax.dot_general(left, right, (((0,), (0,)), ((), ())), preferred_element_...]
    unnamed x288 -> x137, local copies, waits for them, and re-layouts: 71.3 us -> 23.7 us
    ppermute x60 -> x32, waiting for transfers between devices: 162 us -> 117 us  [swap(): return lax.ppermute(value, 'dp', xor_pairs(self.count, 1 << b))]
    ppermute x9, waiting for transfers between devices: 57.3 us -> 20.9 us  [step(): lax.ppermute(up, 'tensor', [(i, i + 1) for i in range(k - 1, size - 1)])]
    ppermute x16 -> x7, starting transfers between devices: 38.4 us -> 7.86 us  [next(): lax.ppermute(self.value, name, xor_pairs(size, m))]
    ppermute x16 -> x7, waiting for transfers between devices: 28.7 us -> 56.1 us  [next(): lax.ppermute(self.value, name, xor_pairs(size, m))]
  transfers between devices with their start and end apart: 99 -> 65, of which waited for: 41 -> 25; matrix products, arithmetic and copies ran while one was open for 11% -> 5% of each run, Pallas kernels for 16% -> 41%
where the time goes in v2:
time: 796 us; the launch traced here: 788 us
  Pallas kernels  371 us (47%)
  waiting for transfers between devices  257 us (32%)
  starting transfers between devices  80.2 us (10%)
  other arithmetic  37.7 us (5%)
  local copies, waits for them, and re-layouts  26.7 us (3%)
  between operations  15 us (2%)
    pallas_call x53, Pallas kernels, run(): pl.pallas_call(whole, grid_spec=pltpu.PrefetchScalarGridSpec(num_scalar_p...  371 us
    ppermute x32, waiting for transfers between devices, swap(): return lax.ppermute(value, 'dp', xor_pairs(self.count, 1 << b))  117 us
    ppermute x7, waiting for transfers between devices, next(): lax.ppermute(self.value, name, xor_pairs(size, m))  56.1 us
    ppermute x9, waiting for transfers between devices, step(): lax.ppermute(down, 'tensor', [(i + 1, i) for i in range(0, size - k)])  47.5 us
    ppermute x32, starting transfers between devices, swap(): return lax.ppermute(value, 'dp', xor_pairs(self.count, 1 << b))  31.9 us
    unnamed x137, local copies, waits for them, and re-layouts  23.7 us
    ppermute x9, waiting for transfers between devices, step(): lax.ppermute(up, 'tensor', [(i, i + 1) for i in range(k - 1, size - 1)])  20.9 us
    select_n x9, other arithmetic, slot(): value = jnp.where(here, arr, value)  19 us
  transfers between devices with their start and end apart: 65, of which 25 were waited for; matrix products, arithmetic and copies ran while one was open for 5% of the time, Pallas kernels for 41%

profile of v2, /device:TPU:0, one launch (start us, length us, event | category | flops | bytes accessed | tf_op | source)
XLA Modules:
  0.0 787.9 jit_solution(13618225449409957933)
XLA Ops:
  28.1 20.9 %collective-permute-done.refs_0_ = bf16[256,2048]{1,0:T(8,128)(2,1)S(1)} collective-permute-done((bf16[256,2048]{1,0:T(8,128)(2,1)}, bf16[256,2048]{1,0:T(8,128)(2,1)S(1)}, u32[]{:S(2)}, u32[]{:S(2)}) %collective-permute-start) | collective-permute-done | bytes 1048608 | tf_op jit(solution)/shard_map/ppermute | solution.py:119
  49.1 10.9 %collective-permute-done.1.refs_1_ = bf16[256,2048]{1,0:T(8,128)(2,1)} collective-permute-done((bf16[256,2048]{1,0:T(8,128)(2,1)}, bf16[256,2048]{1,0:T(8,128)(2,1)}, u32[]{:S(2)}, u32[]{:S(2)}) %collective-permute-start.1) | collective-permute-done | bytes 1048608 | tf_op jit(solution)/shard_map/ppermute | solution.py:120
  74.6 19.5 %collective-permute-done.3.refs_1_ = bf16[256,2048]{1,0:T(8,128)(2,1)S(1)} collective-permute-done((bf16[256,2048]{1,0:T(8,128)(2,1)}, bf16[256,2048]{1,0:T(8,128)(2,1)S(1)}, u32[]{:S(2)}, u32[]{:S(2)}) %collective-permute-start.3) | collective-permute-done | bytes 1048608 | tf_op jit(solution)/shard_map/ppermute | solution.py:120
  112.4 12.3 %collective-permute-done.5 = bf16[256,2048]{1,0:T(8,128)(2,1)S(1)} collective-permute-done((bf16[256,2048]{1,0:T(8,128)(2,1)}, bf16[256,2048]{1,0:T(8,128)(2,1)S(1)}, u32[]{:S(2)}, u32[]{:S(2)}) %collective-permute-start.5) | collective-permute-done | bytes 1048608 | tf_op jit(solution)/shard_map/ppermute | solution.py:120
  131.4 13.6 %attend.1 = (bf16[1024,512]{1,0:T(8,128)(2,1)}, f32[8,128]{1,0:T(8,128)}) custom-call(s32[1024]{0:T(1024)} %refs_0_.4, bf16[1024,512]{1,0:T(8,128)(2,1)} %get-tuple-element.221.refs_1_, bf16[1024,512]{1,0:T(8,128)(2,1)} %get-tuple-element.222.refs_2_, bf16[1024,512]{1,0:T(8,128)(2,1)} %get-tuple-element.223.refs_3_, s32[1024,1]{1,0:T(8,128)} %copy.86.refs_4_.refs_5_, ...), custom_call_target="tpu_custom_call" | custom-call | flops 11000000512 | bytes 11000000 | tf_op jit(solution)/shard_map/attend/pallas_call | solution.py:57
  155.9 15.1 %all-to-all-done = bf16[4,256,512]{2,1,0:T(8,128)(2,1)} async-done(((bf16[4,256,512]{2,1,0:T(8,128)(2,1)}), bf16[4,256,512]{2,1,0:T(8,128)(2,1)}, u32[]{:S(2)}, u32[]{:S(2)}) %all-to-all-start) | async-done | bytes 1048608 | tf_op jit(solution)/shard_map/all_to_all | solution.py:141
  182.0 22.2 %ffn.4 = (bf16[2048,1024]{1,0:T(8,128)(2,1)}, bf16[1024,2048]{1,0:T(8,128)(2,1)}, bf16[1024,2048]{1,0:T(8,128)(2,1)}, bf16[2048,1024]{1,0:T(8,128)(2,1)}, bf16[1...) custom-call(s32[1]{0:T(128)} %bitcast.1.refs_0_, ...), custom_call_target="tpu_custom_call" | custom-call | flops 22000001024 | bytes 22000000 | tf_op jit(solution)/shard_map/ffn/pallas_call | solution.py:57
  214.6 22.4 %ffn.5 = (bf16[2048,1024]{1,0:T(8,128)(2,1)}, bf16[1024,2048]{1,0:T(8,128)(2,1)}, bf16[1024,2048]{1,0:T(8,128)(2,1)}, bf16[2048,1024]{1,0:T(8,128)(2,1)}, bf16[1...) custom-call(s32[1]{0:T(128)} %bitcast.2.refs_0_, ...), custom_call_target="tpu_custom_call", output_to_operand_aliasing={{0}: (6, {}), {1}: (7, {}), {2}: (8, {}), {3}: (9, {}), {4}... | custom-call | flops 22000001024 | bytes 22000000 | tf_op jit(solution)/shard_map/ffn/pallas_call | solution.py:57
  246.6 22.3 %ffn.6 = (bf16[2048,1024]{1,0:T(8,128)(2,1)}, bf16[1024,2048]{1,0:T(8,128)(2,1)}, bf16[1024,2048]{1,0:T(8,128)(2,1)}, bf16[2048,1024]{1,0:T(8,128)(2,1)}, bf16[1...) custom-call(s32[1]{0:T(128)} %bitcast.3.refs_0_, ...), custom_call_target="tpu_custom_call", output_to_operand_aliasing={{0}: (6, {}), {1}: (7, {}), {2}: (8, {}), {3}: (9, {}), {4}... | custom-call | flops 22000001024 | bytes 22000000 | tf_op jit(solution)/shard_map/ffn/pallas_call | solution.py:57
  279.9 22.2 %ffn.7 = (bf16[2048,1024]{1,0:T(8,128)(2,1)}, bf16[1024,2048]{1,0:T(8,128)(2,1)}, bf16[1024,2048]{1,0:T(8,128)(2,1)}, bf16[2048,1024]{1,0:T(8,128)(2,1)}, bf16[1...) custom-call(s32[1]{0:T(128)} %bitcast.refs_0_, ...), custom_call_target="tpu_custom_call", output_to_operand_aliasing={{0}: (6, {}), {1}: (7, {}), {2}: (8, {}), {3}: (9, {}), {4}... | custom-call | flops 22000001024 | bytes 22000000 | tf_op jit(solution)/shard_map/ffn/pallas_call | solution.py:57
  330.5 10.8 %keep.4 = (bf16[512,1024]{1,0:T(8,128)(2,1)}, bf16[512,1024]{1,0:T(8,128)(2,1)}, bf16[512,1024]{1,0:T(8,128)(2,1)}, bf16[512,1024]{1,0:T(8,128)(2,1)}, f32[8,128]{1,0:T(8,128)}) custom-call(s32[3]{0:T(128)} %pad_add_fusion.1.refs_0_, bf16[2048,1024]{1,0:T(8,128)(2,1)} %get-tuple-element.276.refs_1_, bf16[1024,2048]{1,0:T(8,128)(2,1)} %get-tuple-element.277.refs_2_, ...), custom_call_target="tpu_custom_call" | custom-call | flops 10000000000 | bytes 10000000 | tf_op jit(solution)/shard_map/keep/pallas_call | solution.py:57
  384.1 10.9 %collective-permute-done.23.refs_2_ = bf16[256,1024]{1,0:T(8,128)(2,1)S(1)} collective-permute-done((bf16[256,1024]{1,0:T(8,128)(2,1)}, bf16[256,1024]{1,0:T(8,128)(2,1)S(1)}, u32[]{:S(2)}, u32[]{:S(2)}) %collective-permute-start.23) | collective-permute-done | bytes 524320 | tf_op jit(solution)/shard_map/ppermute | solution.py:279
  417.2 33.0 %collective-permute-done.27.refs_2_ = bf16[256,1024]{1,0:T(8,128)(2,1)S(1)} collective-permute-done((bf16[256,1024]{1,0:T(8,128)(2,1)S(1)}, bf16[256,1024]{1,0:T(8,128)(2,1)S(1)}, u32[]{:S(2)}, u32[]{:S(2)}) %collective-permute-start.27) | collective-permute-done | bytes 524320 | tf_op jit(solution)/shard_map/ppermute | solution.py:279
  468.6 21.3 %attend_back.1 = (bf16[1024,1536]{1,0:T(8,128)(2,1)}, f32[8,128]{1,0:T(8,128)}) custom-call(s32[1024]{0:T(1024)} %refs_0_.4, bf16[1024,512]{1,0:T(8,128)(2,1)} %get-tuple-element.221.refs_1_, bf16[1024,512]{1,0:T(8,128)(2,1)} %get-tuple-element.222.refs_2_, bf16[1024,512]{1,0:T(8,128)(2,1)} %get-tuple-element.223.refs_3_, bf16[1024,512]{1,0:T(8,128)(2,1)} %bitcast.27, ...), custom_call_target="tpu_custom_call" | custom-call | flops 16999999488 | bytes 17000000 | tf_op jit(solution)/shard_map/attend_back/pallas_call | solution.py:57
  490.5 11.0 %back_project.1 = (bf16[1024,2048]{1,0:T(8,128)(2,1)}, f32[8,128]{1,0:T(8,128)}) custom-call(bf16[1024,1536]{1,0:T(8,128)(2,1)} %get-tuple-element.313.refs_0_.refs_2_, bf16[2048,512]{1,0:T(8,128)(2,1)} %refs_1_.2, bf16[2048,512]{1,0:T(8,128)(2,1)} %refs_2_.15, bf16[2048,512]{1,0:T(8,128)(2,1)} %refs_3_.17, f32[8,128]{1,0:T(8,128)} %get-tuple-element.314.refs_4_), custom_call_target="tpu_custom_call" | custom-call | flops 11000000512 | bytes 11000000 | tf_op jit(solution)/shard_map/back_project/pallas_call | solution.py:57
  514.3 20.1 %collective-permute-done.33.refs_2_ = bf16[256,2048]{1,0:T(8,128)(2,1)S(1)} collective-permute-done((bf16[256,2048]{1,0:T(8,128)(2,1)}, bf16[256,2048]{1,0:T(8,128)(2,1)S(1)}, u32[]{:S(2)}, u32[]{:S(2)}) %collective-permute-start.33) | collective-permute-done | bytes 1048608 | tf_op jit(solution)/shard_map/ppermute | solution.py:279
  558.6 11.8 %keep.7 = (bf16[512,1024]{1,0:T(8,128)(2,1)}, bf16[512,1024]{1,0:T(8,128)(2,1)}, bf16[512,1024]{1,0:T(8,128)(2,1)}, bf16[512,1024]{1,0:T(8,128)(2,1)}, f32[8,128]{1,0:T(8,128)}) custom-call(s32[3]{0:T(128)} %pad_add_fusion.1.refs_0_, bf16[2048,1024]{1,0:T(8,128)(2,1)} %get-tuple-element.317.refs_1_, bf16[1024,1536]{1,0:T(8,128)(2,1)} %get-tuple-element.313.refs_0_.refs_2_, ...), custom_call_target="tpu_custom_call" | custom-call | flops 10000000000 | bytes 10000000 | tf_op jit(solution)/shard_map/keep/pallas_call | solution.py:57
  570.4 29.0 %collective-permute-done.40.refs_2_ = bf16[512,2048]{1,0:T(8,128)(2,1)S(1)} collective-permute-done((bf16[512,2048]{1,0:T(8,128)(2,1)}, bf16[512,2048]{1,0:T(8,128)(2,1)S(1)}, u32[]{:S(2)}, u32[]{:S(2)}) %collective-permute-start.40) | collective-permute-done | bytes 2097184 | tf_op jit(solution)/shard_map/ppermute | solution.py:279
  617.9 11.0 %finish.4 = (f32[2048,2048]{1,0:T(8,128)}, f32[8,128]{1,0:T(8,128)}) custom-call(s32[1]{0:T(128)} %bitcast.12.refs_0_, bf16[1024,2048]{1,0:T(8,128)(2,1)} %get-tuple-element.337.refs_1_, bf16[1024,2048]{1,0:T(8,128)(2,1)} %collective-permute-done.38.refs_2_, f32[8,128]{1,0:T(8,128)} %get-tuple-element.342.refs_3_), custom_call_target="tpu_custom_call" | custom-call | flops 11000000512 | bytes 11000000 | tf_op jit(solution)/shard_map/finish/pallas_call | solution.py:57
  643.8 11.0 %finish.5 = (f32[2048,2048]{1,0:T(8,128)}, f32[8,128]{1,0:T(8,128)}) custom-call(s32[1]{0:T(128)} %bitcast.12.refs_0_, bf16[1024,2048]{1,0:T(8,128)(2,1)} %get-tuple-element.348.refs_1_, bf16[1024,2048]{1,0:T(8,128)(2,1)} %collective-permute-done.43.refs_2_, f32[8,128]{1,0:T(8,128)} %get-tuple-element.349.refs_3_), custom_call_target="tpu_custom_call" | custom-call | flops 11000000512 | bytes 11000000 | tf_op jit(solution)/shard_map/finish/pallas_call | solution.py:57
  672.5 11.0 %finish.6 = (f32[2048,2048]{1,0:T(8,128)}, f32[8,128]{1,0:T(8,128)}) custom-call(s32[1]{0:T(128)} %bitcast.12.refs_0_, bf16[1024,2048]{1,0:T(8,128)(2,1)} %get-tuple-element.355.refs_1_, bf16[1024,2048]{1,0:T(8,128)(2,1)} %collective-permute-done.47.refs_2_, f32[8,128]{1,0:T(8,128)} %get-tuple-element.356.refs_3_), custom_call_target="tpu_custom_call" | custom-call | flops 11000000512 | bytes 11000000 | tf_op jit(solution)/shard_map/finish/pallas_call | solution.py:57
  691.0 25.5 %collective-permute-done.45.refs_2_ = f32[32,128]{1,0:T(8,128)S(1)} collective-permute-done((f32[32,128]{1,0:T(8,128)S(1)}, f32[32,128]{1,0:T(8,128)S(1)}, u32[]{:S(2)}, u32[]{:S(2)}) %collective-permute-start.45) | collective-permute-done | bytes 16416 | tf_op jit(solution)/shard_map/ppermute | solution.py:448
  727.5 20.8 %collective-permute-done.49.refs_2_ = f32[32,128]{1,0:T(8,128)S(1)} collective-permute-done((f32[32,128]{1,0:T(8,128)S(1)}, f32[32,128]{1,0:T(8,128)S(1)}, u32[]{:S(2)}, u32[]{:S(2)}) %collective-permute-start.49) | collective-permute-done | bytes 16416 | tf_op jit(solution)/shard_map/ppermute | solution.py:448
  769.5 11.4 %finish.7 = (f32[2048,512]{1,0:T(8,128)}, f32[2048,512]{1,0:T(8,128)}, f32[2048,512]{1,0:T(8,128)}, f32[512,2048]{1,0:T(8,128)}, f32[8,128]{1,0:T(8,128)}) custom-call(s32[1]{0:T(128)} %bitcast.12.refs_0_, bf16[1024,2048]{1,0:T(8,128)(2,1)} %get-tuple-element.376.refs_1_, bf16[1024,2048]{1,0:T(8,128)(2,1)} %collective-permute-done.56.refs_2_, ...), custom_call_target="tpu_custom_call" | custom-call | flops 11000000512 | bytes 11000000 | tf_op jit(solution)/shard_map/finish/pallas_call | solution.py:57
  (332 shorter events, 353.0 us)
Async XLA Ops:
  7.2 61.4 %all-gather.6.cloned.1.call-start = ((), (), s32[]{:S(2)}) async-start(), calls=%async_computation.5 | async-start | bytes 1310720 | tf_op jit(solution)/shard_map/all_gather | solution.py:857
  16.4 43.6 %collective-permute-start.1 = (bf16[256,2048]{1,0:T(8,128)(2,1)}, bf16[256,2048]{1,0:T(8,128)(2,1)}, u32[]{:S(2)}, u32[]{:S(2)}) collective-permute-start(bf16[256,2048]{1,0:T(8,128)(2,1)} %fusion.2.refs_1_), channel_id=1, source_target_pairs={{1,0},{2,1},{3,2},{5,4},{6,5},{7,6},{9,8},{10,9},{11,10},{13,12},{... | collective-permute-start | bytes 3145736 | tf_op jit(solution)/shard_map/ppermute | solution.py:120
  18.5 152.5 %all-gather.8.cloned.1.call-start = ((), (), s32[]{:S(2)}) async-start(), calls=%async_computation.8 | async-start | bytes 9437184 | tf_op jit(solution)/shard_map/all_gather | solution.py:880
  149.3 251.9 %reduce-scatter.3.cloned.1.call-start = ((), (), s32[]{:S(2)}) async-start(), calls=%async_computation.6 | async-start | bytes 5242880 | tf_op jit(solution)/shard_map/reduce_scatter | solution.py:901
  151.3 59.3 %collective-permute-start.12 = (bf16[256,2048]{1,0:T(8,128)(2,1)}, bf16[256,2048]{1,0:T(8,128)(2,1)S(1)}, u32[]{:S(2)}, u32[]{:S(2)}) collective-permute-start(bf16[256,2048]{1,0:T(8,128)(2,1)} %get-tuple-element.236), channel_id=1, source_target_pairs={{1,2},{2,3},{5,6},{6,7},{9,10},{10,11},{13,14},{14,15},{17,18},{18... | collective-permute-start | bytes 3145736 | tf_op jit(solution)/shard_map/ppermute | solution.py:119
  152.0 58.6 %collective-permute-start.13 = (bf16[256,2048]{1,0:T(8,128)(2,1)}, bf16[256,2048]{1,0:T(8,128)(2,1)S(1)}, u32[]{:S(2)}, u32[]{:S(2)}) collective-permute-start(bf16[256,2048]{1,0:T(8,128)(2,1)} %get-tuple-element.237), channel_id=1, source_target_pairs={{1,0},{2,1},{5,4},{6,5},{9,8},{10,9},{13,12},{14,13},{17,16},{18,1... | collective-permute-start | bytes 3145736 | tf_op jit(solution)/shard_map/ppermute | solution.py:120
  212.6 56.4 %collective-permute-start.16 = (bf16[256,2048]{1,0:T(8,128)(2,1)}, bf16[256,2048]{1,0:T(8,128)(2,1)S(1)}, u32[]{:S(2)}, u32[]{:S(2)}) collective-permute-start(bf16[256,2048]{1,0:T(8,128)(2,1)} %get-tuple-element.250), channel_id=1, source_target_pairs={{2,3},{6,7},{10,11},{14,15},{18,19},{22,23},{26,27},{30,31}} | collective-permute-start | bytes 3145736 | tf_op jit(solution)/shard_map/ppermute | solution.py:119
  213.3 55.7 %collective-permute-start.17 = (bf16[256,2048]{1,0:T(8,128)(2,1)}, bf16[256,2048]{1,0:T(8,128)(2,1)}, u32[]{:S(2)}, u32[]{:S(2)}) collective-permute-start(bf16[256,2048]{1,0:T(8,128)(2,1)} %get-tuple-element.251), channel_id=1, source_target_pairs={{1,0},{5,4},{9,8},{13,12},{17,16},{21,20},{25,24},{29,28}} | collective-permute-start | bytes 3145736 | tf_op jit(solution)/shard_map/ppermute | solution.py:120
  383.4 74.5 %collective-permute-start.26 = (bf16[512,2048]{1,0:T(8,128)(2,1)}, bf16[512,2048]{1,0:T(8,128)(2,1)}, u32[]{:S(2)}, u32[]{:S(2)}) collective-permute-start(bf16[512,2048]{1,0:T(8,128)(2,1)} %get-tuple-element.305), channel_id=1, source_target_pairs={{0,16},{4,20},{8,24},{12,28},{16,0},{20,4},{24,8},{28,12},{1,17},{... | collective-permute-start | bytes 6291464 | tf_op jit(solution)/shard_map/ppermute | solution.py:279
  383.7 74.3 %collective-permute-start.25 = (bf16[512,2048]{1,0:T(8,128)(2,1)}, bf16[512,2048]{1,0:T(8,128)(2,1)}, u32[]{:S(2)}, u32[]{:S(2)}) collective-permute-start(bf16[512,2048]{1,0:T(8,128)(2,1)} %get-tuple-element.303), channel_id=1, source_target_pairs={{0,8},{4,12},{8,0},{12,4},{16,24},{20,28},{24,16},{28,20},{1,9},{5... | collective-permute-start | bytes 6291464 | tf_op jit(solution)/shard_map/ppermute | solution.py:279
  410.6 57.1 %all-to-all-start.1 = ((bf16[4,256,512]{2,1,0:T(8,128)(2,1)}), bf16[4,256,512]{2,1,0:T(8,128)(2,1)S(1)}, u32[]{:S(2)}, u32[]{:S(2)}) async-start(bf16[4,256,512]{2,1,0:T(8,128)(2,1)} %bitcast.28), calls=%async_computation.2 | async-start | bytes 2097152 | tf_op jit(solution)/shard_map/all_to_all | solution.py:141
  414.1 127.7 %all-gather.10.cloned.1.call-start = ((), (), s32[]{:S(2)}) async-start(), calls=%async_computation.9 | async-start | bytes 5242880 | tf_op jit(solution)/shard_map/all_gather | solution.py:920
  414.7 245.4 %reduce-scatter.5.cloned.1.call-start = ((), (), s32[]{:S(2)}) async-start(), calls=%async_computation.7 | async-start | bytes 5242880 | tf_op jit(solution)/shard_map/reduce_scatter | solution.py:926
  456.3 45.3 %collective-permute-start.31 = (bf16[512,1024]{1,0:T(8,128)(2,1)}, bf16[512,1024]{1,0:T(8,128)(2,1)S(1)}, u32[]{:S(2)}, u32[]{:S(2)}) collective-permute-start(bf16[512,1024]{1,0:T(8,128)(2,1)} %get-tuple-element.323.refs_1_), channel_id=1, source_target_pairs={{0,8},{4,12},{8,0},{12,4},{16,24},{20,28},{24,16},{28,20},{1,9},{5... | collective-permute-start | bytes 3145736 | tf_op jit(solution)/shard_map/ppermute | solution.py:279
  457.4 44.2 %collective-permute-start.32 = (bf16[512,1024]{1,0:T(8,128)(2,1)}, bf16[512,1024]{1,0:T(8,128)(2,1)S(1)}, u32[]{:S(2)}, u32[]{:S(2)}) collective-permute-start(bf16[512,1024]{1,0:T(8,128)(2,1)} %get-tuple-element.324.refs_3_), channel_id=1, source_target_pairs={{0,16},{4,20},{8,24},{12,28},{16,0},{20,4},{24,8},{28,12},{1,17},{... | collective-permute-start | bytes 3145736 | tf_op jit(solution)/shard_map/ppermute | solution.py:279
  551.1 48.3 %collective-permute-start.40 = (bf16[512,2048]{1,0:T(8,128)(2,1)}, bf16[512,2048]{1,0:T(8,128)(2,1)S(1)}, u32[]{:S(2)}, u32[]{:S(2)}) collective-permute-start(bf16[512,2048]{1,0:T(8,128)(2,1)} %get-tuple-element.339.refs_1_), channel_id=1, source_target_pairs={{0,8},{4,12},{8,0},{12,4},{16,24},{20,28},{24,16},{28,20},{1,9},{5... | collective-permute-start | bytes 6291464 | tf_op jit(solution)/shard_map/ppermute | solution.py:279
  552.1 65.8 %collective-permute-start.38 = (bf16[1024,2048]{1,0:T(8,128)(2,1)}, bf16[1024,2048]{1,0:T(8,128)(2,1)}, u32[]{:S(2)}, u32[]{:S(2)}) collective-permute-start(bf16[1024,2048]{1,0:T(8,128)(2,1)} %get-tuple-element.337.refs_1_), channel_id=1, source_target_pairs={{0,4},{4,0},{8,12},{12,8},{16,20},{20,16},{24,28},{28,24},{1,5},{5... | collective-permute-start | bytes 12582920 | tf_op jit(solution)/shard_map/ppermute | solution.py:279
  552.7 52.5 %collective-permute-start.39 = (bf16[512,2048]{1,0:T(8,128)(2,1)S(1)}, bf16[512,2048]{1,0:T(8,128)(2,1)S(1)}, u32[]{:S(2)}, u32[]{:S(2)}) collective-permute-start(bf16[512,2048]{1,0:T(8,128)(2,1)S(1)} %copy-done.42), channel_id=1, source_target_pairs={{0,16},{4,20},{8,24},{12,28},{16,0},{20,4},{24,8},{28,12},{1,17},{... | collective-permute-start | bytes 6291464 | tf_op jit(solution)/shard_map/ppermute | solution.py:279
  611.1 60.6 %collective-permute-start.47 = (bf16[1024,2048]{1,0:T(8,128)(2,1)}, bf16[1024,2048]{1,0:T(8,128)(2,1)}, u32[]{:S(2)}, u32[]{:S(2)}) collective-permute-start(bf16[1024,2048]{1,0:T(8,128)(2,1)} %get-tuple-element.355.refs_1_), channel_id=1, source_target_pairs={{0,4},{4,0},{8,12},{12,8},{16,20},{20,16},{24,28},{28,24},{1,5},{5... | collective-permute-start | bytes 12582920 | tf_op jit(solution)/shard_map/ppermute | solution.py:279
  613.0 149.0 %all-to-all-start.2 = ((bf16[4,256,2048]{2,1,0:T(8,128)(2,1)}), bf16[4,256,2048]{2,1,0:T(8,128)(2,1)}, u32[]{:S(2)}, u32[]{:S(2)}) async-start(bf16[4,256,2048]{2,1,0:T(8,128)(2,1)} %bitcast.25), calls=%async_computation.3 | async-start | bytes 8388608 | tf_op jit(solution)/shard_map/all_to_all | solution.py:141
  665.7 50.7 %collective-permute-start.45 = (f32[32,128]{1,0:T(8,128)S(1)}, f32[32,128]{1,0:T(8,128)S(1)}, u32[]{:S(2)}, u32[]{:S(2)}) collective-permute-start(f32[32,128]{1,0:T(8,128)S(1)} %pad_maximum_fusion.2.refs_0_), channel_id=1, source_target_pairs={{0,2},{1,3},{2,0},{3,1},{4,6},{5,7},{6,4},{7,5},{8,10},{9,11},{10,... | collective-permute-start | bytes 49160 | tf_op jit(solution)/shard_map/ppermute | solution.py:448
  667.1 49.4 %collective-permute-start.46 = (f32[32,128]{1,0:T(8,128)S(1)}, f32[32,128]{1,0:T(8,128)S(1)}, u32[]{:S(2)}, u32[]{:S(2)}) collective-permute-start(f32[32,128]{1,0:T(8,128)S(1)} %pad_maximum_fusion.2.refs_0_), channel_id=1, source_target_pairs={{0,3},{1,2},{2,1},{3,0},{4,7},{5,6},{6,5},{7,4},{8,11},{9,10},{10,... | collective-permute-start | bytes 49160 | tf_op jit(solution)/shard_map/ppermute | solution.py:448
  670.1 47.6 %collective-permute-start.51 = (bf16[256,1024]{1,0:T(8,128)(2,1)S(1)}, bf16[256,1024]{1,0:T(8,128)(2,1)S(1)}, u32[]{:S(2)}, u32[]{:S(2)}) collective-permute-start(bf16[256,1024]{1,0:T(8,128)(2,1)S(1)} %copy-done.56), channel_id=1, source_target_pairs={{0,16},{4,20},{8,24},{12,28},{16,0},{20,4},{24,8},{28,12},{1,17},{... | collective-permute-start | bytes 1572872 | tf_op jit(solution)/shard_map/ppermute | solution.py:279
  671.6 46.1 %collective-permute-start.52 = (bf16[256,1024]{1,0:T(8,128)(2,1)S(1)}, bf16[256,1024]{1,0:T(8,128)(2,1)S(1)}, u32[]{:S(2)}, u32[]{:S(2)}) collective-permute-start(bf16[256,1024]{1,0:T(8,128)(2,1)S(1)} %copy-done.57), channel_id=1, source_target_pairs={{0,8},{4,12},{8,0},{12,4},{16,24},{20,28},{24,16},{28,20},{1,9},{5... | collective-permute-start | bytes 1572872 | tf_op jit(solution)/shard_map/ppermute | solution.py:279
  (109 other events, 1446.8 us)
Sparse Core Ops, SparseCore 0:
  18.6 41.8 all-gather.5
  69.4 53.3 all-gather.7
  302.3 82.5 reduce-scatter.2
  416.9 88.3 all-gather.9
  551.3 79.0 reduce-scatter.4

commit v3 on v2

--- a/solution.py
+++ b/solution.py
@@ -15,7 +15,7 @@
 F32 = jnp.float32
 VMEM = 56 << 20
 COST = {
-    "give": 8, "keep": 10, "fold": 4, "spread": 4, "join": 4.5, "finish": 11, "middle": 9.5, "attend": 11,
+    "give": 8, "give_second": 2.5, "keep": 10, "fold": 4, "spread": 4, "join": 4.5, "finish": 11, "middle": 9.5, "attend": 11,
     "attend_back": 17, "back_project": 11, "qkv": 5.6, "project": 8.6, "ffn": 22, "last": 5, "tie": 0.5,
 }
 
@@ -66,7 +66,7 @@
             out_shape=list(out_shape) + [TOKEN],
             input_output_aliases=aliases or {},
             compiler_params=pltpu.CompilerParams(vmem_limit_bytes=VMEM),
-            cost_estimate=pl.CostEstimate(flops=int(COST[name] * 1e+09), bytes_accessed=int(COST[name] * 1e6), transcendentals=0),
+            cost_estimate=pl.CostEstimate(flops=int(COST[name] * order.worth * 1e9), bytes_accessed=int(COST[name] * 1e6), transcendentals=0),
             name=name,
         )(*operands, *tokens)
         order.give(token)
@@ -77,7 +77,7 @@
 
 class Order:
     def __init__(self):
-        self.tokens = []
+        self.tokens, self.worth = [], 1.3
 
     def take(self):
         return self.tokens
@@ -149,19 +149,12 @@
     return lax.dynamic_slice_in_dim(values, block * cols, cols, axis=1)
 
 
-def give_body(places, *refs, two, last):
-    out = refs[-1]
-    if not two:
-        out[...] = dot(refs[0][...], refs[1][...]).astype(BF)
-        return
-
-    @pl.when(pl.program_id(0) < last)
-    def _():
-        out[...] = dot(refs[0][...], refs[1][...]).astype(BF)
-
-    @pl.when(pl.program_id(0) == last)
-    def _():
-        out[...] = second(refs[2:4], None).astype(BF)
+def give_body(places, left, right, out):
+    out[...] = dot(left[...], right[...]).astype(BF)
+
+
+def give_second_body(places, left, right, out):
+    out[...] = second((left, right), None).astype(BF)
 
 
 def second(refs, rows):
@@ -176,7 +169,7 @@
 
 def keep_body(places, *refs, two, last, lanes, chunks):
     ins = 4 if two else 2
-    got, outs = refs[ins], refs[ins + 1 :]
+    gots, outs = refs[ins : ins + (2 if two else 1)], refs[ins + (2 if two else 1) :]
     step = pl.program_id(0)
     rows = outs[0].shape[0]
     for lane in range(lanes):
@@ -189,14 +182,14 @@
             @pl.when((inside & (step < last)) if two else inside)
             def _():
                 total = dot(refs[0][place, :], refs[1][...])
-                out[...] = (total + got[place, :].astype(F32)).astype(BF)
+                out[...] = (total + gots[0][place, :].astype(F32)).astype(BF)
 
             if two and lane == lanes - 1:
 
                 @pl.when(step == last)
                 def _():
                     total = second(refs[2:4], place)
-                    out[...] = (total + got[place, :].astype(F32)).astype(BF)
+                    out[...] = (total + gots[1][place, :].astype(F32)).astype(BF)
 
 
 def fold_body(places, *refs):
@@ -253,6 +246,7 @@
         self.rows = left.shape[0] // 2
         self.cols = right.shape[1] + (pair[1].shape[1] if pair else 0)
         self.bn = min(512, widths[-1])
+        self.gots = []
 
 
 class Gradients:
@@ -292,19 +286,21 @@
             ]
         return specs, [p.left, p.right, *p.pair], dict(two=bool(p.pair), last=last)
 
-    def give(self, order, at=0):
+    def give(self, order, at=0, second=False):
         p = self.products[at]
         specs, values, facts = self.operands(p, 1 - self.bit(0))
+        some = slice(2, 4) if second else slice(0, 2)
+        cols = values[some][1].shape[1]
         (out,) = call(
-            functools.partial(give_body, **facts),
-            name="give",
-            grid=(p.cols // p.bn,),
+            give_second_body if second else give_body,
+            name="give_second" if second else "give",
+            grid=(cols // p.bn,),
             scalars=1,
-            in_specs=specs,
+            in_specs=specs[some],
             out_specs=[pl.BlockSpec((p.rows, p.bn), lambda n, s: (0, n))],
-            out_shape=[jax.ShapeDtypeStruct((p.rows, p.cols), BF)],
-        )(order, self.scalars(1 - self.bit(0)), *values)
-        p.got = self.swap(out, 0)
+            out_shape=[jax.ShapeDtypeStruct((p.rows, cols), BF)],
+        )(order, self.scalars(1 - self.bit(0)), *values[some])
+        p.gots.append(self.swap(out, 0))
 
     def keep(self, order, at=0):
         p = self.products[at]
@@ -323,10 +319,14 @@
             name="keep",
             grid=(lanes * chunks,),
             scalars=1,
-            in_specs=specs + [pl.BlockSpec((p.rows, p.bn), lambda n, s: (0, n))],
+            in_specs=specs
+            + [
+                pl.BlockSpec((p.rows, p.bn), lambda n, s: (0, jnp.minimum(n, facts["last"] - 1))),
+                pl.BlockSpec((p.rows, p.bn), lambda n, s: (0, 0)),
+            ][: len(p.gots)],
             out_specs=[out_spec(k // 2) for k in range(2 * lanes)],
             out_shape=[jax.ShapeDtypeStruct((rows, cols), BF)] * (2 * lanes),
-        )(order, self.scalars(self.bit(0), *[self.bit(b) for b in p.firsts]), *values, p.got)
+        )(order, self.scalars(self.bit(0), *[self.bit(b) for b in p.firsts]), *values, *p.gots)
         for h in range(lanes):
             self.kept.append(outs[2 * h])
             self.gots.append(self.swap(outs[2 * h + 1], p.firsts[h]))
@@ -352,6 +352,9 @@
             self.gots = [self.swap(outs[1 + 2 * h], self.orders[h][self.step]) for h in (0, 1)]
         else:
             self.ask()
+
+    def hold(self, order):
+        self.gots = order.after(*self.gots)
 
     def ask(self):
         self.step -= 1
@@ -434,13 +437,11 @@
     def __init__(self, parts, dp, tensor):
         self.size = parts[0].size
         self.value = jnp.concatenate([p.reshape(-1, 128) for p in parts], axis=0)
-        self.left = []
-        for name, size in (("tensor", tensor), ("dp", dp)):
-            step = 1
-            while step < size:
-                masks = [step, 2 * step, 3 * step] if 2 * step < size else [step]
-                self.left.append((name, size, masks))
-                step *= 1 + len(masks)
+        self.left = [
+            (name, size, [1 << k])
+            for name, size in (("tensor", tensor), ("dp", dp))
+            for k in range(size.bit_length() - 1)
+        ]
         self.next()
 
     def next(self):
@@ -450,8 +451,6 @@
     def step(self, order):
         self.value, *got = order.after(self.value, *self.got)
         self.value = self.value + got[0]
-        if len(got) == 3:
-            self.value = self.value + (got[1] + got[2])
         if self.left:
             self.next()
 
@@ -922,7 +921,8 @@
         first.spread(order)
     wide.fold(order)
     (d_qkv,) = attend_back(order, doc_ids, query, key, value, d_mix, cos, sin)
-    downs = exchange(order.after(down_part)[0]).reshape(tensor, t, d)
+    attn = Gradients([(normed_t, d_qkv, [width] * 4, d_resid_all, mixed)], dp)
+    attn.give(order)
     d_normed = lax.psum_scatter(
         back_project(order, d_qkv, w_query, w_key, w_value),
         "tensor",
@@ -932,27 +932,38 @@
     first.join(order)
     for _ in more:
         wide.fold(order)
+    attn.give(order, second=True)
+    attn.keep(order)
+    wide.hold(order)
+    usual, order.worth = order.worth, 10
+    attn.fold(order)
+    order.worth = usual
     for _ in more:
         wide.spread(order)
-    attn = Gradients([(normed_t, d_qkv, [width] * 4, d_resid_all, mixed)], dp)
-    attn.give(order)
-    attn.keep(order)
+    (down_grad,) = first.finish(order)
+    in_grad, attn_gain_part = last(order, d_normed, layer_in, d_resid, attn_gain)
+    totals = GainTotals([attn_gain_part, ffn_gain_part], dp, tensor)
+    totals.step(order)
+    totals.step(order)
+    down_sum = lax.psum_scatter(
+        order.after(down_part)[0], "tensor", scatter_dimension=0, tiled=True
+    )
+    totals.step(order)
+    attn.hold(order)
+    order.worth = 0.3
+    wide.hold(order)
     wide.join(order)
-    (down_grad,) = first.finish(order)
-    attn.fold(order)
+    for _ in more:
+        attn.fold(order)
+    totals.step(order)
     (gate_grad,) = wide.finish(order, 0)
     for _ in more:
-        attn.fold(order)
-    in_grad, attn_gain_part = last(order, d_normed, layer_in, d_resid, attn_gain)
-    totals = GainTotals([attn_gain_part, ffn_gain_part], dp, tensor)
+        attn.spread(order)
     (up_grad,) = wide.finish(order, 1)
-    totals.step(order)
-    for _ in more:
-        attn.spread(order)
     attn_gain_grad, ffn_gain_grad = totals.split(order)
     attn.join(order)
     query_grad, key_grad, value_grad, out_grad = attn.finish(order)
-    layer_out = (resid + jnp.sum(downs.astype(F32), axis=0)).astype(BF)
+    layer_out = (resid + down_sum.astype(F32)).astype(BF)
     return (
         layer_out,
         in_grad,

time: 796 us -> 752 us (0.945)
  waiting for transfers between devices: 257 us -> 219 us
  starting transfers between devices: 80.2 us -> 67.4 us
    ppermute x7 -> x5, waiting for transfers between devices: 56.1 us -> 26.3 us  [next(): lax.ppermute(self.value, name, xor_pairs(size, m))]
    ppermute x32 -> x33, waiting for transfers between devices: 117 us -> 103 us  [swap(): return lax.ppermute(value, 'dp', xor_pairs(self.count, 1 << b))]
    pallas_call x53 -> x59, Pallas kernels: 371 us -> 377 us  [run(): pl.pallas_call(whole, grid_spec=pltpu.PrefetchScalarGridSpec(num_scalar_p...]
    ppermute x32 -> x33, starting transfers between devices: 31.9 us -> 26.6 us  [swap(): return lax.ppermute(value, 'dp', xor_pairs(self.count, 1 << b))]
    unnamed x137 -> x129, local copies, waits for them, and re-layouts: 23.7 us -> 24 us
  transfers between devices with their start and end apart: 65 -> 64, of which waited for: 25 -> 25; matrix products, arithmetic and copies ran while one was open for 5% -> 5% of each run, Pallas kernels for 41% -> 44%
where the time goes in v3:
time: 752 us; the launch traced here: 741 us
  Pallas kernels  377 us (50%)
  waiting for transfers between devices  219 us (29%)
  starting transfers between devices  67.4 us (9%)
  other arithmetic  36 us (5%)
  local copies, waits for them, and re-layouts  27 us (4%)
  between operations  15.3 us (2%)
    pallas_call x59, Pallas kernels, run(): pl.pallas_call(whole, grid_spec=pltpu.PrefetchScalarGridSpec(num_scalar_p...  377 us
    ppermute x33, waiting for transfers between devices, swap(): return lax.ppermute(value, 'dp', xor_pairs(self.count, 1 << b))  103 us
    ppermute x9, waiting for transfers between devices, step(): lax.ppermute(down, 'tensor', [(i + 1, i) for i in range(0, size - k)])  52.3 us
    ppermute x33, starting transfers between devices, swap(): return lax.ppermute(value, 'dp', xor_pairs(self.count, 1 << b))  26.6 us
    ppermute x5, waiting for transfers between devices, next(): lax.ppermute(self.value, name, xor_pairs(size, m))  26.3 us
    unnamed x129, local copies, waits for them, and re-layouts  24 us
    ppermute x9, waiting for transfers between devices, step(): lax.ppermute(up, 'tensor', [(i, i + 1) for i in range(k - 1, size - 1)])  21 us
    select_n x9, other arithmetic, slot(): value = jnp.where(here, arr, value)  20.1 us
  transfers between devices with their start and end apart: 64, of which 25 were waited for; matrix products, arithmetic and copies ran while one was open for 5% of the time, Pallas kernels for 44%

profile of v3, /device:TPU:0, one launch (start us, length us, event | category | flops | bytes accessed | tf_op | source)
XLA Modules:
  0.0 741.1 jit_solution(2771814069233135909)
XLA Ops:
  28.1 21.0 %collective-permute-done.refs_0_ = bf16[256,2048]{1,0:T(8,128)(2,1)S(1)} collective-permute-done((bf16[256,2048]{1,0:T(8,128)(2,1)}, bf16[256,2048]{1,0:T(8,128)(2,1)S(1)}, u32[]{:S(2)}, u32[]{:S(2)}) %collective-permute-start) | collective-permute-done | bytes 1048608 | tf_op jit(solution)/shard_map/ppermute | solution.py:119
  49.1 10.8 %collective-permute-done.1.refs_1_ = bf16[256,2048]{1,0:T(8,128)(2,1)} collective-permute-done((bf16[256,2048]{1,0:T(8,128)(2,1)}, bf16[256,2048]{1,0:T(8,128)(2,1)}, u32[]{:S(2)}, u32[]{:S(2)}) %collective-permute-start.1) | collective-permute-done | bytes 1048608 | tf_op jit(solution)/shard_map/ppermute | solution.py:120
  73.4 21.0 %collective-permute-done.3.refs_1_ = bf16[256,2048]{1,0:T(8,128)(2,1)} collective-permute-done((bf16[256,2048]{1,0:T(8,128)(2,1)}, bf16[256,2048]{1,0:T(8,128)(2,1)}, u32[]{:S(2)}, u32[]{:S(2)}) %collective-permute-start.3) | collective-permute-done | bytes 1048608 | tf_op jit(solution)/shard_map/ppermute | solution.py:120
  111.6 12.3 %collective-permute-done.5 = bf16[256,2048]{1,0:T(8,128)(2,1)S(1)} collective-permute-done((bf16[256,2048]{1,0:T(8,128)(2,1)}, bf16[256,2048]{1,0:T(8,128)(2,1)S(1)}, u32[]{:S(2)}, u32[]{:S(2)}) %collective-permute-start.5) | collective-permute-done | bytes 1048608 | tf_op jit(solution)/shard_map/ppermute | solution.py:120
  130.7 13.6 %attend.1 = (bf16[1024,512]{1,0:T(8,128)(2,1)}, f32[8,128]{1,0:T(8,128)}) custom-call(s32[1024]{0:T(1024)} %refs_0_.4, bf16[1024,512]{1,0:T(8,128)(2,1)} %get-tuple-element.234.refs_1_, bf16[1024,512]{1,0:T(8,128)(2,1)} %get-tuple-element.235.refs_2_, bf16[1024,512]{1,0:T(8,128)(2,1)} %get-tuple-element.236.refs_3_, s32[1024,1]{1,0:T(8,128)} %copy.92.refs_4_.refs_5_, ...), custom_call_target="tpu_custom_call" | custom-call | flops 14300000256 | bytes 11000000 | tf_op jit(solution)/shard_map/attend/pallas_call | solution.py:57
  154.4 15.0 %all-to-all-done = bf16[4,256,512]{2,1,0:T(8,128)(2,1)S(1)} async-done(((bf16[4,256,512]{2,1,0:T(8,128)(2,1)}), bf16[4,256,512]{2,1,0:T(8,128)(2,1)S(1)}, u32[]{:S(2)}, u32[]{:S(2)}) %all-to-all-start) | async-done | bytes 1048608 | tf_op jit(solution)/shard_map/all_to_all | solution.py:141
  181.5 22.2 %ffn.4 = (bf16[2048,1024]{1,0:T(8,128)(2,1)}, bf16[1024,2048]{1,0:T(8,128)(2,1)}, bf16[1024,2048]{1,0:T(8,128)(2,1)}, bf16[2048,1024]{1,0:T(8,128)(2,1)}, bf16[1...) custom-call(s32[1]{0:T(128)} %bitcast.1.refs_0_, ...), custom_call_target="tpu_custom_call" | custom-call | flops 28600000512 | bytes 22000000 | tf_op jit(solution)/shard_map/ffn/pallas_call | solution.py:57
  213.8 22.4 %ffn.5 = (bf16[2048,1024]{1,0:T(8,128)(2,1)}, bf16[1024,2048]{1,0:T(8,128)(2,1)}, bf16[1024,2048]{1,0:T(8,128)(2,1)}, bf16[2048,1024]{1,0:T(8,128)(2,1)}, bf16[1...) custom-call(s32[1]{0:T(128)} %bitcast.2.refs_0_, ...), custom_call_target="tpu_custom_call", output_to_operand_aliasing={{0}: (6, {}), {1}: (7, {}), {2}: (8, {}), {3}: (9, {}), {4}... | custom-call | flops 28600000512 | bytes 22000000 | tf_op jit(solution)/shard_map/ffn/pallas_call | solution.py:57
  247.1 22.3 %ffn.6 = (bf16[2048,1024]{1,0:T(8,128)(2,1)}, bf16[1024,2048]{1,0:T(8,128)(2,1)}, bf16[1024,2048]{1,0:T(8,128)(2,1)}, bf16[2048,1024]{1,0:T(8,128)(2,1)}, bf16[1...) custom-call(s32[1]{0:T(128)} %bitcast.3.refs_0_, ...), custom_call_target="tpu_custom_call", output_to_operand_aliasing={{0}: (6, {}), {1}: (7, {}), {2}: (8, {}), {3}: (9, {}), {4}... | custom-call | flops 28600000512 | bytes 22000000 | tf_op jit(solution)/shard_map/ffn/pallas_call | solution.py:57
  283.9 22.2 %ffn.7 = (bf16[2048,1024]{1,0:T(8,128)(2,1)}, bf16[1024,2048]{1,0:T(8,128)(2,1)}, bf16[1024,2048]{1,0:T(8,128)(2,1)}, bf16[2048,1024]{1,0:T(8,128)(2,1)}, bf16[1...) custom-call(s32[1]{0:T(128)} %bitcast.refs_0_, ...), custom_call_target="tpu_custom_call", output_to_operand_aliasing={{0}: (6, {}), {1}: (7, {}), {2}: (8, {}), {3}: (9, {}), {4}... | custom-call | flops 28600000512 | bytes 22000000 | tf_op jit(solution)/shard_map/ffn/pallas_call | solution.py:57
  334.7 10.8 %keep.4 = (bf16[512,1024]{1,0:T(8,128)(2,1)}, bf16[512,1024]{1,0:T(8,128)(2,1)}, bf16[512,1024]{1,0:T(8,128)(2,1)}, bf16[512,1024]{1,0:T(8,128)(2,1)}, f32[8,128]{1,0:T(8,128)}) custom-call(s32[3]{0:T(128)} %pad_add_fusion.1.refs_0_, bf16[2048,1024]{1,0:T(8,128)(2,1)} %get-tuple-element.289.refs_1_, bf16[1024,2048]{1,0:T(8,128)(2,1)} %get-tuple-element.290.refs_2_, ...), custom_call_target="tpu_custom_call" | custom-call | flops 12999999488 | bytes 10000000 | tf_op jit(solution)/shard_map/keep/pallas_call | solution.py:57
  359.1 10.4 %keep.6 = (bf16[512,2048]{1,0:T(8,128)(2,1)}, bf16[512,2048]{1,0:T(8,128)(2,1)}, f32[8,128]{1,0:T(8,128)}) custom-call(s32[2]{0:T(128)} %pad_add_fusion.4.refs_0_, bf16[2048,1024]{1,0:T(8,128)(2,1)} %get-tuple-element.293.refs_1_, bf16[1024,2048]{1,0:T(8,128)(2,1)} %get-tuple-element.294.refs_2_, bf16[1024,2048]{1,0:T(8,128)(2,1)} %collective-permute-done.21.refs_3_, ...), custom_call_target="tpu_custom_call" | custom-call | flops 12999999488 | bytes 10000000 | tf_op jit(solution)/shard_map/keep/pallas_call | solution.py:57
  382.5 10.9 %collective-permute-done.23.refs_2_ = bf16[256,1024]{1,0:T(8,128)(2,1)S(1)} collective-permute-done((bf16[256,1024]{1,0:T(8,128)(2,1)}, bf16[256,1024]{1,0:T(8,128)(2,1)S(1)}, u32[]{:S(2)}, u32[]{:S(2)}) %collective-permute-start.23) | collective-permute-done | bytes 524320 | tf_op jit(solution)/shard_map/ppermute | solution.py:273
  415.0 33.7 %collective-permute-done.27.refs_2_ = bf16[256,1024]{1,0:T(8,128)(2,1)S(1)} collective-permute-done((bf16[256,1024]{1,0:T(8,128)(2,1)S(1)}, bf16[256,1024]{1,0:T(8,128)(2,1)S(1)}, u32[]{:S(2)}, u32[]{:S(2)}) %collective-permute-start.27) | collective-permute-done | bytes 524320 | tf_op jit(solution)/shard_map/ppermute | solution.py:273
  467.2 21.3 %attend_back.1 = (bf16[1024,1536]{1,0:T(8,128)(2,1)}, f32[8,128]{1,0:T(8,128)}) custom-call(s32[1024]{0:T(1024)} %refs_0_.4, bf16[1024,512]{1,0:T(8,128)(2,1)} %get-tuple-element.234.refs_1_, bf16[1024,512]{1,0:T(8,128)(2,1)} %get-tuple-element.235.refs_2_, bf16[1024,512]{1,0:T(8,128)(2,1)} %get-tuple-element.236.refs_3_, bf16[1024,512]{1,0:T(8,128)(2,1)} %bitcast.25, ...), custom_call_target="tpu_custom_call" | custom-call | flops 22100000768 | bytes 17000000 | tf_op jit(solution)/shard_map/attend_back/pallas_call | solution.py:57
  495.5 11.1 %back_project.1 = (bf16[1024,2048]{1,0:T(8,128)(2,1)}, f32[8,128]{1,0:T(8,128)}) custom-call(bf16[1024,1536]{1,0:T(8,128)(2,1)} %get-tuple-element.324.refs_2_.refs_0_, bf16[2048,512]{1,0:T(8,128)(2,1)} %refs_1_.2, bf16[2048,512]{1,0:T(8,128)(2,1)} %refs_2_.15, bf16[2048,512]{1,0:T(8,128)(2,1)} %refs_3_.17, f32[8,128]{1,0:T(8,128)} %get-tuple-element.327.refs_4_), custom_call_target="tpu_custom_call" | custom-call | flops 14300000256 | bytes 11000000 | tf_op jit(solution)/shard_map/back_project/pallas_call | solution.py:57
  524.9 12.8 %keep.7 = (bf16[512,1024]{1,0:T(8,128)(2,1)}, bf16[512,1024]{1,0:T(8,128)(2,1)}, bf16[512,1024]{1,0:T(8,128)(2,1)}, bf16[512,1024]{1,0:T(8,128)(2,1)}, f32[8,128]{1,0:T(8,128)}) custom-call(s32[3]{0:T(128)} %pad_add_fusion.1.refs_0_, bf16[2048,1024]{1,0:T(8,128)(2,1)} %get-tuple-element.325.refs_1_, bf16[1024,1536]{1,0:T(8,128)(2,1)} %get-tuple-element.324.refs_2_.refs_0_, ...), custom_call_target="tpu_custom_call" | custom-call | flops 12999999488 | bytes 10000000 | tf_op jit(solution)/shard_map/keep/pallas_call | solution.py:57
  550.5 20.9 %collective-permute-done.38.refs_2_ = bf16[512,1024]{1,0:T(8,128)(2,1)} collective-permute-done((bf16[512,1024]{1,0:T(8,128)(2,1)}, bf16[512,1024]{1,0:T(8,128)(2,1)}, u32[]{:S(2)}, u32[]{:S(2)}) %collective-permute-start.38) | collective-permute-done | bytes 1048608 | tf_op jit(solution)/shard_map/ppermute | solution.py:273
  585.3 11.0 %finish.4 = (f32[2048,2048]{1,0:T(8,128)}, f32[8,128]{1,0:T(8,128)}) custom-call(s32[1]{0:T(128)} %bitcast.12.refs_0_, bf16[1024,2048]{1,0:T(8,128)(2,1)} %get-tuple-element.333.refs_1_, bf16[1024,2048]{1,0:T(8,128)(2,1)} %collective-permute-done.31.refs_2_, f32[8,128]{1,0:T(8,128)} %get-tuple-element.355.refs_3_), custom_call_target="tpu_custom_call" | custom-call | flops 14300000256 | bytes 11000000 | tf_op jit(solution)/shard_map/finish/pallas_call | solution.py:57
  618.1 17.6 %collective-permute-done.46.refs_0_ = bf16[512,2048]{1,0:T(8,128)(2,1)S(1)} collective-permute-done((bf16[512,2048]{1,0:T(8,128)(2,1)}, bf16[512,2048]{1,0:T(8,128)(2,1)S(1)}, u32[]{:S(2)}, u32[]{:S(2)}) %collective-permute-start.46) | collective-permute-done | bytes 2097184 | tf_op jit(solution)/shard_map/ppermute | solution.py:273
  653.4 12.0 %collective-permute-done.43.refs_1_ = f32[32,128]{1,0:T(8,128)S(1)} collective-permute-done((f32[32,128]{1,0:T(8,128)S(1)}, f32[32,128]{1,0:T(8,128)S(1)}, u32[]{:S(2)}, u32[]{:S(2)}) %collective-permute-start.43) | collective-permute-done | bytes 16416 | tf_op jit(solution)/shard_map/ppermute | solution.py:449
  666.6 11.0 %finish.5 = (f32[2048,2048]{1,0:T(8,128)}, f32[8,128]{1,0:T(8,128)}) custom-call(s32[1]{0:T(128)} %bitcast.12.refs_0_, bf16[1024,2048]{1,0:T(8,128)(2,1)} %get-tuple-element.392.refs_1_, bf16[1024,2048]{1,0:T(8,128)(2,1)} %collective-permute-done.52.refs_2_, f32[8,128]{1,0:T(8,128)} %get-tuple-element.393.refs_3_), custom_call_target="tpu_custom_call" | custom-call | flops 3300000000 | bytes 11000000 | tf_op jit(solution)/shard_map/finish/pallas_call | solution.py:57
  687.0 11.0 %finish.6 = (f32[2048,2048]{1,0:T(8,128)}, f32[8,128]{1,0:T(8,128)}) custom-call(s32[1]{0:T(128)} %bitcast.12.refs_0_, bf16[1024,2048]{1,0:T(8,128)(2,1)} %get-tuple-element.389.refs_1_, bf16[1024,2048]{1,0:T(8,128)(2,1)} %copy-done.45, f32[8,128]{1,0:T(8,128)} %get-tuple-element.395.refs_3_), custom_call_target="tpu_custom_call" | custom-call | flops 3300000000 | bytes 11000000 | tf_op jit(solution)/shard_map/finish/pallas_call | solution.py:57
  722.4 11.4 %finish.7 = (f32[2048,512]{1,0:T(8,128)}, f32[2048,512]{1,0:T(8,128)}, f32[2048,512]{1,0:T(8,128)}, f32[512,2048]{1,0:T(8,128)}, f32[8,128]{1,0:T(8,128)}) custom-call(s32[1]{0:T(128)} %bitcast.12.refs_0_, bf16[1024,2048]{1,0:T(8,128)(2,1)} %get-tuple-element.402.refs_1_, bf16[1024,2048]{1,0:T(8,128)(2,1)} %collective-permute-done.55.refs_2_, ...), custom_call_target="tpu_custom_call" | custom-call | flops 3300000000 | bytes 11000000 | tf_op jit(solution)/shard_map/finish/pallas_call | solution.py:57
  (330 shorter events, 337.2 us)
Async XLA Ops:
  7.2 61.5 %all-gather.6.cloned.1.call-start = ((), (), s32[]{:S(2)}) async-start(), calls=%async_computation.5 | async-start | bytes 1310720 | tf_op jit(solution)/shard_map/all_gather | solution.py:856
  16.4 43.6 %collective-permute-start.1 = (bf16[256,2048]{1,0:T(8,128)(2,1)}, bf16[256,2048]{1,0:T(8,128)(2,1)}, u32[]{:S(2)}, u32[]{:S(2)}) collective-permute-start(bf16[256,2048]{1,0:T(8,128)(2,1)} %fusion.2.refs_1_), channel_id=1, source_target_pairs={{1,0},{2,1},{3,2},{5,4},{6,5},{7,6},{9,8},{10,9},{11,10},{13,12},{... | collective-permute-start | bytes 3145736 | tf_op jit(solution)/shard_map/ppermute | solution.py:120
  18.5 150.9 %all-gather.8.cloned.1.call-start = ((), (), s32[]{:S(2)}) async-start(), calls=%async_computation.9 | async-start | bytes 9437184 | tf_op jit(solution)/shard_map/all_gather | solution.py:879
  105.6 42.3 %collective-permute-start.6 = (bf16[256,2048]{1,0:T(8,128)(2,1)}, bf16[256,2048]{1,0:T(8,128)(2,1)S(1)}, u32[]{:S(2)}, u32[]{:S(2)}) collective-permute-start(bf16[256,2048]{1,0:T(8,128)(2,1)} %get-tuple-element.240), channel_id=1, source_target_pairs={{0,1},{1,2},{2,3},{4,5},{5,6},{6,7},{8,9},{9,10},{10,11},{12,13},{... | collective-permute-start | bytes 3145736 | tf_op jit(solution)/shard_map/ppermute | solution.py:119
  147.8 251.7 %reduce-scatter.4.cloned.1.call-start = ((), (), s32[]{:S(2)}) async-start(), calls=%async_computation.6 | async-start | bytes 5242880 | tf_op jit(solution)/shard_map/reduce_scatter | solution.py:900
  149.8 60.3 %collective-permute-start.12 = (bf16[256,2048]{1,0:T(8,128)(2,1)}, bf16[256,2048]{1,0:T(8,128)(2,1)S(1)}, u32[]{:S(2)}, u32[]{:S(2)}) collective-permute-start(bf16[256,2048]{1,0:T(8,128)(2,1)} %get-tuple-element.249), channel_id=1, source_target_pairs={{1,2},{2,3},{5,6},{6,7},{9,10},{10,11},{13,14},{14,15},{17,18},{18... | collective-permute-start | bytes 3145736 | tf_op jit(solution)/shard_map/ppermute | solution.py:119
  150.5 59.6 %collective-permute-start.13 = (bf16[256,2048]{1,0:T(8,128)(2,1)}, bf16[256,2048]{1,0:T(8,128)(2,1)}, u32[]{:S(2)}, u32[]{:S(2)}) collective-permute-start(bf16[256,2048]{1,0:T(8,128)(2,1)} %get-tuple-element.250), channel_id=1, source_target_pairs={{1,0},{2,1},{5,4},{6,5},{9,8},{10,9},{13,12},{14,13},{17,16},{18,1... | collective-permute-start | bytes 3145736 | tf_op jit(solution)/shard_map/ppermute | solution.py:120
  211.7 57.7 %collective-permute-start.16 = (bf16[256,2048]{1,0:T(8,128)(2,1)}, bf16[256,2048]{1,0:T(8,128)(2,1)S(1)}, u32[]{:S(2)}, u32[]{:S(2)}) collective-permute-start(bf16[256,2048]{1,0:T(8,128)(2,1)} %get-tuple-element.263), channel_id=1, source_target_pairs={{2,3},{6,7},{10,11},{14,15},{18,19},{22,23},{26,27},{30,31}} | collective-permute-start | bytes 3145736 | tf_op jit(solution)/shard_map/ppermute | solution.py:119
  212.5 57.0 %collective-permute-start.17 = (bf16[256,2048]{1,0:T(8,128)(2,1)}, bf16[256,2048]{1,0:T(8,128)(2,1)S(1)}, u32[]{:S(2)}, u32[]{:S(2)}) collective-permute-start(bf16[256,2048]{1,0:T(8,128)(2,1)} %get-tuple-element.264), channel_id=1, source_target_pairs={{1,0},{5,4},{9,8},{13,12},{17,16},{21,20},{25,24},{29,28}} | collective-permute-start | bytes 3145736 | tf_op jit(solution)/shard_map/ppermute | solution.py:120
  381.8 74.7 %collective-permute-start.26 = (bf16[512,2048]{1,0:T(8,128)(2,1)}, bf16[512,2048]{1,0:T(8,128)(2,1)}, u32[]{:S(2)}, u32[]{:S(2)}) collective-permute-start(bf16[512,2048]{1,0:T(8,128)(2,1)} %get-tuple-element.318), channel_id=1, source_target_pairs={{0,16},{4,20},{8,24},{12,28},{16,0},{20,4},{24,8},{28,12},{1,17},{... | collective-permute-start | bytes 6291464 | tf_op jit(solution)/shard_map/ppermute | solution.py:273
  382.1 74.4 %collective-permute-start.25 = (bf16[512,2048]{1,0:T(8,128)(2,1)}, bf16[512,2048]{1,0:T(8,128)(2,1)}, u32[]{:S(2)}, u32[]{:S(2)}) collective-permute-start(bf16[512,2048]{1,0:T(8,128)(2,1)} %get-tuple-element.316), channel_id=1, source_target_pairs={{0,8},{4,12},{8,0},{12,4},{16,24},{20,28},{24,16},{28,20},{1,9},{5... | collective-permute-start | bytes 6291464 | tf_op jit(solution)/shard_map/ppermute | solution.py:273
  409.0 57.2 %all-to-all-start.1 = ((bf16[4,256,512]{2,1,0:T(8,128)(2,1)}), bf16[4,256,512]{2,1,0:T(8,128)(2,1)S(1)}, u32[]{:S(2)}, u32[]{:S(2)}) async-start(bf16[4,256,512]{2,1,0:T(8,128)(2,1)} %bitcast.26), calls=%async_computation.2 | async-start | bytes 2097152 | tf_op jit(solution)/shard_map/all_to_all | solution.py:141
  412.5 105.2 %all-gather.10.cloned.1.call-start = ((), (), s32[]{:S(2)}) async-start(), calls=%async_computation.10 | async-start | bytes 5242880 | tf_op jit(solution)/shard_map/all_gather | solution.py:919
  415.0 181.3 %reduce-scatter.6.cloned.1.call-start = ((), (), s32[]{:S(2)}) async-start(), calls=%async_computation.7 | async-start | bytes 5242880 | tf_op jit(solution)/shard_map/reduce_scatter | solution.py:926
  454.8 51.7 %collective-permute-start.29 = (bf16[512,1024]{1,0:T(8,128)(2,1)}, bf16[512,1024]{1,0:T(8,128)(2,1)S(1)}, u32[]{:S(2)}, u32[]{:S(2)}) collective-permute-start(bf16[512,1024]{1,0:T(8,128)(2,1)} %get-tuple-element.330.refs_1_), channel_id=1, source_target_pairs={{0,8},{4,12},{8,0},{12,4},{16,24},{20,28},{24,16},{28,20},{1,9},{5... | collective-permute-start | bytes 3145736 | tf_op jit(solution)/shard_map/ppermute | solution.py:273
  455.9 50.7 %collective-permute-start.30 = (bf16[512,1024]{1,0:T(8,128)(2,1)}, bf16[512,1024]{1,0:T(8,128)(2,1)S(1)}, u32[]{:S(2)}, u32[]{:S(2)}) collective-permute-start(bf16[512,1024]{1,0:T(8,128)(2,1)} %get-tuple-element.331.refs_3_), channel_id=1, source_target_pairs={{0,16},{4,20},{8,24},{12,28},{16,0},{20,4},{24,8},{28,12},{1,17},{... | collective-permute-start | bytes 3145736 | tf_op jit(solution)/shard_map/ppermute | solution.py:273
  463.8 49.5 %collective-permute-start.32 = (bf16[256,2048]{1,0:T(8,128)(2,1)}, bf16[256,2048]{1,0:T(8,128)(2,1)}, u32[]{:S(2)}, u32[]{:S(2)}) collective-permute-start(bf16[256,2048]{1,0:T(8,128)(2,1)} %get-tuple-element.335), channel_id=1, source_target_pairs={{0,16},{4,20},{8,24},{12,28},{16,0},{20,4},{24,8},{28,12},{1,17},{... | collective-permute-start | bytes 3145736 | tf_op jit(solution)/shard_map/ppermute | solution.py:273
  465.3 48.0 %collective-permute-start.33 = (bf16[256,2048]{1,0:T(8,128)(2,1)}, bf16[256,2048]{1,0:T(8,128)(2,1)}, u32[]{:S(2)}, u32[]{:S(2)}) collective-permute-start(bf16[256,2048]{1,0:T(8,128)(2,1)} %get-tuple-element.337), channel_id=1, source_target_pairs={{0,8},{4,12},{8,0},{12,4},{16,24},{20,28},{24,16},{28,20},{1,9},{5... | collective-permute-start | bytes 3145736 | tf_op jit(solution)/shard_map/ppermute | solution.py:273
  522.3 193.7 %reduce-scatter.8.cloned.1.call-start = ((), (), s32[]{:S(2)}) async-start(), calls=%async_computation.8 | async-start | bytes 5242880 | tf_op jit(solution)/shard_map/reduce_scatter | solution.py:948
  540.2 45.1 %collective-permute-start.31 = (bf16[1024,2048]{1,0:T(8,128)(2,1)S(1)}, bf16[1024,2048]{1,0:T(8,128)(2,1)}, u32[]{:S(2)}, u32[]{:S(2)}) collective-permute-start(bf16[1024,2048]{1,0:T(8,128)(2,1)S(1)} %copy-done.44), channel_id=1, source_target_pairs={{0,4},{4,0},{8,12},{12,8},{16,20},{20,16},{24,28},{28,24},{1,5},{5... | collective-permute-start | bytes 12582920 | tf_op jit(solution)/shard_map/ppermute | solution.py:273
  576.1 40.4 %collective-permute-start.44 = (bf16[256,1024]{1,0:T(8,128)(2,1)}, bf16[256,1024]{1,0:T(8,128)(2,1)S(1)}, u32[]{:S(2)}, u32[]{:S(2)}) collective-permute-start(bf16[256,1024]{1,0:T(8,128)(2,1)} %get-tuple-element.372), channel_id=1, source_target_pairs={{0,16},{4,20},{8,24},{12,28},{16,0},{20,4},{24,8},{28,12},{1,17},{... | collective-permute-start | bytes 1572872 | tf_op jit(solution)/shard_map/ppermute | solution.py:273
  577.6 38.9 %collective-permute-start.45 = (bf16[256,1024]{1,0:T(8,128)(2,1)}, bf16[256,1024]{1,0:T(8,128)(2,1)S(1)}, u32[]{:S(2)}, u32[]{:S(2)}) collective-permute-start(bf16[256,1024]{1,0:T(8,128)(2,1)} %get-tuple-element.373), channel_id=1, source_target_pairs={{0,8},{4,12},{8,0},{12,4},{16,24},{20,28},{24,16},{28,20},{1,9},{5... | collective-permute-start | bytes 1572872 | tf_op jit(solution)/shard_map/ppermute | solution.py:273
  583.7 52.0 %collective-permute-start.46 = (bf16[512,2048]{1,0:T(8,128)(2,1)}, bf16[512,2048]{1,0:T(8,128)(2,1)S(1)}, u32[]{:S(2)}, u32[]{:S(2)}) collective-permute-start(bf16[512,2048]{1,0:T(8,128)(2,1)} %get-tuple-element.379.refs_1_), channel_id=1, source_target_pairs={{0,8},{4,12},{8,0},{12,4},{16,24},{20,28},{24,16},{28,20},{1,9},{5... | collective-permute-start | bytes 6291464 | tf_op jit(solution)/shard_map/ppermute | solution.py:273
  584.7 51.0 %collective-permute-start.47 = (bf16[512,2048]{1,0:T(8,128)(2,1)}, bf16[512,2048]{1,0:T(8,128)(2,1)}, u32[]{:S(2)}, u32[]{:S(2)}) collective-permute-start(bf16[512,2048]{1,0:T(8,128)(2,1)} %get-tuple-element.378.refs_1_), channel_id=1, source_target_pairs={{0,16},{4,20},{8,24},{12,28},{16,0},{20,4},{24,8},{28,12},{1,17},{... | collective-permute-start | bytes 6291464 | tf_op jit(solution)/shard_map/ppermute | solution.py:273
  (104 other events, 1313.1 us)
Sparse Core Ops, SparseCore 0:
  18.6 41.8 all-gather.5
  69.5 53.3 all-gather.7
  314.7 76.0 reduce-scatter.3
  415.3 88.5 all-gather.9
  522.4 73.5 reduce-scatter.5
  642.1 73.8 reduce-scatter.7

commit v4 on v3

--- a/solution.py
+++ b/solution.py
@@ -15,7 +15,7 @@
 F32 = jnp.float32
 VMEM = 56 << 20
 COST = {
-    "give": 8, "give_second": 2.5, "keep": 10, "fold": 4, "spread": 4, "join": 4.5, "finish": 11, "middle": 9.5, "attend": 11,
+    "give": 8, "give_second": 2.5, "keep": 10, "fold": 4, "spread": 4, "join": 4.5, "finish": 5.5, "middle": 9.5, "attend": 11,
     "attend_back": 17, "back_project": 11, "qkv": 5.6, "project": 8.6, "ffn": 22, "last": 5, "tie": 0.5,
 }
 
@@ -226,18 +226,14 @@
             out[...] = piece[...]
 
 
-def finish_body(core, mine, other, *outs, turned):
-    for source, turn in ((mine, 0), (other, 1)):
-
-        @pl.when(pl.program_id(0) == turn)
-        def _():
-            at = 0
-            for k, out in enumerate(outs):
-                flip = turned and k == len(outs) - 1
-                width = out.shape[0] if flip else out.shape[1]
-                value = source[:, at : at + width].astype(F32)
-                out[...] = value.T if flip else value
-                at += width
+def finish_body(place, source, *refs, turned, count):
+    at, outs = 0, refs[-count:]
+    for k, out in enumerate(outs):
+        flip = turned and k == count - 1
+        width = out.shape[0] if flip else out.shape[1]
+        value = source[:, at : at + width].astype(F32)
+        out[...] = value.T if flip else value
+        at += width
 
 
 class Product:
@@ -406,31 +402,31 @@
             p.other = self.swap(p.half, 0)
 
     def finish(self, order, at=0):
+        outs = self.fill(order, at, 0)
+        return self.fill(order, at, 1, outs)
+
+    def fill(self, order, at, other, ahead=()):
         p = self.products[at]
         rows, cols = p.half.shape
         crows = min(256, rows)
         nblk = rows // crows
         turned = bool(p.pair)
-        specs = [
-            pl.BlockSpec((crows, w), lambda g, b, s: ((g ^ s[0]) * nblk + b, 0)) for w in p.widths
-        ]
+        specs = [pl.BlockSpec((crows, w), lambda b, s: (s[0] * nblk + b, 0)) for w in p.widths]
         shapes = [jax.ShapeDtypeStruct((2 * rows, w), F32) for w in p.widths]
         if turned:
             w = p.widths[-1]
-            specs[-1] = pl.BlockSpec((w, crows), lambda g, b, s: (0, (g ^ s[0]) * nblk + b))
+            specs[-1] = pl.BlockSpec((w, crows), lambda b, s: (0, s[0] * nblk + b))
             shapes[-1] = jax.ShapeDtypeStruct((w, 2 * rows), F32)
         return call(
-            functools.partial(finish_body, turned=turned),
+            functools.partial(finish_body, turned=turned, count=len(specs)),
             name="finish",
-            grid=(2, nblk),
+            grid=(nblk,),
             scalars=1,
-            in_specs=[
-                pl.BlockSpec((crows, cols), lambda g, b, s: (jnp.where(g == 0, b, nblk - 1), 0)),
-                pl.BlockSpec((crows, cols), lambda g, b, s: (jnp.where(g == 0, 0, b), 0)),
-            ],
+            in_specs=[pl.BlockSpec((crows, cols), lambda b, s: (b, 0))] + [ANY] * len(ahead),
             out_specs=specs,
             out_shape=shapes,
-        )(order, self.scalars(self.bit(0)), p.half, p.other)
+            aliases={2 + k: k for k in range(len(ahead))},
+        )(order, self.scalars(self.bit(0) ^ other), p.other if other else p.half, *ahead)
 
 
 class GainTotals:
@@ -873,14 +869,19 @@
         if j == tensor - 1:
             cots = LineGather(cotangent, tensor, place)
             cots.step(order)
+        usual, order.worth = order.worth, 20 if j == tensor - 1 else order.worth
         held = qkv_slot(order, chunk[j], line.slot(j), w_query, w_key, w_value, cos, sin, held, tensor)
-        if j == 1:
+        order.worth = usual
+        if j == min(2, tensor - 1):
             (w_cols,) = order.after(w_cols)
             w_out_all = lax.all_gather(w_cols, "dp", axis=0)
     query, key, value, normed_t = held
+    cots.step(order)
     (mixed,) = attend(order, doc_ids, query, key, value)
     mix = exchange(mixed)
+    cot_slots = list(order.after(cots.slot(1)))
     cots.step(order)
+    cot_slots += order.after(cots.slot(2))
     resid, normed2_own = project(order, mix, w_out_all, layer_in, ffn_gain)
 
     weights = (w_gate, w_up, w_down)
@@ -895,7 +896,8 @@
         else:
             cots.hold(order)
             line.hold(order)
-        held = ffn_slot(order, chunk[j], line.slot(j), cots.slot(j), *weights, held, tensor)
+        cot = cot_slots[j - 1] if j < 3 else cots.slot(j)
+        held = ffn_slot(order, chunk[j], line.slot(j), cot, *weights, held, tensor)
     inner_t, d_gate, d_up, normed2_t, cot_all, d_normed2_part, down_part = held
     d_normed2 = lax.psum_scatter(d_normed2_part, "tensor", scatter_dimension=0, tiled=True)
 
@@ -940,29 +942,33 @@
     order.worth = usual
     for _ in more:
         wide.spread(order)
+    for _ in more:
+        attn.fold(order)
+    down_sum = lax.psum_scatter(
+        order.after(down_part)[0], "tensor", scatter_dimension=0, tiled=True
+    )
     (down_grad,) = first.finish(order)
     in_grad, attn_gain_part = last(order, d_normed, layer_in, d_resid, attn_gain)
     totals = GainTotals([attn_gain_part, ffn_gain_part], dp, tensor)
     totals.step(order)
     totals.step(order)
-    down_sum = lax.psum_scatter(
-        order.after(down_part)[0], "tensor", scatter_dimension=0, tiled=True
-    )
     totals.step(order)
+    wide.hold(order)
+    order.worth = 0.3
+    wide.join(order)
     attn.hold(order)
     order.worth = 0.3
-    wide.hold(order)
-    wide.join(order)
-    for _ in more:
-        attn.fold(order)
-    totals.step(order)
-    (gate_grad,) = wide.finish(order, 0)
     for _ in more:
         attn.spread(order)
+    order.worth = 0.3
+    (gate_grad,) = wide.finish(order, 0)
     (up_grad,) = wide.finish(order, 1)
+    (down_sum,) = order.after(down_sum)
+    attn.join(order)
+    totals.step(order)
+    attn_grads = attn.fill(order, 0, 0)
     attn_gain_grad, ffn_gain_grad = totals.split(order)
-    attn.join(order)
-    query_grad, key_grad, value_grad, out_grad = attn.finish(order)
+    query_grad, key_grad, value_grad, out_grad = attn.fill(order, 0, 1, attn_grads)
     layer_out = (resid + down_sum.astype(F32)).astype(BF)
     return (
         layer_out,

time: 752 us -> 754 us (level)
  waiting for transfers between devices: 219 us -> 203 us
  starting transfers between devices: 67.4 us -> 79.3 us
    ppermute x9, waiting for transfers between devices: 52.3 us -> 76.3 us  [step(): lax.ppermute(down, 'tensor', [(i + 1, i) for i in range(0, size - k)])]
    ppermute x9, waiting for transfers between devices: 21 us -> 0.02 us  [step(): lax.ppermute(up, 'tensor', [(i, i + 1) for i in range(k - 1, size - 1)])]
    ppermute x5, waiting for transfers between devices: 26.3 us -> 11.4 us  [next(): lax.ppermute(self.value, name, xor_pairs(size, m))]
    ppermute x9, starting transfers between devices: 15.3 us -> 23.6 us  [step(): lax.ppermute(up, 'tensor', [(i, i + 1) for i in range(k - 1, size - 1)])]
    all_to_all x2, waiting for transfers between devices: 15 us -> 7.22 us  [exchange(): return lax.all_to_all(values, 'tensor', 0, 0, tiled=True)]
    pallas_call x59 -> x66, Pallas kernels: 377 us -> 381 us  [run(): pl.pallas_call(whole, grid_spec=pltpu.PrefetchScalarGridSpec(num_scalar_p...]
    unnamed x129 -> x127, local copies, waits for them, and re-layouts: 24 us -> 26.1 us
  transfers between devices with their start and end apart: 64 -> 64, of which waited for: 25 -> 27; matrix products, arithmetic and copies ran while one was open for 5% -> 5% of each run, Pallas kernels for 44% -> 45%
where the time goes in v4:
time: 754 us; the launch traced here: 743 us
  Pallas kernels  381 us (51%)
  waiting for transfers between devices  203 us (27%)
  starting transfers between devices  79.3 us (11%)
  other arithmetic  36.1 us (5%)
  local copies, waits for them, and re-layouts  29 us (4%)
  between operations  15.2 us (2%)
    pallas_call x66, Pallas kernels, run(): pl.pallas_call(whole, grid_spec=pltpu.PrefetchScalarGridSpec(num_scalar_p...  381 us
    ppermute x33, waiting for transfers between devices, swap(): return lax.ppermute(value, 'dp', xor_pairs(self.count, 1 << b))  108 us
    ppermute x9, waiting for transfers between devices, step(): lax.ppermute(down, 'tensor', [(i + 1, i) for i in range(0, size - k)])  76.3 us
    ppermute x33, starting transfers between devices, swap(): return lax.ppermute(value, 'dp', xor_pairs(self.count, 1 << b))  26.4 us
    unnamed x127, local copies, waits for them, and re-layouts  26.1 us
    ppermute x9, starting transfers between devices, step(): lax.ppermute(up, 'tensor', [(i, i + 1) for i in range(k - 1, size - 1)])  23.6 us
    select_n x9, other arithmetic, slot(): value = jnp.where(here, arr, value)  20 us
  transfers between devices with their start and end apart: 64, of which 27 were waited for; matrix products, arithmetic and copies ran while one was open for 5% of the time, Pallas kernels for 45%

profile of v4, /device:TPU:0, one launch (start us, length us, event | category | flops | bytes accessed | tf_op | source)
XLA Modules:
  0.0 743.4 jit_solution(17202786702753825688)
XLA Ops:
  29.8 26.5 %collective-permute-done.1.refs_1_ = bf16[256,2048]{1,0:T(8,128)(2,1)S(1)} collective-permute-done((bf16[256,2048]{1,0:T(8,128)(2,1)}, bf16[256,2048]{1,0:T(8,128)(2,1)S(1)}, u32[]{:S(2)}, u32[]{:S(2)}) %collective-permute-start.1) | collective-permute-done | bytes 1048608 | tf_op jit(solution)/shard_map/ppermute | solution.py:120
  67.8 19.9 %collective-permute-done.3.refs_1_ = bf16[256,2048]{1,0:T(8,128)(2,1)S(1)} collective-permute-done((bf16[256,2048]{1,0:T(8,128)(2,1)}, bf16[256,2048]{1,0:T(8,128)(2,1)S(1)}, u32[]{:S(2)}, u32[]{:S(2)}) %collective-permute-start.3) | collective-permute-done | bytes 1048608 | tf_op jit(solution)/shard_map/ppermute | solution.py:120
  126.3 10.3 %collective-permute-done.7.refs_1_ = bf16[256,2048]{1,0:T(8,128)(2,1)S(1)} collective-permute-done((bf16[256,2048]{1,0:T(8,128)(2,1)}, bf16[256,2048]{1,0:T(8,128)(2,1)S(1)}, u32[]{:S(2)}, u32[]{:S(2)}) %collective-permute-start.7) | collective-permute-done | bytes 1048608 | tf_op jit(solution)/shard_map/ppermute | solution.py:120
  141.5 13.8 %attend.1 = (bf16[1024,512]{1,0:T(8,128)(2,1)}, f32[8,128]{1,0:T(8,128)}) custom-call(s32[1024]{0:T(1024)} %refs_0_.4, bf16[1024,512]{1,0:T(8,128)(2,1)} %get-tuple-element.251.refs_1_, bf16[1024,512]{1,0:T(8,128)(2,1)} %get-tuple-element.252.refs_2_, bf16[1024,512]{1,0:T(8,128)(2,1)} %get-tuple-element.253.refs_3_, s32[1024,1]{1,0:T(8,128)} %copy.102.refs_4_.refs_5_, ...), custom_call_target="tpu_custom_call" | custom-call | flops 14300000256 | bytes 11000000 | tf_op jit(solution)/shard_map/attend/pallas_call | solution.py:57
  162.5 10.7 %collective-permute-done.9.refs_1_ = bf16[256,2048]{1,0:T(8,128)(2,1)} collective-permute-done((bf16[256,2048]{1,0:T(8,128)(2,1)}, bf16[256,2048]{1,0:T(8,128)(2,1)}, u32[]{:S(2)}, u32[]{:S(2)}) %collective-permute-start.9) | collective-permute-done | bytes 1048608 | tf_op jit(solution)/shard_map/ppermute | solution.py:120
  202.4 22.3 %ffn.4 = (bf16[2048,1024]{1,0:T(8,128)(2,1)}, bf16[1024,2048]{1,0:T(8,128)(2,1)}, bf16[1024,2048]{1,0:T(8,128)(2,1)}, bf16[2048,1024]{1,0:T(8,128)(2,1)}, bf16[1...) custom-call(s32[1]{0:T(128)} %bitcast.1.refs_0_, ...), custom_call_target="tpu_custom_call" | custom-call | flops 28600000512 | bytes 22000000 | tf_op jit(solution)/shard_map/ffn/pallas_call | solution.py:57
  231.6 22.2 %ffn.5 = (bf16[2048,1024]{1,0:T(8,128)(2,1)}, bf16[1024,2048]{1,0:T(8,128)(2,1)}, bf16[1024,2048]{1,0:T(8,128)(2,1)}, bf16[2048,1024]{1,0:T(8,128)(2,1)}, bf16[1...) custom-call(s32[1]{0:T(128)} %bitcast.2.refs_0_, ...), custom_call_target="tpu_custom_call", output_to_operand_aliasing={{0}: (6, {}), {1}: (7, {}), {2}: (8, {}), {3}: (9, {}), {4}... | custom-call | flops 28600000512 | bytes 22000000 | tf_op jit(solution)/shard_map/ffn/pallas_call | solution.py:57
  260.5 22.2 %ffn.6 = (bf16[2048,1024]{1,0:T(8,128)(2,1)}, bf16[1024,2048]{1,0:T(8,128)(2,1)}, bf16[1024,2048]{1,0:T(8,128)(2,1)}, bf16[2048,1024]{1,0:T(8,128)(2,1)}, bf16[1...) custom-call(s32[1]{0:T(128)} %bitcast.3.refs_0_, ...), custom_call_target="tpu_custom_call", output_to_operand_aliasing={{0}: (6, {}), {1}: (7, {}), {2}: (8, {}), {3}: (9, {}), {4}... | custom-call | flops 28600000512 | bytes 22000000 | tf_op jit(solution)/shard_map/ffn/pallas_call | solution.py:57
  290.2 22.2 %ffn.7 = (bf16[2048,1024]{1,0:T(8,128)(2,1)}, bf16[1024,2048]{1,0:T(8,128)(2,1)}, bf16[1024,2048]{1,0:T(8,128)(2,1)}, bf16[2048,1024]{1,0:T(8,128)(2,1)}, bf16[1...) custom-call(s32[1]{0:T(128)} %bitcast.refs_0_, ...), custom_call_target="tpu_custom_call", output_to_operand_aliasing={{0}: (6, {}), {1}: (7, {}), {2}: (8, {}), {3}: (9, {}), {4}... | custom-call | flops 28600000512 | bytes 22000000 | tf_op jit(solution)/shard_map/ffn/pallas_call | solution.py:57
  312.4 8.5 %give.4 = (bf16[1024,2048]{1,0:T(8,128)(2,1)}, f32[8,128]{1,0:T(8,128)}) custom-call(s32[1]{0:T(128)} %bitcast.13.refs_0_, bf16[2048,1024]{1,0:T(8,128)(2,1)} %get-tuple-element.311.refs_1_, bf16[1024,2048]{1,0:T(8,128)(2,1)} %get-tuple-element.312.refs_2_, f32[8,128]{1,0:T(8,128)} %get-tuple-element.313.refs_3_), custom_call_target="tpu_custom_call" | custom-call | flops 10400000000 | bytes 8000000 | tf_op jit(solution)/shard_map/give/pallas_call | solution.py:57
  321.1 8.5 %give.5 = (bf16[1024,2048]{1,0:T(8,128)(2,1)}, f32[8,128]{1,0:T(8,128)}) custom-call(s32[1]{0:T(128)} %bitcast.13.refs_0_, bf16[2048,1024]{1,0:T(8,128)(2,1)} %get-tuple-element.315.refs_1_, bf16[1024,2048]{1,0:T(8,128)(2,1)} %get-tuple-element.317.refs_2_, f32[8,128]{1,0:T(8,128)} %get-tuple-element.318.refs_3_), custom_call_target="tpu_custom_call" | custom-call | flops 10400000000 | bytes 8000000 | tf_op jit(solution)/shard_map/give/pallas_call | solution.py:57
  341.1 10.6 %keep.4 = (bf16[512,1024]{1,0:T(8,128)(2,1)}, bf16[512,1024]{1,0:T(8,128)(2,1)}, bf16[512,1024]{1,0:T(8,128)(2,1)}, bf16[512,1024]{1,0:T(8,128)(2,1)}, f32[8,128]{1,0:T(8,128)}) custom-call(s32[3]{0:T(128)} %pad_add_fusion.1.refs_0_, bf16[2048,1024]{1,0:T(8,128)(2,1)} %get-tuple-element.311.refs_1_, bf16[1024,2048]{1,0:T(8,128)(2,1)} %get-tuple-element.312.refs_2_, ...), custom_call_target="tpu_custom_call" | custom-call | flops 12999999488 | bytes 10000000 | tf_op jit(solution)/shard_map/keep/pallas_call | solution.py:57
  354.6 10.3 %keep.5 = (bf16[512,2048]{1,0:T(8,128)(2,1)}, bf16[512,2048]{1,0:T(8,128)(2,1)}, f32[8,128]{1,0:T(8,128)}) custom-call(s32[2]{0:T(128)} %pad_add_fusion.3.refs_0_, bf16[2048,1024]{1,0:T(8,128)(2,1)} %get-tuple-element.315.refs_1_, bf16[1024,2048]{1,0:T(8,128)(2,1)} %get-tuple-element.317.refs_2_, bf16[1024,2048]{1,0:T(8,128)(2,1)} %collective-permute-done.22.refs_3_, ...), custom_call_target="tpu_custom_call" | custom-call | flops 12999999488 | bytes 10000000 | tf_op jit(solution)/shard_map/keep/pallas_call | solution.py:57
  364.9 10.3 %keep.6 = (bf16[512,2048]{1,0:T(8,128)(2,1)}, bf16[512,2048]{1,0:T(8,128)(2,1)}, f32[8,128]{1,0:T(8,128)}) custom-call(s32[2]{0:T(128)} %pad_add_fusion.4.refs_0_, bf16[2048,1024]{1,0:T(8,128)(2,1)} %get-tuple-element.315.refs_1_, bf16[1024,2048]{1,0:T(8,128)(2,1)} %get-tuple-element.316.refs_2_, bf16[1024,2048]{1,0:T(8,128)(2,1)} %collective-permute-done.21.refs_3_, ...), custom_call_target="tpu_custom_call" | custom-call | flops 12999999488 | bytes 10000000 | tf_op jit(solution)/shard_map/keep/pallas_call | solution.py:57
  388.3 11.0 %collective-permute-done.23.refs_2_ = bf16[256,1024]{1,0:T(8,128)(2,1)S(1)} collective-permute-done((bf16[256,1024]{1,0:T(8,128)(2,1)}, bf16[256,1024]{1,0:T(8,128)(2,1)S(1)}, u32[]{:S(2)}, u32[]{:S(2)}) %collective-permute-start.23) | collective-permute-done | bytes 524320 | tf_op jit(solution)/shard_map/ppermute | solution.py:269
  404.9 9.4 %middle.1 = (bf16[1024,512]{1,0:T(8,128)(2,1)}, f32[256,2048]{1,0:T(8,128)}, bf16[2048,256]{1,0:T(8,128)(2,1)}, f32[1,2048]{1,0:T(1,128)}, f32[8,128]{1,0:T(8,128)}) custom-call(bf16[256,2048]{1,0:T(8,128)(2,1)} %reduce-scatter.4.cloned.1.call-done.refs_0_, f32[256,2048]{1,0:T(8,128)} %get-tuple-element.267.refs_1_, bf16[256,2048]{1,0:T(8,128)(2,1)} %refs_2_.14, ...), custom_call_target="tpu_custom_call" | custom-call | flops 12350000128 | bytes 9500000 | tf_op jit(solution)/shard_map/middle/pallas_call | solution.py:57
  421.7 32.3 %collective-permute-done.27.refs_2_ = bf16[256,1024]{1,0:T(8,128)(2,1)S(1)} collective-permute-done((bf16[256,1024]{1,0:T(8,128)(2,1)S(1)}, bf16[256,1024]{1,0:T(8,128)(2,1)S(1)}, u32[]{:S(2)}, u32[]{:S(2)}) %collective-permute-start.27) | collective-permute-done | bytes 524320 | tf_op jit(solution)/shard_map/ppermute | solution.py:269
  471.9 21.3 %attend_back.1 = (bf16[1024,1536]{1,0:T(8,128)(2,1)}, f32[8,128]{1,0:T(8,128)}) custom-call(s32[1024]{0:T(1024)} %refs_0_.4, bf16[1024,512]{1,0:T(8,128)(2,1)} %get-tuple-element.251.refs_1_, bf16[1024,512]{1,0:T(8,128)(2,1)} %get-tuple-element.252.refs_2_, bf16[1024,512]{1,0:T(8,128)(2,1)} %get-tuple-element.253.refs_3_, bf16[1024,512]{1,0:T(8,128)(2,1)} %bitcast.27, ...), custom_call_target="tpu_custom_call" | custom-call | flops 22100000768 | bytes 17000000 | tf_op jit(solution)/shard_map/attend_back/pallas_call | solution.py:57
  500.2 11.1 %back_project.1 = (bf16[1024,2048]{1,0:T(8,128)(2,1)}, f32[8,128]{1,0:T(8,128)}) custom-call(bf16[1024,1536]{1,0:T(8,128)(2,1)} %get-tuple-element.346.refs_2_.refs_0_, bf16[2048,512]{1,0:T(8,128)(2,1)} %refs_1_.2, bf16[2048,512]{1,0:T(8,128)(2,1)} %refs_2_.15, bf16[2048,512]{1,0:T(8,128)(2,1)} %refs_3_.17, f32[8,128]{1,0:T(8,128)} %get-tuple-element.356.refs_4_), custom_call_target="tpu_custom_call" | custom-call | flops 14300000256 | bytes 11000000 | tf_op jit(solution)/shard_map/back_project/pallas_call | solution.py:57
  531.0 11.9 %keep.7 = (bf16[512,1024]{1,0:T(8,128)(2,1)}, bf16[512,1024]{1,0:T(8,128)(2,1)}, bf16[512,1024]{1,0:T(8,128)(2,1)}, bf16[512,1024]{1,0:T(8,128)(2,1)}, f32[8,128]{1,0:T(8,128)}) custom-call(s32[3]{0:T(128)} %pad_add_fusion.1.refs_0_, bf16[2048,1024]{1,0:T(8,128)(2,1)} %get-tuple-element.309.refs_1_, bf16[1024,1536]{1,0:T(8,128)(2,1)} %get-tuple-element.346.refs_2_.refs_0_, ...), custom_call_target="tpu_custom_call" | custom-call | flops 12999999488 | bytes 10000000 | tf_op jit(solution)/shard_map/keep/pallas_call | solution.py:57
  545.0 8.5 %collective-permute-done.37.refs_0_ = bf16[256,2048]{1,0:T(8,128)(2,1)S(1)} collective-permute-done((bf16[256,2048]{1,0:T(8,128)(2,1)S(1)}, bf16[256,2048]{1,0:T(8,128)(2,1)S(1)}, u32[]{:S(2)}, u32[]{:S(2)}) %collective-permute-start.37) | collective-permute-done | bytes 1048608 | tf_op jit(solution)/shard_map/ppermute | solution.py:269
  555.5 19.7 %collective-permute-done.35.refs_2_ = bf16[512,1024]{1,0:T(8,128)(2,1)S(1)} collective-permute-done((bf16[512,1024]{1,0:T(8,128)(2,1)}, bf16[512,1024]{1,0:T(8,128)(2,1)S(1)}, u32[]{:S(2)}, u32[]{:S(2)}) %collective-permute-start.35) | collective-permute-done | bytes 1048608 | tf_op jit(solution)/shard_map/ppermute | solution.py:269
  636.9 9.2 %collective-permute-done.42.refs_1_ = bf16[512,2048]{1,0:T(8,128)(2,1)S(1)} collective-permute-done((bf16[512,2048]{1,0:T(8,128)(2,1)}, bf16[512,2048]{1,0:T(8,128)(2,1)S(1)}, u32[]{:S(2)}, u32[]{:S(2)}) %collective-permute-start.42) | collective-permute-done | bytes 2097184 | tf_op jit(solution)/shard_map/ppermute | solution.py:269
  659.9 11.5 %collective-permute-done.49.refs_0_ = bf16[256,1024]{1,0:T(8,128)(2,1)S(1)} collective-permute-done((bf16[256,1024]{1,0:T(8,128)(2,1)S(1)}, bf16[256,1024]{1,0:T(8,128)(2,1)S(1)}, u32[]{:S(2)}, u32[]{:S(2)}) %collective-permute-start.49) | collective-permute-done | bytes 524320 | tf_op jit(solution)/shard_map/ppermute | solution.py:269
  (335 shorter events, 364.2 us)
Async XLA Ops:
  7.2 92.1 %all-gather.6.cloned.1.call-start = ((), (), s32[]{:S(2)}) async-start(), calls=%async_computation.5 | async-start | bytes 1310720 | tf_op jit(solution)/shard_map/all_gather | solution.py:852
  11.4 44.8 %collective-permute-start.1 = (bf16[256,2048]{1,0:T(8,128)(2,1)}, bf16[256,2048]{1,0:T(8,128)(2,1)S(1)}, u32[]{:S(2)}, u32[]{:S(2)}) collective-permute-start(bf16[256,2048]{1,0:T(8,128)(2,1)} %fusion.2.refs_1_), channel_id=1, source_target_pairs={{1,0},{2,1},{3,2},{5,4},{6,5},{7,6},{9,8},{10,9},{11,10},{13,12},{... | collective-permute-start | bytes 3145736 | tf_op jit(solution)/shard_map/ppermute | solution.py:120
  12.7 43.6 %collective-permute-start = (bf16[256,2048]{1,0:T(8,128)(2,1)}, bf16[256,2048]{1,0:T(8,128)(2,1)}, u32[]{:S(2)}, u32[]{:S(2)}) collective-permute-start(bf16[256,2048]{1,0:T(8,128)(2,1)} %fusion.2.refs_1_), channel_id=1, source_target_pairs={{0,1},{1,2},{2,3},{4,5},{5,6},{6,7},{8,9},{9,10},{10,11},{12,13},{... | collective-permute-start | bytes 3145736 | tf_op jit(solution)/shard_map/ppermute | solution.py:119
  20.1 167.1 %all-gather.8.cloned.1.call-start = ((), (), s32[]{:S(2)}) async-start(), calls=%async_computation.9 | async-start | bytes 9437184 | tf_op jit(solution)/shard_map/all_gather | solution.py:877
  102.6 34.1 %collective-permute-start.7 = (bf16[256,2048]{1,0:T(8,128)(2,1)}, bf16[256,2048]{1,0:T(8,128)(2,1)S(1)}, u32[]{:S(2)}, u32[]{:S(2)}) collective-permute-start(bf16[256,2048]{1,0:T(8,128)(2,1)} %get-tuple-element.254), channel_id=1, source_target_pairs={{1,0},{2,1},{3,2},{5,4},{6,5},{7,6},{9,8},{10,9},{11,10},{13,12},{... | collective-permute-start | bytes 3145736 | tf_op jit(solution)/shard_map/ppermute | solution.py:120
  160.8 244.1 %reduce-scatter.4.cloned.1.call-start = ((), (), s32[]{:S(2)}) async-start(), calls=%async_computation.6 | async-start | bytes 5242880 | tf_op jit(solution)/shard_map/reduce_scatter | solution.py:902
  173.8 108.9 %collective-permute-start.16 = (bf16[256,2048]{1,0:T(8,128)(2,1)}, bf16[256,2048]{1,0:T(8,128)(2,1)}, u32[]{:S(2)}, u32[]{:S(2)}) collective-permute-start(bf16[256,2048]{1,0:T(8,128)(2,1)} %get-tuple-element.263), channel_id=1, source_target_pairs={{2,3},{6,7},{10,11},{14,15},{18,19},{22,23},{26,27},{30,31}} | collective-permute-start | bytes 3145736 | tf_op jit(solution)/shard_map/ppermute | solution.py:119
  175.5 107.2 %collective-permute-start.17 = (bf16[256,2048]{1,0:T(8,128)(2,1)}, bf16[256,2048]{1,0:T(8,128)(2,1)}, u32[]{:S(2)}, u32[]{:S(2)}) collective-permute-start(bf16[256,2048]{1,0:T(8,128)(2,1)} %get-tuple-element.264), channel_id=1, source_target_pairs={{1,0},{5,4},{9,8},{13,12},{17,16},{21,20},{25,24},{29,28}} | collective-permute-start | bytes 3145736 | tf_op jit(solution)/shard_map/ppermute | solution.py:120
  320.9 201.8 %all-gather.10.cloned.1.call-start = ((), (), s32[]{:S(2)}) async-start(), calls=%async_computation.10 | async-start | bytes 5242880 | tf_op jit(solution)/shard_map/all_gather | solution.py:921
  386.4 74.7 %collective-permute-start.26 = (bf16[512,2048]{1,0:T(8,128)(2,1)}, bf16[512,2048]{1,0:T(8,128)(2,1)}, u32[]{:S(2)}, u32[]{:S(2)}) collective-permute-start(bf16[512,2048]{1,0:T(8,128)(2,1)} %get-tuple-element.340), channel_id=1, source_target_pairs={{0,16},{4,20},{8,24},{12,28},{16,0},{20,4},{24,8},{28,12},{1,17},{... | collective-permute-start | bytes 6291464 | tf_op jit(solution)/shard_map/ppermute | solution.py:269
  387.0 74.2 %collective-permute-start.25 = (bf16[512,2048]{1,0:T(8,128)(2,1)}, bf16[512,2048]{1,0:T(8,128)(2,1)}, u32[]{:S(2)}, u32[]{:S(2)}) collective-permute-start(bf16[512,2048]{1,0:T(8,128)(2,1)} %get-tuple-element.338), channel_id=1, source_target_pairs={{0,8},{4,12},{8,0},{12,4},{16,24},{20,28},{24,16},{28,20},{1,9},{5... | collective-permute-start | bytes 6291464 | tf_op jit(solution)/shard_map/ppermute | solution.py:269
  414.4 56.6 %all-to-all-start.1 = ((bf16[4,256,512]{2,1,0:T(8,128)(2,1)}), bf16[4,256,512]{2,1,0:T(8,128)(2,1)S(1)}, u32[]{:S(2)}, u32[]{:S(2)}) async-start(bf16[4,256,512]{2,1,0:T(8,128)(2,1)} %bitcast.26), calls=%async_computation.2 | async-start | bytes 2097152 | tf_op jit(solution)/shard_map/all_to_all | solution.py:141
  420.2 194.5 %reduce-scatter.8.cloned.1.call-start = ((), (), s32[]{:S(2)}) async-start(), calls=%async_computation.8 | async-start | bytes 5242880 | tf_op jit(solution)/shard_map/reduce_scatter | solution.py:928
  420.4 33.5 %collective-permute-start.27 = (bf16[256,1024]{1,0:T(8,128)(2,1)S(1)}, bf16[256,1024]{1,0:T(8,128)(2,1)S(1)}, u32[]{:S(2)}, u32[]{:S(2)}) collective-permute-start(bf16[256,1024]{1,0:T(8,128)(2,1)S(1)} %copy-done.55), channel_id=1, source_target_pairs={{0,16},{4,20},{8,24},{12,28},{16,0},{20,4},{24,8},{28,12},{1,17},{... | collective-permute-start | bytes 1572872 | tf_op jit(solution)/shard_map/ppermute | solution.py:269
  420.7 34.5 %collective-permute-start.28 = (bf16[256,1024]{1,0:T(8,128)(2,1)S(1)}, bf16[256,1024]{1,0:T(8,128)(2,1)S(1)}, u32[]{:S(2)}, u32[]{:S(2)}) collective-permute-start(bf16[256,1024]{1,0:T(8,128)(2,1)S(1)} %copy-done.56), channel_id=1, source_target_pairs={{0,8},{4,12},{8,0},{12,4},{16,24},{20,28},{24,16},{28,20},{1,9},{5... | collective-permute-start | bytes 1572872 | tf_op jit(solution)/shard_map/ppermute | solution.py:269
  459.6 52.0 %collective-permute-start.32 = (bf16[512,1024]{1,0:T(8,128)(2,1)}, bf16[512,1024]{1,0:T(8,128)(2,1)S(1)}, u32[]{:S(2)}, u32[]{:S(2)}) collective-permute-start(bf16[512,1024]{1,0:T(8,128)(2,1)} %get-tuple-element.354.refs_1_), channel_id=1, source_target_pairs={{0,8},{4,12},{8,0},{12,4},{16,24},{20,28},{24,16},{28,20},{1,9},{5... | collective-permute-start | bytes 3145736 | tf_op jit(solution)/shard_map/ppermute | solution.py:269
  460.6 51.0 %collective-permute-start.33 = (bf16[512,1024]{1,0:T(8,128)(2,1)}, bf16[512,1024]{1,0:T(8,128)(2,1)S(1)}, u32[]{:S(2)}, u32[]{:S(2)}) collective-permute-start(bf16[512,1024]{1,0:T(8,128)(2,1)} %get-tuple-element.355.refs_3_), channel_id=1, source_target_pairs={{0,16},{4,20},{8,24},{12,28},{16,0},{20,4},{24,8},{28,12},{1,17},{... | collective-permute-start | bytes 3145736 | tf_op jit(solution)/shard_map/ppermute | solution.py:269
  468.3 50.0 %collective-permute-start.30 = (bf16[256,2048]{1,0:T(8,128)(2,1)}, bf16[256,2048]{1,0:T(8,128)(2,1)}, u32[]{:S(2)}, u32[]{:S(2)}) collective-permute-start(bf16[256,2048]{1,0:T(8,128)(2,1)} %get-tuple-element.351), channel_id=1, source_target_pairs={{0,16},{4,20},{8,24},{12,28},{16,0},{20,4},{24,8},{28,12},{1,17},{... | collective-permute-start | bytes 3145736 | tf_op jit(solution)/shard_map/ppermute | solution.py:269
  469.9 48.5 %collective-permute-start.31 = (bf16[256,2048]{1,0:T(8,128)(2,1)}, bf16[256,2048]{1,0:T(8,128)(2,1)}, u32[]{:S(2)}, u32[]{:S(2)}) collective-permute-start(bf16[256,2048]{1,0:T(8,128)(2,1)} %get-tuple-element.353), channel_id=1, source_target_pairs={{0,8},{4,12},{8,0},{12,4},{16,24},{20,28},{24,16},{28,20},{1,9},{5... | collective-permute-start | bytes 3145736 | tf_op jit(solution)/shard_map/ppermute | solution.py:269
  511.3 193.9 %reduce-scatter.6.cloned.1.call-start = ((), (), s32[]{:S(2)}) async-start(), calls=%async_computation.7 | async-start | bytes 5242880 | tf_op jit(solution)/shard_map/reduce_scatter | solution.py:947
  545.0 63.8 %collective-permute-start.43 = (bf16[1024,2048]{1,0:T(8,128)(2,1)}, bf16[1024,2048]{1,0:T(8,128)(2,1)}, u32[]{:S(2)}, u32[]{:S(2)}) collective-permute-start(bf16[1024,2048]{1,0:T(8,128)(2,1)} %get-tuple-element.384.refs_1_), channel_id=1, source_target_pairs={{0,4},{4,0},{8,12},{12,8},{16,20},{20,16},{24,28},{28,24},{1,5},{5... | collective-permute-start | bytes 12582920 | tf_op jit(solution)/shard_map/ppermute | solution.py:269
  600.4 45.7 %collective-permute-start.42 = (bf16[512,2048]{1,0:T(8,128)(2,1)}, bf16[512,2048]{1,0:T(8,128)(2,1)S(1)}, u32[]{:S(2)}, u32[]{:S(2)}) collective-permute-start(bf16[512,2048]{1,0:T(8,128)(2,1)} %get-tuple-element.380.refs_1_), channel_id=1, source_target_pairs={{0,16},{4,20},{8,24},{12,28},{16,0},{20,4},{24,8},{28,12},{1,17},{... | collective-permute-start | bytes 6291464 | tf_op jit(solution)/shard_map/ppermute | solution.py:269
  601.2 45.8 %collective-permute-start.41 = (bf16[512,2048]{1,0:T(8,128)(2,1)}, bf16[512,2048]{1,0:T(8,128)(2,1)}, u32[]{:S(2)}, u32[]{:S(2)}) collective-permute-start(bf16[512,2048]{1,0:T(8,128)(2,1)} %get-tuple-element.381.refs_1_), channel_id=1, source_target_pairs={{0,8},{4,12},{8,0},{12,4},{16,24},{20,28},{24,16},{28,20},{1,9},{5... | collective-permute-start | bytes 6291464 | tf_op jit(solution)/shard_map/ppermute | solution.py:269
  657.0 40.3 %collective-permute-start.47 = (bf16[1024,2048]{1,0:T(8,128)(2,1)}, bf16[1024,2048]{1,0:T(8,128)(2,1)S(1)}, u32[]{:S(2)}, u32[]{:S(2)}) collective-permute-start(bf16[1024,2048]{1,0:T(8,128)(2,1)} %get-tuple-element.403.refs_1_), channel_id=1, source_target_pairs={{0,4},{4,0},{8,12},{12,8},{16,20},{20,16},{24,28},{28,24},{1,5},{5... | collective-permute-start | bytes 12582920 | tf_op jit(solution)/shard_map/ppermute | solution.py:269
  (103 other events, 1138.6 us)
Sparse Core Ops, SparseCore 0:
  20.2 37.6 all-gather.5
  100.1 55.8 all-gather.7
  321.0 78.7 reduce-scatter.3
  414.5 96.1 all-gather.9
  513.5 75.4 reduce-scatter.7
  600.5 77.9 reduce-scatter.5

commit v5 on v4

--- a/solution.py
+++ b/solution.py
@@ -876,12 +876,10 @@
             (w_cols,) = order.after(w_cols)
             w_out_all = lax.all_gather(w_cols, "dp", axis=0)
     query, key, value, normed_t = held
-    cots.step(order)
     (mixed,) = attend(order, doc_ids, query, key, value)
     mix = exchange(mixed)
-    cot_slots = list(order.after(cots.slot(1)))
     cots.step(order)
-    cot_slots += order.after(cots.slot(2))
+    (cot_first,) = order.after(cots.slot(1))
     resid, normed2_own = project(order, mix, w_out_all, layer_in, ffn_gain)
 
     weights = (w_gate, w_up, w_down)
@@ -896,7 +894,7 @@
         else:
             cots.hold(order)
             line.hold(order)
-        cot = cot_slots[j - 1] if j < 3 else cots.slot(j)
+        cot = cot_first if j == 1 else cots.slot(j)
         held = ffn_slot(order, chunk[j], line.slot(j), cot, *weights, held, tensor)
     inner_t, d_gate, d_up, normed2_t, cot_all, d_normed2_part, down_part = held
     d_normed2 = lax.psum_scatter(d_normed2_part, "tensor", scatter_dimension=0, tiled=True)
@@ -940,13 +938,13 @@
     usual, order.worth = order.worth, 10
     attn.fold(order)
     order.worth = usual
+    down_sum = lax.psum_scatter(
+        order.after(down_part)[0], "tensor", scatter_dimension=0, tiled=True
+    )
     for _ in more:
         wide.spread(order)
     for _ in more:
         attn.fold(order)
-    down_sum = lax.psum_scatter(
-        order.after(down_part)[0], "tensor", scatter_dimension=0, tiled=True
-    )
     (down_grad,) = first.finish(order)
     in_grad, attn_gain_part = last(order, d_normed, layer_in, d_resid, attn_gain)
     totals = GainTotals([attn_gain_part, ffn_gain_part], dp, tensor)
@@ -961,14 +959,18 @@
     for _ in more:
         attn.spread(order)
     order.worth = 0.3
-    (gate_grad,) = wide.finish(order, 0)
-    (up_grad,) = wide.finish(order, 1)
+    order.worth = 5
+    gate_grad = wide.fill(order, 0, 0)
+    up_grad = wide.fill(order, 1, 0)
+    order.worth = 0.02
+    (gate_grad,) = wide.fill(order, 0, 1, gate_grad)
+    (up_grad,) = wide.fill(order, 1, 1, up_grad)
     (down_sum,) = order.after(down_sum)
     attn.join(order)
+    attn_grads = attn.fill(order, 0, 0)
     totals.step(order)
-    attn_grads = attn.fill(order, 0, 0)
+    query_grad, key_grad, value_grad, out_grad = attn.fill(order, 0, 1, attn_grads)
     attn_gain_grad, ffn_gain_grad = totals.split(order)
-    query_grad, key_grad, value_grad, out_grad = attn.fill(order, 0, 1, attn_grads)
     layer_out = (resid + down_sum.astype(F32)).astype(BF)
     return (
         layer_out,

time: 754 us -> 728 us (0.966)
  waiting for transfers between devices: 203 us -> 184 us
    ppermute x9, waiting for transfers between devices: 76.3 us -> 62.8 us  [step(): lax.ppermute(down, 'tensor', [(i + 1, i) for i in range(0, size - k)])]
    ppermute x33, waiting for transfers between devices: 108 us -> 94.6 us  [swap(): return lax.ppermute(value, 'dp', xor_pairs(self.count, 1 << b))]
    all_to_all x2, waiting for transfers between devices: 7.22 us -> 15.3 us  [exchange(): return lax.all_to_all(values, 'tensor', 0, 0, tiled=True)]
    pallas_call x66 -> x65, Pallas kernels: 381 us -> 374 us  [run(): pl.pallas_call(whole, grid_spec=pltpu.PrefetchScalarGridSpec(num_scalar_p...]
    unnamed x127 -> x129, local copies, waits for them, and re-layouts: 26.1 us -> 25.3 us
  transfers between devices with their start and end apart: 64 -> 64, of which waited for: 27 -> 23; matrix products, arithmetic and copies ran while one was open for 5% -> 5% of each run, Pallas kernels for 45% -> 47%
where the time goes in v5:
time: 728 us; the launch traced here: 717 us
  Pallas kernels  374 us (51%)
  waiting for transfers between devices  184 us (25%)
  starting transfers between devices  77.3 us (11%)
  other arithmetic  39.1 us (5%)
  local copies, waits for them, and re-layouts  28.2 us (4%)
  between operations  15.2 us (2%)
    pallas_call x65, Pallas kernels, run(): pl.pallas_call(whole, grid_spec=pltpu.PrefetchScalarGridSpec(num_scalar_p...  374 us
    ppermute x33, waiting for transfers between devices, swap(): return lax.ppermute(value, 'dp', xor_pairs(self.count, 1 << b))  94.6 us
    ppermute x9, waiting for transfers between devices, step(): lax.ppermute(down, 'tensor', [(i + 1, i) for i in range(0, size - k)])  62.8 us
    ppermute x33, starting transfers between devices, swap(): return lax.ppermute(value, 'dp', xor_pairs(self.count, 1 << b))  32.8 us
    unnamed x129, local copies, waits for them, and re-layouts  25.3 us
    ppermute x9, starting transfers between devices, step(): lax.ppermute(up, 'tensor', [(i, i + 1) for i in range(k - 1, size - 1)])  22.7 us
    select_n x9, other arithmetic, slot(): value = jnp.where(here, arr, value)  21.3 us
    all_to_all x2, waiting for transfers between devices, exchange(): return lax.all_to_all(values, 'tensor', 0, 0, tiled=True)  15.3 us
  transfers between devices with their start and end apart: 64, of which 23 were waited for; matrix products, arithmetic and copies ran while one was open for 5% of the time, Pallas kernels for 47%

profile of v5, /device:TPU:0, one launch (start us, length us, event | category | flops | bytes accessed | tf_op | source)
XLA Modules:
  0.0 717.4 jit_solution(17090919879794203532)
XLA Ops:
  29.7 26.5 %collective-permute-done.1.refs_1_ = bf16[256,2048]{1,0:T(8,128)(2,1)S(1)} collective-permute-done((bf16[256,2048]{1,0:T(8,128)(2,1)}, bf16[256,2048]{1,0:T(8,128)(2,1)S(1)}, u32[]{:S(2)}, u32[]{:S(2)}) %collective-permute-start.1) | collective-permute-done | bytes 1048608 | tf_op jit(solution)/shard_map/ppermute | solution.py:120
  67.8 19.9 %collective-permute-done.3.refs_1_ = bf16[256,2048]{1,0:T(8,128)(2,1)S(1)} collective-permute-done((bf16[256,2048]{1,0:T(8,128)(2,1)}, bf16[256,2048]{1,0:T(8,128)(2,1)S(1)}, u32[]{:S(2)}, u32[]{:S(2)}) %collective-permute-start.3) | collective-permute-done | bytes 1048608 | tf_op jit(solution)/shard_map/ppermute | solution.py:120
  111.0 8.2 %collective-permute-done.5 = bf16[256,2048]{1,0:T(8,128)(2,1)} collective-permute-done((bf16[256,2048]{1,0:T(8,128)(2,1)}, bf16[256,2048]{1,0:T(8,128)(2,1)}, u32[]{:S(2)}, u32[]{:S(2)}) %collective-permute-start.5) | collective-permute-done | bytes 1048608 | tf_op jit(solution)/shard_map/ppermute | solution.py:120
  127.3 10.9 %attend.1 = (bf16[1024,512]{1,0:T(8,128)(2,1)}, f32[8,128]{1,0:T(8,128)}) custom-call(s32[1024]{0:T(1024)} %refs_0_.4, bf16[1024,512]{1,0:T(8,128)(2,1)} %get-tuple-element.249.refs_1_, bf16[1024,512]{1,0:T(8,128)(2,1)} %get-tuple-element.250.refs_2_, bf16[1024,512]{1,0:T(8,128)(2,1)} %get-tuple-element.251.refs_3_, s32[1024,1]{1,0:T(8,128)} %copy.101.refs_4_.refs_5_, ...), custom_call_target="tpu_custom_call" | custom-call | flops 14300000256 | bytes 11000000 | tf_op jit(solution)/shard_map/attend/pallas_call | solution.py:57
  149.6 15.3 %all-to-all-done = bf16[4,256,512]{2,1,0:T(8,128)(2,1)} async-done(((bf16[4,256,512]{2,1,0:T(8,128)(2,1)}), bf16[4,256,512]{2,1,0:T(8,128)(2,1)}, u32[]{:S(2)}, u32[]{:S(2)}) %all-to-all-start) | async-done | bytes 1048608 | tf_op jit(solution)/shard_map/all_to_all | solution.py:141
  164.9 8.4 %project.1 = (f32[256,2048]{1,0:T(8,128)}, bf16[256,2048]{1,0:T(8,128)(2,1)}, f32[8,128]{1,0:T(8,128)}) custom-call(bf16[1024,512]{1,0:T(8,128)(2,1)} %bitcast.7.refs_0_, bf16[8,2048,256]{2,1,0:T(8,128)(2,1)} %bitcast.34, bf16[256,2048]{1,0:T(8,128)(2,1)} %refs_1_.3, f32[1,2048]{1,0:T(1,128)} %bitcast.38, f32[8,128]{1,0:T(8,128)} %get-tuple-element.260.refs_4_), custom_call_target="tpu_custom_call" | custom-call | flops 11180000256 | bytes 8600000 | tf_op jit(solution)/shard_map/project/pallas_call | solution.py:57
  179.2 22.2 %ffn.4 = (bf16[2048,1024]{1,0:T(8,128)(2,1)}, bf16[1024,2048]{1,0:T(8,128)(2,1)}, bf16[1024,2048]{1,0:T(8,128)(2,1)}, bf16[2048,1024]{1,0:T(8,128)(2,1)}, bf16[1...) custom-call(s32[1]{0:T(128)} %bitcast.1.refs_0_, ...), custom_call_target="tpu_custom_call" | custom-call | flops 28600000512 | bytes 22000000 | tf_op jit(solution)/shard_map/ffn/pallas_call | solution.py:57
  211.4 22.3 %ffn.5 = (bf16[2048,1024]{1,0:T(8,128)(2,1)}, bf16[1024,2048]{1,0:T(8,128)(2,1)}, bf16[1024,2048]{1,0:T(8,128)(2,1)}, bf16[2048,1024]{1,0:T(8,128)(2,1)}, bf16[1...) custom-call(s32[1]{0:T(128)} %bitcast.2.refs_0_, ...), custom_call_target="tpu_custom_call", output_to_operand_aliasing={{0}: (6, {}), {1}: (7, {}), {2}: (8, {}), {3}: (9, {}), {4}... | custom-call | flops 28600000512 | bytes 22000000 | tf_op jit(solution)/shard_map/ffn/pallas_call | solution.py:57
  243.1 22.3 %ffn.6 = (bf16[2048,1024]{1,0:T(8,128)(2,1)}, bf16[1024,2048]{1,0:T(8,128)(2,1)}, bf16[1024,2048]{1,0:T(8,128)(2,1)}, bf16[2048,1024]{1,0:T(8,128)(2,1)}, bf16[1...) custom-call(s32[1]{0:T(128)} %bitcast.3.refs_0_, ...), custom_call_target="tpu_custom_call", output_to_operand_aliasing={{0}: (6, {}), {1}: (7, {}), {2}: (8, {}), {3}: (9, {}), {4}... | custom-call | flops 28600000512 | bytes 22000000 | tf_op jit(solution)/shard_map/ffn/pallas_call | solution.py:57
  270.0 7.6 %collective-permute-done.15.refs_1_ = bf16[256,2048]{1,0:T(8,128)(2,1)S(1)} collective-permute-done((bf16[256,2048]{1,0:T(8,128)(2,1)}, bf16[256,2048]{1,0:T(8,128)(2,1)S(1)}, u32[]{:S(2)}, u32[]{:S(2)}) %collective-permute-start.15) | collective-permute-done | bytes 1048608 | tf_op jit(solution)/shard_map/ppermute | solution.py:120
  281.5 22.2 %ffn.7 = (bf16[2048,1024]{1,0:T(8,128)(2,1)}, bf16[1024,2048]{1,0:T(8,128)(2,1)}, bf16[1024,2048]{1,0:T(8,128)(2,1)}, bf16[2048,1024]{1,0:T(8,128)(2,1)}, bf16[1...) custom-call(s32[1]{0:T(128)} %bitcast.refs_0_, ...), custom_call_target="tpu_custom_call", output_to_operand_aliasing={{0}: (6, {}), {1}: (7, {}), {2}: (8, {}), {3}: (9, {}), {4}... | custom-call | flops 28600000512 | bytes 22000000 | tf_op jit(solution)/shard_map/ffn/pallas_call | solution.py:57
  303.8 8.5 %give.4 = (bf16[1024,2048]{1,0:T(8,128)(2,1)}, f32[8,128]{1,0:T(8,128)}) custom-call(s32[1]{0:T(128)} %bitcast.13.refs_0_, bf16[2048,1024]{1,0:T(8,128)(2,1)} %get-tuple-element.307.refs_1_, bf16[1024,2048]{1,0:T(8,128)(2,1)} %get-tuple-element.308.refs_2_, f32[8,128]{1,0:T(8,128)} %get-tuple-element.309.refs_3_), custom_call_target="tpu_custom_call" | custom-call | flops 10400000000 | bytes 8000000 | tf_op jit(solution)/shard_map/give/pallas_call | solution.py:57
  312.5 8.4 %give.5 = (bf16[1024,2048]{1,0:T(8,128)(2,1)}, f32[8,128]{1,0:T(8,128)}) custom-call(s32[1]{0:T(128)} %bitcast.13.refs_0_, bf16[2048,1024]{1,0:T(8,128)(2,1)} %get-tuple-element.311.refs_1_, bf16[1024,2048]{1,0:T(8,128)(2,1)} %get-tuple-element.313.refs_2_, f32[8,128]{1,0:T(8,128)} %get-tuple-element.314.refs_3_), custom_call_target="tpu_custom_call" | custom-call | flops 10400000000 | bytes 8000000 | tf_op jit(solution)/shard_map/give/pallas_call | solution.py:57
  321.4 8.4 %give.6 = (bf16[1024,2048]{1,0:T(8,128)(2,1)}, f32[8,128]{1,0:T(8,128)}) custom-call(s32[1]{0:T(128)} %bitcast.13.refs_0_, bf16[2048,1024]{1,0:T(8,128)(2,1)} %get-tuple-element.311.refs_1_, bf16[1024,2048]{1,0:T(8,128)(2,1)} %get-tuple-element.312.refs_2_, f32[8,128]{1,0:T(8,128)} %get-tuple-element.315.refs_3_), custom_call_target="tpu_custom_call" | custom-call | flops 10400000000 | bytes 8000000 | tf_op jit(solution)/shard_map/give/pallas_call | solution.py:57
  332.4 10.7 %keep.4 = (bf16[512,1024]{1,0:T(8,128)(2,1)}, bf16[512,1024]{1,0:T(8,128)(2,1)}, bf16[512,1024]{1,0:T(8,128)(2,1)}, bf16[512,1024]{1,0:T(8,128)(2,1)}, f32[8,128]{1,0:T(8,128)}) custom-call(s32[3]{0:T(128)} %pad_add_fusion.1.refs_0_, bf16[2048,1024]{1,0:T(8,128)(2,1)} %get-tuple-element.307.refs_1_, bf16[1024,2048]{1,0:T(8,128)(2,1)} %get-tuple-element.308.refs_2_, ...), custom_call_target="tpu_custom_call" | custom-call | flops 12999999488 | bytes 10000000 | tf_op jit(solution)/shard_map/keep/pallas_call | solution.py:57
  348.6 10.3 %keep.5 = (bf16[512,2048]{1,0:T(8,128)(2,1)}, bf16[512,2048]{1,0:T(8,128)(2,1)}, f32[8,128]{1,0:T(8,128)}) custom-call(s32[2]{0:T(128)} %pad_add_fusion.3.refs_0_, bf16[2048,1024]{1,0:T(8,128)(2,1)} %get-tuple-element.311.refs_1_, bf16[1024,2048]{1,0:T(8,128)(2,1)} %get-tuple-element.313.refs_2_, bf16[1024,2048]{1,0:T(8,128)(2,1)} %collective-permute-done.22.refs_3_, ...), custom_call_target="tpu_custom_call" | custom-call | flops 12999999488 | bytes 10000000 | tf_op jit(solution)/shard_map/keep/pallas_call | solution.py:57
  358.8 10.4 %keep.6 = (bf16[512,2048]{1,0:T(8,128)(2,1)}, bf16[512,2048]{1,0:T(8,128)(2,1)}, f32[8,128]{1,0:T(8,128)}) custom-call(s32[2]{0:T(128)} %pad_add_fusion.4.refs_0_, bf16[2048,1024]{1,0:T(8,128)(2,1)} %get-tuple-element.311.refs_1_, bf16[1024,2048]{1,0:T(8,128)(2,1)} %get-tuple-element.312.refs_2_, bf16[1024,2048]{1,0:T(8,128)(2,1)} %collective-permute-done.21.refs_3_, ...), custom_call_target="tpu_custom_call" | custom-call | flops 12999999488 | bytes 10000000 | tf_op jit(solution)/shard_map/keep/pallas_call | solution.py:57
  382.0 11.0 %collective-permute-done.23.refs_2_ = bf16[256,1024]{1,0:T(8,128)(2,1)S(1)} collective-permute-done((bf16[256,1024]{1,0:T(8,128)(2,1)}, bf16[256,1024]{1,0:T(8,128)(2,1)S(1)}, u32[]{:S(2)}, u32[]{:S(2)}) %collective-permute-start.23) | collective-permute-done | bytes 524320 | tf_op jit(solution)/shard_map/ppermute | solution.py:269
  398.8 9.4 %middle.1 = (bf16[1024,512]{1,0:T(8,128)(2,1)}, f32[256,2048]{1,0:T(8,128)}, bf16[2048,256]{1,0:T(8,128)(2,1)}, f32[1,2048]{1,0:T(1,128)}, f32[8,128]{1,0:T(8,128)}) custom-call(bf16[256,2048]{1,0:T(8,128)(2,1)} %reduce-scatter.4.cloned.1.call-done.refs_0_, f32[256,2048]{1,0:T(8,128)} %get-tuple-element.261.refs_1_, bf16[256,2048]{1,0:T(8,128)(2,1)} %refs_2_.14, ...), custom_call_target="tpu_custom_call" | custom-call | flops 12350000128 | bytes 9500000 | tf_op jit(solution)/shard_map/middle/pallas_call | solution.py:57
  413.5 34.4 %collective-permute-done.27.refs_2_ = bf16[256,1024]{1,0:T(8,128)(2,1)S(1)} collective-permute-done((bf16[256,1024]{1,0:T(8,128)(2,1)S(1)}, bf16[256,1024]{1,0:T(8,128)(2,1)S(1)}, u32[]{:S(2)}, u32[]{:S(2)}) %collective-permute-start.27) | collective-permute-done | bytes 524320 | tf_op jit(solution)/shard_map/ppermute | solution.py:269
  466.0 16.9 %attend_back.1 = (bf16[1024,1536]{1,0:T(8,128)(2,1)}, f32[8,128]{1,0:T(8,128)}) custom-call(s32[1024]{0:T(1024)} %refs_0_.4, bf16[1024,512]{1,0:T(8,128)(2,1)} %get-tuple-element.249.refs_1_, bf16[1024,512]{1,0:T(8,128)(2,1)} %get-tuple-element.250.refs_2_, bf16[1024,512]{1,0:T(8,128)(2,1)} %get-tuple-element.251.refs_3_, bf16[1024,512]{1,0:T(8,128)(2,1)} %bitcast.27, ...), custom_call_target="tpu_custom_call" | custom-call | flops 22100000768 | bytes 17000000 | tf_op jit(solution)/shard_map/attend_back/pallas_call | solution.py:57
  489.9 11.1 %back_project.1 = (bf16[1024,2048]{1,0:T(8,128)(2,1)}, f32[8,128]{1,0:T(8,128)}) custom-call(bf16[1024,1536]{1,0:T(8,128)(2,1)} %get-tuple-element.342.refs_2_.refs_0_, bf16[2048,512]{1,0:T(8,128)(2,1)} %refs_1_.2, bf16[2048,512]{1,0:T(8,128)(2,1)} %refs_2_.15, bf16[2048,512]{1,0:T(8,128)(2,1)} %refs_3_.17, f32[8,128]{1,0:T(8,128)} %get-tuple-element.352.refs_4_), custom_call_target="tpu_custom_call" | custom-call | flops 14300000256 | bytes 11000000 | tf_op jit(solution)/shard_map/back_project/pallas_call | solution.py:57
  523.7 11.8 %keep.7 = (bf16[512,1024]{1,0:T(8,128)(2,1)}, bf16[512,1024]{1,0:T(8,128)(2,1)}, bf16[512,1024]{1,0:T(8,128)(2,1)}, bf16[512,1024]{1,0:T(8,128)(2,1)}, f32[8,128]{1,0:T(8,128)}) custom-call(s32[3]{0:T(128)} %pad_add_fusion.1.refs_0_, bf16[2048,1024]{1,0:T(8,128)(2,1)} %get-tuple-element.305.refs_1_, bf16[1024,1536]{1,0:T(8,128)(2,1)} %get-tuple-element.342.refs_2_.refs_0_, ...), custom_call_target="tpu_custom_call" | custom-call | flops 12999999488 | bytes 10000000 | tf_op jit(solution)/shard_map/keep/pallas_call | solution.py:57
  547.3 21.3 %collective-permute-done.35.refs_2_ = bf16[512,1024]{1,0:T(8,128)(2,1)} collective-permute-done((bf16[512,1024]{1,0:T(8,128)(2,1)}, bf16[512,1024]{1,0:T(8,128)(2,1)}, u32[]{:S(2)}, u32[]{:S(2)}) %collective-permute-start.35) | collective-permute-done | bytes 1048608 | tf_op jit(solution)/shard_map/ppermute | solution.py:269
  (336 shorter events, 343.7 us)
Async XLA Ops:
  7.2 93.1 %all-gather.6.cloned.1.call-start = ((), (), s32[]{:S(2)}) async-start(), calls=%async_computation.5 | async-start | bytes 1310720 | tf_op jit(solution)/shard_map/all_gather | solution.py:852
  11.4 44.8 %collective-permute-start.1 = (bf16[256,2048]{1,0:T(8,128)(2,1)}, bf16[256,2048]{1,0:T(8,128)(2,1)S(1)}, u32[]{:S(2)}, u32[]{:S(2)}) collective-permute-start(bf16[256,2048]{1,0:T(8,128)(2,1)} %fusion.2.refs_1_), channel_id=1, source_target_pairs={{1,0},{2,1},{3,2},{5,4},{6,5},{7,6},{9,8},{10,9},{11,10},{13,12},{... | collective-permute-start | bytes 3145736 | tf_op jit(solution)/shard_map/ppermute | solution.py:120
  12.7 43.6 %collective-permute-start = (bf16[256,2048]{1,0:T(8,128)(2,1)}, bf16[256,2048]{1,0:T(8,128)(2,1)}, u32[]{:S(2)}, u32[]{:S(2)}) collective-permute-start(bf16[256,2048]{1,0:T(8,128)(2,1)} %fusion.2.refs_1_), channel_id=1, source_target_pairs={{0,1},{1,2},{2,3},{4,5},{5,6},{6,7},{8,9},{9,10},{10,11},{12,13},{... | collective-permute-start | bytes 3145736 | tf_op jit(solution)/shard_map/ppermute | solution.py:119
  20.0 144.9 %all-gather.8.cloned.1.call-start = ((), (), s32[]{:S(2)}) async-start(), calls=%async_computation.9 | async-start | bytes 9437184 | tf_op jit(solution)/shard_map/all_gather | solution.py:877
  103.5 39.0 %collective-permute-start.7 = (bf16[256,2048]{1,0:T(8,128)(2,1)}, bf16[256,2048]{1,0:T(8,128)(2,1)S(1)}, u32[]{:S(2)}, u32[]{:S(2)}) collective-permute-start(bf16[256,2048]{1,0:T(8,128)(2,1)} %get-tuple-element.255), channel_id=1, source_target_pairs={{1,0},{2,1},{3,2},{5,4},{6,5},{7,6},{9,8},{10,9},{11,10},{13,12},{... | collective-permute-start | bytes 3145736 | tf_op jit(solution)/shard_map/ppermute | solution.py:120
  104.8 37.7 %collective-permute-start.6 = (bf16[256,2048]{1,0:T(8,128)(2,1)}, bf16[256,2048]{1,0:T(8,128)(2,1)S(1)}, u32[]{:S(2)}, u32[]{:S(2)}) collective-permute-start(bf16[256,2048]{1,0:T(8,128)(2,1)} %get-tuple-element.255), channel_id=1, source_target_pairs={{0,1},{1,2},{2,3},{4,5},{5,6},{6,7},{8,9},{9,10},{10,11},{12,13},{... | collective-permute-start | bytes 3145736 | tf_op jit(solution)/shard_map/ppermute | solution.py:119
  142.4 256.4 %reduce-scatter.4.cloned.1.call-start = ((), (), s32[]{:S(2)}) async-start(), calls=%async_computation.6 | async-start | bytes 5242880 | tf_op jit(solution)/shard_map/reduce_scatter | solution.py:900
  144.4 63.4 %collective-permute-start.12 = (bf16[256,2048]{1,0:T(8,128)(2,1)}, bf16[256,2048]{1,0:T(8,128)(2,1)S(1)}, u32[]{:S(2)}, u32[]{:S(2)}) collective-permute-start(bf16[256,2048]{1,0:T(8,128)(2,1)} %get-tuple-element.257), channel_id=1, source_target_pairs={{1,2},{2,3},{5,6},{6,7},{9,10},{10,11},{13,14},{14,15},{17,18},{18... | collective-permute-start | bytes 3145736 | tf_op jit(solution)/shard_map/ppermute | solution.py:119
  145.1 62.6 %collective-permute-start.13 = (bf16[256,2048]{1,0:T(8,128)(2,1)}, bf16[256,2048]{1,0:T(8,128)(2,1)}, u32[]{:S(2)}, u32[]{:S(2)}) collective-permute-start(bf16[256,2048]{1,0:T(8,128)(2,1)} %get-tuple-element.258), channel_id=1, source_target_pairs={{1,0},{2,1},{5,4},{6,5},{9,8},{10,9},{13,12},{14,13},{17,16},{18,1... | collective-permute-start | bytes 3145736 | tf_op jit(solution)/shard_map/ppermute | solution.py:120
  209.4 56.1 %collective-permute-start.16 = (bf16[256,2048]{1,0:T(8,128)(2,1)}, bf16[256,2048]{1,0:T(8,128)(2,1)S(1)}, u32[]{:S(2)}, u32[]{:S(2)}) collective-permute-start(bf16[256,2048]{1,0:T(8,128)(2,1)} %get-tuple-element.280), channel_id=1, source_target_pairs={{2,3},{6,7},{10,11},{14,15},{18,19},{22,23},{26,27},{30,31}} | collective-permute-start | bytes 3145736 | tf_op jit(solution)/shard_map/ppermute | solution.py:119
  210.1 55.4 %collective-permute-start.17 = (bf16[256,2048]{1,0:T(8,128)(2,1)}, bf16[256,2048]{1,0:T(8,128)(2,1)S(1)}, u32[]{:S(2)}, u32[]{:S(2)}) collective-permute-start(bf16[256,2048]{1,0:T(8,128)(2,1)} %get-tuple-element.281), channel_id=1, source_target_pairs={{1,0},{5,4},{9,8},{13,12},{17,16},{21,20},{25,24},{29,28}} | collective-permute-start | bytes 3145736 | tf_op jit(solution)/shard_map/ppermute | solution.py:120
  312.2 200.8 %all-gather.10.cloned.1.call-start = ((), (), s32[]{:S(2)}) async-start(), calls=%async_computation.10 | async-start | bytes 5242880 | tf_op jit(solution)/shard_map/all_gather | solution.py:919
  380.3 74.7 %collective-permute-start.26 = (bf16[512,2048]{1,0:T(8,128)(2,1)}, bf16[512,2048]{1,0:T(8,128)(2,1)}, u32[]{:S(2)}, u32[]{:S(2)}) collective-permute-start(bf16[512,2048]{1,0:T(8,128)(2,1)} %get-tuple-element.336), channel_id=1, source_target_pairs={{0,16},{4,20},{8,24},{12,28},{16,0},{20,4},{24,8},{28,12},{1,17},{... | collective-permute-start | bytes 6291464 | tf_op jit(solution)/shard_map/ppermute | solution.py:269
  380.5 74.6 %collective-permute-start.25 = (bf16[512,2048]{1,0:T(8,128)(2,1)}, bf16[512,2048]{1,0:T(8,128)(2,1)}, u32[]{:S(2)}, u32[]{:S(2)}) collective-permute-start(bf16[512,2048]{1,0:T(8,128)(2,1)} %get-tuple-element.334), channel_id=1, source_target_pairs={{0,8},{4,12},{8,0},{12,4},{16,24},{20,28},{24,16},{28,20},{1,9},{5... | collective-permute-start | bytes 6291464 | tf_op jit(solution)/shard_map/ppermute | solution.py:269
  408.2 56.8 %all-to-all-start.1 = ((bf16[4,256,512]{2,1,0:T(8,128)(2,1)}), bf16[4,256,512]{2,1,0:T(8,128)(2,1)S(1)}, u32[]{:S(2)}, u32[]{:S(2)}) async-start(bf16[4,256,512]{2,1,0:T(8,128)(2,1)} %bitcast.26), calls=%async_computation.2 | async-start | bytes 2097152 | tf_op jit(solution)/shard_map/all_to_all | solution.py:141
  411.8 194.3 %reduce-scatter.8.cloned.1.call-start = ((), (), s32[]{:S(2)}) async-start(), calls=%async_computation.8 | async-start | bytes 5242880 | tf_op jit(solution)/shard_map/reduce_scatter | solution.py:926
  453.6 47.5 %collective-permute-start.32 = (bf16[512,1024]{1,0:T(8,128)(2,1)}, bf16[512,1024]{1,0:T(8,128)(2,1)S(1)}, u32[]{:S(2)}, u32[]{:S(2)}) collective-permute-start(bf16[512,1024]{1,0:T(8,128)(2,1)} %get-tuple-element.350.refs_1_), channel_id=1, source_target_pairs={{0,8},{4,12},{8,0},{12,4},{16,24},{20,28},{24,16},{28,20},{1,9},{5... | collective-permute-start | bytes 3145736 | tf_op jit(solution)/shard_map/ppermute | solution.py:269
  454.6 46.5 %collective-permute-start.33 = (bf16[512,1024]{1,0:T(8,128)(2,1)}, bf16[512,1024]{1,0:T(8,128)(2,1)S(1)}, u32[]{:S(2)}, u32[]{:S(2)}) collective-permute-start(bf16[512,1024]{1,0:T(8,128)(2,1)} %get-tuple-element.351.refs_3_), channel_id=1, source_target_pairs={{0,16},{4,20},{8,24},{12,28},{16,0},{20,4},{24,8},{28,12},{1,17},{... | collective-permute-start | bytes 3145736 | tf_op jit(solution)/shard_map/ppermute | solution.py:269
  462.3 45.7 %collective-permute-start.30 = (bf16[256,2048]{1,0:T(8,128)(2,1)}, bf16[256,2048]{1,0:T(8,128)(2,1)}, u32[]{:S(2)}, u32[]{:S(2)}) collective-permute-start(bf16[256,2048]{1,0:T(8,128)(2,1)} %get-tuple-element.347), channel_id=1, source_target_pairs={{0,16},{4,20},{8,24},{12,28},{16,0},{20,4},{24,8},{28,12},{1,17},{... | collective-permute-start | bytes 3145736 | tf_op jit(solution)/shard_map/ppermute | solution.py:269
  463.9 44.1 %collective-permute-start.31 = (bf16[256,2048]{1,0:T(8,128)(2,1)}, bf16[256,2048]{1,0:T(8,128)(2,1)}, u32[]{:S(2)}, u32[]{:S(2)}) collective-permute-start(bf16[256,2048]{1,0:T(8,128)(2,1)} %get-tuple-element.349), channel_id=1, source_target_pairs={{0,8},{4,12},{8,0},{12,4},{16,24},{20,28},{24,16},{28,20},{1,9},{5... | collective-permute-start | bytes 3145736 | tf_op jit(solution)/shard_map/ppermute | solution.py:269
  501.0 179.1 %reduce-scatter.6.cloned.1.call-start = ((), (), s32[]{:S(2)}) async-start(), calls=%async_computation.7 | async-start | bytes 5242880 | tf_op jit(solution)/shard_map/reduce_scatter | solution.py:941
  537.9 62.2 %collective-permute-start.41 = (bf16[1024,2048]{1,0:T(8,128)(2,1)}, bf16[1024,2048]{1,0:T(8,128)(2,1)}, u32[]{:S(2)}, u32[]{:S(2)}) collective-permute-start(bf16[1024,2048]{1,0:T(8,128)(2,1)} %get-tuple-element.375.refs_1_), channel_id=1, source_target_pairs={{0,4},{4,0},{8,12},{12,8},{16,20},{20,16},{24,28},{28,24},{1,5},{5... | collective-permute-start | bytes 12582920 | tf_op jit(solution)/shard_map/ppermute | solution.py:269
  582.4 51.0 %collective-permute-start.40 = (bf16[512,2048]{1,0:T(8,128)(2,1)}, bf16[512,2048]{1,0:T(8,128)(2,1)S(1)}, u32[]{:S(2)}, u32[]{:S(2)}) collective-permute-start(bf16[512,2048]{1,0:T(8,128)(2,1)} %get-tuple-element.371.refs_1_), channel_id=1, source_target_pairs={{0,16},{4,20},{8,24},{12,28},{16,0},{20,4},{24,8},{28,12},{1,17},{... | collective-permute-start | bytes 6291464 | tf_op jit(solution)/shard_map/ppermute | solution.py:269
  582.8 52.4 %collective-permute-start.39 = (bf16[512,2048]{1,0:T(8,128)(2,1)}, bf16[512,2048]{1,0:T(8,128)(2,1)}, u32[]{:S(2)}, u32[]{:S(2)}) collective-permute-start(bf16[512,2048]{1,0:T(8,128)(2,1)} %get-tuple-element.372.refs_1_), channel_id=1, source_target_pairs={{0,8},{4,12},{8,0},{12,4},{16,24},{20,28},{24,16},{28,20},{1,9},{5... | collective-permute-start | bytes 6291464 | tf_op jit(solution)/shard_map/ppermute | solution.py:269
  (104 other events, 1253.0 us)
Sparse Core Ops, SparseCore 0:
  20.1 37.6 all-gather.5
  101.0 55.7 all-gather.7
  312.4 77.5 reduce-scatter.3
  408.4 93.9 all-gather.9
  505.2 74.8 reduce-scatter.7
  583.2 77.0 reduce-scatter.5

commit v6 on v5

--- a/solution.py
+++ b/solution.py
@@ -16,7 +16,7 @@
 VMEM = 56 << 20
 COST = {
     "give": 8, "give_second": 2.5, "keep": 10, "fold": 4, "spread": 4, "join": 4.5, "finish": 5.5, "middle": 9.5, "attend": 11,
-    "attend_back": 17, "back_project": 11, "qkv": 5.6, "project": 8.6, "ffn": 22, "last": 5, "tie": 0.5,
+    "attend_back": 17, "back_project": 11, "qkv": 5.6, "project": 8.6, "ffn": 22, "ffn_forward": 9, "ffn_back": 14, "last": 5, "tie": 0.5,
 }
 
 
@@ -822,6 +822,111 @@
     )(order, chunk, rows, cot, w_gate, w_up, w_down, *held)
 
 
+def ffn_forward_body(*refs):
+    chunk, rows, cot, wg, wu = refs[:5]
+    inner, rows_out, cot_out, gate_out, up_out = refs[-5:]
+    step = pl.program_id(0)
+    x = rows[...]
+    gate = dot(x, wg[...])
+    up = dot(x, wu[...])
+    gate_out[...] = gate
+    up_out[...] = up
+    inner[...] = (gate * sigmoid(gate) * up).astype(BF).T
+    part = rows_out.shape[0]
+    rows_out[...] = rows[:, pl.ds(pl.multiple_of(step * part, part), part)].T
+
+    @pl.when(step == 0)
+    def _():
+        cot_out[...] = cot[...]
+
+
+def ffn_back_body(*refs):
+    chunk, cot, gate_ref, up_ref, wg, wu, wd = refs[:7]
+    d_gate, d_up, d_rows, down, acc_d, acc_o = refs[-6:]
+    step, last = pl.program_id(0), pl.num_programs(0) - 1
+    gate, up = gate_ref[...], up_ref[...]
+    sig = sigmoid(gate)
+    silu = gate * sig
+    d_inner = dot_nt(cot[...], wd[...])
+    dg = (d_inner * up * (sig * (1.0 + gate * (1.0 - sig)))).astype(BF)
+    du = (d_inner * silu).astype(BF)
+    d_gate[...] = dg
+    d_up[...] = du
+    term_o = dot((silu * up).astype(BF), wd[...])
+    term_d = dot_nt(dg, wg[...]) + dot_nt(du, wu[...])
+
+    @pl.when(step == 0)
+    def _():
+        acc_o[...] = term_o
+        acc_d[...] = term_d
+
+    @pl.when(step > 0)
+    def _():
+        acc_o[...] += term_o
+        acc_d[...] += term_d
+
+    @pl.when(step == last)
+    def _():
+        d_rows[...] = acc_d[...].astype(BF)
+        down[...] = acc_o[...].astype(BF)
+
+
+def ffn_forward(order, chunk, rows, cot, w_gate, w_up, held):
+    t, d = rows.shape
+    hidden = w_gate.shape[1]
+    bh = min(512, hidden)
+    steps = hidden // bh
+    whole = pl.BlockSpec((t, d), lambda i, s: (0, 0))
+    wcol = pl.BlockSpec((d, bh), lambda i, s: (0, i))
+    own = pl.BlockSpec((t, bh), lambda i, s: (0, i))
+    return call(
+        ffn_forward_body,
+        name="ffn_forward",
+        grid=(steps,),
+        scalars=1,
+        in_specs=[whole, whole, wcol, wcol] + [ANY] * 3,
+        out_specs=[
+            pl.BlockSpec((bh, t), lambda i, s: (i, s[0])),
+            pl.BlockSpec((d // steps, t), lambda i, s: (i, s[0])),
+            pl.BlockSpec((t, d), lambda i, s: (s[0], 0)),
+            own,
+            own,
+        ],
+        out_shape=[jax.ShapeDtypeStruct(v.shape, v.dtype) for v in held]
+        + [jax.ShapeDtypeStruct((t, hidden), F32)] * 2,
+        aliases={5 + i: i for i in range(3)},
+    )(order, chunk, rows, cot, w_gate, w_up, *held)
+
+
+def ffn_back(order, chunk, cot, gate, up, w_gate, w_up, w_down, held):
+    t, d = cot.shape
+    hidden = w_gate.shape[1]
+    bh = min(512, hidden)
+    wcol = pl.BlockSpec((d, bh), lambda i, s: (0, i))
+    own = pl.BlockSpec((t, bh), lambda i, s: (0, i))
+    part = pl.BlockSpec((t, bh), lambda i, s: (s[0], i))
+    line = pl.BlockSpec((t, d), lambda i, s: (s[0], 0))
+    return call(
+        ffn_back_body,
+        name="ffn_back",
+        grid=(hidden // bh,),
+        scalars=1,
+        in_specs=[
+            pl.BlockSpec((t, d), lambda i, s: (0, 0)),
+            own,
+            own,
+            wcol,
+            wcol,
+            pl.BlockSpec((bh, d), lambda i, s: (i, 0)),
+        ]
+        + [ANY] * 4,
+        out_specs=[part, part, line, line],
+        out_shape=[jax.ShapeDtypeStruct(v.shape, v.dtype) for v in held],
+        scratch=[pltpu.VMEM((t, d), F32)] * 2,
+        aliases={7 + i: i for i in range(4)},
+    )(order, chunk, cot, gate, up, w_gate, w_up, w_down, *held)
+
+
 def local(
     layer_in,
     cotangent,
@@ -895,21 +1000,32 @@
             cots.hold(order)
             line.hold(order)
         cot = cot_first if j == 1 else cots.slot(j)
-        held = ffn_slot(order, chunk[j], line.slot(j), cot, *weights, held, tensor)
+        if j < tensor - 1:
+            held = ffn_slot(order, chunk[j], line.slot(j), cot, *weights, held, tensor)
     inner_t, d_gate, d_up, normed2_t, cot_all, d_normed2_part, down_part = held
+    inner_t, normed2_t, cot_all, gate_last, up_last = ffn_forward(
+        order, chunk[j], line.slot(j), cot, w_gate, w_up, [inner_t, normed2_t, cot_all]
+    )
+    first = Gradients([(inner_t, cot_all, [d])], dp)
+    first.give(order)
+    d_gate, d_up, d_normed2_part, down_part = ffn_back(
+        order, chunk[j], cot, gate_last, up_last, *weights,
+        [d_gate, d_up, d_normed2_part, down_part],
+    )
     d_normed2 = lax.psum_scatter(d_normed2_part, "tensor", scatter_dimension=0, tiled=True)
 
-    first = Gradients([(inner_t, cot_all, [d])], dp)
     wide = Gradients([(normed2_t, d_gate, [hidden]), (normed2_t, d_up, [hidden])], dp)
     more = range(first.bits - 2)
-
-    first.give(order)
+    usual = order.worth
+
+    first.keep(order)
     wide.give(order, 0)
     wide.give(order, 1)
-    first.keep(order)
+    order.worth = 25
+    first.fold(order)
+    order.worth = usual
     wide.keep(order, 0)
     wide.keep(order, 1)
-    first.fold(order)
     for _ in more:
         first.fold(order)
     d_mix, d_resid, d_resid_t, ffn_gain_part = middle(
@@ -923,13 +1039,13 @@
     (d_qkv,) = attend_back(order, doc_ids, query, key, value, d_mix, cos, sin)
     attn = Gradients([(normed_t, d_qkv, [width] * 4, d_resid_all, mixed)], dp)
     attn.give(order)
+    first.join(order)
     d_normed = lax.psum_scatter(
         back_project(order, d_qkv, w_query, w_key, w_value),
         "tensor",
         scatter_dimension=0,
         tiled=True,
     )
-    first.join(order)
     for _ in more:
         wide.fold(order)
     attn.give(order, second=True)

time: 728 us -> 734 us (level)
  Pallas kernels: 374 us -> 391 us
  starting transfers between devices: 77.3 us -> 66.9 us
    pallas_call x65 -> x66, Pallas kernels: 374 us -> 391 us  [run(): pl.pallas_call(whole, grid_spec=pltpu.PrefetchScalarGridSpec(num_scalar_p...]
    ppermute x33, starting transfers between devices: 32.8 us -> 21.7 us  [swap(): return lax.ppermute(value, 'dp', xor_pairs(self.count, 1 << b))]
    unnamed x129 -> x131, local copies, waits for them, and re-layouts: 25.3 us -> 29 us
  transfers between devices with their start and end apart: 64 -> 64, of which waited for: 23 -> 22; matrix products, arithmetic and copies ran while one was open for 5% -> 5% of each run, Pallas kernels for 47% -> 50%
where the time goes in v6:
time: 734 us; the launch traced here: 723 us
  Pallas kernels  391 us (53%)
  waiting for transfers between devices  179 us (24%)
  starting transfers between devices  66.9 us (9%)
  other arithmetic  39 us (5%)
  local copies, waits for them, and re-layouts  32 us (4%)
  between operations  15.2 us (2%)
    pallas_call x66, Pallas kernels, run(): pl.pallas_call(whole, grid_spec=pltpu.PrefetchScalarGridSpec(num_scalar_p...  391 us
    ppermute x33, waiting for transfers between devices, swap(): return lax.ppermute(value, 'dp', xor_pairs(self.count, 1 << b))  90.4 us
    ppermute x9, waiting for transfers between devices, step(): lax.ppermute(down, 'tensor', [(i + 1, i) for i in range(0, size - k)])  62.8 us
    unnamed x131, local copies, waits for them, and re-layouts  29 us
    ppermute x9, starting transfers between devices, step(): lax.ppermute(up, 'tensor', [(i, i + 1) for i in range(k - 1, size - 1)])  22.6 us
    ppermute x33, starting transfers between devices, swap(): return lax.ppermute(value, 'dp', xor_pairs(self.count, 1 << b))  21.7 us
    select_n x9, other arithmetic, slot(): value = jnp.where(here, arr, value)  21.2 us
    all_to_all x2, waiting for transfers between devices, exchange(): return lax.all_to_all(values, 'tensor', 0, 0, tiled=True)  15.3 us
  transfers between devices with their start and end apart: 64, of which 22 were waited for; matrix products, arithmetic and copies ran while one was open for 5% of the time, Pallas kernels for 50%

profile of v6, /device:TPU:0, one launch (start us, length us, event | category | flops | bytes accessed | tf_op | source)
XLA Modules:
  0.0 723.1 jit_solution(12757091826538355668)
XLA Ops:
  29.7 26.5 %collective-permute-done.1.refs_1_ = bf16[256,2048]{1,0:T(8,128)(2,1)S(1)} collective-permute-done((bf16[256,2048]{1,0:T(8,128)(2,1)}, bf16[256,2048]{1,0:T(8,128)(2,1)S(1)}, u32[]{:S(2)}, u32[]{:S(2)}) %collective-permute-start.1) | collective-permute-done | bytes 1048608 | tf_op jit(solution)/shard_map/ppermute | solution.py:120
  67.8 19.9 %collective-permute-done.3.refs_1_ = bf16[256,2048]{1,0:T(8,128)(2,1)S(1)} collective-permute-done((bf16[256,2048]{1,0:T(8,128)(2,1)}, bf16[256,2048]{1,0:T(8,128)(2,1)S(1)}, u32[]{:S(2)}, u32[]{:S(2)}) %collective-permute-start.3) | collective-permute-done | bytes 1048608 | tf_op jit(solution)/shard_map/ppermute | solution.py:120
  127.3 13.7 %attend.1 = (bf16[1024,512]{1,0:T(8,128)(2,1)}, f32[8,128]{1,0:T(8,128)}) custom-call(s32[1024]{0:T(1024)} %refs_0_.4, bf16[1024,512]{1,0:T(8,128)(2,1)} %get-tuple-element.252.refs_1_, bf16[1024,512]{1,0:T(8,128)(2,1)} %get-tuple-element.253.refs_2_, bf16[1024,512]{1,0:T(8,128)(2,1)} %get-tuple-element.254.refs_3_, s32[1024,1]{1,0:T(8,128)} %copy.101.refs_4_.refs_5_, ...), custom_call_target="tpu_custom_call" | custom-call | flops 14300000256 | bytes 11000000 | tf_op jit(solution)/shard_map/attend/pallas_call | solution.py:57
  152.3 15.3 %all-to-all-done = bf16[4,256,512]{2,1,0:T(8,128)(2,1)} async-done(((bf16[4,256,512]{2,1,0:T(8,128)(2,1)}), bf16[4,256,512]{2,1,0:T(8,128)(2,1)}, u32[]{:S(2)}, u32[]{:S(2)}) %all-to-all-start) | async-done | bytes 1048608 | tf_op jit(solution)/shard_map/all_to_all | solution.py:141
  167.7 8.5 %project.1 = (f32[256,2048]{1,0:T(8,128)}, bf16[256,2048]{1,0:T(8,128)(2,1)}, f32[8,128]{1,0:T(8,128)}) custom-call(bf16[1024,512]{1,0:T(8,128)(2,1)} %bitcast.7.refs_0_, bf16[8,2048,256]{2,1,0:T(8,128)(2,1)} %bitcast.34, bf16[256,2048]{1,0:T(8,128)(2,1)} %refs_1_.3, f32[1,2048]{1,0:T(1,128)} %bitcast.38, f32[8,128]{1,0:T(8,128)} %get-tuple-element.263.refs_4_), custom_call_target="tpu_custom_call" | custom-call | flops 11180000256 | bytes 8600000 | tf_op jit(solution)/shard_map/project/pallas_call | solution.py:57
  182.1 22.2 %ffn.3 = (bf16[2048,1024]{1,0:T(8,128)(2,1)}, bf16[1024,2048]{1,0:T(8,128)(2,1)}, bf16[1024,2048]{1,0:T(8,128)(2,1)}, bf16[2048,1024]{1,0:T(8,128)(2,1)}, bf16[1...) custom-call(s32[1]{0:T(128)} %bitcast.1.refs_0_, ...), custom_call_target="tpu_custom_call" | custom-call | flops 28600000512 | bytes 22000000 | tf_op jit(solution)/shard_map/ffn/pallas_call | solution.py:57
  214.3 22.3 %ffn.4 = (bf16[2048,1024]{1,0:T(8,128)(2,1)}, bf16[1024,2048]{1,0:T(8,128)(2,1)}, bf16[1024,2048]{1,0:T(8,128)(2,1)}, bf16[2048,1024]{1,0:T(8,128)(2,1)}, bf16[1...) custom-call(s32[1]{0:T(128)} %bitcast.2.refs_0_, ...), custom_call_target="tpu_custom_call", output_to_operand_aliasing={{0}: (6, {}), {1}: (7, {}), {2}: (8, {}), {3}: (9, {}), {4}... | custom-call | flops 28600000512 | bytes 22000000 | tf_op jit(solution)/shard_map/ffn/pallas_call | solution.py:57
  245.8 22.4 %ffn.5 = (bf16[2048,1024]{1,0:T(8,128)(2,1)}, bf16[1024,2048]{1,0:T(8,128)(2,1)}, bf16[1024,2048]{1,0:T(8,128)(2,1)}, bf16[2048,1024]{1,0:T(8,128)(2,1)}, bf16[1...) custom-call(s32[1]{0:T(128)} %bitcast.3.refs_0_, ...), custom_call_target="tpu_custom_call", output_to_operand_aliasing={{0}: (6, {}), {1}: (7, {}), {2}: (8, {}), {3}: (9, {}), {4}... | custom-call | flops 28600000512 | bytes 22000000 | tf_op jit(solution)/shard_map/ffn/pallas_call | solution.py:57
  284.3 12.0 %ffn_forward.1 = (bf16[2048,1024]{1,0:T(8,128)(2,1)}, bf16[2048,1024]{1,0:T(8,128)(2,1)}, bf16[1024,2048]{1,0:T(8,128)(2,1)}, f32[256,2048]{1,0:T(8,128)}, f32[256,2048]{1,0:T(8,128)}, /*index=5*/f32[8,128]{1,0:T(8,128)}) custom-call(s32[1]{0:T(128)} %bitcast.refs_0_, ...), custom_call_target="tpu_custom_call", output_to_operand_aliasing={{0}: (5, {}), {1}: (6, {}), {2}: (7, {})} | custom-call | flops 11699999744 | bytes 9000000 | tf_op jit(solution)/shard_map/ffn_forward/pallas_call | solution.py:57
  296.3 8.5 %give.4 = (bf16[1024,2048]{1,0:T(8,128)(2,1)}, f32[8,128]{1,0:T(8,128)}) custom-call(s32[1]{0:T(128)} %bitcast.10.refs_0_, bf16[2048,1024]{1,0:T(8,128)(2,1)} %get-tuple-element.309.refs_1_, bf16[1024,2048]{1,0:T(8,128)(2,1)} %get-tuple-element.310.refs_2_, f32[8,128]{1,0:T(8,128)} %get-tuple-element.311.refs_3_), custom_call_target="tpu_custom_call" | custom-call | flops 10400000000 | bytes 8000000 | tf_op jit(solution)/shard_map/give/pallas_call | solution.py:57
  307.2 18.9 %ffn_back.1 = (bf16[1024,2048]{1,0:T(8,128)(2,1)}, bf16[1024,2048]{1,0:T(8,128)(2,1)}, bf16[1024,2048]{1,0:T(8,128)(2,1)}, bf16[1024,2048]{1,0:T(8,128)(2,1)}, f32[8,128]{1,0:T(8,128)}) custom-call(s32[1]{0:T(128)} %bitcast.refs_0_, ...), custom_call_target="tpu_custom_call", output_to_operand_aliasing={{0}: (7, {}), {1}: (8, {}), {2}: (9, {}), {3}: (10, {})} | custom-call | flops 18200000512 | bytes 14000000 | tf_op jit(solution)/shard_map/ffn_back/pallas_call | solution.py:57
  326.1 11.1 %keep.4 = (bf16[512,1024]{1,0:T(8,128)(2,1)}, bf16[512,1024]{1,0:T(8,128)(2,1)}, bf16[512,1024]{1,0:T(8,128)(2,1)}, bf16[512,1024]{1,0:T(8,128)(2,1)}, f32[8,128]{1,0:T(8,128)}) custom-call(s32[3]{0:T(128)} %pad_add_fusion.1.refs_0_, bf16[2048,1024]{1,0:T(8,128)(2,1)} %get-tuple-element.309.refs_1_, bf16[1024,2048]{1,0:T(8,128)(2,1)} %get-tuple-element.310.refs_2_, ...), custom_call_target="tpu_custom_call" | custom-call | flops 12999999488 | bytes 10000000 | tf_op jit(solution)/shard_map/keep/pallas_call | solution.py:57
  337.4 8.4 %give.5 = (bf16[1024,2048]{1,0:T(8,128)(2,1)}, f32[8,128]{1,0:T(8,128)}) custom-call(s32[1]{0:T(128)} %bitcast.10.refs_0_, bf16[2048,1024]{1,0:T(8,128)(2,1)} %get-tuple-element.322.refs_1_, bf16[1024,2048]{1,0:T(8,128)(2,1)} %get-tuple-element.324.refs_2_, f32[8,128]{1,0:T(8,128)} %get-tuple-element.325.refs_3_), custom_call_target="tpu_custom_call" | custom-call | flops 10400000000 | bytes 8000000 | tf_op jit(solution)/shard_map/give/pallas_call | solution.py:57
  345.8 8.5 %give.6 = (bf16[1024,2048]{1,0:T(8,128)(2,1)}, f32[8,128]{1,0:T(8,128)}) custom-call(s32[1]{0:T(128)} %bitcast.10.refs_0_, bf16[2048,1024]{1,0:T(8,128)(2,1)} %get-tuple-element.322.refs_1_, bf16[1024,2048]{1,0:T(8,128)(2,1)} %get-tuple-element.323.refs_2_, f32[8,128]{1,0:T(8,128)} %get-tuple-element.326.refs_3_), custom_call_target="tpu_custom_call" | custom-call | flops 10400000000 | bytes 8000000 | tf_op jit(solution)/shard_map/give/pallas_call | solution.py:57
  354.9 8.2 %collective-permute-done.19.refs_2_ = bf16[512,1024]{1,0:T(8,128)(2,1)S(1)} collective-permute-done((bf16[512,1024]{1,0:T(8,128)(2,1)}, bf16[512,1024]{1,0:T(8,128)(2,1)S(1)}, u32[]{:S(2)}, u32[]{:S(2)}) %collective-permute-start.19) | collective-permute-done | bytes 1048608 | tf_op jit(solution)/shard_map/ppermute | solution.py:269
  370.9 10.3 %keep.5 = (bf16[512,2048]{1,0:T(8,128)(2,1)}, bf16[512,2048]{1,0:T(8,128)(2,1)}, f32[8,128]{1,0:T(8,128)}) custom-call(s32[2]{0:T(128)} %pad_add_fusion.3.refs_0_, bf16[2048,1024]{1,0:T(8,128)(2,1)} %get-tuple-element.322.refs_1_, bf16[1024,2048]{1,0:T(8,128)(2,1)} %get-tuple-element.324.refs_2_, bf16[1024,2048]{1,0:T(8,128)(2,1)} %collective-permute-done.24.refs_3_, ...), custom_call_target="tpu_custom_call" | custom-call | flops 12999999488 | bytes 10000000 | tf_op jit(solution)/shard_map/keep/pallas_call | solution.py:57
  383.2 10.3 %keep.6 = (bf16[512,2048]{1,0:T(8,128)(2,1)}, bf16[512,2048]{1,0:T(8,128)(2,1)}, f32[8,128]{1,0:T(8,128)}) custom-call(s32[2]{0:T(128)} %pad_add_fusion.4.refs_0_, bf16[2048,1024]{1,0:T(8,128)(2,1)} %get-tuple-element.322.refs_1_, bf16[1024,2048]{1,0:T(8,128)(2,1)} %get-tuple-element.323.refs_2_, bf16[1024,2048]{1,0:T(8,128)(2,1)} %copy-done.46, ...), custom_call_target="tpu_custom_call" | custom-call | flops 12999999488 | bytes 10000000 | tf_op jit(solution)/shard_map/keep/pallas_call | solution.py:57
  400.2 9.4 %middle.1 = (bf16[1024,512]{1,0:T(8,128)(2,1)}, f32[256,2048]{1,0:T(8,128)}, bf16[2048,256]{1,0:T(8,128)(2,1)}, f32[1,2048]{1,0:T(1,128)}, f32[8,128]{1,0:T(8,128)}) custom-call(bf16[256,2048]{1,0:T(8,128)(2,1)} %reduce-scatter.4.cloned.1.call-done.refs_0_, f32[256,2048]{1,0:T(8,128)} %get-tuple-element.264.refs_1_, bf16[256,2048]{1,0:T(8,128)(2,1)} %refs_2_.14, ...), custom_call_target="tpu_custom_call" | custom-call | flops 12350000128 | bytes 9500000 | tf_op jit(solution)/shard_map/middle/pallas_call | solution.py:57
  416.8 35.1 %collective-permute-done.27.refs_2_ = bf16[256,1024]{1,0:T(8,128)(2,1)S(1)} collective-permute-done((bf16[256,1024]{1,0:T(8,128)(2,1)S(1)}, bf16[256,1024]{1,0:T(8,128)(2,1)S(1)}, u32[]{:S(2)}, u32[]{:S(2)}) %collective-permute-start.27) | collective-permute-done | bytes 524320 | tf_op jit(solution)/shard_map/ppermute | solution.py:269
  469.9 21.3 %attend_back.1 = (bf16[1024,1536]{1,0:T(8,128)(2,1)}, f32[8,128]{1,0:T(8,128)}) custom-call(s32[1024]{0:T(1024)} %refs_0_.4, bf16[1024,512]{1,0:T(8,128)(2,1)} %get-tuple-element.252.refs_1_, bf16[1024,512]{1,0:T(8,128)(2,1)} %get-tuple-element.253.refs_2_, bf16[1024,512]{1,0:T(8,128)(2,1)} %get-tuple-element.254.refs_3_, bf16[1024,512]{1,0:T(8,128)(2,1)} %bitcast.26, ...), custom_call_target="tpu_custom_call" | custom-call | flops 22100000768 | bytes 17000000 | tf_op jit(solution)/shard_map/attend_back/pallas_call | solution.py:57
  504.5 11.0 %back_project.1 = (bf16[1024,2048]{1,0:T(8,128)(2,1)}, f32[8,128]{1,0:T(8,128)}) custom-call(bf16[1024,1536]{1,0:T(8,128)(2,1)} %get-tuple-element.348.refs_2_.refs_0_, bf16[2048,512]{1,0:T(8,128)(2,1)} %refs_1_.2, bf16[2048,512]{1,0:T(8,128)(2,1)} %refs_2_.15, bf16[2048,512]{1,0:T(8,128)(2,1)} %refs_3_.17, f32[8,128]{1,0:T(8,128)} %get-tuple-element.359.refs_4_), custom_call_target="tpu_custom_call" | custom-call | flops 14300000256 | bytes 11000000 | tf_op jit(solution)/shard_map/back_project/pallas_call | solution.py:57
  530.0 12.1 %keep.7 = (bf16[512,1024]{1,0:T(8,128)(2,1)}, bf16[512,1024]{1,0:T(8,128)(2,1)}, bf16[512,1024]{1,0:T(8,128)(2,1)}, bf16[512,1024]{1,0:T(8,128)(2,1)}, f32[8,128]{1,0:T(8,128)}) custom-call(s32[3]{0:T(128)} %pad_add_fusion.1.refs_0_, bf16[2048,1024]{1,0:T(8,128)(2,1)} %get-tuple-element.314.refs_1_, bf16[1024,1536]{1,0:T(8,128)(2,1)} %get-tuple-element.348.refs_2_.refs_0_, ...), custom_call_target="tpu_custom_call" | custom-call | flops 12999999488 | bytes 10000000 | tf_op jit(solution)/shard_map/keep/pallas_call | solution.py:57
  543.6 8.9 %collective-permute-done.37.refs_0_ = bf16[256,2048]{1,0:T(8,128)(2,1)S(1)} collective-permute-done((bf16[256,2048]{1,0:T(8,128)(2,1)S(1)}, bf16[256,2048]{1,0:T(8,128)(2,1)S(1)}, u32[]{:S(2)}, u32[]{:S(2)}) %collective-permute-start.37) | collective-permute-done | bytes 1048608 | tf_op jit(solution)/shard_map/ppermute | solution.py:269
  554.1 20.2 %collective-permute-done.35.refs_2_ = bf16[512,1024]{1,0:T(8,128)(2,1)} collective-permute-done((bf16[512,1024]{1,0:T(8,128)(2,1)}, bf16[512,1024]{1,0:T(8,128)(2,1)}, u32[]{:S(2)}, u32[]{:S(2)}) %collective-permute-start.35) | collective-permute-done | bytes 1048608 | tf_op jit(solution)/shard_map/ppermute | solution.py:269
  (339 shorter events, 342.8 us)
Async XLA Ops:
  7.2 93.0 %all-gather.6.cloned.1.call-start = ((), (), s32[]{:S(2)}) async-start(), calls=%async_computation.5 | async-start | bytes 1310720 | tf_op jit(solution)/shard_map/all_gather | solution.py:957
  11.4 44.8 %collective-permute-start.1 = (bf16[256,2048]{1,0:T(8,128)(2,1)}, bf16[256,2048]{1,0:T(8,128)(2,1)S(1)}, u32[]{:S(2)}, u32[]{:S(2)}) collective-permute-start(bf16[256,2048]{1,0:T(8,128)(2,1)} %fusion.2.refs_1_), channel_id=1, source_target_pairs={{1,0},{2,1},{3,2},{5,4},{6,5},{7,6},{9,8},{10,9},{11,10},{13,12},{... | collective-permute-start | bytes 3145736 | tf_op jit(solution)/shard_map/ppermute | solution.py:120
  12.7 43.6 %collective-permute-start = (bf16[256,2048]{1,0:T(8,128)(2,1)}, bf16[256,2048]{1,0:T(8,128)(2,1)}, u32[]{:S(2)}, u32[]{:S(2)}) collective-permute-start(bf16[256,2048]{1,0:T(8,128)(2,1)} %fusion.2.refs_1_), channel_id=1, source_target_pairs={{0,1},{1,2},{2,3},{4,5},{5,6},{6,7},{8,9},{9,10},{10,11},{12,13},{... | collective-permute-start | bytes 3145736 | tf_op jit(solution)/shard_map/ppermute | solution.py:119
  20.0 147.7 %all-gather.8.cloned.1.call-start = ((), (), s32[]{:S(2)}) async-start(), calls=%async_computation.9 | async-start | bytes 9437184 | tf_op jit(solution)/shard_map/all_gather | solution.py:982
  103.5 41.8 %collective-permute-start.7 = (bf16[256,2048]{1,0:T(8,128)(2,1)}, bf16[256,2048]{1,0:T(8,128)(2,1)S(1)}, u32[]{:S(2)}, u32[]{:S(2)}) collective-permute-start(bf16[256,2048]{1,0:T(8,128)(2,1)} %get-tuple-element.258), channel_id=1, source_target_pairs={{1,0},{2,1},{3,2},{5,4},{6,5},{7,6},{9,8},{10,9},{11,10},{13,12},{... | collective-permute-start | bytes 3145736 | tf_op jit(solution)/shard_map/ppermute | solution.py:120
  104.8 40.5 %collective-permute-start.6 = (bf16[256,2048]{1,0:T(8,128)(2,1)}, bf16[256,2048]{1,0:T(8,128)(2,1)S(1)}, u32[]{:S(2)}, u32[]{:S(2)}) collective-permute-start(bf16[256,2048]{1,0:T(8,128)(2,1)} %get-tuple-element.258), channel_id=1, source_target_pairs={{0,1},{1,2},{2,3},{4,5},{5,6},{6,7},{8,9},{9,10},{10,11},{12,13},{... | collective-permute-start | bytes 3145736 | tf_op jit(solution)/shard_map/ppermute | solution.py:119
  145.2 254.9 %reduce-scatter.4.cloned.1.call-start = ((), (), s32[]{:S(2)}) async-start(), calls=%async_computation.6 | async-start | bytes 5242880 | tf_op jit(solution)/shard_map/reduce_scatter | solution.py:1015
  147.2 63.5 %collective-permute-start.8 = (bf16[256,2048]{1,0:T(8,128)(2,1)}, bf16[256,2048]{1,0:T(8,128)(2,1)S(1)}, u32[]{:S(2)}, u32[]{:S(2)}) collective-permute-start(bf16[256,2048]{1,0:T(8,128)(2,1)} %get-tuple-element.260), channel_id=1, source_target_pairs={{1,2},{2,3},{5,6},{6,7},{9,10},{10,11},{13,14},{14,15},{17,18},{18... | collective-permute-start | bytes 3145736 | tf_op jit(solution)/shard_map/ppermute | solution.py:119
  147.9 62.8 %collective-permute-start.9 = (bf16[256,2048]{1,0:T(8,128)(2,1)}, bf16[256,2048]{1,0:T(8,128)(2,1)}, u32[]{:S(2)}, u32[]{:S(2)}) collective-permute-start(bf16[256,2048]{1,0:T(8,128)(2,1)} %get-tuple-element.261), channel_id=1, source_target_pairs={{1,0},{2,1},{5,4},{6,5},{9,8},{10,9},{13,12},{14,13},{17,16},{18,1... | collective-permute-start | bytes 3145736 | tf_op jit(solution)/shard_map/ppermute | solution.py:120
  212.3 55.9 %collective-permute-start.12 = (bf16[256,2048]{1,0:T(8,128)(2,1)}, bf16[256,2048]{1,0:T(8,128)(2,1)S(1)}, u32[]{:S(2)}, u32[]{:S(2)}) collective-permute-start(bf16[256,2048]{1,0:T(8,128)(2,1)} %get-tuple-element.269), channel_id=1, source_target_pairs={{2,3},{6,7},{10,11},{14,15},{18,19},{22,23},{26,27},{30,31}} | collective-permute-start | bytes 3145736 | tf_op jit(solution)/shard_map/ppermute | solution.py:119
  213.0 55.2 %collective-permute-start.13 = (bf16[256,2048]{1,0:T(8,128)(2,1)}, bf16[256,2048]{1,0:T(8,128)(2,1)S(1)}, u32[]{:S(2)}, u32[]{:S(2)}) collective-permute-start(bf16[256,2048]{1,0:T(8,128)(2,1)} %get-tuple-element.270), channel_id=1, source_target_pairs={{1,0},{5,4},{9,8},{13,12},{17,16},{21,20},{25,24},{29,28}} | collective-permute-start | bytes 3145736 | tf_op jit(solution)/shard_map/ppermute | solution.py:120
  393.5 65.4 %collective-permute-start.26 = (bf16[512,2048]{1,0:T(8,128)(2,1)}, bf16[512,2048]{1,0:T(8,128)(2,1)}, u32[]{:S(2)}, u32[]{:S(2)}) collective-permute-start(bf16[512,2048]{1,0:T(8,128)(2,1)} %get-tuple-element.342), channel_id=1, source_target_pairs={{0,16},{4,20},{8,24},{12,28},{16,0},{20,4},{24,8},{28,12},{1,17},{... | collective-permute-start | bytes 6291464 | tf_op jit(solution)/shard_map/ppermute | solution.py:269
  395.3 63.6 %collective-permute-start.25 = (bf16[512,2048]{1,0:T(8,128)(2,1)}, bf16[512,2048]{1,0:T(8,128)(2,1)}, u32[]{:S(2)}, u32[]{:S(2)}) collective-permute-start(bf16[512,2048]{1,0:T(8,128)(2,1)} %get-tuple-element.340), channel_id=1, source_target_pairs={{0,8},{4,12},{8,0},{12,4},{16,24},{20,28},{24,16},{28,20},{1,9},{5... | collective-permute-start | bytes 6291464 | tf_op jit(solution)/shard_map/ppermute | solution.py:269
  409.6 59.3 %all-to-all-start.1 = ((bf16[4,256,512]{2,1,0:T(8,128)(2,1)}), bf16[4,256,512]{2,1,0:T(8,128)(2,1)S(1)}, u32[]{:S(2)}, u32[]{:S(2)}) async-start(bf16[4,256,512]{2,1,0:T(8,128)(2,1)} %bitcast.27), calls=%async_computation.2 | async-start | bytes 2097152 | tf_op jit(solution)/shard_map/all_to_all | solution.py:141
  413.1 108.6 %all-gather.10.cloned.1.call-start = ((), (), s32[]{:S(2)}) async-start(), calls=%async_computation.10 | async-start | bytes 5242880 | tf_op jit(solution)/shard_map/all_gather | solution.py:1035
  416.1 196.2 %reduce-scatter.8.cloned.1.call-start = ((), (), s32[]{:S(2)}) async-start(), calls=%async_computation.8 | async-start | bytes 5242880 | tf_op jit(solution)/shard_map/reduce_scatter | solution.py:1043
  457.6 40.6 %collective-permute-start.32 = (bf16[512,1024]{1,0:T(8,128)(2,1)}, bf16[512,1024]{1,0:T(8,128)(2,1)S(1)}, u32[]{:S(2)}, u32[]{:S(2)}) collective-permute-start(bf16[512,1024]{1,0:T(8,128)(2,1)} %get-tuple-element.356.refs_1_), channel_id=1, source_target_pairs={{0,8},{4,12},{8,0},{12,4},{16,24},{20,28},{24,16},{28,20},{1,9},{5... | collective-permute-start | bytes 3145736 | tf_op jit(solution)/shard_map/ppermute | solution.py:269
  458.4 39.8 %collective-permute-start.33 = (bf16[512,1024]{1,0:T(8,128)(2,1)}, bf16[512,1024]{1,0:T(8,128)(2,1)}, u32[]{:S(2)}, u32[]{:S(2)}) collective-permute-start(bf16[512,1024]{1,0:T(8,128)(2,1)} %get-tuple-element.357.refs_3_), channel_id=1, source_target_pairs={{0,16},{4,20},{8,24},{12,28},{16,0},{20,4},{24,8},{28,12},{1,17},{... | collective-permute-start | bytes 3145736 | tf_op jit(solution)/shard_map/ppermute | solution.py:269
  466.2 49.4 %collective-permute-start.30 = (bf16[256,2048]{1,0:T(8,128)(2,1)}, bf16[256,2048]{1,0:T(8,128)(2,1)S(1)}, u32[]{:S(2)}, u32[]{:S(2)}) collective-permute-start(bf16[256,2048]{1,0:T(8,128)(2,1)} %get-tuple-element.353), channel_id=1, source_target_pairs={{0,16},{4,20},{8,24},{12,28},{16,0},{20,4},{24,8},{28,12},{1,17},{... | collective-permute-start | bytes 3145736 | tf_op jit(solution)/shard_map/ppermute | solution.py:269
  467.8 47.9 %collective-permute-start.31 = (bf16[256,2048]{1,0:T(8,128)(2,1)}, bf16[256,2048]{1,0:T(8,128)(2,1)}, u32[]{:S(2)}, u32[]{:S(2)}) collective-permute-start(bf16[256,2048]{1,0:T(8,128)(2,1)} %get-tuple-element.355), channel_id=1, source_target_pairs={{0,8},{4,12},{8,0},{12,4},{16,24},{20,28},{24,16},{28,20},{1,9},{5... | collective-permute-start | bytes 3145736 | tf_op jit(solution)/shard_map/ppermute | solution.py:269
  515.6 169.0 %reduce-scatter.6.cloned.1.call-start = ((), (), s32[]{:S(2)}) async-start(), calls=%async_computation.7 | async-start | bytes 5242880 | tf_op jit(solution)/shard_map/reduce_scatter | solution.py:1057
  543.6 62.7 %collective-permute-start.41 = (bf16[1024,2048]{1,0:T(8,128)(2,1)}, bf16[1024,2048]{1,0:T(8,128)(2,1)}, u32[]{:S(2)}, u32[]{:S(2)}) collective-permute-start(bf16[1024,2048]{1,0:T(8,128)(2,1)} %get-tuple-element.381.refs_1_), channel_id=1, source_target_pairs={{0,4},{4,0},{8,12},{12,8},{16,20},{20,16},{24,28},{28,24},{1,5},{5... | collective-permute-start | bytes 12582920 | tf_op jit(solution)/shard_map/ppermute | solution.py:269
  586.9 52.1 %collective-permute-start.40 = (bf16[512,2048]{1,0:T(8,128)(2,1)}, bf16[512,2048]{1,0:T(8,128)(2,1)S(1)}, u32[]{:S(2)}, u32[]{:S(2)}) collective-permute-start(bf16[512,2048]{1,0:T(8,128)(2,1)} %get-tuple-element.377.refs_1_), channel_id=1, source_target_pairs={{0,16},{4,20},{8,24},{12,28},{16,0},{20,4},{24,8},{28,12},{1,17},{... | collective-permute-start | bytes 6291464 | tf_op jit(solution)/shard_map/ppermute | solution.py:269
  587.2 53.5 %collective-permute-start.39 = (bf16[512,2048]{1,0:T(8,128)(2,1)}, bf16[512,2048]{1,0:T(8,128)(2,1)}, u32[]{:S(2)}, u32[]{:S(2)}) collective-permute-start(bf16[512,2048]{1,0:T(8,128)(2,1)} %get-tuple-element.378.refs_1_), channel_id=1, source_target_pairs={{0,8},{4,12},{8,0},{12,4},{16,24},{20,28},{24,16},{28,20},{1,9},{5... | collective-permute-start | bytes 6291464 | tf_op jit(solution)/shard_map/ppermute | solution.py:269
  (105 other events, 1253.9 us)
Sparse Core Ops, SparseCore 0:
  20.1 37.6 all-gather.5
  101.0 55.7 all-gather.7
  326.3 73.2 reduce-scatter.3
  416.3 90.7 all-gather.9
  515.7 73.6 reduce-scatter.7
  591.5 77.9 reduce-scatter.5

commit v7 on v5

--- a/solution.py
+++ b/solution.py
@@ -903,72 +903,74 @@
     wide = Gradients([(normed2_t, d_gate, [hidden]), (normed2_t, d_up, [hidden])], dp)
     more = range(first.bits - 2)
 
+    usual = order.worth
     first.give(order)
     wide.give(order, 0)
+    first.keep(order)
     wide.give(order, 1)
-    first.keep(order)
+    order.worth = 10
+    first.fold(order)
+    order.worth = usual
     wide.keep(order, 0)
     wide.keep(order, 1)
-    first.fold(order)
-    for _ in more:
-        first.fold(order)
     d_mix, d_resid, d_resid_t, ffn_gain_part = middle(
         order, d_normed2, resid, cotangent, ffn_gain, w_out_all, width
     )
     d_mix = exchange(d_mix)
     d_resid_all = lax.all_gather(d_resid_t, "tensor", axis=0)
     for _ in more:
+        first.fold(order)
+    wide.fold(order)
+    for _ in more:
         first.spread(order)
-    wide.fold(order)
     (d_qkv,) = attend_back(order, doc_ids, query, key, value, d_mix, cos, sin)
     attn = Gradients([(normed_t, d_qkv, [width] * 4, d_resid_all, mixed)], dp)
     attn.give(order)
+    for _ in more:
+        wide.fold(order)
+    first.join(order)
+    attn.give(order, second=True)
     d_normed = lax.psum_scatter(
         back_project(order, d_qkv, w_query, w_key, w_value),
         "tensor",
         scatter_dimension=0,
         tiled=True,
     )
-    first.join(order)
-    for _ in more:
-        wide.fold(order)
-    attn.give(order, second=True)
-    attn.keep(order)
     wide.hold(order)
-    usual, order.worth = order.worth, 10
-    attn.fold(order)
-    order.worth = usual
-    down_sum = lax.psum_scatter(
-        order.after(down_part)[0], "tensor", scatter_dimension=0, tiled=True
-    )
     for _ in more:
         wide.spread(order)
-    for _ in more:
-        attn.fold(order)
-    (down_grad,) = first.finish(order)
-    in_grad, attn_gain_part = last(order, d_normed, layer_in, d_resid, attn_gain)
-    totals = GainTotals([attn_gain_part, ffn_gain_part], dp, tensor)
-    totals.step(order)
-    totals.step(order)
-    totals.step(order)
+    attn.keep(order)
+    down_grad = first.fill(order, 0, 0)
+    (down_grad,) = first.fill(order, 0, 1, down_grad)
     wide.hold(order)
     order.worth = 0.3
     wide.join(order)
     attn.hold(order)
-    order.worth = 0.3
+    order.worth = 10
+    attn.fold(order)
+    down_sum = lax.psum_scatter(
+        order.after(down_part)[0], "tensor", scatter_dimension=0, tiled=True
+    )
+    gate_grad = wide.fill(order, 0, 0)
+    order.worth = 1.3
+    for _ in more:
+        attn.fold(order)
+    up_grad = wide.fill(order, 1, 0)
+    in_grad, attn_gain_part = last(order, d_normed, layer_in, d_resid, attn_gain)
+    totals = GainTotals([attn_gain_part, ffn_gain_part], dp, tensor)
+    attn.hold(order)
     for _ in more:
         attn.spread(order)
-    order.worth = 0.3
-    order.worth = 5
-    gate_grad = wide.fill(order, 0, 0)
-    up_grad = wide.fill(order, 1, 0)
+    totals.step(order)
+    (gate_grad,) = wide.fill(order, 0, 1, gate_grad)
+    totals.step(order)
+    (up_grad,) = wide.fill(order, 1, 1, up_grad)
     order.worth = 0.02
-    (gate_grad,) = wide.fill(order, 0, 1, gate_grad)
-    (up_grad,) = wide.fill(order, 1, 1, up_grad)
-    (down_sum,) = order.after(down_sum)
+    totals.step(order)
     attn.join(order)
     attn_grads = attn.fill(order, 0, 0)
     totals.step(order)
+    (down_sum,) = order.after(down_sum)
     query_grad, key_grad, value_grad, out_grad = attn.fill(order, 0, 1, attn_grads)
     attn_gain_grad, ffn_gain_grad = totals.split(order)
     layer_out = (resid + down_sum.astype(F32)).astype(BF)

time: 728 us -> 732 us (level)
  waiting for transfers between devices: 184 us -> 197 us
    ppermute x9, waiting for transfers between devices: 0.02 us -> 21 us  [step(): lax.ppermute(up, 'tensor', [(i, i + 1) for i in range(k - 1, size - 1)])]
    ppermute x9, waiting for transfers between devices: 62.8 us -> 47.7 us  [step(): lax.ppermute(down, 'tensor', [(i + 1, i) for i in range(0, size - k)])]
    ppermute x33, waiting for transfers between devices: 94.6 us -> 109 us  [swap(): return lax.ppermute(value, 'dp', xor_pairs(self.count, 1 << b))]
    ppermute x5, waiting for transfers between devices: 11.2 us -> 0.6 us  [next(): lax.ppermute(self.value, name, xor_pairs(size, m))]
    unnamed x129 -> x115, local copies, waits for them, and re-layouts: 25.3 us -> 21.8 us
    pallas_call x65 -> x66, Pallas kernels: 374 us -> 375 us  [run(): pl.pallas_call(whole, grid_spec=pltpu.PrefetchScalarGridSpec(num_scalar_p...]
  transfers between devices with their start and end apart: 64 -> 64, of which waited for: 23 -> 25; matrix products, arithmetic and copies ran while one was open for 5% -> 5% of each run, Pallas kernels for 47% -> 48%
where the time goes in v7:
time: 732 us; the launch traced here: 721 us
  Pallas kernels  375 us (51%)
  waiting for transfers between devices  197 us (27%)
  starting transfers between devices  72.6 us (10%)
  other arithmetic  37.3 us (5%)
  local copies, waits for them, and re-layouts  24.7 us (3%)
  between operations  15.2 us (2%)
    pallas_call x66, Pallas kernels, run(): pl.pallas_call(whole, grid_spec=pltpu.PrefetchScalarGridSpec(num_scalar_p...  375 us
    ppermute x33, waiting for transfers between devices, swap(): return lax.ppermute(value, 'dp', xor_pairs(self.count, 1 << b))  109 us
    ppermute x9, waiting for transfers between devices, step(): lax.ppermute(down, 'tensor', [(i + 1, i) for i in range(0, size - k)])  47.7 us
    ppermute x33, starting transfers between devices, swap(): return lax.ppermute(value, 'dp', xor_pairs(self.count, 1 << b))  30.1 us
    unnamed x115, local copies, waits for them, and re-layouts  21.8 us
    ppermute x9, waiting for transfers between devices, step(): lax.ppermute(up, 'tensor', [(i, i + 1) for i in range(k - 1, size - 1)])  21 us
    select_n x9, other arithmetic, slot(): value = jnp.where(here, arr, value)  20.1 us
    ppermute x9, starting transfers between devices, step(): lax.ppermute(up, 'tensor', [(i, i + 1) for i in range(k - 1, size - 1)])  17.1 us
  transfers between devices with their start and end apart: 64, of which 25 were waited for; matrix products, arithmetic and copies ran while one was open for 5% of the time, Pallas kernels for 48%

profile of v7, /device:TPU:0, one launch (start us, length us, event | category | flops | bytes accessed | tf_op | source)
XLA Modules:
  0.0 721.4 jit_solution(8645065518322721511)
XLA Ops:
  28.1 21.0 %collective-permute-done.refs_0_ = bf16[256,2048]{1,0:T(8,128)(2,1)S(1)} collective-permute-done((bf16[256,2048]{1,0:T(8,128)(2,1)}, bf16[256,2048]{1,0:T(8,128)(2,1)S(1)}, u32[]{:S(2)}, u32[]{:S(2)}) %collective-permute-start) | collective-permute-done | bytes 1048608 | tf_op jit(solution)/shard_map/ppermute | solution.py:119
  49.1 10.8 %collective-permute-done.1.refs_1_ = bf16[256,2048]{1,0:T(8,128)(2,1)} collective-permute-done((bf16[256,2048]{1,0:T(8,128)(2,1)}, bf16[256,2048]{1,0:T(8,128)(2,1)}, u32[]{:S(2)}, u32[]{:S(2)}) %collective-permute-start.1) | collective-permute-done | bytes 1048608 | tf_op jit(solution)/shard_map/ppermute | solution.py:120
  70.6 14.9 %collective-permute-done.3.refs_1_ = bf16[256,2048]{1,0:T(8,128)(2,1)S(1)} collective-permute-done((bf16[256,2048]{1,0:T(8,128)(2,1)}, bf16[256,2048]{1,0:T(8,128)(2,1)S(1)}, u32[]{:S(2)}, u32[]{:S(2)}) %collective-permute-start.3) | collective-permute-done | bytes 1048608 | tf_op jit(solution)/shard_map/ppermute | solution.py:120
  108.2 8.7 %collective-permute-done.5 = bf16[256,2048]{1,0:T(8,128)(2,1)} collective-permute-done((bf16[256,2048]{1,0:T(8,128)(2,1)}, bf16[256,2048]{1,0:T(8,128)(2,1)}, u32[]{:S(2)}, u32[]{:S(2)}) %collective-permute-start.5) | collective-permute-done | bytes 1048608 | tf_op jit(solution)/shard_map/ppermute | solution.py:120
  125.0 10.9 %attend.1 = (bf16[1024,512]{1,0:T(8,128)(2,1)}, f32[8,128]{1,0:T(8,128)}) custom-call(s32[1024]{0:T(1024)} %refs_0_.4, bf16[1024,512]{1,0:T(8,128)(2,1)} %get-tuple-element.252.refs_1_, bf16[1024,512]{1,0:T(8,128)(2,1)} %get-tuple-element.253.refs_2_, bf16[1024,512]{1,0:T(8,128)(2,1)} %get-tuple-element.254.refs_3_, s32[1024,1]{1,0:T(8,128)} %copy.103.refs_4_.refs_5_, ...), custom_call_target="tpu_custom_call" | custom-call | flops 14300000256 | bytes 11000000 | tf_op jit(solution)/shard_map/attend/pallas_call | solution.py:57
  147.3 16.4 %all-to-all-done = bf16[4,256,512]{2,1,0:T(8,128)(2,1)} async-done(((bf16[4,256,512]{2,1,0:T(8,128)(2,1)}), bf16[4,256,512]{2,1,0:T(8,128)(2,1)}, u32[]{:S(2)}, u32[]{:S(2)}) %all-to-all-start) | async-done | bytes 1048608 | tf_op jit(solution)/shard_map/all_to_all | solution.py:141
  163.6 8.5 %project.1 = (f32[256,2048]{1,0:T(8,128)}, bf16[256,2048]{1,0:T(8,128)(2,1)}, f32[8,128]{1,0:T(8,128)}) custom-call(bf16[1024,512]{1,0:T(8,128)(2,1)} %bitcast.7.refs_0_, bf16[8,2048,256]{2,1,0:T(8,128)(2,1)} %bitcast.34, bf16[256,2048]{1,0:T(8,128)(2,1)} %refs_1_.3, f32[1,2048]{1,0:T(1,128)} %bitcast.38, f32[8,128]{1,0:T(8,128)} %get-tuple-element.263.refs_4_), custom_call_target="tpu_custom_call" | custom-call | flops 11180000256 | bytes 8600000 | tf_op jit(solution)/shard_map/project/pallas_call | solution.py:57
  174.8 22.2 %ffn.4 = (bf16[2048,1024]{1,0:T(8,128)(2,1)}, bf16[1024,2048]{1,0:T(8,128)(2,1)}, bf16[1024,2048]{1,0:T(8,128)(2,1)}, bf16[2048,1024]{1,0:T(8,128)(2,1)}, bf16[1...) custom-call(s32[1]{0:T(128)} %bitcast.1.refs_0_, ...), custom_call_target="tpu_custom_call" | custom-call | flops 28600000512 | bytes 22000000 | tf_op jit(solution)/shard_map/ffn/pallas_call | solution.py:57
  208.8 22.4 %ffn.5 = (bf16[2048,1024]{1,0:T(8,128)(2,1)}, bf16[1024,2048]{1,0:T(8,128)(2,1)}, bf16[1024,2048]{1,0:T(8,128)(2,1)}, bf16[2048,1024]{1,0:T(8,128)(2,1)}, bf16[1...) custom-call(s32[1]{0:T(128)} %bitcast.2.refs_0_, ...), custom_call_target="tpu_custom_call", output_to_operand_aliasing={{0}: (6, {}), {1}: (7, {}), {2}: (8, {}), {3}: (9, {}), {4}... | custom-call | flops 28600000512 | bytes 22000000 | tf_op jit(solution)/shard_map/ffn/pallas_call | solution.py:57
  242.1 22.3 %ffn.6 = (bf16[2048,1024]{1,0:T(8,128)(2,1)}, bf16[1024,2048]{1,0:T(8,128)(2,1)}, bf16[1024,2048]{1,0:T(8,128)(2,1)}, bf16[2048,1024]{1,0:T(8,128)(2,1)}, bf16[1...) custom-call(s32[1]{0:T(128)} %bitcast.3.refs_0_, ...), custom_call_target="tpu_custom_call", output_to_operand_aliasing={{0}: (6, {}), {1}: (7, {}), {2}: (8, {}), {3}: (9, {}), {4}... | custom-call | flops 28600000512 | bytes 22000000 | tf_op jit(solution)/shard_map/ffn/pallas_call | solution.py:57
  279.9 22.2 %ffn.7 = (bf16[2048,1024]{1,0:T(8,128)(2,1)}, bf16[1024,2048]{1,0:T(8,128)(2,1)}, bf16[1024,2048]{1,0:T(8,128)(2,1)}, bf16[2048,1024]{1,0:T(8,128)(2,1)}, bf16[1...) custom-call(s32[1]{0:T(128)} %bitcast.refs_0_, ...), custom_call_target="tpu_custom_call", output_to_operand_aliasing={{0}: (6, {}), {1}: (7, {}), {2}: (8, {}), {3}: (9, {}), {4}... | custom-call | flops 28600000512 | bytes 22000000 | tf_op jit(solution)/shard_map/ffn/pallas_call | solution.py:57
  312.7 8.6 %give.5 = (bf16[1024,2048]{1,0:T(8,128)(2,1)}, f32[8,128]{1,0:T(8,128)}) custom-call(s32[1]{0:T(128)} %bitcast.13.refs_0_, bf16[2048,1024]{1,0:T(8,128)(2,1)} %get-tuple-element.310.refs_1_, bf16[1024,2048]{1,0:T(8,128)(2,1)} %get-tuple-element.316.refs_2_, f32[8,128]{1,0:T(8,128)} %get-tuple-element.317.refs_3_), custom_call_target="tpu_custom_call" | custom-call | flops 10400000000 | bytes 8000000 | tf_op jit(solution)/shard_map/give/pallas_call | solution.py:57
  321.3 11.2 %keep.4 = (bf16[512,1024]{1,0:T(8,128)(2,1)}, bf16[512,1024]{1,0:T(8,128)(2,1)}, bf16[512,1024]{1,0:T(8,128)(2,1)}, bf16[512,1024]{1,0:T(8,128)(2,1)}, f32[8,128]{1,0:T(8,128)}) custom-call(s32[3]{0:T(128)} %pad_add_fusion.1.refs_0_, bf16[2048,1024]{1,0:T(8,128)(2,1)} %get-tuple-element.312.refs_1_, bf16[1024,2048]{1,0:T(8,128)(2,1)} %get-tuple-element.313.refs_2_, ...), custom_call_target="tpu_custom_call" | custom-call | flops 12999999488 | bytes 10000000 | tf_op jit(solution)/shard_map/keep/pallas_call | solution.py:57
  345.1 13.2 %collective-permute-done.21.refs_2_ = bf16[512,1024]{1,0:T(8,128)(2,1)S(1)} collective-permute-done((bf16[512,1024]{1,0:T(8,128)(2,1)}, bf16[512,1024]{1,0:T(8,128)(2,1)S(1)}, u32[]{:S(2)}, u32[]{:S(2)}) %collective-permute-start.21) | collective-permute-done | bytes 1048608 | tf_op jit(solution)/shard_map/ppermute | solution.py:269
  365.2 10.4 %keep.5 = (bf16[512,2048]{1,0:T(8,128)(2,1)}, bf16[512,2048]{1,0:T(8,128)(2,1)}, f32[8,128]{1,0:T(8,128)}) custom-call(s32[2]{0:T(128)} %pad_add_fusion.3.refs_0_, bf16[2048,1024]{1,0:T(8,128)(2,1)} %get-tuple-element.310.refs_1_, bf16[1024,2048]{1,0:T(8,128)(2,1)} %get-tuple-element.316.refs_2_, bf16[1024,2048]{1,0:T(8,128)(2,1)} %collective-permute-done.20.refs_3_, ...), custom_call_target="tpu_custom_call" | custom-call | flops 12999999488 | bytes 10000000 | tf_op jit(solution)/shard_map/keep/pallas_call | solution.py:57
  376.2 10.3 %keep.6 = (bf16[512,2048]{1,0:T(8,128)(2,1)}, bf16[512,2048]{1,0:T(8,128)(2,1)}, f32[8,128]{1,0:T(8,128)}) custom-call(s32[2]{0:T(128)} %pad_add_fusion.4.refs_0_, bf16[2048,1024]{1,0:T(8,128)(2,1)} %get-tuple-element.310.refs_1_, bf16[1024,2048]{1,0:T(8,128)(2,1)} %get-tuple-element.311.refs_2_, bf16[1024,2048]{1,0:T(8,128)(2,1)} %collective-permute-done.19.refs_3_, ...), custom_call_target="tpu_custom_call" | custom-call | flops 12999999488 | bytes 10000000 | tf_op jit(solution)/shard_map/keep/pallas_call | solution.py:57
  388.5 9.3 %middle.1 = (bf16[1024,512]{1,0:T(8,128)(2,1)}, f32[256,2048]{1,0:T(8,128)}, bf16[2048,256]{1,0:T(8,128)(2,1)}, f32[1,2048]{1,0:T(1,128)}, f32[8,128]{1,0:T(8,128)}) custom-call(bf16[256,2048]{1,0:T(8,128)(2,1)} %reduce-scatter.4.cloned.1.call-done.refs_0_, f32[256,2048]{1,0:T(8,128)} %get-tuple-element.264.refs_1_, bf16[256,2048]{1,0:T(8,128)(2,1)} %refs_2_.14, ...), custom_call_target="tpu_custom_call" | custom-call | flops 12350000128 | bytes 9500000 | tf_op jit(solution)/shard_map/middle/pallas_call | solution.py:57
  405.2 40.0 %collective-permute-done.23.refs_2_ = bf16[256,1024]{1,0:T(8,128)(2,1)} collective-permute-done((bf16[256,1024]{1,0:T(8,128)(2,1)}, bf16[256,1024]{1,0:T(8,128)(2,1)}, u32[]{:S(2)}, u32[]{:S(2)}) %collective-permute-start.23) | collective-permute-done | bytes 524320 | tf_op jit(solution)/shard_map/ppermute | solution.py:269
  472.3 16.9 %attend_back.1 = (bf16[1024,1536]{1,0:T(8,128)(2,1)}, f32[8,128]{1,0:T(8,128)}) custom-call(s32[1024]{0:T(1024)} %refs_0_.4, bf16[1024,512]{1,0:T(8,128)(2,1)} %get-tuple-element.252.refs_1_, bf16[1024,512]{1,0:T(8,128)(2,1)} %get-tuple-element.253.refs_2_, bf16[1024,512]{1,0:T(8,128)(2,1)} %get-tuple-element.254.refs_3_, bf16[1024,512]{1,0:T(8,128)(2,1)} %bitcast.27, ...), custom_call_target="tpu_custom_call" | custom-call | flops 22100000768 | bytes 17000000 | tf_op jit(solution)/shard_map/attend_back/pallas_call | solution.py:57
  497.0 15.9 %collective-permute-done.32.refs_2_ = bf16[256,2048]{1,0:T(8,128)(2,1)} collective-permute-done((bf16[256,2048]{1,0:T(8,128)(2,1)}, bf16[256,2048]{1,0:T(8,128)(2,1)}, u32[]{:S(2)}, u32[]{:S(2)}) %collective-permute-start.32) | collective-permute-done | bytes 1048608 | tf_op jit(solution)/shard_map/ppermute | solution.py:269
  528.9 11.0 %back_project.1 = (bf16[1024,2048]{1,0:T(8,128)(2,1)}, f32[8,128]{1,0:T(8,128)}) custom-call(bf16[1024,1536]{1,0:T(8,128)(2,1)} %get-tuple-element.345.refs_2_.refs_0_, bf16[2048,512]{1,0:T(8,128)(2,1)} %refs_1_.2, bf16[2048,512]{1,0:T(8,128)(2,1)} %refs_2_.15, bf16[2048,512]{1,0:T(8,128)(2,1)} %refs_3_.17, f32[8,128]{1,0:T(8,128)} %get-tuple-element.361.refs_4_), custom_call_target="tpu_custom_call" | custom-call | flops 14300000256 | bytes 11000000 | tf_op jit(solution)/shard_map/back_project/pallas_call | solution.py:57
  550.2 11.9 %keep.7 = (bf16[512,1024]{1,0:T(8,128)(2,1)}, bf16[512,1024]{1,0:T(8,128)(2,1)}, bf16[512,1024]{1,0:T(8,128)(2,1)}, bf16[512,1024]{1,0:T(8,128)(2,1)}, f32[8,128]{1,0:T(8,128)}) custom-call(s32[3]{0:T(128)} %pad_add_fusion.1.refs_0_, bf16[2048,1024]{1,0:T(8,128)(2,1)} %get-tuple-element.308.refs_1_, bf16[1024,1536]{1,0:T(8,128)(2,1)} %get-tuple-element.345.refs_2_.refs_0_, ...), custom_call_target="tpu_custom_call" | custom-call | flops 12999999488 | bytes 10000000 | tf_op jit(solution)/shard_map/keep/pallas_call | solution.py:57
  576.2 19.2 %collective-permute-done.39.refs_0_ = bf16[512,2048]{1,0:T(8,128)(2,1)S(1)} collective-permute-done((bf16[512,2048]{1,0:T(8,128)(2,1)}, bf16[512,2048]{1,0:T(8,128)(2,1)S(1)}, u32[]{:S(2)}, u32[]{:S(2)}) %collective-permute-start.39) | collective-permute-done | bytes 2097184 | tf_op jit(solution)/shard_map/ppermute | solution.py:269
  606.8 9.9 %collective-permute-done.37.refs_0_ = bf16[512,1024]{1,0:T(8,128)(2,1)S(1)} collective-permute-done((bf16[512,1024]{1,0:T(8,128)(2,1)}, bf16[512,1024]{1,0:T(8,128)(2,1)S(1)}, u32[]{:S(2)}, u32[]{:S(2)}) %collective-permute-start.37) | collective-permute-done | bytes 1048608 | tf_op jit(solution)/shard_map/ppermute | solution.py:269
  (323 shorter events, 338.1 us)
Async XLA Ops:
  7.2 90.9 %all-gather.6.cloned.1.call-start = ((), (), s32[]{:S(2)}) async-start(), calls=%async_computation.5 | async-start | bytes 1310720 | tf_op jit(solution)/shard_map/all_gather | solution.py:852
  18.5 145.2 %all-gather.8.cloned.1.call-start = ((), (), s32[]{:S(2)}) async-start(), calls=%async_computation.9 | async-start | bytes 9437184 | tf_op jit(solution)/shard_map/all_gather | solution.py:877
  140.1 248.4 %reduce-scatter.4.cloned.1.call-start = ((), (), s32[]{:S(2)}) async-start(), calls=%async_computation.6 | async-start | bytes 5242880 | tf_op jit(solution)/shard_map/reduce_scatter | solution.py:900
  142.1 62.8 %collective-permute-start.12 = (bf16[256,2048]{1,0:T(8,128)(2,1)}, bf16[256,2048]{1,0:T(8,128)(2,1)S(1)}, u32[]{:S(2)}, u32[]{:S(2)}) collective-permute-start(bf16[256,2048]{1,0:T(8,128)(2,1)} %get-tuple-element.260), channel_id=1, source_target_pairs={{1,2},{2,3},{5,6},{6,7},{9,10},{10,11},{13,14},{14,15},{17,18},{18... | collective-permute-start | bytes 3145736 | tf_op jit(solution)/shard_map/ppermute | solution.py:119
  142.8 62.1 %collective-permute-start.13 = (bf16[256,2048]{1,0:T(8,128)(2,1)}, bf16[256,2048]{1,0:T(8,128)(2,1)S(1)}, u32[]{:S(2)}, u32[]{:S(2)}) collective-permute-start(bf16[256,2048]{1,0:T(8,128)(2,1)} %get-tuple-element.261), channel_id=1, source_target_pairs={{1,0},{2,1},{5,4},{6,5},{9,8},{10,9},{13,12},{14,13},{17,16},{18,1... | collective-permute-start | bytes 3145736 | tf_op jit(solution)/shard_map/ppermute | solution.py:120
  206.8 57.6 %collective-permute-start.16 = (bf16[256,2048]{1,0:T(8,128)(2,1)}, bf16[256,2048]{1,0:T(8,128)(2,1)S(1)}, u32[]{:S(2)}, u32[]{:S(2)}) collective-permute-start(bf16[256,2048]{1,0:T(8,128)(2,1)} %get-tuple-element.283), channel_id=1, source_target_pairs={{2,3},{6,7},{10,11},{14,15},{18,19},{22,23},{26,27},{30,31}} | collective-permute-start | bytes 3145736 | tf_op jit(solution)/shard_map/ppermute | solution.py:119
  207.5 56.9 %collective-permute-start.17 = (bf16[256,2048]{1,0:T(8,128)(2,1)}, bf16[256,2048]{1,0:T(8,128)(2,1)S(1)}, u32[]{:S(2)}, u32[]{:S(2)}) collective-permute-start(bf16[256,2048]{1,0:T(8,128)(2,1)} %get-tuple-element.284), channel_id=1, source_target_pairs={{1,0},{5,4},{9,8},{13,12},{17,16},{21,20},{25,24},{29,28}} | collective-permute-start | bytes 3145736 | tf_op jit(solution)/shard_map/ppermute | solution.py:120
  312.5 212.4 %all-gather.10.cloned.1.call-start = ((), (), s32[]{:S(2)}) async-start(), calls=%async_computation.10 | async-start | bytes 5242880 | tf_op jit(solution)/shard_map/all_gather | solution.py:920
  375.6 76.6 %collective-permute-start.27 = (bf16[512,2048]{1,0:T(8,128)(2,1)}, bf16[512,2048]{1,0:T(8,128)(2,1)S(1)}, u32[]{:S(2)}, u32[]{:S(2)}) collective-permute-start(bf16[512,2048]{1,0:T(8,128)(2,1)} %get-tuple-element.339), channel_id=1, source_target_pairs={{0,8},{4,12},{8,0},{12,4},{16,24},{20,28},{24,16},{28,20},{1,9},{5... | collective-permute-start | bytes 6291464 | tf_op jit(solution)/shard_map/ppermute | solution.py:269
  386.6 65.6 %collective-permute-start.28 = (bf16[512,2048]{1,0:T(8,128)(2,1)}, bf16[512,2048]{1,0:T(8,128)(2,1)}, u32[]{:S(2)}, u32[]{:S(2)}) collective-permute-start(bf16[512,2048]{1,0:T(8,128)(2,1)} %get-tuple-element.341), channel_id=1, source_target_pairs={{0,16},{4,20},{8,24},{12,28},{16,0},{20,4},{24,8},{28,12},{1,17},{... | collective-permute-start | bytes 6291464 | tf_op jit(solution)/shard_map/ppermute | solution.py:269
  397.8 47.4 %collective-permute-start.23 = (bf16[256,1024]{1,0:T(8,128)(2,1)}, bf16[256,1024]{1,0:T(8,128)(2,1)}, u32[]{:S(2)}, u32[]{:S(2)}) collective-permute-start(bf16[256,1024]{1,0:T(8,128)(2,1)} %get-tuple-element.332), channel_id=1, source_target_pairs={{0,16},{4,20},{8,24},{12,28},{16,0},{20,4},{24,8},{28,12},{1,17},{... | collective-permute-start | bytes 1572872 | tf_op jit(solution)/shard_map/ppermute | solution.py:269
  399.4 45.9 %collective-permute-start.24 = (bf16[256,1024]{1,0:T(8,128)(2,1)}, bf16[256,1024]{1,0:T(8,128)(2,1)}, u32[]{:S(2)}, u32[]{:S(2)}) collective-permute-start(bf16[256,1024]{1,0:T(8,128)(2,1)} %get-tuple-element.334), channel_id=1, source_target_pairs={{0,8},{4,12},{8,0},{12,4},{16,24},{20,28},{24,16},{28,20},{1,9},{5... | collective-permute-start | bytes 1572872 | tf_op jit(solution)/shard_map/ppermute | solution.py:269
  400.8 70.5 %all-to-all-start.1 = ((bf16[4,256,512]{2,1,0:T(8,128)(2,1)}), bf16[4,256,512]{2,1,0:T(8,128)(2,1)S(1)}, u32[]{:S(2)}, u32[]{:S(2)}) async-start(bf16[4,256,512]{2,1,0:T(8,128)(2,1)} %bitcast.26), calls=%async_computation.2 | async-start | bytes 2097152 | tf_op jit(solution)/shard_map/all_to_all | solution.py:141
  405.0 244.3 %reduce-scatter.8.cloned.1.call-start = ((), (), s32[]{:S(2)}) async-start(), calls=%async_computation.8 | async-start | bytes 5242880 | tf_op jit(solution)/shard_map/reduce_scatter | solution.py:933
  467.3 52.2 %collective-permute-start.30 = (bf16[512,1024]{1,0:T(8,128)(2,1)}, bf16[512,1024]{1,0:T(8,128)(2,1)}, u32[]{:S(2)}, u32[]{:S(2)}) collective-permute-start(bf16[512,1024]{1,0:T(8,128)(2,1)} %get-tuple-element.349.refs_1_), channel_id=1, source_target_pairs={{0,8},{4,12},{8,0},{12,4},{16,24},{20,28},{24,16},{28,20},{1,9},{5... | collective-permute-start | bytes 3145736 | tf_op jit(solution)/shard_map/ppermute | solution.py:269
  468.1 51.4 %collective-permute-start.31 = (bf16[512,1024]{1,0:T(8,128)(2,1)}, bf16[512,1024]{1,0:T(8,128)(2,1)}, u32[]{:S(2)}, u32[]{:S(2)}) collective-permute-start(bf16[512,1024]{1,0:T(8,128)(2,1)} %get-tuple-element.350.refs_3_), channel_id=1, source_target_pairs={{0,16},{4,20},{8,24},{12,28},{16,0},{20,4},{24,8},{28,12},{1,17},{... | collective-permute-start | bytes 3145736 | tf_op jit(solution)/shard_map/ppermute | solution.py:269
  496.2 52.3 %collective-permute-start.29 = (bf16[1024,1536]{1,0:T(8,128)(2,1)}, bf16[1024,1536]{1,0:T(8,128)(2,1)S(1)}, u32[]{:S(2)}, u32[]{:S(2)}) collective-permute-start(bf16[1024,1536]{1,0:T(8,128)(2,1)} %get-tuple-element.348), channel_id=1, source_target_pairs={{0,4},{4,0},{8,12},{12,8},{16,20},{20,16},{24,28},{28,24},{1,5},{5... | collective-permute-start | bytes 9437192 | tf_op jit(solution)/shard_map/ppermute | solution.py:269
  524.8 45.4 %collective-permute-start.41 = (bf16[1024,2048]{1,0:T(8,128)(2,1)}, bf16[1024,2048]{1,0:T(8,128)(2,1)}, u32[]{:S(2)}, u32[]{:S(2)}) collective-permute-start(bf16[1024,2048]{1,0:T(8,128)(2,1)} %get-tuple-element.372.refs_1_), channel_id=1, source_target_pairs={{0,4},{4,0},{8,12},{12,8},{16,20},{20,16},{24,28},{28,24},{1,5},{5... | collective-permute-start | bytes 12582920 | tf_op jit(solution)/shard_map/ppermute | solution.py:269
  540.0 162.5 %reduce-scatter.6.cloned.1.call-start = ((), (), s32[]{:S(2)}) async-start(), calls=%async_computation.7 | async-start | bytes 5242880 | tf_op jit(solution)/shard_map/reduce_scatter | solution.py:951
  546.6 48.7 %collective-permute-start.39 = (bf16[512,2048]{1,0:T(8,128)(2,1)}, bf16[512,2048]{1,0:T(8,128)(2,1)S(1)}, u32[]{:S(2)}, u32[]{:S(2)}) collective-permute-start(bf16[512,2048]{1,0:T(8,128)(2,1)} %get-tuple-element.371.refs_1_), channel_id=1, source_target_pairs={{0,8},{4,12},{8,0},{12,4},{16,24},{20,28},{24,16},{28,20},{1,9},{5... | collective-permute-start | bytes 6291464 | tf_op jit(solution)/shard_map/ppermute | solution.py:269
  547.3 48.7 %collective-permute-start.40 = (bf16[512,2048]{1,0:T(8,128)(2,1)}, bf16[512,2048]{1,0:T(8,128)(2,1)S(1)}, u32[]{:S(2)}, u32[]{:S(2)}) collective-permute-start(bf16[512,2048]{1,0:T(8,128)(2,1)} %get-tuple-element.370.refs_1_), channel_id=1, source_target_pairs={{0,16},{4,20},{8,24},{12,28},{16,0},{20,4},{24,8},{28,12},{1,17},{... | collective-permute-start | bytes 6291464 | tf_op jit(solution)/shard_map/ppermute | solution.py:269
  562.1 54.7 %collective-permute-start.37 = (bf16[512,1024]{1,0:T(8,128)(2,1)}, bf16[512,1024]{1,0:T(8,128)(2,1)S(1)}, u32[]{:S(2)}, u32[]{:S(2)}) collective-permute-start(bf16[512,1024]{1,0:T(8,128)(2,1)} %get-tuple-element.368), channel_id=1, source_target_pairs={{0,8},{4,12},{8,0},{12,4},{16,24},{20,28},{24,16},{28,20},{1,9},{5... | collective-permute-start | bytes 3145736 | tf_op jit(solution)/shard_map/ppermute | solution.py:269
  563.4 53.8 %collective-permute-start.38 = (bf16[512,1024]{1,0:T(8,128)(2,1)}, bf16[512,1024]{1,0:T(8,128)(2,1)S(1)}, u32[]{:S(2)}, u32[]{:S(2)}) collective-permute-start(bf16[512,1024]{1,0:T(8,128)(2,1)} %get-tuple-element.369), channel_id=1, source_target_pairs={{0,16},{4,20},{8,24},{12,28},{16,0},{20,4},{24,8},{28,12},{1,17},{... | collective-permute-start | bytes 3145736 | tf_op jit(solution)/shard_map/ppermute | solution.py:269
  626.1 48.5 %collective-permute-start.50 = (bf16[1024,2048]{1,0:T(8,128)(2,1)}, bf16[1024,2048]{1,0:T(8,128)(2,1)}, u32[]{:S(2)}, u32[]{:S(2)}) collective-permute-start(bf16[1024,2048]{1,0:T(8,128)(2,1)} %get-tuple-element.390.refs_1_), channel_id=1, source_target_pairs={{0,4},{4,0},{8,12},{12,8},{16,20},{20,16},{24,28},{28,24},{1,5},{5... | collective-permute-start | bytes 12582920 | tf_op jit(solution)/shard_map/ppermute | solution.py:269
  (97 other events, 1259.9 us)
Sparse Core Ops, SparseCore 0:
  18.6 41.8 all-gather.5
  98.9 55.6 all-gather.7
  312.6 75.8 reduce-scatter.3
  397.9 100.3 all-gather.9
  540.1 74.9 reduce-scatter.7
  627.3 75.1 reduce-scatter.5

commit v8 on v5

--- a/solution.py
+++ b/solution.py
@@ -909,30 +909,33 @@
     first.keep(order)
     wide.keep(order, 0)
     wide.keep(order, 1)
+    usual = order.worth
     first.fold(order)
-    for _ in more:
-        first.fold(order)
     d_mix, d_resid, d_resid_t, ffn_gain_part = middle(
         order, d_normed2, resid, cotangent, ffn_gain, w_out_all, width
     )
     d_mix = exchange(d_mix)
     d_resid_all = lax.all_gather(d_resid_t, "tensor", axis=0)
     for _ in more:
+        first.fold(order)
+    wide.fold(order)
+    for _ in more:
         first.spread(order)
-    wide.fold(order)
+    order.worth = 1.3
     (d_qkv,) = attend_back(order, doc_ids, query, key, value, d_mix, cos, sin)
+    order.worth = usual
     attn = Gradients([(normed_t, d_qkv, [width] * 4, d_resid_all, mixed)], dp)
     attn.give(order)
+    for _ in more:
+        wide.fold(order)
+    first.join(order)
+    attn.give(order, second=True)
     d_normed = lax.psum_scatter(
         back_project(order, d_qkv, w_query, w_key, w_value),
         "tensor",
         scatter_dimension=0,
         tiled=True,
     )
-    first.join(order)
-    for _ in more:
-        wide.fold(order)
-    attn.give(order, second=True)
     attn.keep(order)
     wide.hold(order)
     usual, order.worth = order.worth, 10
@@ -964,11 +967,11 @@
     up_grad = wide.fill(order, 1, 0)
     order.worth = 0.02
     (gate_grad,) = wide.fill(order, 0, 1, gate_grad)
+    attn.join(order)
     (up_grad,) = wide.fill(order, 1, 1, up_grad)
-    (down_sum,) = order.after(down_sum)
-    attn.join(order)
     attn_grads = attn.fill(order, 0, 0)
     totals.step(order)
+    (down_sum,) = order.after(down_sum)
     query_grad, key_grad, value_grad, out_grad = attn.fill(order, 0, 1, attn_grads)
     attn_gain_grad, ffn_gain_grad = totals.split(order)
     layer_out = (resid + down_sum.astype(F32)).astype(BF)

time: 728 us -> 712 us (0.978)
  waiting for transfers between devices: 184 us -> 171 us
  starting transfers between devices: 77.3 us -> 65.4 us
    ppermute x9, waiting for transfers between devices: 0.02 us -> 21 us  [step(): lax.ppermute(up, 'tensor', [(i, i + 1) for i in range(k - 1, size - 1)])]
    ppermute x9, waiting for transfers between devices: 62.8 us -> 44 us  [step(): lax.ppermute(down, 'tensor', [(i + 1, i) for i in range(0, size - k)])]
    ppermute x33, waiting for transfers between devices: 94.6 us -> 82.8 us  [swap(): return lax.ppermute(value, 'dp', xor_pairs(self.count, 1 << b))]
    ppermute x33, starting transfers between devices: 32.8 us -> 24.5 us  [swap(): return lax.ppermute(value, 'dp', xor_pairs(self.count, 1 << b))]
    unnamed x129 -> x121, local copies, waits for them, and re-layouts: 25.3 us -> 27.3 us
  transfers between devices with their start and end apart: 64 -> 64, of which waited for: 23 -> 26; matrix products, arithmetic and copies ran while one was open for 5% -> 5% of each run, Pallas kernels for 47% -> 51%
where the time goes in v8:
time: 712 us; the launch traced here: 701 us
  Pallas kernels  381 us (54%)
  waiting for transfers between devices  171 us (24%)
  starting transfers between devices  65.4 us (9%)
  other arithmetic  38.6 us (5%)
  local copies, waits for them, and re-layouts  30.2 us (4%)
  between operations  15.2 us (2%)
    pallas_call x65, Pallas kernels, run(): pl.pallas_call(whole, grid_spec=pltpu.PrefetchScalarGridSpec(num_scalar_p...  381 us
    ppermute x33, waiting for transfers between devices, swap(): return lax.ppermute(value, 'dp', xor_pairs(self.count, 1 << b))  82.8 us
    ppermute x9, waiting for transfers between devices, step(): lax.ppermute(down, 'tensor', [(i + 1, i) for i in range(0, size - k)])  44 us
    unnamed x121, local copies, waits for them, and re-layouts  27.3 us
    ppermute x33, starting transfers between devices, swap(): return lax.ppermute(value, 'dp', xor_pairs(self.count, 1 << b))  24.5 us
    select_n x9, other arithmetic, slot(): value = jnp.where(here, arr, value)  21.3 us
    ppermute x9, waiting for transfers between devices, step(): lax.ppermute(up, 'tensor', [(i, i + 1) for i in range(k - 1, size - 1)])  21 us
    ppermute x9, starting transfers between devices, step(): lax.ppermute(up, 'tensor', [(i, i + 1) for i in range(k - 1, size - 1)])  17.2 us
  transfers between devices with their start and end apart: 64, of which 26 were waited for; matrix products, arithmetic and copies ran while one was open for 5% of the time, Pallas kernels for 51%

profile of v8, /device:TPU:0, one launch (start us, length us, event | category | flops | bytes accessed | tf_op | source)
XLA Modules:
  0.0 701.3 jit_solution(12908939392664436124)
XLA Ops:
  28.1 21.0 %collective-permute-done.refs_0_ = bf16[256,2048]{1,0:T(8,128)(2,1)S(1)} collective-permute-done((bf16[256,2048]{1,0:T(8,128)(2,1)}, bf16[256,2048]{1,0:T(8,128)(2,1)S(1)}, u32[]{:S(2)}, u32[]{:S(2)}) %collective-permute-start) | collective-permute-done | bytes 1048608 | tf_op jit(solution)/shard_map/ppermute | solution.py:119
  49.1 10.9 %collective-permute-done.1.refs_1_ = bf16[256,2048]{1,0:T(8,128)(2,1)} collective-permute-done((bf16[256,2048]{1,0:T(8,128)(2,1)}, bf16[256,2048]{1,0:T(8,128)(2,1)}, u32[]{:S(2)}, u32[]{:S(2)}) %collective-permute-start.1) | collective-permute-done | bytes 1048608 | tf_op jit(solution)/shard_map/ppermute | solution.py:120
  70.6 14.9 %collective-permute-done.3.refs_1_ = bf16[256,2048]{1,0:T(8,128)(2,1)S(1)} collective-permute-done((bf16[256,2048]{1,0:T(8,128)(2,1)}, bf16[256,2048]{1,0:T(8,128)(2,1)S(1)}, u32[]{:S(2)}, u32[]{:S(2)}) %collective-permute-start.3) | collective-permute-done | bytes 1048608 | tf_op jit(solution)/shard_map/ppermute | solution.py:120
  108.3 8.6 %collective-permute-done.5 = bf16[256,2048]{1,0:T(8,128)(2,1)} collective-permute-done((bf16[256,2048]{1,0:T(8,128)(2,1)}, bf16[256,2048]{1,0:T(8,128)(2,1)}, u32[]{:S(2)}, u32[]{:S(2)}) %collective-permute-start.5) | collective-permute-done | bytes 1048608 | tf_op jit(solution)/shard_map/ppermute | solution.py:120
  124.9 13.7 %attend.1 = (bf16[1024,512]{1,0:T(8,128)(2,1)}, f32[8,128]{1,0:T(8,128)}) custom-call(s32[1024]{0:T(1024)} %refs_0_.4, bf16[1024,512]{1,0:T(8,128)(2,1)} %get-tuple-element.249.refs_1_, bf16[1024,512]{1,0:T(8,128)(2,1)} %get-tuple-element.250.refs_2_, bf16[1024,512]{1,0:T(8,128)(2,1)} %get-tuple-element.251.refs_3_, s32[1024,1]{1,0:T(8,128)} %copy.101.refs_4_.refs_5_, ...), custom_call_target="tpu_custom_call" | custom-call | flops 14300000256 | bytes 11000000 | tf_op jit(solution)/shard_map/attend/pallas_call | solution.py:57
  150.0 14.5 %all-to-all-done = bf16[4,256,512]{2,1,0:T(8,128)(2,1)} async-done(((bf16[4,256,512]{2,1,0:T(8,128)(2,1)}), bf16[4,256,512]{2,1,0:T(8,128)(2,1)}, u32[]{:S(2)}, u32[]{:S(2)}) %all-to-all-start) | async-done | bytes 1048608 | tf_op jit(solution)/shard_map/all_to_all | solution.py:141
  164.5 8.4 %project.1 = (f32[256,2048]{1,0:T(8,128)}, bf16[256,2048]{1,0:T(8,128)(2,1)}, f32[8,128]{1,0:T(8,128)}) custom-call(bf16[1024,512]{1,0:T(8,128)(2,1)} %bitcast.7.refs_0_, bf16[8,2048,256]{2,1,0:T(8,128)(2,1)} %bitcast.34, bf16[256,2048]{1,0:T(8,128)(2,1)} %refs_1_.3, f32[1,2048]{1,0:T(1,128)} %bitcast.38, f32[8,128]{1,0:T(8,128)} %get-tuple-element.260.refs_4_), custom_call_target="tpu_custom_call" | custom-call | flops 11180000256 | bytes 8600000 | tf_op jit(solution)/shard_map/project/pallas_call | solution.py:57
  175.6 22.2 %ffn.4 = (bf16[2048,1024]{1,0:T(8,128)(2,1)}, bf16[1024,2048]{1,0:T(8,128)(2,1)}, bf16[1024,2048]{1,0:T(8,128)(2,1)}, bf16[2048,1024]{1,0:T(8,128)(2,1)}, bf16[1...) custom-call(s32[1]{0:T(128)} %bitcast.1.refs_0_, ...), custom_call_target="tpu_custom_call" | custom-call | flops 28600000512 | bytes 22000000 | tf_op jit(solution)/shard_map/ffn/pallas_call | solution.py:57
  208.5 22.3 %ffn.5 = (bf16[2048,1024]{1,0:T(8,128)(2,1)}, bf16[1024,2048]{1,0:T(8,128)(2,1)}, bf16[1024,2048]{1,0:T(8,128)(2,1)}, bf16[2048,1024]{1,0:T(8,128)(2,1)}, bf16[1...) custom-call(s32[1]{0:T(128)} %bitcast.2.refs_0_, ...), custom_call_target="tpu_custom_call", output_to_operand_aliasing={{0}: (6, {}), {1}: (7, {}), {2}: (8, {}), {3}: (9, {}), {4}... | custom-call | flops 28600000512 | bytes 22000000 | tf_op jit(solution)/shard_map/ffn/pallas_call | solution.py:57
  242.1 22.3 %ffn.6 = (bf16[2048,1024]{1,0:T(8,128)(2,1)}, bf16[1024,2048]{1,0:T(8,128)(2,1)}, bf16[1024,2048]{1,0:T(8,128)(2,1)}, bf16[2048,1024]{1,0:T(8,128)(2,1)}, bf16[1...) custom-call(s32[1]{0:T(128)} %bitcast.3.refs_0_, ...), custom_call_target="tpu_custom_call", output_to_operand_aliasing={{0}: (6, {}), {1}: (7, {}), {2}: (8, {}), {3}: (9, {}), {4}... | custom-call | flops 28600000512 | bytes 22000000 | tf_op jit(solution)/shard_map/ffn/pallas_call | solution.py:57
  279.0 22.2 %ffn.7 = (bf16[2048,1024]{1,0:T(8,128)(2,1)}, bf16[1024,2048]{1,0:T(8,128)(2,1)}, bf16[1024,2048]{1,0:T(8,128)(2,1)}, bf16[2048,1024]{1,0:T(8,128)(2,1)}, bf16[1...) custom-call(s32[1]{0:T(128)} %bitcast.refs_0_, ...), custom_call_target="tpu_custom_call", output_to_operand_aliasing={{0}: (6, {}), {1}: (7, {}), {2}: (8, {}), {3}: (9, {}), {4}... | custom-call | flops 28600000512 | bytes 22000000 | tf_op jit(solution)/shard_map/ffn/pallas_call | solution.py:57
  301.4 8.6 %give.4 = (bf16[1024,2048]{1,0:T(8,128)(2,1)}, f32[8,128]{1,0:T(8,128)}) custom-call(s32[1]{0:T(128)} %bitcast.13.refs_0_, bf16[2048,1024]{1,0:T(8,128)(2,1)} %get-tuple-element.307.refs_1_, bf16[1024,2048]{1,0:T(8,128)(2,1)} %get-tuple-element.308.refs_2_, f32[8,128]{1,0:T(8,128)} %get-tuple-element.309.refs_3_), custom_call_target="tpu_custom_call" | custom-call | flops 10400000000 | bytes 8000000 | tf_op jit(solution)/shard_map/give/pallas_call | solution.py:57
  310.1 8.4 %give.5 = (bf16[1024,2048]{1,0:T(8,128)(2,1)}, f32[8,128]{1,0:T(8,128)}) custom-call(s32[1]{0:T(128)} %bitcast.13.refs_0_, bf16[2048,1024]{1,0:T(8,128)(2,1)} %get-tuple-element.311.refs_1_, bf16[1024,2048]{1,0:T(8,128)(2,1)} %get-tuple-element.313.refs_2_, f32[8,128]{1,0:T(8,128)} %get-tuple-element.314.refs_3_), custom_call_target="tpu_custom_call" | custom-call | flops 10400000000 | bytes 8000000 | tf_op jit(solution)/shard_map/give/pallas_call | solution.py:57
  319.0 8.4 %give.6 = (bf16[1024,2048]{1,0:T(8,128)(2,1)}, f32[8,128]{1,0:T(8,128)}) custom-call(s32[1]{0:T(128)} %bitcast.13.refs_0_, bf16[2048,1024]{1,0:T(8,128)(2,1)} %get-tuple-element.311.refs_1_, bf16[1024,2048]{1,0:T(8,128)(2,1)} %get-tuple-element.312.refs_2_, f32[8,128]{1,0:T(8,128)} %get-tuple-element.315.refs_3_), custom_call_target="tpu_custom_call" | custom-call | flops 10400000000 | bytes 8000000 | tf_op jit(solution)/shard_map/give/pallas_call | solution.py:57
  329.9 10.6 %keep.4 = (bf16[512,1024]{1,0:T(8,128)(2,1)}, bf16[512,1024]{1,0:T(8,128)(2,1)}, bf16[512,1024]{1,0:T(8,128)(2,1)}, bf16[512,1024]{1,0:T(8,128)(2,1)}, f32[8,128]{1,0:T(8,128)}) custom-call(s32[3]{0:T(128)} %pad_add_fusion.1.refs_0_, bf16[2048,1024]{1,0:T(8,128)(2,1)} %get-tuple-element.307.refs_1_, bf16[1024,2048]{1,0:T(8,128)(2,1)} %get-tuple-element.308.refs_2_, ...), custom_call_target="tpu_custom_call" | custom-call | flops 12999999488 | bytes 10000000 | tf_op jit(solution)/shard_map/keep/pallas_call | solution.py:57
  345.4 10.3 %keep.5 = (bf16[512,2048]{1,0:T(8,128)(2,1)}, bf16[512,2048]{1,0:T(8,128)(2,1)}, f32[8,128]{1,0:T(8,128)}) custom-call(s32[2]{0:T(128)} %pad_add_fusion.3.refs_0_, bf16[2048,1024]{1,0:T(8,128)(2,1)} %get-tuple-element.311.refs_1_, bf16[1024,2048]{1,0:T(8,128)(2,1)} %get-tuple-element.313.refs_2_, bf16[1024,2048]{1,0:T(8,128)(2,1)} %collective-permute-done.22.refs_3_, ...), custom_call_target="tpu_custom_call" | custom-call | flops 12999999488 | bytes 10000000 | tf_op jit(solution)/shard_map/keep/pallas_call | solution.py:57
  356.3 10.3 %keep.6 = (bf16[512,2048]{1,0:T(8,128)(2,1)}, bf16[512,2048]{1,0:T(8,128)(2,1)}, f32[8,128]{1,0:T(8,128)}) custom-call(s32[2]{0:T(128)} %pad_add_fusion.4.refs_0_, bf16[2048,1024]{1,0:T(8,128)(2,1)} %get-tuple-element.311.refs_1_, bf16[1024,2048]{1,0:T(8,128)(2,1)} %get-tuple-element.312.refs_2_, bf16[1024,2048]{1,0:T(8,128)(2,1)} %collective-permute-done.21.refs_3_, ...), custom_call_target="tpu_custom_call" | custom-call | flops 12999999488 | bytes 10000000 | tf_op jit(solution)/shard_map/keep/pallas_call | solution.py:57
  378.2 9.3 %middle.1 = (bf16[1024,512]{1,0:T(8,128)(2,1)}, f32[256,2048]{1,0:T(8,128)}, bf16[2048,256]{1,0:T(8,128)(2,1)}, f32[1,2048]{1,0:T(1,128)}, f32[8,128]{1,0:T(8,128)}) custom-call(bf16[256,2048]{1,0:T(8,128)(2,1)} %reduce-scatter.4.cloned.1.call-done.refs_0_, f32[256,2048]{1,0:T(8,128)} %get-tuple-element.261.refs_1_, bf16[256,2048]{1,0:T(8,128)(2,1)} %refs_2_.14, ...), custom_call_target="tpu_custom_call" | custom-call | flops 12350000128 | bytes 9500000 | tf_op jit(solution)/shard_map/middle/pallas_call | solution.py:57
  392.0 33.3 %collective-permute-done.23.refs_2_ = bf16[256,1024]{1,0:T(8,128)(2,1)S(1)} collective-permute-done((bf16[256,1024]{1,0:T(8,128)(2,1)}, bf16[256,1024]{1,0:T(8,128)(2,1)S(1)}, u32[]{:S(2)}, u32[]{:S(2)}) %collective-permute-start.23) | collective-permute-done | bytes 524320 | tf_op jit(solution)/shard_map/ppermute | solution.py:269
  431.8 7.2 %fold.8 = (bf16[256,2048]{1,0:T(8,128)(2,1)}, bf16[256,2048]{1,0:T(8,128)(2,1)}, bf16[256,2048]{1,0:T(8,128)(2,1)}, bf16[256,2048]{1,0:T(8,128)(2,1)}, f32[8,128]{1,0:T(8,128)}) custom-call(s32[2]{0:T(128)} %pad_add_fusion.refs_0_, bf16[512,2048]{1,0:T(8,128)(2,1)} %get-tuple-element.335.refs_1_, bf16[512,2048]{1,0:T(8,128)(2,1)} %collective-permute-done.27.refs_2_, ...), custom_call_target="tpu_custom_call" | custom-call | flops 5200000000 | bytes 4000000 | tf_op jit(solution)/shard_map/fold/pallas_call | solution.py:57
  452.5 21.3 %attend_back.1 = (bf16[1024,1536]{1,0:T(8,128)(2,1)}, f32[8,128]{1,0:T(8,128)}) custom-call(s32[1024]{0:T(1024)} %refs_0_.4, bf16[1024,512]{1,0:T(8,128)(2,1)} %get-tuple-element.249.refs_1_, bf16[1024,512]{1,0:T(8,128)(2,1)} %get-tuple-element.250.refs_2_, bf16[1024,512]{1,0:T(8,128)(2,1)} %get-tuple-element.251.refs_3_, bf16[1024,512]{1,0:T(8,128)(2,1)} %bitcast.27, ...), custom_call_target="tpu_custom_call" | custom-call | flops 22100000768 | bytes 17000000 | tf_op jit(solution)/shard_map/attend_back/pallas_call | solution.py:57
  499.8 11.1 %back_project.1 = (bf16[1024,2048]{1,0:T(8,128)(2,1)}, f32[8,128]{1,0:T(8,128)}) custom-call(bf16[1024,1536]{1,0:T(8,128)(2,1)} %get-tuple-element.342.refs_2_.refs_0_, bf16[2048,512]{1,0:T(8,128)(2,1)} %refs_1_.2, bf16[2048,512]{1,0:T(8,128)(2,1)} %refs_2_.15, bf16[2048,512]{1,0:T(8,128)(2,1)} %refs_3_.17, f32[8,128]{1,0:T(8,128)} %get-tuple-element.356.refs_4_), custom_call_target="tpu_custom_call" | custom-call | flops 14300000256 | bytes 11000000 | tf_op jit(solution)/shard_map/back_project/pallas_call | solution.py:57
  512.1 12.5 %keep.7 = (bf16[512,1024]{1,0:T(8,128)(2,1)}, bf16[512,1024]{1,0:T(8,128)(2,1)}, bf16[512,1024]{1,0:T(8,128)(2,1)}, bf16[512,1024]{1,0:T(8,128)(2,1)}, f32[8,128]{1,0:T(8,128)}) custom-call(s32[3]{0:T(128)} %pad_add_fusion.1.refs_0_, bf16[2048,1024]{1,0:T(8,128)(2,1)} %get-tuple-element.305.refs_1_, bf16[1024,1536]{1,0:T(8,128)(2,1)} %get-tuple-element.342.refs_2_.refs_0_, ...), custom_call_target="tpu_custom_call" | custom-call | flops 12999999488 | bytes 10000000 | tf_op jit(solution)/shard_map/keep/pallas_call | solution.py:57
  528.1 22.3 %collective-permute-done.35.refs_2_ = bf16[512,1024]{1,0:T(8,128)(2,1)S(1)} collective-permute-done((bf16[512,1024]{1,0:T(8,128)(2,1)}, bf16[512,1024]{1,0:T(8,128)(2,1)S(1)}, u32[]{:S(2)}, u32[]{:S(2)}) %collective-permute-start.35) | collective-permute-done | bytes 1048608 | tf_op jit(solution)/shard_map/ppermute | solution.py:269
  (328 shorter events, 331.4 us)
Async XLA Ops:
  7.2 90.9 %all-gather.6.cloned.1.call-start = ((), (), s32[]{:S(2)}) async-start(), calls=%async_computation.5 | async-start | bytes 1310720 | tf_op jit(solution)/shard_map/all_gather | solution.py:852
  16.4 43.6 %collective-permute-start.1 = (bf16[256,2048]{1,0:T(8,128)(2,1)}, bf16[256,2048]{1,0:T(8,128)(2,1)}, u32[]{:S(2)}, u32[]{:S(2)}) collective-permute-start(bf16[256,2048]{1,0:T(8,128)(2,1)} %fusion.2.refs_1_), channel_id=1, source_target_pairs={{1,0},{2,1},{3,2},{5,4},{6,5},{7,6},{9,8},{10,9},{11,10},{13,12},{... | collective-permute-start | bytes 3145736 | tf_op jit(solution)/shard_map/ppermute | solution.py:120
  18.5 146.1 %all-gather.8.cloned.1.call-start = ((), (), s32[]{:S(2)}) async-start(), calls=%async_computation.9 | async-start | bytes 9437184 | tf_op jit(solution)/shard_map/all_gather | solution.py:877
  101.4 41.5 %collective-permute-start.6 = (bf16[256,2048]{1,0:T(8,128)(2,1)}, bf16[256,2048]{1,0:T(8,128)(2,1)S(1)}, u32[]{:S(2)}, u32[]{:S(2)}) collective-permute-start(bf16[256,2048]{1,0:T(8,128)(2,1)} %get-tuple-element.255), channel_id=1, source_target_pairs={{0,1},{1,2},{2,3},{4,5},{5,6},{6,7},{8,9},{9,10},{10,11},{12,13},{... | collective-permute-start | bytes 3145736 | tf_op jit(solution)/shard_map/ppermute | solution.py:119
  142.8 235.3 %reduce-scatter.4.cloned.1.call-start = ((), (), s32[]{:S(2)}) async-start(), calls=%async_computation.6 | async-start | bytes 5242880 | tf_op jit(solution)/shard_map/reduce_scatter | solution.py:900
  144.9 60.0 %collective-permute-start.12 = (bf16[256,2048]{1,0:T(8,128)(2,1)}, bf16[256,2048]{1,0:T(8,128)(2,1)S(1)}, u32[]{:S(2)}, u32[]{:S(2)}) collective-permute-start(bf16[256,2048]{1,0:T(8,128)(2,1)} %get-tuple-element.257), channel_id=1, source_target_pairs={{1,2},{2,3},{5,6},{6,7},{9,10},{10,11},{13,14},{14,15},{17,18},{18... | collective-permute-start | bytes 3145736 | tf_op jit(solution)/shard_map/ppermute | solution.py:119
  145.6 59.3 %collective-permute-start.13 = (bf16[256,2048]{1,0:T(8,128)(2,1)}, bf16[256,2048]{1,0:T(8,128)(2,1)}, u32[]{:S(2)}, u32[]{:S(2)}) collective-permute-start(bf16[256,2048]{1,0:T(8,128)(2,1)} %get-tuple-element.258), channel_id=1, source_target_pairs={{1,0},{2,1},{5,4},{6,5},{9,8},{10,9},{13,12},{14,13},{17,16},{18,1... | collective-permute-start | bytes 3145736 | tf_op jit(solution)/shard_map/ppermute | solution.py:120
  206.4 58.0 %collective-permute-start.16 = (bf16[256,2048]{1,0:T(8,128)(2,1)}, bf16[256,2048]{1,0:T(8,128)(2,1)S(1)}, u32[]{:S(2)}, u32[]{:S(2)}) collective-permute-start(bf16[256,2048]{1,0:T(8,128)(2,1)} %get-tuple-element.280), channel_id=1, source_target_pairs={{2,3},{6,7},{10,11},{14,15},{18,19},{22,23},{26,27},{30,31}} | collective-permute-start | bytes 3145736 | tf_op jit(solution)/shard_map/ppermute | solution.py:119
  207.2 57.3 %collective-permute-start.17 = (bf16[256,2048]{1,0:T(8,128)(2,1)}, bf16[256,2048]{1,0:T(8,128)(2,1)S(1)}, u32[]{:S(2)}, u32[]{:S(2)}) collective-permute-start(bf16[256,2048]{1,0:T(8,128)(2,1)} %get-tuple-element.281), channel_id=1, source_target_pairs={{1,0},{5,4},{9,8},{13,12},{17,16},{21,20},{25,24},{29,28}} | collective-permute-start | bytes 3145736 | tf_op jit(solution)/shard_map/ppermute | solution.py:120
  301.2 194.5 %all-gather.10.cloned.1.call-start = ((), (), s32[]{:S(2)}) async-start(), calls=%async_computation.10 | async-start | bytes 5242880 | tf_op jit(solution)/shard_map/all_gather | solution.py:918
  355.8 76.1 %collective-permute-start.27 = (bf16[512,2048]{1,0:T(8,128)(2,1)}, bf16[512,2048]{1,0:T(8,128)(2,1)}, u32[]{:S(2)}, u32[]{:S(2)}) collective-permute-start(bf16[512,2048]{1,0:T(8,128)(2,1)} %get-tuple-element.336), channel_id=1, source_target_pairs={{0,8},{4,12},{8,0},{12,4},{16,24},{20,28},{24,16},{28,20},{1,9},{5... | collective-permute-start | bytes 6291464 | tf_op jit(solution)/shard_map/ppermute | solution.py:269
  366.6 65.2 %collective-permute-start.28 = (bf16[512,2048]{1,0:T(8,128)(2,1)}, bf16[512,2048]{1,0:T(8,128)(2,1)}, u32[]{:S(2)}, u32[]{:S(2)}) collective-permute-start(bf16[512,2048]{1,0:T(8,128)(2,1)} %get-tuple-element.338), channel_id=1, source_target_pairs={{0,16},{4,20},{8,24},{12,28},{16,0},{20,4},{24,8},{28,12},{1,17},{... | collective-permute-start | bytes 6291464 | tf_op jit(solution)/shard_map/ppermute | solution.py:269
  375.0 50.3 %collective-permute-start.23 = (bf16[256,1024]{1,0:T(8,128)(2,1)}, bf16[256,1024]{1,0:T(8,128)(2,1)S(1)}, u32[]{:S(2)}, u32[]{:S(2)}) collective-permute-start(bf16[256,1024]{1,0:T(8,128)(2,1)} %get-tuple-element.329), channel_id=1, source_target_pairs={{0,16},{4,20},{8,24},{12,28},{16,0},{20,4},{24,8},{28,12},{1,17},{... | collective-permute-start | bytes 1572872 | tf_op jit(solution)/shard_map/ppermute | solution.py:269
  377.4 47.9 %collective-permute-start.24 = (bf16[256,1024]{1,0:T(8,128)(2,1)}, bf16[256,1024]{1,0:T(8,128)(2,1)S(1)}, u32[]{:S(2)}, u32[]{:S(2)}) collective-permute-start(bf16[256,1024]{1,0:T(8,128)(2,1)} %get-tuple-element.331), channel_id=1, source_target_pairs={{0,8},{4,12},{8,0},{12,4},{16,24},{20,28},{24,16},{28,20},{1,9},{5... | collective-permute-start | bytes 1572872 | tf_op jit(solution)/shard_map/ppermute | solution.py:269
  387.5 64.0 %all-to-all-start.1 = ((bf16[4,256,512]{2,1,0:T(8,128)(2,1)}), bf16[4,256,512]{2,1,0:T(8,128)(2,1)S(1)}, u32[]{:S(2)}, u32[]{:S(2)}) async-start(bf16[4,256,512]{2,1,0:T(8,128)(2,1)} %bitcast.26), calls=%async_computation.2 | async-start | bytes 2097152 | tf_op jit(solution)/shard_map/all_to_all | solution.py:141
  391.8 198.0 %reduce-scatter.8.cloned.1.call-start = ((), (), s32[]{:S(2)}) async-start(), calls=%async_computation.8 | async-start | bytes 5242880 | tf_op jit(solution)/shard_map/reduce_scatter | solution.py:933
  439.0 42.3 %collective-permute-start.32 = (bf16[256,2048]{1,0:T(8,128)(2,1)}, bf16[256,2048]{1,0:T(8,128)(2,1)S(1)}, u32[]{:S(2)}, u32[]{:S(2)}) collective-permute-start(bf16[256,2048]{1,0:T(8,128)(2,1)} %get-tuple-element.349), channel_id=1, source_target_pairs={{0,16},{4,20},{8,24},{12,28},{16,0},{20,4},{24,8},{28,12},{1,17},{... | collective-permute-start | bytes 3145736 | tf_op jit(solution)/shard_map/ppermute | solution.py:269
  440.2 41.2 %collective-permute-start.33 = (bf16[256,2048]{1,0:T(8,128)(2,1)}, bf16[256,2048]{1,0:T(8,128)(2,1)}, u32[]{:S(2)}, u32[]{:S(2)}) collective-permute-start(bf16[256,2048]{1,0:T(8,128)(2,1)} %get-tuple-element.351), channel_id=1, source_target_pairs={{0,8},{4,12},{8,0},{12,4},{16,24},{20,28},{24,16},{28,20},{1,9},{5... | collective-permute-start | bytes 3145736 | tf_op jit(solution)/shard_map/ppermute | solution.py:269
  486.8 39.5 %collective-permute-start.37 = (bf16[256,2048]{1,0:T(8,128)(2,1)}, bf16[256,2048]{1,0:T(8,128)(2,1)S(1)}, u32[]{:S(2)}, u32[]{:S(2)}) collective-permute-start(bf16[256,2048]{1,0:T(8,128)(2,1)} %get-tuple-element.362.refs_1_), channel_id=1, source_target_pairs={{0,16},{4,20},{8,24},{12,28},{16,0},{20,4},{24,8},{28,12},{1,17},{... | collective-permute-start | bytes 3145736 | tf_op jit(solution)/shard_map/ppermute | solution.py:269
  486.8 39.5 %collective-permute-start.38 = (bf16[256,2048]{1,0:T(8,128)(2,1)}, bf16[256,2048]{1,0:T(8,128)(2,1)S(1)}, u32[]{:S(2)}, u32[]{:S(2)}) collective-permute-start(bf16[256,2048]{1,0:T(8,128)(2,1)} %get-tuple-element.363.refs_3_), channel_id=1, source_target_pairs={{0,8},{4,12},{8,0},{12,4},{16,24},{20,28},{24,16},{28,20},{1,9},{5... | collective-permute-start | bytes 3145736 | tf_op jit(solution)/shard_map/ppermute | solution.py:269
  510.9 171.4 %reduce-scatter.6.cloned.1.call-start = ((), (), s32[]{:S(2)}) async-start(), calls=%async_computation.7 | async-start | bytes 5242880 | tf_op jit(solution)/shard_map/reduce_scatter | solution.py:944
  526.2 55.6 %collective-permute-start.39 = (bf16[1024,2048]{1,0:T(8,128)(2,1)}, bf16[1024,2048]{1,0:T(8,128)(2,1)S(1)}, u32[]{:S(2)}, u32[]{:S(2)}) collective-permute-start(bf16[1024,2048]{1,0:T(8,128)(2,1)} %get-tuple-element.370.refs_1_), channel_id=1, source_target_pairs={{0,4},{4,0},{8,12},{12,8},{16,20},{20,16},{24,28},{28,24},{1,5},{5... | collective-permute-start | bytes 12582920 | tf_op jit(solution)/shard_map/ppermute | solution.py:269
  563.4 53.2 %collective-permute-start.48 = (bf16[512,2048]{1,0:T(8,128)(2,1)}, bf16[512,2048]{1,0:T(8,128)(2,1)S(1)}, u32[]{:S(2)}, u32[]{:S(2)}) collective-permute-start(bf16[512,2048]{1,0:T(8,128)(2,1)} %get-tuple-element.397.refs_1_), channel_id=1, source_target_pairs={{0,8},{4,12},{8,0},{12,4},{16,24},{20,28},{24,16},{28,20},{1,9},{5... | collective-permute-start | bytes 6291464 | tf_op jit(solution)/shard_map/ppermute | solution.py:269
  564.3 52.3 %collective-permute-start.49 = (bf16[512,2048]{1,0:T(8,128)(2,1)}, bf16[512,2048]{1,0:T(8,128)(2,1)}, u32[]{:S(2)}, u32[]{:S(2)}) collective-permute-start(bf16[512,2048]{1,0:T(8,128)(2,1)} %get-tuple-element.396.refs_1_), channel_id=1, source_target_pairs={{0,16},{4,20},{8,24},{12,28},{16,0},{20,4},{24,8},{28,12},{1,17},{... | collective-permute-start | bytes 6291464 | tf_op jit(solution)/shard_map/ppermute | solution.py:269
  (100 other events, 1218.9 us)
Sparse Core Ops, SparseCore 0:
  18.6 41.8 all-gather.5
  98.9 55.6 all-gather.7
  301.3 76.8 reduce-scatter.3
  387.6 97.9 all-gather.9
  511.0 73.6 reduce-scatter.7
  607.7 74.4 reduce-scatter.5

commit v9 on v8

--- a/solution.py
+++ b/solution.py
@@ -916,15 +916,13 @@
     )
     d_mix = exchange(d_mix)
     d_resid_all = lax.all_gather(d_resid_t, "tensor", axis=0)
+    wide.fold(order)
     for _ in more:
         first.fold(order)
-    wide.fold(order)
+    (d_qkv,) = attend_back(order, doc_ids, query, key, value, d_mix, cos, sin)
+    attn = Gradients([(normed_t, d_qkv, [width] * 4, d_resid_all, mixed)], dp)
     for _ in more:
         first.spread(order)
-    order.worth = 1.3
-    (d_qkv,) = attend_back(order, doc_ids, query, key, value, d_mix, cos, sin)
-    order.worth = usual
-    attn = Gradients([(normed_t, d_qkv, [width] * 4, d_resid_all, mixed)], dp)
     attn.give(order)
     for _ in more:
         wide.fold(order)

time: 712 us -> 714 us (level)
    unnamed x121 -> x125, local copies, waits for them, and re-layouts: 27.3 us -> 26.5 us
  transfers between devices with their start and end apart: 64 -> 64, of which waited for: 26 -> 27; matrix products, arithmetic and copies ran while one was open for 5% -> 5% of each run, Pallas kernels for 51% -> 50%
where the time goes in v9:
time: 714 us; the launch traced here: 703 us
  Pallas kernels  374 us (52%)
  waiting for transfers between devices  175 us (25%)
  starting transfers between devices  69.8 us (10%)
  other arithmetic  38.7 us (5%)
  local copies, waits for them, and re-layouts  29.4 us (4%)
  between operations  15.2 us (2%)
    pallas_call x65, Pallas kernels, run(): pl.pallas_call(whole, grid_spec=pltpu.PrefetchScalarGridSpec(num_scalar_p...  374 us
    ppermute x33, waiting for transfers between devices, swap(): return lax.ppermute(value, 'dp', xor_pairs(self.count, 1 << b))  79.8 us
    ppermute x9, waiting for transfers between devices, step(): lax.ppermute(down, 'tensor', [(i + 1, i) for i in range(0, size - k)])  46.8 us
    ppermute x33, starting transfers between devices, swap(): return lax.ppermute(value, 'dp', xor_pairs(self.count, 1 << b))  30.1 us
    unnamed x125, local copies, waits for them, and re-layouts  26.5 us
    select_n x9, other arithmetic, slot(): value = jnp.where(here, arr, value)  21.3 us
    ppermute x9, waiting for transfers between devices, step(): lax.ppermute(up, 'tensor', [(i, i + 1) for i in range(k - 1, size - 1)])  21 us
    ppermute x9, starting transfers between devices, step(): lax.ppermute(up, 'tensor', [(i, i + 1) for i in range(k - 1, size - 1)])  17.1 us
  transfers between devices with their start and end apart: 64, of which 27 were waited for; matrix products, arithmetic and copies ran while one was open for 5% of the time, Pallas kernels for 50%

profile of v9, /device:TPU:0, one launch (start us, length us, event | category | flops | bytes accessed | tf_op | source)
XLA Modules:
  0.0 702.6 jit_solution(9110000904182782445)
XLA Ops:
  28.1 21.0 %collective-permute-done.refs_0_ = bf16[256,2048]{1,0:T(8,128)(2,1)S(1)} collective-permute-done((bf16[256,2048]{1,0:T(8,128)(2,1)}, bf16[256,2048]{1,0:T(8,128)(2,1)S(1)}, u32[]{:S(2)}, u32[]{:S(2)}) %collective-permute-start) | collective-permute-done | bytes 1048608 | tf_op jit(solution)/shard_map/ppermute | solution.py:119
  49.1 10.9 %collective-permute-done.1.refs_1_ = bf16[256,2048]{1,0:T(8,128)(2,1)} collective-permute-done((bf16[256,2048]{1,0:T(8,128)(2,1)}, bf16[256,2048]{1,0:T(8,128)(2,1)}, u32[]{:S(2)}, u32[]{:S(2)}) %collective-permute-start.1) | collective-permute-done | bytes 1048608 | tf_op jit(solution)/shard_map/ppermute | solution.py:120
  70.6 14.9 %collective-permute-done.3.refs_1_ = bf16[256,2048]{1,0:T(8,128)(2,1)S(1)} collective-permute-done((bf16[256,2048]{1,0:T(8,128)(2,1)}, bf16[256,2048]{1,0:T(8,128)(2,1)S(1)}, u32[]{:S(2)}, u32[]{:S(2)}) %collective-permute-start.3) | collective-permute-done | bytes 1048608 | tf_op jit(solution)/shard_map/ppermute | solution.py:120
  108.2 8.6 %collective-permute-done.5 = bf16[256,2048]{1,0:T(8,128)(2,1)} collective-permute-done((bf16[256,2048]{1,0:T(8,128)(2,1)}, bf16[256,2048]{1,0:T(8,128)(2,1)}, u32[]{:S(2)}, u32[]{:S(2)}) %collective-permute-start.5) | collective-permute-done | bytes 1048608 | tf_op jit(solution)/shard_map/ppermute | solution.py:120
  124.9 10.9 %attend.1 = (bf16[1024,512]{1,0:T(8,128)(2,1)}, f32[8,128]{1,0:T(8,128)}) custom-call(s32[1024]{0:T(1024)} %refs_0_.4, bf16[1024,512]{1,0:T(8,128)(2,1)} %get-tuple-element.249.refs_1_, bf16[1024,512]{1,0:T(8,128)(2,1)} %get-tuple-element.250.refs_2_, bf16[1024,512]{1,0:T(8,128)(2,1)} %get-tuple-element.251.refs_3_, s32[1024,1]{1,0:T(8,128)} %copy.101.refs_4_.refs_5_, ...), custom_call_target="tpu_custom_call" | custom-call | flops 14300000256 | bytes 11000000 | tf_op jit(solution)/shard_map/attend/pallas_call | solution.py:57
  147.2 16.4 %all-to-all-done = bf16[4,256,512]{2,1,0:T(8,128)(2,1)} async-done(((bf16[4,256,512]{2,1,0:T(8,128)(2,1)}), bf16[4,256,512]{2,1,0:T(8,128)(2,1)}, u32[]{:S(2)}, u32[]{:S(2)}) %all-to-all-start) | async-done | bytes 1048608 | tf_op jit(solution)/shard_map/all_to_all | solution.py:141
  163.6 8.4 %project.1 = (f32[256,2048]{1,0:T(8,128)}, bf16[256,2048]{1,0:T(8,128)(2,1)}, f32[8,128]{1,0:T(8,128)}) custom-call(bf16[1024,512]{1,0:T(8,128)(2,1)} %bitcast.7.refs_0_, bf16[8,2048,256]{2,1,0:T(8,128)(2,1)} %bitcast.34, bf16[256,2048]{1,0:T(8,128)(2,1)} %refs_1_.3, f32[1,2048]{1,0:T(1,128)} %bitcast.38, f32[8,128]{1,0:T(8,128)} %get-tuple-element.260.refs_4_), custom_call_target="tpu_custom_call" | custom-call | flops 11180000256 | bytes 8600000 | tf_op jit(solution)/shard_map/project/pallas_call | solution.py:57
  174.7 22.2 %ffn.4 = (bf16[2048,1024]{1,0:T(8,128)(2,1)}, bf16[1024,2048]{1,0:T(8,128)(2,1)}, bf16[1024,2048]{1,0:T(8,128)(2,1)}, bf16[2048,1024]{1,0:T(8,128)(2,1)}, bf16[1...) custom-call(s32[1]{0:T(128)} %bitcast.1.refs_0_, ...), custom_call_target="tpu_custom_call" | custom-call | flops 28600000512 | bytes 22000000 | tf_op jit(solution)/shard_map/ffn/pallas_call | solution.py:57
  208.5 22.3 %ffn.5 = (bf16[2048,1024]{1,0:T(8,128)(2,1)}, bf16[1024,2048]{1,0:T(8,128)(2,1)}, bf16[1024,2048]{1,0:T(8,128)(2,1)}, bf16[2048,1024]{1,0:T(8,128)(2,1)}, bf16[1...) custom-call(s32[1]{0:T(128)} %bitcast.2.refs_0_, ...), custom_call_target="tpu_custom_call", output_to_operand_aliasing={{0}: (6, {}), {1}: (7, {}), {2}: (8, {}), {3}: (9, {}), {4}... | custom-call | flops 28600000512 | bytes 22000000 | tf_op jit(solution)/shard_map/ffn/pallas_call | solution.py:57
  242.1 22.3 %ffn.6 = (bf16[2048,1024]{1,0:T(8,128)(2,1)}, bf16[1024,2048]{1,0:T(8,128)(2,1)}, bf16[1024,2048]{1,0:T(8,128)(2,1)}, bf16[2048,1024]{1,0:T(8,128)(2,1)}, bf16[1...) custom-call(s32[1]{0:T(128)} %bitcast.3.refs_0_, ...), custom_call_target="tpu_custom_call", output_to_operand_aliasing={{0}: (6, {}), {1}: (7, {}), {2}: (8, {}), {3}: (9, {}), {4}... | custom-call | flops 28600000512 | bytes 22000000 | tf_op jit(solution)/shard_map/ffn/pallas_call | solution.py:57
  280.8 22.2 %ffn.7 = (bf16[2048,1024]{1,0:T(8,128)(2,1)}, bf16[1024,2048]{1,0:T(8,128)(2,1)}, bf16[1024,2048]{1,0:T(8,128)(2,1)}, bf16[2048,1024]{1,0:T(8,128)(2,1)}, bf16[1...) custom-call(s32[1]{0:T(128)} %bitcast.refs_0_, ...), custom_call_target="tpu_custom_call", output_to_operand_aliasing={{0}: (6, {}), {1}: (7, {}), {2}: (8, {}), {3}: (9, {}), {4}... | custom-call | flops 28600000512 | bytes 22000000 | tf_op jit(solution)/shard_map/ffn/pallas_call | solution.py:57
  303.0 8.5 %give.4 = (bf16[1024,2048]{1,0:T(8,128)(2,1)}, f32[8,128]{1,0:T(8,128)}) custom-call(s32[1]{0:T(128)} %bitcast.13.refs_0_, bf16[2048,1024]{1,0:T(8,128)(2,1)} %get-tuple-element.307.refs_1_, bf16[1024,2048]{1,0:T(8,128)(2,1)} %get-tuple-element.308.refs_2_, f32[8,128]{1,0:T(8,128)} %get-tuple-element.309.refs_3_), custom_call_target="tpu_custom_call" | custom-call | flops 10400000000 | bytes 8000000 | tf_op jit(solution)/shard_map/give/pallas_call | solution.py:57
  311.5 8.4 %give.5 = (bf16[1024,2048]{1,0:T(8,128)(2,1)}, f32[8,128]{1,0:T(8,128)}) custom-call(s32[1]{0:T(128)} %bitcast.13.refs_0_, bf16[2048,1024]{1,0:T(8,128)(2,1)} %get-tuple-element.311.refs_1_, bf16[1024,2048]{1,0:T(8,128)(2,1)} %get-tuple-element.313.refs_2_, f32[8,128]{1,0:T(8,128)} %get-tuple-element.314.refs_3_), custom_call_target="tpu_custom_call" | custom-call | flops 10400000000 | bytes 8000000 | tf_op jit(solution)/shard_map/give/pallas_call | solution.py:57
  320.5 8.4 %give.6 = (bf16[1024,2048]{1,0:T(8,128)(2,1)}, f32[8,128]{1,0:T(8,128)}) custom-call(s32[1]{0:T(128)} %bitcast.13.refs_0_, bf16[2048,1024]{1,0:T(8,128)(2,1)} %get-tuple-element.311.refs_1_, bf16[1024,2048]{1,0:T(8,128)(2,1)} %get-tuple-element.312.refs_2_, f32[8,128]{1,0:T(8,128)} %get-tuple-element.315.refs_3_), custom_call_target="tpu_custom_call" | custom-call | flops 10400000000 | bytes 8000000 | tf_op jit(solution)/shard_map/give/pallas_call | solution.py:57
  331.4 10.8 %keep.4 = (bf16[512,1024]{1,0:T(8,128)(2,1)}, bf16[512,1024]{1,0:T(8,128)(2,1)}, bf16[512,1024]{1,0:T(8,128)(2,1)}, bf16[512,1024]{1,0:T(8,128)(2,1)}, f32[8,128]{1,0:T(8,128)}) custom-call(s32[3]{0:T(128)} %pad_add_fusion.1.refs_0_, bf16[2048,1024]{1,0:T(8,128)(2,1)} %get-tuple-element.307.refs_1_, bf16[1024,2048]{1,0:T(8,128)(2,1)} %get-tuple-element.308.refs_2_, ...), custom_call_target="tpu_custom_call" | custom-call | flops 12999999488 | bytes 10000000 | tf_op jit(solution)/shard_map/keep/pallas_call | solution.py:57
  342.4 10.3 %keep.5 = (bf16[512,2048]{1,0:T(8,128)(2,1)}, bf16[512,2048]{1,0:T(8,128)(2,1)}, f32[8,128]{1,0:T(8,128)}) custom-call(s32[2]{0:T(128)} %pad_add_fusion.3.refs_0_, bf16[2048,1024]{1,0:T(8,128)(2,1)} %get-tuple-element.311.refs_1_, bf16[1024,2048]{1,0:T(8,128)(2,1)} %get-tuple-element.313.refs_2_, bf16[1024,2048]{1,0:T(8,128)(2,1)} %collective-permute-done.22.refs_3_, ...), custom_call_target="tpu_custom_call" | custom-call | flops 12999999488 | bytes 10000000 | tf_op jit(solution)/shard_map/keep/pallas_call | solution.py:57
  354.6 10.3 %keep.6 = (bf16[512,2048]{1,0:T(8,128)(2,1)}, bf16[512,2048]{1,0:T(8,128)(2,1)}, f32[8,128]{1,0:T(8,128)}) custom-call(s32[2]{0:T(128)} %pad_add_fusion.4.refs_0_, bf16[2048,1024]{1,0:T(8,128)(2,1)} %get-tuple-element.311.refs_1_, bf16[1024,2048]{1,0:T(8,128)(2,1)} %get-tuple-element.312.refs_2_, bf16[1024,2048]{1,0:T(8,128)(2,1)} %collective-permute-done.21.refs_3_, ...), custom_call_target="tpu_custom_call" | custom-call | flops 12999999488 | bytes 10000000 | tf_op jit(solution)/shard_map/keep/pallas_call | solution.py:57
  375.8 9.4 %middle.1 = (bf16[1024,512]{1,0:T(8,128)(2,1)}, f32[256,2048]{1,0:T(8,128)}, bf16[2048,256]{1,0:T(8,128)(2,1)}, f32[1,2048]{1,0:T(1,128)}, f32[8,128]{1,0:T(8,128)}) custom-call(bf16[256,2048]{1,0:T(8,128)(2,1)} %reduce-scatter.4.cloned.1.call-done.refs_0_, f32[256,2048]{1,0:T(8,128)} %get-tuple-element.261.refs_1_, bf16[256,2048]{1,0:T(8,128)(2,1)} %refs_2_.14, ...), custom_call_target="tpu_custom_call" | custom-call | flops 12350000128 | bytes 9500000 | tf_op jit(solution)/shard_map/middle/pallas_call | solution.py:57
  393.1 20.4 %collective-permute-done.25.refs_2_ = bf16[512,2048]{1,0:T(8,128)(2,1)} collective-permute-done((bf16[512,2048]{1,0:T(8,128)(2,1)}, bf16[512,2048]{1,0:T(8,128)(2,1)}, u32[]{:S(2)}, u32[]{:S(2)}) %collective-permute-start.25) | collective-permute-done | bytes 2097184 | tf_op jit(solution)/shard_map/ppermute | solution.py:269
  433.8 16.9 %attend_back.1 = (bf16[1024,1536]{1,0:T(8,128)(2,1)}, f32[8,128]{1,0:T(8,128)}) custom-call(s32[1024]{0:T(1024)} %refs_0_.4, bf16[1024,512]{1,0:T(8,128)(2,1)} %get-tuple-element.249.refs_1_, bf16[1024,512]{1,0:T(8,128)(2,1)} %get-tuple-element.250.refs_2_, bf16[1024,512]{1,0:T(8,128)(2,1)} %get-tuple-element.251.refs_3_, bf16[1024,512]{1,0:T(8,128)(2,1)} %bitcast.26, ...), custom_call_target="tpu_custom_call" | custom-call | flops 22100000768 | bytes 17000000 | tf_op jit(solution)/shard_map/attend_back/pallas_call | solution.py:57
  474.6 15.5 %collective-permute-done.30.refs_2_ = bf16[512,1024]{1,0:T(8,128)(2,1)S(1)} collective-permute-done((bf16[512,1024]{1,0:T(8,128)(2,1)}, bf16[512,1024]{1,0:T(8,128)(2,1)S(1)}, u32[]{:S(2)}, u32[]{:S(2)}) %collective-permute-start.30) | collective-permute-done | bytes 1048608 | tf_op jit(solution)/shard_map/ppermute | solution.py:269
  500.9 11.1 %back_project.1 = (bf16[1024,2048]{1,0:T(8,128)(2,1)}, f32[8,128]{1,0:T(8,128)}) custom-call(bf16[1024,1536]{1,0:T(8,128)(2,1)} %get-tuple-element.339.refs_2_.refs_0_, bf16[2048,512]{1,0:T(8,128)(2,1)} %refs_1_.2, bf16[2048,512]{1,0:T(8,128)(2,1)} %refs_2_.15, bf16[2048,512]{1,0:T(8,128)(2,1)} %refs_3_.17, f32[8,128]{1,0:T(8,128)} %get-tuple-element.356.refs_4_), custom_call_target="tpu_custom_call" | custom-call | flops 14300000256 | bytes 11000000 | tf_op jit(solution)/shard_map/back_project/pallas_call | solution.py:57
  513.0 12.8 %keep.7 = (bf16[512,1024]{1,0:T(8,128)(2,1)}, bf16[512,1024]{1,0:T(8,128)(2,1)}, bf16[512,1024]{1,0:T(8,128)(2,1)}, bf16[512,1024]{1,0:T(8,128)(2,1)}, f32[8,128]{1,0:T(8,128)}) custom-call(s32[3]{0:T(128)} %pad_add_fusion.1.refs_0_, bf16[2048,1024]{1,0:T(8,128)(2,1)} %get-tuple-element.305.refs_1_, bf16[1024,1536]{1,0:T(8,128)(2,1)} %get-tuple-element.339.refs_2_.refs_0_, ...), custom_call_target="tpu_custom_call" | custom-call | flops 12999999488 | bytes 10000000 | tf_op jit(solution)/shard_map/keep/pallas_call | solution.py:57
  530.0 21.7 %collective-permute-done.35.refs_2_ = bf16[512,1024]{1,0:T(8,128)(2,1)S(1)} collective-permute-done((bf16[512,1024]{1,0:T(8,128)(2,1)}, bf16[512,1024]{1,0:T(8,128)(2,1)S(1)}, u32[]{:S(2)}, u32[]{:S(2)}) %collective-permute-start.35) | collective-permute-done | bytes 1048608 | tf_op jit(solution)/shard_map/ppermute | solution.py:269
  (332 shorter events, 342.7 us)
Async XLA Ops:
  7.2 90.9 %all-gather.6.cloned.1.call-start = ((), (), s32[]{:S(2)}) async-start(), calls=%async_computation.5 | async-start | bytes 1310720 | tf_op jit(solution)/shard_map/all_gather | solution.py:852
  11.4 37.7 %collective-permute-start = (bf16[256,2048]{1,0:T(8,128)(2,1)}, bf16[256,2048]{1,0:T(8,128)(2,1)S(1)}, u32[]{:S(2)}, u32[]{:S(2)}) collective-permute-start(bf16[256,2048]{1,0:T(8,128)(2,1)} %fusion.2.refs_1_), channel_id=1, source_target_pairs={{0,1},{1,2},{2,3},{4,5},{5,6},{6,7},{8,9},{9,10},{10,11},{12,13},{... | collective-permute-start | bytes 3145736 | tf_op jit(solution)/shard_map/ppermute | solution.py:119
  16.4 43.6 %collective-permute-start.1 = (bf16[256,2048]{1,0:T(8,128)(2,1)}, bf16[256,2048]{1,0:T(8,128)(2,1)}, u32[]{:S(2)}, u32[]{:S(2)}) collective-permute-start(bf16[256,2048]{1,0:T(8,128)(2,1)} %fusion.2.refs_1_), channel_id=1, source_target_pairs={{1,0},{2,1},{3,2},{5,4},{6,5},{7,6},{9,8},{10,9},{11,10},{13,12},{... | collective-permute-start | bytes 3145736 | tf_op jit(solution)/shard_map/ppermute | solution.py:120
  18.5 145.2 %all-gather.8.cloned.1.call-start = ((), (), s32[]{:S(2)}) async-start(), calls=%async_computation.9 | async-start | bytes 9437184 | tf_op jit(solution)/shard_map/all_gather | solution.py:877
  101.4 38.8 %collective-permute-start.6 = (bf16[256,2048]{1,0:T(8,128)(2,1)}, bf16[256,2048]{1,0:T(8,128)(2,1)S(1)}, u32[]{:S(2)}, u32[]{:S(2)}) collective-permute-start(bf16[256,2048]{1,0:T(8,128)(2,1)} %get-tuple-element.255), channel_id=1, source_target_pairs={{0,1},{1,2},{2,3},{4,5},{5,6},{6,7},{8,9},{9,10},{10,11},{12,13},{... | collective-permute-start | bytes 3145736 | tf_op jit(solution)/shard_map/ppermute | solution.py:119
  140.1 235.8 %reduce-scatter.4.cloned.1.call-start = ((), (), s32[]{:S(2)}) async-start(), calls=%async_computation.6 | async-start | bytes 5242880 | tf_op jit(solution)/shard_map/reduce_scatter | solution.py:900
  142.1 62.8 %collective-permute-start.12 = (bf16[256,2048]{1,0:T(8,128)(2,1)}, bf16[256,2048]{1,0:T(8,128)(2,1)S(1)}, u32[]{:S(2)}, u32[]{:S(2)}) collective-permute-start(bf16[256,2048]{1,0:T(8,128)(2,1)} %get-tuple-element.257), channel_id=1, source_target_pairs={{1,2},{2,3},{5,6},{6,7},{9,10},{10,11},{13,14},{14,15},{17,18},{18... | collective-permute-start | bytes 3145736 | tf_op jit(solution)/shard_map/ppermute | solution.py:119
  142.8 62.0 %collective-permute-start.13 = (bf16[256,2048]{1,0:T(8,128)(2,1)}, bf16[256,2048]{1,0:T(8,128)(2,1)}, u32[]{:S(2)}, u32[]{:S(2)}) collective-permute-start(bf16[256,2048]{1,0:T(8,128)(2,1)} %get-tuple-element.258), channel_id=1, source_target_pairs={{1,0},{2,1},{5,4},{6,5},{9,8},{10,9},{13,12},{14,13},{17,16},{18,1... | collective-permute-start | bytes 3145736 | tf_op jit(solution)/shard_map/ppermute | solution.py:120
  206.4 58.0 %collective-permute-start.16 = (bf16[256,2048]{1,0:T(8,128)(2,1)}, bf16[256,2048]{1,0:T(8,128)(2,1)S(1)}, u32[]{:S(2)}, u32[]{:S(2)}) collective-permute-start(bf16[256,2048]{1,0:T(8,128)(2,1)} %get-tuple-element.280), channel_id=1, source_target_pairs={{2,3},{6,7},{10,11},{14,15},{18,19},{22,23},{26,27},{30,31}} | collective-permute-start | bytes 3145736 | tf_op jit(solution)/shard_map/ppermute | solution.py:119
  207.2 57.3 %collective-permute-start.17 = (bf16[256,2048]{1,0:T(8,128)(2,1)}, bf16[256,2048]{1,0:T(8,128)(2,1)S(1)}, u32[]{:S(2)}, u32[]{:S(2)}) collective-permute-start(bf16[256,2048]{1,0:T(8,128)(2,1)} %get-tuple-element.281), channel_id=1, source_target_pairs={{1,0},{5,4},{9,8},{13,12},{17,16},{21,20},{25,24},{29,28}} | collective-permute-start | bytes 3145736 | tf_op jit(solution)/shard_map/ppermute | solution.py:120
  238.0 38.8 %collective-permute-start.15 = (bf16[256,2048]{1,0:T(8,128)(2,1)}, bf16[256,2048]{1,0:T(8,128)(2,1)S(1)}, u32[]{:S(2)}, u32[]{:S(2)}) collective-permute-start(bf16[256,2048]{1,0:T(8,128)(2,1)} %get-tuple-element.279), channel_id=1, source_target_pairs={{1,0},{5,4},{9,8},{13,12},{17,16},{21,20},{25,24},{29,28}} | collective-permute-start | bytes 3145736 | tf_op jit(solution)/shard_map/ppermute | solution.py:120
  352.6 60.8 %collective-permute-start.25 = (bf16[512,2048]{1,0:T(8,128)(2,1)}, bf16[512,2048]{1,0:T(8,128)(2,1)}, u32[]{:S(2)}, u32[]{:S(2)}) collective-permute-start(bf16[512,2048]{1,0:T(8,128)(2,1)} %get-tuple-element.333), channel_id=1, source_target_pairs={{0,8},{4,12},{8,0},{12,4},{16,24},{20,28},{24,16},{28,20},{1,9},{5... | collective-permute-start | bytes 6291464 | tf_op jit(solution)/shard_map/ppermute | solution.py:269
  364.9 48.9 %collective-permute-start.26 = (bf16[512,2048]{1,0:T(8,128)(2,1)}, bf16[512,2048]{1,0:T(8,128)(2,1)}, u32[]{:S(2)}, u32[]{:S(2)}) collective-permute-start(bf16[512,2048]{1,0:T(8,128)(2,1)} %get-tuple-element.335), channel_id=1, source_target_pairs={{0,16},{4,20},{8,24},{12,28},{16,0},{20,4},{24,8},{28,12},{1,17},{... | collective-permute-start | bytes 6291464 | tf_op jit(solution)/shard_map/ppermute | solution.py:269
  385.2 47.6 %all-to-all-start.1 = ((bf16[4,256,512]{2,1,0:T(8,128)(2,1)}), bf16[4,256,512]{2,1,0:T(8,128)(2,1)S(1)}, u32[]{:S(2)}, u32[]{:S(2)}) async-start(bf16[4,256,512]{2,1,0:T(8,128)(2,1)} %bitcast.27), calls=%async_computation.2 | async-start | bytes 2097152 | tf_op jit(solution)/shard_map/all_to_all | solution.py:141
  389.4 107.4 %all-gather.10.cloned.1.call-start = ((), (), s32[]{:S(2)}) async-start(), calls=%async_computation.10 | async-start | bytes 5242880 | tf_op jit(solution)/shard_map/all_gather | solution.py:918
  390.0 201.6 %reduce-scatter.8.cloned.1.call-start = ((), (), s32[]{:S(2)}) async-start(), calls=%async_computation.8 | async-start | bytes 5242880 | tf_op jit(solution)/shard_map/reduce_scatter | solution.py:931
  430.7 38.2 %collective-permute-start.32 = (bf16[256,2048]{1,0:T(8,128)(2,1)S(1)}, bf16[256,2048]{1,0:T(8,128)(2,1)}, u32[]{:S(2)}, u32[]{:S(2)}) collective-permute-start(bf16[256,2048]{1,0:T(8,128)(2,1)S(1)} %copy-done.47), channel_id=1, source_target_pairs={{0,16},{4,20},{8,24},{12,28},{16,0},{20,4},{24,8},{28,12},{1,17},{... | collective-permute-start | bytes 3145736 | tf_op jit(solution)/shard_map/ppermute | solution.py:269
  468.3 43.8 %collective-permute-start.29 = (bf16[1024,1536]{1,0:T(8,128)(2,1)}, bf16[1024,1536]{1,0:T(8,128)(2,1)}, u32[]{:S(2)}, u32[]{:S(2)}) collective-permute-start(bf16[1024,1536]{1,0:T(8,128)(2,1)} %get-tuple-element.345), channel_id=1, source_target_pairs={{0,4},{4,0},{8,12},{12,8},{16,20},{20,16},{24,28},{28,24},{1,5},{5... | collective-permute-start | bytes 9437192 | tf_op jit(solution)/shard_map/ppermute | solution.py:269
  473.3 54.8 %collective-permute-start.37 = (bf16[256,2048]{1,0:T(8,128)(2,1)}, bf16[256,2048]{1,0:T(8,128)(2,1)S(1)}, u32[]{:S(2)}, u32[]{:S(2)}) collective-permute-start(bf16[256,2048]{1,0:T(8,128)(2,1)} %get-tuple-element.362.refs_1_), channel_id=1, source_target_pairs={{0,16},{4,20},{8,24},{12,28},{16,0},{20,4},{24,8},{28,12},{1,17},{... | collective-permute-start | bytes 3145736 | tf_op jit(solution)/shard_map/ppermute | solution.py:269
  474.6 53.5 %collective-permute-start.38 = (bf16[256,2048]{1,0:T(8,128)(2,1)}, bf16[256,2048]{1,0:T(8,128)(2,1)S(1)}, u32[]{:S(2)}, u32[]{:S(2)}) collective-permute-start(bf16[256,2048]{1,0:T(8,128)(2,1)} %get-tuple-element.363.refs_3_), channel_id=1, source_target_pairs={{0,8},{4,12},{8,0},{12,4},{16,24},{20,28},{24,16},{28,20},{1,9},{5... | collective-permute-start | bytes 3145736 | tf_op jit(solution)/shard_map/ppermute | solution.py:269
  512.0 171.6 %reduce-scatter.6.cloned.1.call-start = ((), (), s32[]{:S(2)}) async-start(), calls=%async_computation.7 | async-start | bytes 5242880 | tf_op jit(solution)/shard_map/reduce_scatter | solution.py:942
  528.0 55.6 %collective-permute-start.39 = (bf16[1024,2048]{1,0:T(8,128)(2,1)}, bf16[1024,2048]{1,0:T(8,128)(2,1)S(1)}, u32[]{:S(2)}, u32[]{:S(2)}) collective-permute-start(bf16[1024,2048]{1,0:T(8,128)(2,1)} %get-tuple-element.370.refs_1_), channel_id=1, source_target_pairs={{0,4},{4,0},{8,12},{12,8},{16,20},{20,16},{24,28},{28,24},{1,5},{5... | collective-permute-start | bytes 12582920 | tf_op jit(solution)/shard_map/ppermute | solution.py:269
  565.3 53.2 %collective-permute-start.48 = (bf16[512,2048]{1,0:T(8,128)(2,1)}, bf16[512,2048]{1,0:T(8,128)(2,1)S(1)}, u32[]{:S(2)}, u32[]{:S(2)}) collective-permute-start(bf16[512,2048]{1,0:T(8,128)(2,1)} %get-tuple-element.397.refs_1_), channel_id=1, source_target_pairs={{0,8},{4,12},{8,0},{12,4},{16,24},{20,28},{24,16},{28,20},{1,9},{5... | collective-permute-start | bytes 6291464 | tf_op jit(solution)/shard_map/ppermute | solution.py:269
  566.2 52.3 %collective-permute-start.49 = (bf16[512,2048]{1,0:T(8,128)(2,1)}, bf16[512,2048]{1,0:T(8,128)(2,1)}, u32[]{:S(2)}, u32[]{:S(2)}) collective-permute-start(bf16[512,2048]{1,0:T(8,128)(2,1)} %get-tuple-element.396.refs_1_), channel_id=1, source_target_pairs={{0,16},{4,20},{8,24},{12,28},{16,0},{20,4},{24,8},{28,12},{1,17},{... | collective-permute-start | bytes 6291464 | tf_op jit(solution)/shard_map/ppermute | solution.py:269
  (102 other events, 1254.7 us)
Sparse Core Ops, SparseCore 0:
  18.6 41.8 all-gather.5
  98.9 55.6 all-gather.7
  303.2 72.6 reduce-scatter.3
  392.2 91.1 all-gather.9
  512.1 74.5 reduce-scatter.7
  609.6 73.9 reduce-scatter.5

commit v10 on v8

--- a/solution.py
+++ b/solution.py
@@ -962,7 +962,7 @@
     for _ in more:
         attn.spread(order)
     order.worth = 0.3
-    order.worth = 5
+    order.worth = 4
     gate_grad = wide.fill(order, 0, 0)
     up_grad = wide.fill(order, 1, 0)
     order.worth = 0.02

time: 712 us -> 712 us (level)
    unnamed x121 -> x123, local copies, waits for them, and re-layouts: 27.3 us -> 27.4 us
  transfers between devices with their start and end apart: 64 -> 64, of which waited for: 26 -> 23; matrix products, arithmetic and copies ran while one was open for 5% -> 5% of each run, Pallas kernels for 51% -> 51%
where the time goes in v10:
time: 712 us; the launch traced here: 701 us
  Pallas kernels  381 us (54%)
  waiting for transfers between devices  167 us (23%)
  starting transfers between devices  68.7 us (10%)
  other arithmetic  38.8 us (5%)
  local copies, waits for them, and re-layouts  30.4 us (4%)
  between operations  15.2 us (2%)
    pallas_call x65, Pallas kernels, run(): pl.pallas_call(whole, grid_spec=pltpu.PrefetchScalarGridSpec(num_scalar_p...  381 us
    ppermute x33, waiting for transfers between devices, swap(): return lax.ppermute(value, 'dp', xor_pairs(self.count, 1 << b))  78.1 us
    ppermute x9, waiting for transfers between devices, step(): lax.ppermute(down, 'tensor', [(i + 1, i) for i in range(0, size - k)])  44 us
    ppermute x33, starting transfers between devices, swap(): return lax.ppermute(value, 'dp', xor_pairs(self.count, 1 << b))  28.5 us
    unnamed x123, local copies, waits for them, and re-layouts  27.4 us
    select_n x9, other arithmetic, slot(): value = jnp.where(here, arr, value)  21.3 us
    ppermute x9, waiting for transfers between devices, step(): lax.ppermute(up, 'tensor', [(i, i + 1) for i in range(k - 1, size - 1)])  21 us
    ppermute x9, starting transfers between devices, step(): lax.ppermute(up, 'tensor', [(i, i + 1) for i in range(k - 1, size - 1)])  17.2 us
  transfers between devices with their start and end apart: 64, of which 23 were waited for; matrix products, arithmetic and copies ran while one was open for 5% of the time, Pallas kernels for 51%

profile of v10, /device:TPU:0, one launch (start us, length us, event | category | flops | bytes accessed | tf_op | source)
XLA Modules:
  0.0 700.8 jit_solution(7334254326885249154)
XLA Ops:
  28.1 21.0 %collective-permute-done.refs_0_ = bf16[256,2048]{1,0:T(8,128)(2,1)S(1)} collective-permute-done((bf16[256,2048]{1,0:T(8,128)(2,1)}, bf16[256,2048]{1,0:T(8,128)(2,1)S(1)}, u32[]{:S(2)}, u32[]{:S(2)}) %collective-permute-start) | collective-permute-done | bytes 1048608 | tf_op jit(solution)/shard_map/ppermute | solution.py:119
  49.1 10.9 %collective-permute-done.1.refs_1_ = bf16[256,2048]{1,0:T(8,128)(2,1)} collective-permute-done((bf16[256,2048]{1,0:T(8,128)(2,1)}, bf16[256,2048]{1,0:T(8,128)(2,1)}, u32[]{:S(2)}, u32[]{:S(2)}) %collective-permute-start.1) | collective-permute-done | bytes 1048608 | tf_op jit(solution)/shard_map/ppermute | solution.py:120
  70.6 14.9 %collective-permute-done.3.refs_1_ = bf16[256,2048]{1,0:T(8,128)(2,1)S(1)} collective-permute-done((bf16[256,2048]{1,0:T(8,128)(2,1)}, bf16[256,2048]{1,0:T(8,128)(2,1)S(1)}, u32[]{:S(2)}, u32[]{:S(2)}) %collective-permute-start.3) | collective-permute-done | bytes 1048608 | tf_op jit(solution)/shard_map/ppermute | solution.py:120
  108.3 8.6 %collective-permute-done.5 = bf16[256,2048]{1,0:T(8,128)(2,1)} collective-permute-done((bf16[256,2048]{1,0:T(8,128)(2,1)}, bf16[256,2048]{1,0:T(8,128)(2,1)}, u32[]{:S(2)}, u32[]{:S(2)}) %collective-permute-start.5) | collective-permute-done | bytes 1048608 | tf_op jit(solution)/shard_map/ppermute | solution.py:120
  124.9 13.7 %attend.1 = (bf16[1024,512]{1,0:T(8,128)(2,1)}, f32[8,128]{1,0:T(8,128)}) custom-call(s32[1024]{0:T(1024)} %refs_0_.4, bf16[1024,512]{1,0:T(8,128)(2,1)} %get-tuple-element.249.refs_1_, bf16[1024,512]{1,0:T(8,128)(2,1)} %get-tuple-element.250.refs_2_, bf16[1024,512]{1,0:T(8,128)(2,1)} %get-tuple-element.251.refs_3_, s32[1024,1]{1,0:T(8,128)} %copy.101.refs_4_.refs_5_, ...), custom_call_target="tpu_custom_call" | custom-call | flops 14300000256 | bytes 11000000 | tf_op jit(solution)/shard_map/attend/pallas_call | solution.py:57
  150.0 14.5 %all-to-all-done = bf16[4,256,512]{2,1,0:T(8,128)(2,1)} async-done(((bf16[4,256,512]{2,1,0:T(8,128)(2,1)}), bf16[4,256,512]{2,1,0:T(8,128)(2,1)}, u32[]{:S(2)}, u32[]{:S(2)}) %all-to-all-start) | async-done | bytes 1048608 | tf_op jit(solution)/shard_map/all_to_all | solution.py:141
  164.5 8.4 %project.1 = (f32[256,2048]{1,0:T(8,128)}, bf16[256,2048]{1,0:T(8,128)(2,1)}, f32[8,128]{1,0:T(8,128)}) custom-call(bf16[1024,512]{1,0:T(8,128)(2,1)} %bitcast.7.refs_0_, bf16[8,2048,256]{2,1,0:T(8,128)(2,1)} %bitcast.34, bf16[256,2048]{1,0:T(8,128)(2,1)} %refs_1_.3, f32[1,2048]{1,0:T(1,128)} %bitcast.38, f32[8,128]{1,0:T(8,128)} %get-tuple-element.260.refs_4_), custom_call_target="tpu_custom_call" | custom-call | flops 11180000256 | bytes 8600000 | tf_op jit(solution)/shard_map/project/pallas_call | solution.py:57
  175.6 22.2 %ffn.4 = (bf16[2048,1024]{1,0:T(8,128)(2,1)}, bf16[1024,2048]{1,0:T(8,128)(2,1)}, bf16[1024,2048]{1,0:T(8,128)(2,1)}, bf16[2048,1024]{1,0:T(8,128)(2,1)}, bf16[1...) custom-call(s32[1]{0:T(128)} %bitcast.1.refs_0_, ...), custom_call_target="tpu_custom_call" | custom-call | flops 28600000512 | bytes 22000000 | tf_op jit(solution)/shard_map/ffn/pallas_call | solution.py:57
  208.5 22.3 %ffn.5 = (bf16[2048,1024]{1,0:T(8,128)(2,1)}, bf16[1024,2048]{1,0:T(8,128)(2,1)}, bf16[1024,2048]{1,0:T(8,128)(2,1)}, bf16[2048,1024]{1,0:T(8,128)(2,1)}, bf16[1...) custom-call(s32[1]{0:T(128)} %bitcast.2.refs_0_, ...), custom_call_target="tpu_custom_call", output_to_operand_aliasing={{0}: (6, {}), {1}: (7, {}), {2}: (8, {}), {3}: (9, {}), {4}... | custom-call | flops 28600000512 | bytes 22000000 | tf_op jit(solution)/shard_map/ffn/pallas_call | solution.py:57
  242.1 22.3 %ffn.6 = (bf16[2048,1024]{1,0:T(8,128)(2,1)}, bf16[1024,2048]{1,0:T(8,128)(2,1)}, bf16[1024,2048]{1,0:T(8,128)(2,1)}, bf16[2048,1024]{1,0:T(8,128)(2,1)}, bf16[1...) custom-call(s32[1]{0:T(128)} %bitcast.3.refs_0_, ...), custom_call_target="tpu_custom_call", output_to_operand_aliasing={{0}: (6, {}), {1}: (7, {}), {2}: (8, {}), {3}: (9, {}), {4}... | custom-call | flops 28600000512 | bytes 22000000 | tf_op jit(solution)/shard_map/ffn/pallas_call | solution.py:57
  278.9 22.2 %ffn.7 = (bf16[2048,1024]{1,0:T(8,128)(2,1)}, bf16[1024,2048]{1,0:T(8,128)(2,1)}, bf16[1024,2048]{1,0:T(8,128)(2,1)}, bf16[2048,1024]{1,0:T(8,128)(2,1)}, bf16[1...) custom-call(s32[1]{0:T(128)} %bitcast.refs_0_, ...), custom_call_target="tpu_custom_call", output_to_operand_aliasing={{0}: (6, {}), {1}: (7, {}), {2}: (8, {}), {3}: (9, {}), {4}... | custom-call | flops 28600000512 | bytes 22000000 | tf_op jit(solution)/shard_map/ffn/pallas_call | solution.py:57
  301.4 8.6 %give.4 = (bf16[1024,2048]{1,0:T(8,128)(2,1)}, f32[8,128]{1,0:T(8,128)}) custom-call(s32[1]{0:T(128)} %bitcast.13.refs_0_, bf16[2048,1024]{1,0:T(8,128)(2,1)} %get-tuple-element.307.refs_1_, bf16[1024,2048]{1,0:T(8,128)(2,1)} %get-tuple-element.308.refs_2_, f32[8,128]{1,0:T(8,128)} %get-tuple-element.309.refs_3_), custom_call_target="tpu_custom_call" | custom-call | flops 10400000000 | bytes 8000000 | tf_op jit(solution)/shard_map/give/pallas_call | solution.py:57
  310.0 8.5 %give.5 = (bf16[1024,2048]{1,0:T(8,128)(2,1)}, f32[8,128]{1,0:T(8,128)}) custom-call(s32[1]{0:T(128)} %bitcast.13.refs_0_, bf16[2048,1024]{1,0:T(8,128)(2,1)} %get-tuple-element.311.refs_1_, bf16[1024,2048]{1,0:T(8,128)(2,1)} %get-tuple-element.313.refs_2_, f32[8,128]{1,0:T(8,128)} %get-tuple-element.314.refs_3_), custom_call_target="tpu_custom_call" | custom-call | flops 10400000000 | bytes 8000000 | tf_op jit(solution)/shard_map/give/pallas_call | solution.py:57
  319.0 8.5 %give.6 = (bf16[1024,2048]{1,0:T(8,128)(2,1)}, f32[8,128]{1,0:T(8,128)}) custom-call(s32[1]{0:T(128)} %bitcast.13.refs_0_, bf16[2048,1024]{1,0:T(8,128)(2,1)} %get-tuple-element.311.refs_1_, bf16[1024,2048]{1,0:T(8,128)(2,1)} %get-tuple-element.312.refs_2_, f32[8,128]{1,0:T(8,128)} %get-tuple-element.315.refs_3_), custom_call_target="tpu_custom_call" | custom-call | flops 10400000000 | bytes 8000000 | tf_op jit(solution)/shard_map/give/pallas_call | solution.py:57
  330.0 10.6 %keep.4 = (bf16[512,1024]{1,0:T(8,128)(2,1)}, bf16[512,1024]{1,0:T(8,128)(2,1)}, bf16[512,1024]{1,0:T(8,128)(2,1)}, bf16[512,1024]{1,0:T(8,128)(2,1)}, f32[8,128]{1,0:T(8,128)}) custom-call(s32[3]{0:T(128)} %pad_add_fusion.1.refs_0_, bf16[2048,1024]{1,0:T(8,128)(2,1)} %get-tuple-element.307.refs_1_, bf16[1024,2048]{1,0:T(8,128)(2,1)} %get-tuple-element.308.refs_2_, ...), custom_call_target="tpu_custom_call" | custom-call | flops 12999999488 | bytes 10000000 | tf_op jit(solution)/shard_map/keep/pallas_call | solution.py:57
  344.0 10.3 %keep.5 = (bf16[512,2048]{1,0:T(8,128)(2,1)}, bf16[512,2048]{1,0:T(8,128)(2,1)}, f32[8,128]{1,0:T(8,128)}) custom-call(s32[2]{0:T(128)} %pad_add_fusion.3.refs_0_, bf16[2048,1024]{1,0:T(8,128)(2,1)} %get-tuple-element.311.refs_1_, bf16[1024,2048]{1,0:T(8,128)(2,1)} %get-tuple-element.313.refs_2_, bf16[1024,2048]{1,0:T(8,128)(2,1)} %collective-permute-done.22.refs_3_, ...), custom_call_target="tpu_custom_call" | custom-call | flops 12999999488 | bytes 10000000 | tf_op jit(solution)/shard_map/keep/pallas_call | solution.py:57
  356.2 10.3 %keep.6 = (bf16[512,2048]{1,0:T(8,128)(2,1)}, bf16[512,2048]{1,0:T(8,128)(2,1)}, f32[8,128]{1,0:T(8,128)}) custom-call(s32[2]{0:T(128)} %pad_add_fusion.4.refs_0_, bf16[2048,1024]{1,0:T(8,128)(2,1)} %get-tuple-element.311.refs_1_, bf16[1024,2048]{1,0:T(8,128)(2,1)} %get-tuple-element.312.refs_2_, bf16[1024,2048]{1,0:T(8,128)(2,1)} %collective-permute-done.21.refs_3_, ...), custom_call_target="tpu_custom_call" | custom-call | flops 12999999488 | bytes 10000000 | tf_op jit(solution)/shard_map/keep/pallas_call | solution.py:57
  377.9 9.3 %middle.1 = (bf16[1024,512]{1,0:T(8,128)(2,1)}, f32[256,2048]{1,0:T(8,128)}, bf16[2048,256]{1,0:T(8,128)(2,1)}, f32[1,2048]{1,0:T(1,128)}, f32[8,128]{1,0:T(8,128)}) custom-call(bf16[256,2048]{1,0:T(8,128)(2,1)} %reduce-scatter.4.cloned.1.call-done.refs_0_, f32[256,2048]{1,0:T(8,128)} %get-tuple-element.261.refs_1_, bf16[256,2048]{1,0:T(8,128)(2,1)} %refs_2_.14, ...), custom_call_target="tpu_custom_call" | custom-call | flops 12350000128 | bytes 9500000 | tf_op jit(solution)/shard_map/middle/pallas_call | solution.py:57
  391.0 34.2 %collective-permute-done.23.refs_2_ = bf16[256,1024]{1,0:T(8,128)(2,1)S(1)} collective-permute-done((bf16[256,1024]{1,0:T(8,128)(2,1)}, bf16[256,1024]{1,0:T(8,128)(2,1)S(1)}, u32[]{:S(2)}, u32[]{:S(2)}) %collective-permute-start.23) | collective-permute-done | bytes 524320 | tf_op jit(solution)/shard_map/ppermute | solution.py:269
  431.9 7.2 %fold.8 = (bf16[256,2048]{1,0:T(8,128)(2,1)}, bf16[256,2048]{1,0:T(8,128)(2,1)}, bf16[256,2048]{1,0:T(8,128)(2,1)}, bf16[256,2048]{1,0:T(8,128)(2,1)}, f32[8,128]{1,0:T(8,128)}) custom-call(s32[2]{0:T(128)} %pad_add_fusion.refs_0_, bf16[512,2048]{1,0:T(8,128)(2,1)} %get-tuple-element.335.refs_1_, bf16[512,2048]{1,0:T(8,128)(2,1)} %collective-permute-done.27.refs_2_, ...), custom_call_target="tpu_custom_call" | custom-call | flops 5200000000 | bytes 4000000 | tf_op jit(solution)/shard_map/fold/pallas_call | solution.py:57
  452.7 21.3 %attend_back.1 = (bf16[1024,1536]{1,0:T(8,128)(2,1)}, f32[8,128]{1,0:T(8,128)}) custom-call(s32[1024]{0:T(1024)} %refs_0_.4, bf16[1024,512]{1,0:T(8,128)(2,1)} %get-tuple-element.249.refs_1_, bf16[1024,512]{1,0:T(8,128)(2,1)} %get-tuple-element.250.refs_2_, bf16[1024,512]{1,0:T(8,128)(2,1)} %get-tuple-element.251.refs_3_, bf16[1024,512]{1,0:T(8,128)(2,1)} %bitcast.27, ...), custom_call_target="tpu_custom_call" | custom-call | flops 22100000768 | bytes 17000000 | tf_op jit(solution)/shard_map/attend_back/pallas_call | solution.py:57
  499.5 11.1 %back_project.1 = (bf16[1024,2048]{1,0:T(8,128)(2,1)}, f32[8,128]{1,0:T(8,128)}) custom-call(bf16[1024,1536]{1,0:T(8,128)(2,1)} %get-tuple-element.342.refs_2_.refs_0_, bf16[2048,512]{1,0:T(8,128)(2,1)} %refs_1_.2, bf16[2048,512]{1,0:T(8,128)(2,1)} %refs_2_.15, bf16[2048,512]{1,0:T(8,128)(2,1)} %refs_3_.17, f32[8,128]{1,0:T(8,128)} %get-tuple-element.356.refs_4_), custom_call_target="tpu_custom_call" | custom-call | flops 14300000256 | bytes 11000000 | tf_op jit(solution)/shard_map/back_project/pallas_call | solution.py:57
  511.8 12.6 %keep.7 = (bf16[512,1024]{1,0:T(8,128)(2,1)}, bf16[512,1024]{1,0:T(8,128)(2,1)}, bf16[512,1024]{1,0:T(8,128)(2,1)}, bf16[512,1024]{1,0:T(8,128)(2,1)}, f32[8,128]{1,0:T(8,128)}) custom-call(s32[3]{0:T(128)} %pad_add_fusion.1.refs_0_, bf16[2048,1024]{1,0:T(8,128)(2,1)} %get-tuple-element.305.refs_1_, bf16[1024,1536]{1,0:T(8,128)(2,1)} %get-tuple-element.342.refs_2_.refs_0_, ...), custom_call_target="tpu_custom_call" | custom-call | flops 12999999488 | bytes 10000000 | tf_op jit(solution)/shard_map/keep/pallas_call | solution.py:57
  528.3 22.0 %collective-permute-done.35.refs_2_ = bf16[512,1024]{1,0:T(8,128)(2,1)S(1)} collective-permute-done((bf16[512,1024]{1,0:T(8,128)(2,1)}, bf16[512,1024]{1,0:T(8,128)(2,1)S(1)}, u32[]{:S(2)}, u32[]{:S(2)}) %collective-permute-start.35) | collective-permute-done | bytes 1048608 | tf_op jit(solution)/shard_map/ppermute | solution.py:269
  (330 shorter events, 330.2 us)
Async XLA Ops:
  7.2 90.9 %all-gather.6.cloned.1.call-start = ((), (), s32[]{:S(2)}) async-start(), calls=%async_computation.5 | async-start | bytes 1310720 | tf_op jit(solution)/shard_map/all_gather | solution.py:852
  16.4 43.6 %collective-permute-start.1 = (bf16[256,2048]{1,0:T(8,128)(2,1)}, bf16[256,2048]{1,0:T(8,128)(2,1)}, u32[]{:S(2)}, u32[]{:S(2)}) collective-permute-start(bf16[256,2048]{1,0:T(8,128)(2,1)} %fusion.2.refs_1_), channel_id=1, source_target_pairs={{1,0},{2,1},{3,2},{5,4},{6,5},{7,6},{9,8},{10,9},{11,10},{13,12},{... | collective-permute-start | bytes 3145736 | tf_op jit(solution)/shard_map/ppermute | solution.py:120
  18.5 146.1 %all-gather.8.cloned.1.call-start = ((), (), s32[]{:S(2)}) async-start(), calls=%async_computation.9 | async-start | bytes 9437184 | tf_op jit(solution)/shard_map/all_gather | solution.py:877
  101.4 41.5 %collective-permute-start.6 = (bf16[256,2048]{1,0:T(8,128)(2,1)}, bf16[256,2048]{1,0:T(8,128)(2,1)S(1)}, u32[]{:S(2)}, u32[]{:S(2)}) collective-permute-start(bf16[256,2048]{1,0:T(8,128)(2,1)} %get-tuple-element.255), channel_id=1, source_target_pairs={{0,1},{1,2},{2,3},{4,5},{5,6},{6,7},{8,9},{9,10},{10,11},{12,13},{... | collective-permute-start | bytes 3145736 | tf_op jit(solution)/shard_map/ppermute | solution.py:119
  142.9 235.0 %reduce-scatter.4.cloned.1.call-start = ((), (), s32[]{:S(2)}) async-start(), calls=%async_computation.6 | async-start | bytes 5242880 | tf_op jit(solution)/shard_map/reduce_scatter | solution.py:900
  144.9 60.0 %collective-permute-start.12 = (bf16[256,2048]{1,0:T(8,128)(2,1)}, bf16[256,2048]{1,0:T(8,128)(2,1)S(1)}, u32[]{:S(2)}, u32[]{:S(2)}) collective-permute-start(bf16[256,2048]{1,0:T(8,128)(2,1)} %get-tuple-element.257), channel_id=1, source_target_pairs={{1,2},{2,3},{5,6},{6,7},{9,10},{10,11},{13,14},{14,15},{17,18},{18... | collective-permute-start | bytes 3145736 | tf_op jit(solution)/shard_map/ppermute | solution.py:119
  145.6 59.3 %collective-permute-start.13 = (bf16[256,2048]{1,0:T(8,128)(2,1)}, bf16[256,2048]{1,0:T(8,128)(2,1)}, u32[]{:S(2)}, u32[]{:S(2)}) collective-permute-start(bf16[256,2048]{1,0:T(8,128)(2,1)} %get-tuple-element.258), channel_id=1, source_target_pairs={{1,0},{2,1},{5,4},{6,5},{9,8},{10,9},{13,12},{14,13},{17,16},{18,1... | collective-permute-start | bytes 3145736 | tf_op jit(solution)/shard_map/ppermute | solution.py:120
  206.4 58.0 %collective-permute-start.16 = (bf16[256,2048]{1,0:T(8,128)(2,1)}, bf16[256,2048]{1,0:T(8,128)(2,1)S(1)}, u32[]{:S(2)}, u32[]{:S(2)}) collective-permute-start(bf16[256,2048]{1,0:T(8,128)(2,1)} %get-tuple-element.280), channel_id=1, source_target_pairs={{2,3},{6,7},{10,11},{14,15},{18,19},{22,23},{26,27},{30,31}} | collective-permute-start | bytes 3145736 | tf_op jit(solution)/shard_map/ppermute | solution.py:119
  207.1 57.3 %collective-permute-start.17 = (bf16[256,2048]{1,0:T(8,128)(2,1)}, bf16[256,2048]{1,0:T(8,128)(2,1)S(1)}, u32[]{:S(2)}, u32[]{:S(2)}) collective-permute-start(bf16[256,2048]{1,0:T(8,128)(2,1)} %get-tuple-element.281), channel_id=1, source_target_pairs={{1,0},{5,4},{9,8},{13,12},{17,16},{21,20},{25,24},{29,28}} | collective-permute-start | bytes 3145736 | tf_op jit(solution)/shard_map/ppermute | solution.py:120
  301.2 194.2 %all-gather.10.cloned.1.call-start = ((), (), s32[]{:S(2)}) async-start(), calls=%async_computation.10 | async-start | bytes 5242880 | tf_op jit(solution)/shard_map/all_gather | solution.py:918
  354.2 77.6 %collective-permute-start.27 = (bf16[512,2048]{1,0:T(8,128)(2,1)}, bf16[512,2048]{1,0:T(8,128)(2,1)}, u32[]{:S(2)}, u32[]{:S(2)}) collective-permute-start(bf16[512,2048]{1,0:T(8,128)(2,1)} %get-tuple-element.336), channel_id=1, source_target_pairs={{0,8},{4,12},{8,0},{12,4},{16,24},{20,28},{24,16},{28,20},{1,9},{5... | collective-permute-start | bytes 6291464 | tf_op jit(solution)/shard_map/ppermute | solution.py:269
  366.6 65.3 %collective-permute-start.28 = (bf16[512,2048]{1,0:T(8,128)(2,1)}, bf16[512,2048]{1,0:T(8,128)(2,1)}, u32[]{:S(2)}, u32[]{:S(2)}) collective-permute-start(bf16[512,2048]{1,0:T(8,128)(2,1)} %get-tuple-element.338), channel_id=1, source_target_pairs={{0,16},{4,20},{8,24},{12,28},{16,0},{20,4},{24,8},{28,12},{1,17},{... | collective-permute-start | bytes 6291464 | tf_op jit(solution)/shard_map/ppermute | solution.py:269
  373.7 51.6 %collective-permute-start.23 = (bf16[256,1024]{1,0:T(8,128)(2,1)}, bf16[256,1024]{1,0:T(8,128)(2,1)S(1)}, u32[]{:S(2)}, u32[]{:S(2)}) collective-permute-start(bf16[256,1024]{1,0:T(8,128)(2,1)} %get-tuple-element.329), channel_id=1, source_target_pairs={{0,16},{4,20},{8,24},{12,28},{16,0},{20,4},{24,8},{28,12},{1,17},{... | collective-permute-start | bytes 1572872 | tf_op jit(solution)/shard_map/ppermute | solution.py:269
  376.2 49.1 %collective-permute-start.24 = (bf16[256,1024]{1,0:T(8,128)(2,1)}, bf16[256,1024]{1,0:T(8,128)(2,1)S(1)}, u32[]{:S(2)}, u32[]{:S(2)}) collective-permute-start(bf16[256,1024]{1,0:T(8,128)(2,1)} %get-tuple-element.331), channel_id=1, source_target_pairs={{0,8},{4,12},{8,0},{12,4},{16,24},{20,28},{24,16},{28,20},{1,9},{5... | collective-permute-start | bytes 1572872 | tf_op jit(solution)/shard_map/ppermute | solution.py:269
  387.2 64.5 %all-to-all-start.1 = ((bf16[4,256,512]{2,1,0:T(8,128)(2,1)}), bf16[4,256,512]{2,1,0:T(8,128)(2,1)S(1)}, u32[]{:S(2)}, u32[]{:S(2)}) async-start(bf16[4,256,512]{2,1,0:T(8,128)(2,1)} %bitcast.26), calls=%async_computation.2 | async-start | bytes 2097152 | tf_op jit(solution)/shard_map/all_to_all | solution.py:141
  390.8 199.1 %reduce-scatter.8.cloned.1.call-start = ((), (), s32[]{:S(2)}) async-start(), calls=%async_computation.8 | async-start | bytes 5242880 | tf_op jit(solution)/shard_map/reduce_scatter | solution.py:933
  439.1 42.5 %collective-permute-start.32 = (bf16[256,2048]{1,0:T(8,128)(2,1)}, bf16[256,2048]{1,0:T(8,128)(2,1)S(1)}, u32[]{:S(2)}, u32[]{:S(2)}) collective-permute-start(bf16[256,2048]{1,0:T(8,128)(2,1)} %get-tuple-element.349), channel_id=1, source_target_pairs={{0,16},{4,20},{8,24},{12,28},{16,0},{20,4},{24,8},{28,12},{1,17},{... | collective-permute-start | bytes 3145736 | tf_op jit(solution)/shard_map/ppermute | solution.py:269
  439.3 42.3 %collective-permute-start.33 = (bf16[256,2048]{1,0:T(8,128)(2,1)}, bf16[256,2048]{1,0:T(8,128)(2,1)}, u32[]{:S(2)}, u32[]{:S(2)}) collective-permute-start(bf16[256,2048]{1,0:T(8,128)(2,1)} %get-tuple-element.351), channel_id=1, source_target_pairs={{0,8},{4,12},{8,0},{12,4},{16,24},{20,28},{24,16},{28,20},{1,9},{5... | collective-permute-start | bytes 3145736 | tf_op jit(solution)/shard_map/ppermute | solution.py:269
  449.6 39.4 %collective-permute-start.30 = (bf16[512,1024]{1,0:T(8,128)(2,1)}, bf16[512,1024]{1,0:T(8,128)(2,1)S(1)}, u32[]{:S(2)}, u32[]{:S(2)}) collective-permute-start(bf16[512,1024]{1,0:T(8,128)(2,1)} %get-tuple-element.346.refs_1_), channel_id=1, source_target_pairs={{0,8},{4,12},{8,0},{12,4},{16,24},{20,28},{24,16},{28,20},{1,9},{5... | collective-permute-start | bytes 3145736 | tf_op jit(solution)/shard_map/ppermute | solution.py:269
  487.0 39.3 %collective-permute-start.38 = (bf16[256,2048]{1,0:T(8,128)(2,1)}, bf16[256,2048]{1,0:T(8,128)(2,1)S(1)}, u32[]{:S(2)}, u32[]{:S(2)}) collective-permute-start(bf16[256,2048]{1,0:T(8,128)(2,1)} %get-tuple-element.363.refs_3_), channel_id=1, source_target_pairs={{0,8},{4,12},{8,0},{12,4},{16,24},{20,28},{24,16},{28,20},{1,9},{5... | collective-permute-start | bytes 3145736 | tf_op jit(solution)/shard_map/ppermute | solution.py:269
  510.5 171.3 %reduce-scatter.6.cloned.1.call-start = ((), (), s32[]{:S(2)}) async-start(), calls=%async_computation.7 | async-start | bytes 5242880 | tf_op jit(solution)/shard_map/reduce_scatter | solution.py:944
  526.3 55.6 %collective-permute-start.39 = (bf16[1024,2048]{1,0:T(8,128)(2,1)}, bf16[1024,2048]{1,0:T(8,128)(2,1)S(1)}, u32[]{:S(2)}, u32[]{:S(2)}) collective-permute-start(bf16[1024,2048]{1,0:T(8,128)(2,1)} %get-tuple-element.370.refs_1_), channel_id=1, source_target_pairs={{0,4},{4,0},{8,12},{12,8},{16,20},{20,16},{24,28},{28,24},{1,5},{5... | collective-permute-start | bytes 12582920 | tf_op jit(solution)/shard_map/ppermute | solution.py:269
  563.6 53.2 %collective-permute-start.48 = (bf16[512,2048]{1,0:T(8,128)(2,1)}, bf16[512,2048]{1,0:T(8,128)(2,1)S(1)}, u32[]{:S(2)}, u32[]{:S(2)}) collective-permute-start(bf16[512,2048]{1,0:T(8,128)(2,1)} %get-tuple-element.397.refs_1_), channel_id=1, source_target_pairs={{0,8},{4,12},{8,0},{12,4},{16,24},{20,28},{24,16},{28,20},{1,9},{5... | collective-permute-start | bytes 6291464 | tf_op jit(solution)/shard_map/ppermute | solution.py:269
  564.4 52.3 %collective-permute-start.49 = (bf16[512,2048]{1,0:T(8,128)(2,1)}, bf16[512,2048]{1,0:T(8,128)(2,1)}, u32[]{:S(2)}, u32[]{:S(2)}) collective-permute-start(bf16[512,2048]{1,0:T(8,128)(2,1)} %get-tuple-element.396.refs_1_), channel_id=1, source_target_pairs={{0,16},{4,20},{8,24},{12,28},{16,0},{20,4},{24,8},{28,12},{1,17},{... | collective-permute-start | bytes 6291464 | tf_op jit(solution)/shard_map/ppermute | solution.py:269
  (101 other events, 1223.9 us)
Sparse Core Ops, SparseCore 0:
  18.6 41.8 all-gather.5
  98.9 55.6 all-gather.7
  301.3 75.9 reduce-scatter.3
  387.3 97.3 all-gather.9
  510.7 74.0 reduce-scatter.7
  595.7 75.6 reduce-scatter.5
